TPU v7x, 128 devices: a whole 4x4x4 slice. The times are simulated.
128 devices in a mesh: gx: 8 (over y, core), gy: 16 (over x, z).
Axes of the slice: x: 4, y: 4, z: 4, core: 2. Of those that a mesh axis runs over, the one named last changes fastest.
Arguments:
- level_set: float32 [256, 512, 256], P('gx', 'gy'), may hold values from -16 to 16, as said below
- velocity: bfloat16 [3, 256, 512, 256], P(None, 'gx', 'gy'), may hold values from -2 to 2
- stress_field: float32 [6, 256, 512, 256], P(None, 'gx', 'gy'), may hold values from -6 to 6
- band_tiles: int32 [8, 16, 32], P('gx', 'gy'), may hold values from 0 to 63, as said below
Outputs:
- new_level: float32 [256, 512, 256], P('gx', 'gy')
- new_stress: float32 [6, 256, 512, 256], P(None, 'gx', 'gy')
Inputs may be any that keep to these rules, and one draw needn't show every extreme that they name: `level_set`: A jet-like level set clipped to 8 cells, times a cell-wise positive factor up to 2. `band_tiles`: A device lists 1 to 32 distinct tiles; the slots after its last tile repeat its first entry.
All inputs are finite; a program needn't handle non-finite values.
Results may differ from a plain program's by a relative error of at most 0.0003.
Values sent between devices are 32-bit elements; how exact they have to be, the bound alone decides.
No kernel may reach another device: no remote copies, remote signals or barrier semaphores. Data moves between devices by JAX's collectives and lax.ppermute only.
A program may use at most 192 MiB of HBM per device.

v0:
```python
import functools

import jax
import jax.numpy as jnp
from jax import lax
from jax.experimental import pallas as pl
from jax.experimental.pallas import tpu as pltpu
from jax.sharding import PartitionSpec as P

TILE = 16
SWEEPS = 5
EPSILON = 1e-06
TIME_STEP = 0.4
PSEUDO_STEP = 0.3

CX = 32
CY = 32
LANES = 128
DEEP = 7
ROWS = 64
OWN = 16
UNIT = 16
COMPS = 6
F32 = jnp.float32
LIMIT = 60 * 1024 * 1024
ANY = pl.BlockSpec(memory_space=pl.ANY)
VMEM = pl.BlockSpec(memory_space=pltpu.VMEM)
SMEM = pl.BlockSpec(memory_space=pltpu.SMEM)


def half(h):
    return pl.ds(h * LANES, LANES)


def recip(x):
    return pl.reciprocal(x, approx=True)


def lane_shift(pair, k):
    lane = lax.broadcasted_iota(jnp.int32, pair[0].shape, pair[0].ndim - 1)
    turned = [pltpu.roll(p, (-k) % LANES, p.ndim - 1) for p in pair]
    edge = lane >= LANES - k if k > 0 else lane < -k
    return [jnp.where(edge, turned[1 - h], turned[h]) for h in range(2)]


def weno(d, positive):
    v = [jnp.where(positive, d[k], d[5 - k]) for k in range(5)]
    d1, d2, d3, d4 = (v[k + 1] - v[k] for k in range(4))
    u1, u2, u3 = d2 - d1, d3 - d2, d4 - d3
    g1 = d2 + d2 + u1
    g2 = d2 + d3
    g3 = u3 - (d3 + d3)
    scale = 13.0 / 3.0
    a1 = recip(4.0 * EPSILON + (scale * u1 * u1 + g1 * g1))
    a2 = recip(4.0 * EPSILON + (scale * u2 * u2 + g2 * g2))
    a3 = recip(4.0 * EPSILON + (scale * u3 * u3 + g3 * g3))
    a1 = a1 * a1
    a2 = 6.0 * (a2 * a2)
    a3 = 3.0 * (a3 * a3)
    top = a1 * (u1 - u2) + 0.5 * (a3 * (u2 - u3))
    mid = v[2] + (d3 + d3 + d2) * (1.0 / 6.0)
    return mid + top * (recip(a1 + a2 + a3) * (1.0 / 3.0))


def band_table(tiles_ref):
    shape = (8, LANES)
    row = lax.broadcasted_iota(jnp.int32, shape, 0)
    lane = lax.broadcasted_iota(jnp.int32, shape, 1)
    numbers = (row // 2) * 16 + (row % 2) * 8 + lane // TILE
    flags = jnp.zeros(shape, F32)
    for slot in range(tiles_ref.shape[-1]):
        flags = jnp.where(numbers == tiles_ref[0, 0, slot], 1.0, flags)
    return flags


def advect_kernel(
    tiles, level, xlo, xhi, ylo, yhi, speed,
    adv, to_xp, to_xn, to_yp, to_yn, c_pp, c_pn, c_np, c_nn,
    pad, table, sems,
):
    copies = []
    for h in range(2):
        for n, (src, at, size) in enumerate(((level, 3, CX), (xlo, 0, 3), (xhi, CX + 3, 3))):
            copies.append(
                pltpu.make_async_copy(
                    src.at[:, :, half(h)], pad.at[pl.ds(at, size), h, pl.ds(8, CY), :], sems.at[h, n]
                )
            )
    for copy in copies:
        copy.start()
    table[...] = band_table(tiles)
    for copy in copies:
        copy.wait()
    for h in range(2):
        pad[3 : CX + 3, h, 5:8, :] = ylo[:, :, half(h)]
        pad[3 : CX + 3, h, 8 + CY : 11 + CY, :] = yhi[:, :, half(h)]

    def plane(x, carry):
        for unit in range(CY // UNIT):
            at = 8 + unit * UNIT
            rows = pl.ds(unit * UNIT, UNIT)
            center = [pad[x + 3, h, pl.ds(at, UNIT), :] for h in range(2)]
            ups = [lane_shift(center, k) for k in (1, 2, 3)]
            downs = [lane_shift(center, -k) for k in (3, 2, 1)]
            for h in range(2):
                v = [speed[d, x, rows, half(h)].astype(F32) for d in range(3)]
                lx = [pad[x + 3 + k, h, pl.ds(at, UNIT), :] for k in range(-3, 4)]
                ly = [pad[x + 3, h, pl.ds(at + k, UNIT), :] for k in range(-3, 4)]
                lz = [s[h] for s in downs] + [center[h]] + [s[h] for s in ups]
                drift = None
                for vd, line in zip(v, (lx, ly, lz)):
                    steps = [line[k + 1] - line[k] for k in range(6)]
                    term = vd * weno(steps, vd > 0)
                    drift = term if drift is None else drift + term
                adv[x, rows, half(h)] = center[h] - TIME_STEP * drift
        return carry

    lax.fori_loop(0, CX, plane, 0)
    low, high = CX - DEEP, CX
    to_xp[0:DEEP] = adv[0:DEEP]
    to_xn[0:DEEP] = adv[low:high]
    row8 = lax.broadcasted_iota(jnp.int32, (8, LANES), 0)
    for h in range(2):
        for j in range(2):
            rows = pl.ds(j * TILE, TILE)
            for i, face in ((0, to_xp), (1, to_xn)):
                r = i * 4 + j * 2 + h
                face[DEEP, rows, half(h)] = jnp.broadcast_to(table[r : r + 1, :], (TILE, LANES))
        for i in range(2):
            first = table[i * 4 + h : i * 4 + h + 1, :]
            last = table[i * 4 + 2 + h : i * 4 + 3 + h, :]
            for x in range(i * TILE, i * TILE + TILE):
                to_yp[x, :, half(h)] = jnp.where(row8 == 7, first, adv[x, 0:8, half(h)])
                to_yn[x, :, half(h)] = jnp.where(row8 == 0, last, adv[x, CY - 8 : CY, half(h)])
    c_pp[...] = to_yp[0:DEEP]
    c_pn[...] = to_yn[0:DEEP]
    c_np[...] = to_yp[low:high]
    c_nn[...] = to_yn[low:high]


def advect(tiles, level, xlo, xhi, ylo, yhi, speed):
    shape = lambda *s: jax.ShapeDtypeStruct(s, F32)
    z = 2 * LANES
    return pl.pallas_call(
        advect_kernel,
        out_shape=[shape(CX, CY, z)]
        + [shape(8, CY, z)] * 2
        + [shape(CX, 8, z)] * 2
        + [shape(DEEP, 8, z)] * 4,
        in_specs=[SMEM, ANY, ANY, ANY, VMEM, VMEM, VMEM],
        out_specs=[VMEM] * 9,
        scratch_shapes=[
            pltpu.VMEM((CX + 6, 2, 48, LANES), F32),
            pltpu.VMEM((8, LANES), F32),
            pltpu.SemaphoreType.DMA((2, 3)),
        ],
        compiler_params=pltpu.CompilerParams(vmem_limit_bytes=LIMIT),
        name="advect",
    )(tiles, level, xlo, xhi, ylo, yhi, speed)


WIDE = CX + 2 * DEEP


def sweep_kernel(
    tiles, adv, xlo, xhi, ylo, yhi, c_ll, c_lh, c_hl, c_hh,
    cur_out, weight_out, part,
    first, second, factor, masks, table, sums, sems,
):
    copies = []
    for h in range(2):
        pieces = (
            (adv, DEEP, CX, OWN, CY),
            (xlo.at[pl.ds(0, DEEP)], 0, DEEP, OWN, CY),
            (xhi.at[pl.ds(0, DEEP)], DEEP + CX, DEEP, OWN, CY),
            (ylo, DEEP, CX, OWN - 8, 8),
            (yhi, DEEP, CX, OWN + CY, 8),
            (c_ll, 0, DEEP, OWN - 8, 8),
            (c_lh, 0, DEEP, OWN + CY, 8),
            (c_hl, DEEP + CX, DEEP, OWN - 8, 8),
            (c_hh, DEEP + CX, DEEP, OWN + CY, 8),
        )
        for n, (src, x, nx, y, ny) in enumerate(pieces):
            copies.append(
                pltpu.make_async_copy(
                    src.at[:, :, half(h)],
                    first.at[pl.ds(x, nx), h, pl.ds(y, ny), :],
                    sems.at[h, n],
                )
            )
        for n, src in enumerate((xlo, xhi)):
            copies.append(
                pltpu.make_async_copy(
                    src.at[pl.ds(DEEP, 1), :, half(h)], masks.at[pl.ds(n, 1), h], sems.at[h, 9 + n]
                )
            )
    for copy in copies:
        copy.start()
    table[...] = band_table(tiles)
    sums[...] = jnp.zeros(sums.shape, F32)
    for copy in copies:
        copy.wait()

    def prepare(x, bands):
        for h in range(2):
            for group in range(-1, 5):
                rows = pl.ds(OWN + 8 * group, 8)
                value = first[x, h, rows, :]
                if group == -1:
                    band = jnp.broadcast_to(value[0:1], value.shape)
                elif group == 4:
                    band = jnp.broadcast_to(value[7:8], value.shape)
                else:
                    band = bands(group, h)
                square = value * value
                weight = band * recip(1.0 + square * (1.0 / 36.0))
                sign = value * lax.rsqrt(square + 1.0)
                factor[x, h, rows, :] = PSEUDO_STEP * sign * weight
                weight_out[x, h, rows, :] = weight

    def halo_bands(n):
        return lambda group, h: masks[n, h, pl.ds(8 * group, 8), :]

    def own_bands(i):
        def bands(group, h):
            r = i * 4 + (group // 2) * 2 + h
            return jnp.broadcast_to(table[r : r + 1, :], (8, LANES))

        return bands

    def run(start, stop, bands):
        def body(x, carry):
            prepare(x, bands)
            return carry

        lax.fori_loop(start, stop, body, 0)

    run(0, DEEP, halo_bands(0))
    run(DEEP, DEEP + TILE, own_bands(0))
    run(DEEP + TILE, DEEP + CX, own_bands(1))
    run(DEEP + CX, WIDE, halo_bands(1))

    def sweep_plane(src, x):
        for unit in range(3):
            at = OWN - 8 + unit * UNIT
            rows = pl.ds(at, UNIT)
            center = [src[x, h, rows, :] for h in range(2)]
            up, down = lane_shift(center, 1), lane_shift(center, -1)
            for h in range(2):
                c = center[h]
                step = factor[x, h, rows, :]
                positive = step > 0
                pairs = (
                    (src[x - 1, h, rows, :], src[x + 1, h, rows, :]),
                    (src[x, h, pl.ds(at - 1, UNIT), :], src[x, h, pl.ds(at + 1, UNIT), :]),
                    (down[h], up[h]),
                )
                total = None
                for l, r in pairs:
                    low = jnp.minimum(jnp.minimum(l, r), c)
                    high = jnp.maximum(jnp.maximum(l, r), c)
                    diff = c - jnp.where(positive, low, high)
                    total = diff * diff if total is None else total + diff * diff
                yield unit, h, c - step * (jnp.sqrt(total) - 1.0)

    source, target = first, second
    for sweep in range(1, SWEEPS):

        def body(x, carry, source=source, target=target):
            for unit, h, value in sweep_plane(source, x):
                target[x, h, pl.ds(OWN - 8 + unit * UNIT, UNIT), :] = value
            return carry

        lax.fori_loop(sweep, WIDE - sweep, body, 0)
        source, target = target, source

    shift = SWEEPS

    def last(x, carry):
        for unit, h, value in sweep_plane(source, x):
            cur_out[x - shift, h, pl.ds(OWN - 8 + unit * UNIT, UNIT), :] = value
        return carry

    lax.fori_loop(shift, WIDE - shift, last, 0)

    def count(x, carry):
        for h in range(2):
            for unit in range(CY // UNIT):
                rows = pl.ds(OWN + unit * UNIT, UNIT)
                after = jnp.tanh(cur_out[x + 2, h, rows, :])
                before = jnp.tanh(adv[x, pl.ds(unit * UNIT, UNIT), half(h)])
                sums[0] += after - before
                sums[1] += 1.0 - after * after
        return carry

    lax.fori_loop(0, CX, count, 0)
    lane = lax.broadcasted_iota(jnp.int32, (1, LANES), 1)
    part[...] = jnp.where(lane < 64, jnp.sum(sums[0]), jnp.sum(sums[1]))


def sweeps(tiles, adv, halos):
    shape = lambda *s: jax.ShapeDtypeStruct(s, F32)
    return pl.pallas_call(
        sweep_kernel,
        out_shape=[shape(CX + 4, 2, ROWS, LANES), shape(WIDE, 2, ROWS, LANES), shape(1, LANES)],
        in_specs=[SMEM, VMEM] + [ANY] * 8,
        out_specs=[VMEM] * 3,
        scratch_shapes=[
            pltpu.VMEM((WIDE, 2, ROWS, LANES), F32),
            pltpu.VMEM((WIDE, 2, ROWS, LANES), F32),
            pltpu.VMEM((WIDE, 2, ROWS, LANES), F32),
            pltpu.VMEM((2, 2, CY, LANES), F32),
            pltpu.VMEM((8, LANES), F32),
            pltpu.VMEM((2, UNIT, LANES), F32),
            pltpu.SemaphoreType.DMA((2, 11)),
        ],
        compiler_params=pltpu.CompilerParams(vmem_limit_bytes=LIMIT),
        name="sweeps",
    )(tiles, adv, *halos)


def extend_kernel(
    parts, cur, weight, stress, xlo, xhi, ylo, yhi,
    level_out, stress_out,
    pad, ring, mix, sems,
):
    copies = []
    for h in range(2):
        for n, (src, at, size) in enumerate(((stress, 2, CX), (xlo, 0, 2), (xhi, CX + 2, 2))):
            copies.append(
                pltpu.make_async_copy(
                    src.at[:, :, :, half(h)],
                    pad.at[:, pl.ds(at, size), h, pl.ds(OWN, CY), :],
                    sems.at[h, n],
                )
            )
    for copy in copies:
        copy.start()
    sums = jnp.sum(parts[...], axis=0, keepdims=True)
    shift = sums[:, 0:1] / sums[:, 64:65]
    for copy in copies:
        copy.wait()
    for h in range(2):
        for c in range(COMPS):
            pad[c, :, h, OWN - 2 : OWN, :] = ylo[c, :, :, half(h)]
            pad[c, :, h, OWN + CY : OWN + CY + 2, :] = yhi[c, :, :, half(h)]

    def neighbours(load, at):
        center = [load(0, h, at) for h in range(2)]
        up, down = lane_shift(center, 1), lane_shift(center, -1)
        return center, [
            [
                load(-1, h, at), load(1, h, at), load(0, h, at - 1), load(0, h, at + 1),
                down[h], up[h],
            ]
            for h in range(2)
        ]

    def first_step(i, slot):
        for unit in range(3):
            at = OWN - 8 + unit * UNIT
            rows = pl.ds(at, UNIT)
            center, around = neighbours(lambda dx, h, r: cur[i + 1 + dx, h, pl.ds(r, UNIT), :], at)
            mixes = []
            for h in range(2):
                c = center[h]
                w = [
                    recip(1.0 + jnp.exp(jnp.minimum(2.0 * (n - c), 87.0)))
                    for n in around[h]
                ]
                total = w[0] + w[1] + w[2] + w[3] + w[4] + w[5]
                gate = weight[i + DEEP - 1, h, rows, :] * 0.5 * (1.0 + jnp.tanh(2.0 * (c - shift)))
                scaled = gate * recip(total)
                w = [scaled * n for n in w] + [1.0 - gate]
                mixes.append(w)
                for n in range(7):
                    mix[slot % 2, n, h, rows, :] = w[n]
            for comp in range(COMPS):
                center, around = neighbours(
                    lambda dx, h, r: pad[comp, i + 1 + dx, h, pl.ds(r, UNIT), :], at
                )
                for h in range(2):
                    value = mixes[h][6] * center[h]
                    for n in range(6):
                        value = value + mixes[h][n] * around[h][n]
                    ring[slot, comp, h, rows, :] = value

    def second_step(x, slot):
        slots = {dx: (slot + dx) % 4 for dx in (-1, 0, 1)}
        for unit in range(CY // UNIT):
            at = OWN + unit * UNIT
            rows = pl.ds(at, UNIT)
            own = pl.ds(unit * UNIT, UNIT)
            mixes = [[mix[slot % 2, n, h, rows, :] for n in range(7)] for h in range(2)]
            for comp in range(COMPS):
                center, around = neighbours(
                    lambda dx, h, r: ring[slots[dx], comp, h, pl.ds(r, UNIT), :], at
                )
                for h in range(2):
                    value = mixes[h][6] * center[h]
                    for n in range(6):
                        value = value + mixes[h][n] * around[h][n]
                    stress_out[comp, x, own, half(h)] = value
            for h in range(2):
                level_out[x, own, half(h)] = cur[x + 2, h, rows, :] - shift

    def body(group, carry):
        for k in range(4):
            i = group * 4 + k
            first_step(i, k)

            @pl.when(i >= 2)
            def _():
                second_step(i - 2, (k + 3) % 4)

        return carry

    lax.fori_loop(0, 8, body, 0)
    for i in (32, 33):
        first_step(i, i % 4)
        second_step(i - 2, (i + 3) % 4)


def extend(parts, cur, weight, stress, halos):
    shape = lambda *s: jax.ShapeDtypeStruct(s, F32)
    z = 2 * LANES
    return pl.pallas_call(
        extend_kernel,
        out_shape=[shape(CX, CY, z), shape(COMPS, CX, CY, z)],
        in_specs=[VMEM, VMEM, VMEM, ANY, ANY, ANY, VMEM, VMEM],
        out_specs=[VMEM] * 2,
        scratch_shapes=[
            pltpu.VMEM((COMPS, CX + 4, 2, ROWS, LANES), F32),
            pltpu.VMEM((4, COMPS, 2, ROWS, LANES), F32),
            pltpu.VMEM((2, 7, 2, ROWS, LANES), F32),
            pltpu.SemaphoreType.DMA((2, 3)),
        ],
        compiler_params=pltpu.CompilerParams(vmem_limit_bytes=LIMIT),
        name="extend",
    )(parts, cur, weight, stress, *halos)


def on_device(level, velocity, stress, tiles):
    nx, ny = lax.axis_size("gx"), lax.axis_size("gy")

    def send(value, dx, dy):
        if dy == 0:
            return lax.ppermute(value, "gx", [(i, (i + dx) % nx) for i in range(nx)])
        if dx == 0:
            return lax.ppermute(value, "gy", [(i, (i + dy) % ny) for i in range(ny)])
        pairs = [
            (i * ny + j, (i + dx) % nx * ny + (j + dy) % ny) for i in range(nx) for j in range(ny)
        ]
        return lax.ppermute(value, ("gx", "gy"), pairs)

    xlo = send(level[-3:], 1, 0)
    xhi = send(level[:3], -1, 0)
    ylo = send(level[:, -3:], 0, 1)
    yhi = send(level[:, :3], 0, -1)
    adv, to_xp, to_xn, to_yp, to_yn, c_pp, c_pn, c_np, c_nn = advect(
        tiles, level, xlo, xhi, ylo, yhi, velocity
    )
    halos = (
        send(to_xn, 1, 0),
        send(to_xp, -1, 0),
        send(to_yn, 0, 1),
        send(to_yp, 0, -1),
        send(c_nn, 1, 1),
        send(c_np, 1, -1),
        send(c_pn, -1, 1),
        send(c_pp, -1, -1),
    )
    cur, weight, part = sweeps(tiles, adv, halos)
    sxlo = send(stress[:, -2:], 1, 0)
    sxhi = send(stress[:, :2], -1, 0)
    edge = lambda s: jnp.concatenate((sxlo[:, :, s], stress[:, :, s], sxhi[:, :, s]), axis=1)
    sylo = send(edge(slice(-2, None)), 0, 1)
    syhi = send(edge(slice(0, 2)), 0, -1)
    parts = lax.all_gather(part, ("gx", "gy"), axis=0, tiled=True)
    return extend(parts, cur, weight, stress, (sxlo, sxhi, sylo, syhi))


def solution(mesh):
    in_specs = (
        P("gx", "gy", None),
        P(None, "gx", "gy", None),
        P(None, "gx", "gy", None),
        P("gx", "gy", None),
    )
    out_specs = (P("gx", "gy", None), P(None, "gx", "gy", None))
    return jax.shard_map(
        on_device, mesh=mesh, in_specs=in_specs, out_specs=out_specs, check_vma=False
    )
```

profile of v0, /device:TPU:0, one launch (start us, length us, event | category | flops | bytes accessed | tf_op | source)
XLA Modules:
  0.0 182.4 jit_solution(695338303251545649)
XLA Ops:
  0.6 1.0 fusion.3
  1.6 2.5 %collective-permute-start.1 = (f32[3,32,256]{2,1,0:T(8,128)S(1)}, f32[3,32,256]{2,1,0:T(8,128)S(1)}, u32[]{:S(2)}, u32[]{:S(2)}) collective-permute-start(f32[3,32,256]{2,1,0:T(8,128)S(1)} %get-tuple-element.32), channel_id=1, source_target_pairs={{0,112},{16,0},{32,16},{48,32},{64,48},{80,64},{96,80},{112,96},{1... | collective-permute-start | bytes 294920 | tf_op jit(solution)/shard_map/ppermute | solution.py:448
  4.1 0.0 collective-permute-start
  4.1 1.2 fusion.1
  5.3 3.0 %collective-permute-start.13 = (f32[6,2,32,256]{3,2,1,0:T(8,128)S(1)}, f32[6,2,32,256]{3,2,1,0:T(8,128)S(1)}, u32[]{:S(2)}, u32[]{:S(2)}) collective-permute-start(f32[6,2,32,256]{3,2,1,0:T(8,128)S(1)} %get-tuple-element.28), channel_id=1, source_target_pairs={{0,112},{16,0},{32,16},{48,32},{64,48},{80,64},{96,80},{112,96},{1... | collective-permute-start | bytes 1179656 | tf_op jit(solution)/shard_map/ppermute | solution.py:448
  8.3 1.1 fusion.2
  9.4 6.3 %collective-permute-start.3 = (f32[32,3,256]{2,1,0:T(4,128)S(1)}, f32[32,3,256]{2,1,0:T(4,128)S(1)}, u32[]{:S(2)}, u32[]{:S(2)}) collective-permute-start(f32[32,3,256]{2,1,0:T(4,128)S(1)} %get-tuple-element.30), channel_id=1, source_target_pairs={{0,15},{1,0},{2,1},{3,2},{4,3},{5,4},{6,5},{7,6},{8,7},{9,8},{10,9... | collective-permute-start | bytes 294920 | tf_op jit(solution)/shard_map/ppermute | solution.py:450
  15.7 0.0 collective-permute-start.2
  15.7 0.0 collective-permute-done.1.xhi
  15.7 0.0 collective-permute-start.12
  15.7 2.2 %fusion = (f32[6,32,2,256]{3,2,1,0:T(2,128)S(1)}, f32[6,32,2,256]{3,2,1,0:T(2,128)S(1)}) fusion(f32[6,32,32,256]{3,2,1,0:T(8,128)} %stress.1), kind=kLoop, calls=%fused_computation.2 | loop fusion | bytes 1572864 | tf_op jit(solution)/shard_map/slice | solution.py:476
  17.9 0.0 collective-permute-done.xlo
  17.9 0.0 copy-start.11
  17.9 0.3 collective-permute-done.3.yhi
  18.2 5.8 %collective-permute-done.2.ylo = f32[32,3,256]{2,1,0:T(4,128)S(1)} collective-permute-done((f32[32,3,256]{2,1,0:T(4,128)S(1)}, f32[32,3,256]{2,1,0:T(4,128)S(1)}, u32[]{:S(2)}, u32[]{:S(2)}) %collective-permute-start.2) | collective-permute-done | bytes 98336 | tf_op jit(solution)/shard_map/ppermute | solution.py:450
  24.0 0.0 copy-done.10
  24.0 0.0 copy-done.11
  24.0 0.0 copy-done.8
  24.0 0.0 copy-start.9
  24.0 0.6 copy-done.9
  24.6 13.7 %advect.1 = (f32[32,32,256]{2,1,0:T(8,128)}, f32[8,32,256]{2,1,0:T(8,128)}, f32[8,32,256]{2,1,0:T(8,128)}, f32[32,8,256]{2,1,0:T(8,128)}, f32[32,8,256]{2,1,0:T(...) custom-call(s32[1,1,32]{2,1,0:T(1,128)} %tiles.3, ...), custom_call_target="tpu_custom_call" | custom-call | tf_op jit(solution)/shard_map/advect/pallas_call | solution.py:144
  38.3 0.0 collective-permute-start.4
  38.4 0.0 collective-permute-done.13.xhi
  38.4 0.0 copy-start
  38.4 0.0 collective-permute-done.12.xlo
  38.4 0.0 copy-start.1
  38.5 0.2 pad_maximum_fusion
  38.7 0.1 collective-permute-start.14
  38.8 0.2 pad_maximum_fusion.1
  39.0 5.4 %collective-permute-start.15 = (f32[6,36,2,256]{3,2,1,0:T(2,128)S(1)}, f32[6,36,2,256]{3,2,1,0:T(2,128)S(1)}, u32[]{:S(2)}, u32[]{:S(2)}) collective-permute-start(f32[6,36,2,256]{3,2,1,0:T(2,128)S(1)} %pad_maximum_fusion.1), channel_id=1, source_target_pairs={{0,15},{1,0},{2,1},{3,2},{4,3},{5,4},{6,5},{7,6},{8,7},{9,8},{10,9... | collective-permute-start | bytes 1327112 | tf_op jit(solution)/shard_map/ppermute | solution.py:450
  44.4 0.0 collective-permute-start.8
  44.4 2.6 %collective-permute-start.9 = (f32[7,8,256]{2,1,0:T(8,128)}, f32[7,8,256]{2,1,0:T(8,128)S(1)}, u32[]{:S(2)}, u32[]{:S(2)}) collective-permute-start(f32[7,8,256]{2,1,0:T(8,128)} %get-tuple-element.20), channel_id=1, source_target_pairs={{0,31},{1,16},{2,17},{3,18},{4,19},{5,20},{6,21},{7,22},{8,23},{9,... | collective-permute-start | bytes 172040 | tf_op jit(solution)/shard_map/ppermute | solution.py:454
  46.9 9.4 %collective-permute-done.8.c_ll = f32[7,8,256]{2,1,0:T(8,128)S(1)} collective-permute-done((f32[7,8,256]{2,1,0:T(8,128)}, f32[7,8,256]{2,1,0:T(8,128)S(1)}, u32[]{:S(2)}, u32[]{:S(2)}) %collective-permute-start.8) | collective-permute-done | bytes 57376 | tf_op jit(solution)/shard_map/ppermute | solution.py:454
  56.3 0.0 collective-permute-start.10
  56.3 0.0 collective-permute-done.9.c_lh
  56.3 0.0 copy-start.13
  56.4 4.7 %collective-permute-start.11 = (f32[7,8,256]{2,1,0:T(8,128)}, f32[7,8,256]{2,1,0:T(8,128)S(1)}, u32[]{:S(2)}, u32[]{:S(2)}) collective-permute-start(f32[7,8,256]{2,1,0:T(8,128)} %get-tuple-element.22), channel_id=1, source_target_pairs={{0,127},{1,112},{2,113},{3,114},{4,115},{5,116},{6,117},{7,118},{8... | collective-permute-start | bytes 172040 | tf_op jit(solution)/shard_map/ppermute | solution.py:454
  61.0 2.5 %collective-permute-done.10.c_hl = f32[7,8,256]{2,1,0:T(8,128)S(1)} collective-permute-done((f32[7,8,256]{2,1,0:T(8,128)}, f32[7,8,256]{2,1,0:T(8,128)S(1)}, u32[]{:S(2)}, u32[]{:S(2)}) %collective-permute-start.10) | collective-permute-done | bytes 57376 | tf_op jit(solution)/shard_map/ppermute | solution.py:454
  63.5 0.4 collective-permute-start.5
  63.9 0.0 collective-permute-done.11.c_hh
  63.9 0.0 collective-permute-start.6
  63.9 0.0 collective-permute-done.4.xlo
  63.9 0.0 copy-start.4
  63.9 5.5 %collective-permute-start.7 = (f32[32,8,256]{2,1,0:T(8,128)}, f32[32,8,256]{2,1,0:T(8,128)S(1)}, u32[]{:S(2)}, u32[]{:S(2)}) collective-permute-start(f32[32,8,256]{2,1,0:T(8,128)} %get-tuple-element.18), channel_id=1, source_target_pairs={{0,15},{1,0},{2,1},{3,2},{4,3},{5,4},{6,5},{7,6},{8,7},{9,8},{10,9... | collective-permute-start | bytes 786440 | tf_op jit(solution)/shard_map/ppermute | solution.py:450
  69.4 0.0 collective-permute-done.5.xhi
  69.4 7.1 %collective-permute-done.6.ylo = f32[32,8,256]{2,1,0:T(8,128)S(1)} collective-permute-done((f32[32,8,256]{2,1,0:T(8,128)}, f32[32,8,256]{2,1,0:T(8,128)S(1)}, u32[]{:S(2)}, u32[]{:S(2)}) %collective-permute-start.6) | collective-permute-done | bytes 262176 | tf_op jit(solution)/shard_map/ppermute | solution.py:450
  76.5 0.0 collective-permute-done.7.yhi
  76.5 0.0 copy-done.12
  76.5 0.0 copy-done.13
  76.5 0.0 copy-done.14
  76.6 0.0 copy-done.15
  76.6 0.0 copy-done.4
  76.6 0.6 copy-done.6
  77.2 0.1 copy-done.7
  77.3 30.8 %sweeps.1 = (f32[36,2,64,128]{3,2,1,0:T(8,128)}, f32[46,2,64,128]{3,2,1,0:T(8,128)}, f32[1,128]{1,0:T(1,128)}) custom-call(s32[1,1,32]{2,1,0:T(1,128)} %tiles.3, f32[32,32,256]{2,1,0:T(8,128)} %get-tuple-element.14.adv, f32[8,32,256]{2,1,0:T(8,128)} %copy-done.4, f32[8,32,256]{2,1,0:T(8,128)} %copy-done.5, f32[32,8,256]{2,1,0:T(8,128)} %copy-done.6, ...), custom_call_target="tpu_custom_call" | custom-call | tf_op jit(solution)/shard_map/sweeps/pallas_call | solution.py:303
  108.1 46.5 %all-gather = f32[128,1,128]{2,1,0:T(1,128)} all-gather(f32[1,1,128]{2,1,0:T(1,128)} %bitcast.3), channel_id=1, replica_groups=mesh['gx'=8,'gy'=16] {'gx','gy'}, dimensions={0}, use_global_device_ids=true | all-gather | bytes 66048 | tf_op jit(solution)/shard_map/all_gather | solution.py:479
  154.7 0.0 collective-permute-done.14.ylo
  154.7 0.0 collective-permute-done.15.yhi
  154.7 0.0 copy-start.3
  154.7 0.0 copy-done
  154.7 0.0 copy-done.1
  154.7 0.7 copy-done.2
  155.4 0.2 copy-done.3
  155.6 26.8 %extend.1 = (f32[32,32,256]{2,1,0:T(8,128)}, f32[6,32,32,256]{3,2,1,0:T(8,128)}) custom-call(f32[128,128]{1,0:T(8,128)} %bitcast.2, f32[36,2,64,128]{3,2,1,0:T(8,128)} %get-tuple-element.24.cur, f32[46,2,64,128]{3,2,1,0:T(8,128)} %get-tuple-element.25.weight, f32[6,32,32,256]{3,2,1,0:T(8,128)} %stress.1, f32[6,2,32,256]{3,2,1,0:T(8,128)} %copy-done.1, ...), custom_call_target="tpu_custom_call" | custom-call | tf_op jit(solution)/shard_map/extend/pallas_call | solution.py:427
  (12 shorter events, 0.1 us)
Async XLA Ops:
  1.6 14.1 %collective-permute-start.1 = (f32[3,32,256]{2,1,0:T(8,128)S(1)}, f32[3,32,256]{2,1,0:T(8,128)S(1)}, u32[]{:S(2)}, u32[]{:S(2)}) collective-permute-start(f32[3,32,256]{2,1,0:T(8,128)S(1)} %get-tuple-element.32), channel_id=1, source_target_pairs={{0,112},{16,0},{32,16},{48,32},{64,48},{80,64},{96,80},{112,96},{1... | collective-permute-start | bytes 294920 | tf_op jit(solution)/shard_map/ppermute | solution.py:448
  4.1 13.8 %collective-permute-start = (f32[3,32,256]{2,1,0:T(8,128)S(1)}, f32[3,32,256]{2,1,0:T(8,128)S(1)}, u32[]{:S(2)}, u32[]{:S(2)}) collective-permute-start(f32[3,32,256]{2,1,0:T(8,128)S(1)} %get-tuple-element.33), channel_id=1, source_target_pairs={{0,16},{16,32},{32,48},{48,64},{64,80},{80,96},{96,112},{112,0},{1... | collective-permute-start | bytes 294920 | tf_op jit(solution)/shard_map/ppermute | solution.py:448
  5.3 33.0 %collective-permute-start.13 = (f32[6,2,32,256]{3,2,1,0:T(8,128)S(1)}, f32[6,2,32,256]{3,2,1,0:T(8,128)S(1)}, u32[]{:S(2)}, u32[]{:S(2)}) collective-permute-start(f32[6,2,32,256]{3,2,1,0:T(8,128)S(1)} %get-tuple-element.28), channel_id=1, source_target_pairs={{0,112},{16,0},{32,16},{48,32},{64,48},{80,64},{96,80},{112,96},{1... | collective-permute-start | bytes 1179656 | tf_op jit(solution)/shard_map/ppermute | solution.py:448
  9.4 8.8 %collective-permute-start.3 = (f32[32,3,256]{2,1,0:T(4,128)S(1)}, f32[32,3,256]{2,1,0:T(4,128)S(1)}, u32[]{:S(2)}, u32[]{:S(2)}) collective-permute-start(f32[32,3,256]{2,1,0:T(4,128)S(1)} %get-tuple-element.30), channel_id=1, source_target_pairs={{0,15},{1,0},{2,1},{3,2},{4,3},{5,4},{6,5},{7,6},{8,7},{9,8},{10,9... | collective-permute-start | bytes 294920 | tf_op jit(solution)/shard_map/ppermute | solution.py:450
  15.7 8.3 %collective-permute-start.2 = (f32[32,3,256]{2,1,0:T(4,128)S(1)}, f32[32,3,256]{2,1,0:T(4,128)S(1)}, u32[]{:S(2)}, u32[]{:S(2)}) collective-permute-start(f32[32,3,256]{2,1,0:T(4,128)S(1)} %get-tuple-element.31), channel_id=1, source_target_pairs={{0,1},{1,2},{2,3},{3,4},{4,5},{5,6},{6,7},{7,8},{8,9},{9,10},{10,1... | collective-permute-start | bytes 294920 | tf_op jit(solution)/shard_map/ppermute | solution.py:450
  15.7 8.3 %copy-start.10 = (f32[3,32,256]{2,1,0:T(8,128)}, f32[3,32,256]{2,1,0:T(8,128)S(1)}, u32[]{:S(2)}) copy-start(f32[3,32,256]{2,1,0:T(8,128)S(1)} %collective-permute-done.1.xhi) | copy-start | bytes 294916
  15.7 22.7 %collective-permute-start.12 = (f32[6,2,32,256]{3,2,1,0:T(8,128)S(1)}, f32[6,2,32,256]{3,2,1,0:T(8,128)S(1)}, u32[]{:S(2)}, u32[]{:S(2)}) collective-permute-start(f32[6,2,32,256]{3,2,1,0:T(8,128)S(1)} %get-tuple-element.29), channel_id=1, source_target_pairs={{0,16},{16,32},{32,48},{48,64},{64,80},{80,96},{96,112},{112,0},{1... | collective-permute-start | bytes 1179656 | tf_op jit(solution)/shard_map/ppermute | solution.py:448
  17.9 6.0 %copy-start.11 = (f32[3,32,256]{2,1,0:T(8,128)}, f32[3,32,256]{2,1,0:T(8,128)S(1)}, u32[]{:S(2)}) copy-start(f32[3,32,256]{2,1,0:T(8,128)S(1)} %collective-permute-done.xlo) | copy-start | bytes 294916
  18.2 5.8 %copy-start.8 = (f32[32,3,256]{2,1,0:T(4,128)}, f32[32,3,256]{2,1,0:T(4,128)S(1)}, u32[]{:S(2)}) copy-start(f32[32,3,256]{2,1,0:T(4,128)S(1)} %collective-permute-done.3.yhi) | copy-start | bytes 294916
  24.0 0.7 copy-start.9
  38.3 25.6 %collective-permute-start.4 = (f32[8,32,256]{2,1,0:T(8,128)}, f32[8,32,256]{2,1,0:T(8,128)S(1)}, u32[]{:S(2)}, u32[]{:S(2)}) collective-permute-start(f32[8,32,256]{2,1,0:T(8,128)} %get-tuple-element.15), channel_id=1, source_target_pairs={{0,16},{16,32},{32,48},{48,64},{64,80},{80,96},{96,112},{112,0},{1... | collective-permute-start | bytes 786440 | tf_op jit(solution)/shard_map/ppermute | solution.py:448
  38.4 116.3 %copy-start = (f32[6,2,32,256]{3,2,1,0:T(8,128)}, f32[6,2,32,256]{3,2,1,0:T(8,128)S(1)}, u32[]{:S(2)}) copy-start(f32[6,2,32,256]{3,2,1,0:T(8,128)S(1)} %collective-permute-done.13.xhi) | copy-start | bytes 1179652
  38.4 116.3 %copy-start.1 = (f32[6,2,32,256]{3,2,1,0:T(8,128)}, f32[6,2,32,256]{3,2,1,0:T(8,128)S(1)}, u32[]{:S(2)}) copy-start(f32[6,2,32,256]{3,2,1,0:T(8,128)S(1)} %collective-permute-done.12.xlo) | copy-start | bytes 1179652
  38.7 116.0 %collective-permute-start.14 = (f32[6,36,2,256]{3,2,1,0:T(2,128)S(1)}, f32[6,36,2,256]{3,2,1,0:T(2,128)S(1)}, u32[]{:S(2)}, u32[]{:S(2)}) collective-permute-start(f32[6,36,2,256]{3,2,1,0:T(2,128)S(1)} %pad_maximum_fusion), channel_id=1, source_target_pairs={{0,1},{1,2},{2,3},{3,4},{4,5},{5,6},{6,7},{7,8},{8,9},{9,10},{10,1... | collective-permute-start | bytes 1327112 | tf_op jit(solution)/shard_map/ppermute | solution.py:450
  39.0 115.7 %collective-permute-start.15 = (f32[6,36,2,256]{3,2,1,0:T(2,128)S(1)}, f32[6,36,2,256]{3,2,1,0:T(2,128)S(1)}, u32[]{:S(2)}, u32[]{:S(2)}) collective-permute-start(f32[6,36,2,256]{3,2,1,0:T(2,128)S(1)} %pad_maximum_fusion.1), channel_id=1, source_target_pairs={{0,15},{1,0},{2,1},{3,2},{4,3},{5,4},{6,5},{7,6},{8,7},{9,8},{10,9... | collective-permute-start | bytes 1327112 | tf_op jit(solution)/shard_map/ppermute | solution.py:450
  44.4 12.0 %collective-permute-start.8 = (f32[7,8,256]{2,1,0:T(8,128)}, f32[7,8,256]{2,1,0:T(8,128)S(1)}, u32[]{:S(2)}, u32[]{:S(2)}) collective-permute-start(f32[7,8,256]{2,1,0:T(8,128)} %get-tuple-element.19), channel_id=1, source_target_pairs={{0,17},{1,18},{2,19},{3,20},{4,21},{5,22},{6,23},{7,24},{8,25},{9,... | collective-permute-start | bytes 172040 | tf_op jit(solution)/shard_map/ppermute | solution.py:454
  44.4 12.0 %collective-permute-start.9 = (f32[7,8,256]{2,1,0:T(8,128)}, f32[7,8,256]{2,1,0:T(8,128)S(1)}, u32[]{:S(2)}, u32[]{:S(2)}) collective-permute-start(f32[7,8,256]{2,1,0:T(8,128)} %get-tuple-element.20), channel_id=1, source_target_pairs={{0,31},{1,16},{2,17},{3,18},{4,19},{5,20},{6,21},{7,22},{8,23},{9,... | collective-permute-start | bytes 172040 | tf_op jit(solution)/shard_map/ppermute | solution.py:454
  56.3 20.2 %copy-start.12 = (f32[7,8,256]{2,1,0:T(8,128)}, f32[7,8,256]{2,1,0:T(8,128)S(1)}, u32[]{:S(2)}) copy-start(f32[7,8,256]{2,1,0:T(8,128)S(1)} %collective-permute-done.8.c_ll) | copy-start | bytes 172036
  56.3 7.1 %collective-permute-start.10 = (f32[7,8,256]{2,1,0:T(8,128)}, f32[7,8,256]{2,1,0:T(8,128)S(1)}, u32[]{:S(2)}, u32[]{:S(2)}) collective-permute-start(f32[7,8,256]{2,1,0:T(8,128)} %get-tuple-element.21), channel_id=1, source_target_pairs={{0,113},{1,114},{2,115},{3,116},{4,117},{5,118},{6,119},{7,120},{8... | collective-permute-start | bytes 172040 | tf_op jit(solution)/shard_map/ppermute | solution.py:454
  56.3 20.2 %copy-start.13 = (f32[7,8,256]{2,1,0:T(8,128)}, f32[7,8,256]{2,1,0:T(8,128)S(1)}, u32[]{:S(2)}) copy-start(f32[7,8,256]{2,1,0:T(8,128)S(1)} %collective-permute-done.9.c_lh) | copy-start | bytes 172036
  56.4 7.5 %collective-permute-start.11 = (f32[7,8,256]{2,1,0:T(8,128)}, f32[7,8,256]{2,1,0:T(8,128)S(1)}, u32[]{:S(2)}, u32[]{:S(2)}) collective-permute-start(f32[7,8,256]{2,1,0:T(8,128)} %get-tuple-element.22), channel_id=1, source_target_pairs={{0,127},{1,112},{2,113},{3,114},{4,115},{5,116},{6,117},{7,118},{8... | collective-permute-start | bytes 172040 | tf_op jit(solution)/shard_map/ppermute | solution.py:454
  63.5 13.1 %copy-start.14 = (f32[7,8,256]{2,1,0:T(8,128)}, f32[7,8,256]{2,1,0:T(8,128)S(1)}, u32[]{:S(2)}) copy-start(f32[7,8,256]{2,1,0:T(8,128)S(1)} %collective-permute-done.10.c_hl) | copy-start | bytes 172036
  63.5 6.0 %collective-permute-start.5 = (f32[8,32,256]{2,1,0:T(8,128)}, f32[8,32,256]{2,1,0:T(8,128)S(1)}, u32[]{:S(2)}, u32[]{:S(2)}) collective-permute-start(f32[8,32,256]{2,1,0:T(8,128)} %get-tuple-element.16), channel_id=1, source_target_pairs={{0,112},{16,0},{32,16},{48,32},{64,48},{80,64},{96,80},{112,96},{1... | collective-permute-start | bytes 786440 | tf_op jit(solution)/shard_map/ppermute | solution.py:448
  63.9 12.7 %copy-start.15 = (f32[7,8,256]{2,1,0:T(8,128)}, f32[7,8,256]{2,1,0:T(8,128)S(1)}, u32[]{:S(2)}) copy-start(f32[7,8,256]{2,1,0:T(8,128)S(1)} %collective-permute-done.11.c_hh) | copy-start | bytes 172036
  63.9 12.6 %collective-permute-start.6 = (f32[32,8,256]{2,1,0:T(8,128)}, f32[32,8,256]{2,1,0:T(8,128)S(1)}, u32[]{:S(2)}, u32[]{:S(2)}) collective-permute-start(f32[32,8,256]{2,1,0:T(8,128)} %get-tuple-element.17), channel_id=1, source_target_pairs={{0,1},{1,2},{2,3},{3,4},{4,5},{5,6},{6,7},{7,8},{8,9},{9,10},{10,1... | collective-permute-start | bytes 786440 | tf_op jit(solution)/shard_map/ppermute | solution.py:450
  63.9 12.6 %copy-start.4 = (f32[8,32,256]{2,1,0:T(8,128)}, f32[8,32,256]{2,1,0:T(8,128)S(1)}, u32[]{:S(2)}) copy-start(f32[8,32,256]{2,1,0:T(8,128)S(1)} %collective-permute-done.4.xlo) | copy-start | bytes 786436
  63.9 12.6 %collective-permute-start.7 = (f32[32,8,256]{2,1,0:T(8,128)}, f32[32,8,256]{2,1,0:T(8,128)S(1)}, u32[]{:S(2)}, u32[]{:S(2)}) collective-permute-start(f32[32,8,256]{2,1,0:T(8,128)} %get-tuple-element.18), channel_id=1, source_target_pairs={{0,15},{1,0},{2,1},{3,2},{4,3},{5,4},{6,5},{7,6},{8,7},{9,8},{10,9... | collective-permute-start | bytes 786440 | tf_op jit(solution)/shard_map/ppermute | solution.py:450
  69.4 7.1 %copy-start.5 = (f32[8,32,256]{2,1,0:T(8,128)}, f32[8,32,256]{2,1,0:T(8,128)S(1)}, u32[]{:S(2)}) copy-start(f32[8,32,256]{2,1,0:T(8,128)S(1)} %collective-permute-done.5.xhi) | copy-start | bytes 786436
  76.5 0.7 copy-start.6
  76.5 0.8 copy-start.7
  154.7 0.8 copy-start.2
  154.7 0.9 copy-start.3
where the time goes:
time: 184 us; the launch traced here: 182 us
  Pallas kernels  71.3 us (39%)
  blocking collectives  46.5 us (25%)
  starting transfers between devices  30.5 us (17%)
  waiting for transfers between devices  25 us (14%)
  local copies, waits for them, and re-layouts  7.78 us (4%)
    all_gather x1, blocking collectives, on_device(): parts = lax.all_gather(part, ('gx', 'gy'), axis=0, tiled=True)  46.5 us
    pallas_call x1, Pallas kernels, sweeps(): pl.pallas_call(sweep_kernel, out_shape=[shape(CX + 4, 2, ROWS, LANES), sh...  30.8 us
    pallas_call x1, Pallas kernels, extend(): pl.pallas_call(extend_kernel, out_shape=[shape(CX, CY, z), shape(COMPS, C...  26.8 us
    ppermute x6, starting transfers between devices, send(): return lax.ppermute(value, 'gy', [(i, (i + dy) % ny) for i in range(ny)])  17.3 us
    pallas_call x1, Pallas kernels, advect(): pl.pallas_call(advect_kernel, out_shape=[shape(CX, CY, z)] + [shape(8, CY...  13.7 us
    ppermute x6, waiting for transfers between devices, send(): return lax.ppermute(value, 'gy', [(i, (i + dy) % ny) for i in range(ny)])  13.1 us
    ppermute x4, waiting for transfers between devices, send(): return lax.ppermute(value, ('gx', 'gy'), pairs)  11.9 us
    ppermute x4, starting transfers between devices, send(): return lax.ppermute(value, ('gx', 'gy'), pairs)  7.21 us
  transfers between devices with their start and end apart: 16, of which 5 were waited for; matrix products, arithmetic and copies ran while one was open for 3% of the time, Pallas kernels for 24%

commit v1 on v0

--- a/solution.py
+++ b/solution.py
@@ -75,7 +75,7 @@
 
 def advect_kernel(
     tiles, level, xlo, xhi, ylo, yhi, speed,
-    adv, to_xp, to_xn, to_yp, to_yn, c_pp, c_pn, c_np, c_nn,
+    adv, to_xp, to_xn, to_yp, to_yn,
     pad, table, sems,
 ):
     copies = []
@@ -115,7 +115,7 @@
                 adv[x, rows, half(h)] = center[h] - TIME_STEP * drift
         return carry
 
-    lax.fori_loop(0, CX, plane, 0)
+    lax.fori_loop(0, CX, plane, 0, unroll=2)
     low, high = CX - DEEP, CX
     to_xp[0:DEEP] = adv[0:DEEP]
     to_xn[0:DEEP] = adv[low:high]
@@ -132,10 +132,6 @@
             for x in range(i * TILE, i * TILE + TILE):
                 to_yp[x, :, half(h)] = jnp.where(row8 == 7, first, adv[x, 0:8, half(h)])
                 to_yn[x, :, half(h)] = jnp.where(row8 == 0, last, adv[x, CY - 8 : CY, half(h)])
-    c_pp[...] = to_yp[0:DEEP]
-    c_pn[...] = to_yn[0:DEEP]
-    c_np[...] = to_yp[low:high]
-    c_nn[...] = to_yn[low:high]
 
 
 def advect(tiles, level, xlo, xhi, ylo, yhi, speed):
@@ -145,10 +141,9 @@
         advect_kernel,
         out_shape=[shape(CX, CY, z)]
         + [shape(8, CY, z)] * 2
-        + [shape(CX, 8, z)] * 2
-        + [shape(DEEP, 8, z)] * 4,
+        + [shape(CX, 8, z)] * 2,
         in_specs=[SMEM, ANY, ANY, ANY, VMEM, VMEM, VMEM],
-        out_specs=[VMEM] * 9,
+        out_specs=[VMEM] * 5,
         scratch_shapes=[
             pltpu.VMEM((CX + 6, 2, 48, LANES), F32),
             pltpu.VMEM((8, LANES), F32),
@@ -163,7 +158,7 @@
 
 
 def sweep_kernel(
-    tiles, adv, xlo, xhi, ylo, yhi, c_ll, c_lh, c_hl, c_hh,
+    tiles, adv, xlo, xhi, ylo, yhi,
     cur_out, weight_out, part,
     first, second, factor, masks, table, sums, sems,
 ):
@@ -173,12 +168,8 @@
             (adv, DEEP, CX, OWN, CY),
             (xlo.at[pl.ds(0, DEEP)], 0, DEEP, OWN, CY),
             (xhi.at[pl.ds(0, DEEP)], DEEP + CX, DEEP, OWN, CY),
-            (ylo, DEEP, CX, OWN - 8, 8),
-            (yhi, DEEP, CX, OWN + CY, 8),
-            (c_ll, 0, DEEP, OWN - 8, 8),
-            (c_lh, 0, DEEP, OWN + CY, 8),
-            (c_hl, DEEP + CX, DEEP, OWN - 8, 8),
-            (c_hh, DEEP + CX, DEEP, OWN + CY, 8),
+            (ylo, 0, WIDE, OWN - 8, 8),
+            (yhi, 0, WIDE, OWN + CY, 8),
         )
         for n, (src, x, nx, y, ny) in enumerate(pieces):
             copies.append(
@@ -191,7 +182,7 @@
         for n, src in enumerate((xlo, xhi)):
             copies.append(
                 pltpu.make_async_copy(
-                    src.at[pl.ds(DEEP, 1), :, half(h)], masks.at[pl.ds(n, 1), h], sems.at[h, 9 + n]
+                    src.at[pl.ds(DEEP, 1), :, half(h)], masks.at[pl.ds(n, 1), h], sems.at[h, 5 + n]
                 )
             )
     for copy in copies:
@@ -271,7 +262,7 @@
                 target[x, h, pl.ds(OWN - 8 + unit * UNIT, UNIT), :] = value
             return carry
 
-        lax.fori_loop(sweep, WIDE - sweep, body, 0)
+        lax.fori_loop(sweep, WIDE - sweep, body, 0, unroll=2)
         source, target = target, source
 
     shift = SWEEPS
@@ -281,7 +272,7 @@
             cur_out[x - shift, h, pl.ds(OWN - 8 + unit * UNIT, UNIT), :] = value
         return carry
 
-    lax.fori_loop(shift, WIDE - shift, last, 0)
+    lax.fori_loop(shift, WIDE - shift, last, 0, unroll=2)
 
     def count(x, carry):
         for h in range(2):
@@ -293,7 +284,7 @@
                 sums[1] += 1.0 - after * after
         return carry
 
-    lax.fori_loop(0, CX, count, 0)
+    lax.fori_loop(0, CX, count, 0, unroll=2)
     lane = lax.broadcasted_iota(jnp.int32, (1, LANES), 1)
     part[...] = jnp.where(lane < 64, jnp.sum(sums[0]), jnp.sum(sums[1]))
 
@@ -303,7 +294,7 @@
     return pl.pallas_call(
         sweep_kernel,
         out_shape=[shape(CX + 4, 2, ROWS, LANES), shape(WIDE, 2, ROWS, LANES), shape(1, LANES)],
-        in_specs=[SMEM, VMEM] + [ANY] * 8,
+        in_specs=[SMEM, VMEM] + [ANY] * 4,
         out_specs=[VMEM] * 3,
         scratch_shapes=[
             pltpu.VMEM((WIDE, 2, ROWS, LANES), F32),
@@ -312,7 +303,7 @@
             pltpu.VMEM((2, 2, CY, LANES), F32),
             pltpu.VMEM((8, LANES), F32),
             pltpu.VMEM((2, UNIT, LANES), F32),
-            pltpu.SemaphoreType.DMA((2, 11)),
+            pltpu.SemaphoreType.DMA((2, 7)),
         ],
         compiler_params=pltpu.CompilerParams(vmem_limit_bytes=LIMIT),
         name="sweeps",
@@ -336,7 +327,7 @@
             )
     for copy in copies:
         copy.start()
-    sums = jnp.sum(parts[...], axis=0, keepdims=True)
+    sums = jnp.sum(parts[...], axis=0)
     shift = sums[:, 0:1] / sums[:, 64:65]
     for copy in copies:
         copy.wait()
@@ -457,26 +448,24 @@
     xhi = send(level[:3], -1, 0)
     ylo = send(level[:, -3:], 0, 1)
     yhi = send(level[:, :3], 0, -1)
-    adv, to_xp, to_xn, to_yp, to_yn, c_pp, c_pn, c_np, c_nn = advect(
-        tiles, level, xlo, xhi, ylo, yhi, velocity
+    adv, to_xp, to_xn, to_yp, to_yn = advect(tiles, level, xlo, xhi, ylo, yhi, velocity)
+    stress_after, to_xp, to_xn = lax.optimization_barrier((stress, to_xp, to_xn))
+    axlo, axhi = send(to_xn, 1, 0), send(to_xp, -1, 0)
+    sxlo = send(stress_after[:, -2:], 1, 0)
+    sxhi = send(stress_after[:, :2], -1, 0)
+    row = lax.broadcasted_iota(jnp.int32, (1, 8, 1), 1)
+    low = lambda face: jnp.where(row == 7, face[DEEP:, :8], face[:DEEP, :8])
+    high = lambda face: jnp.where(row == 0, face[DEEP:, -8:], face[:DEEP, -8:])
+    aylo = send(jnp.concatenate((high(axlo), to_yn, high(axhi)), axis=0), 0, 1)
+    ayhi = send(jnp.concatenate((low(axlo), to_yp, low(axhi)), axis=0), 0, -1)
+    edge = lambda s: jnp.concatenate(
+        (sxlo[:, :, s], stress_after[:, :, s], sxhi[:, :, s]), axis=1
     )
-    halos = (
-        send(to_xn, 1, 0),
-        send(to_xp, -1, 0),
-        send(to_yn, 0, 1),
-        send(to_yp, 0, -1),
-        send(c_nn, 1, 1),
-        send(c_np, 1, -1),
-        send(c_pn, -1, 1),
-        send(c_pp, -1, -1),
-    )
-    cur, weight, part = sweeps(tiles, adv, halos)
-    sxlo = send(stress[:, -2:], 1, 0)
-    sxhi = send(stress[:, :2], -1, 0)
-    edge = lambda s: jnp.concatenate((sxlo[:, :, s], stress[:, :, s], sxhi[:, :, s]), axis=1)
     sylo = send(edge(slice(-2, None)), 0, 1)
     syhi = send(edge(slice(0, 2)), 0, -1)
-    parts = lax.all_gather(part, ("gx", "gy"), axis=0, tiled=True)
+    cur, weight, part = sweeps(tiles, adv, (axlo, axhi, aylo, ayhi))
+    copies = jnp.broadcast_to(part[None], (nx * ny, 1, LANES))
+    parts = lax.all_to_all(copies, ("gx", "gy"), 0, 0, tiled=True)
     return extend(parts, cur, weight, stress, (sxlo, sxhi, sylo, syhi))
 
 

time: 184 us -> 140 us (0.76)
  blocking collectives: 46.5 us -> 19.8 us
  starting transfers between devices: 30.5 us -> 18 us
  Pallas kernels: 71.3 us -> 60.8 us
  waiting for transfers between devices: 25 us -> 29.4 us
    all_gather x1 -> x0, blocking collectives: 46.5 us -> none  [on_device(): parts = lax.all_gather(part, ('gx', 'gy'), axis=0, tiled=True)]
    all_to_all x0 -> x1, blocking collectives: none -> 19.8 us  [on_device(): parts = lax.all_to_all(copies, ('gx', 'gy'), 0, 0, tiled=True)]
    ppermute x4 -> x0, waiting for transfers between devices: 11.9 us -> none  [send(): return lax.ppermute(value, ('gx', 'gy'), pairs)]
    ppermute x6, waiting for transfers between devices: 13.1 us -> 22.8 us  [send(): return lax.ppermute(value, 'gy', [(i, (i + dy) % ny) for i in range(ny)])]
    pallas_call x1, Pallas kernels: 30.8 us -> 22 us  [sweeps(): pl.pallas_call(sweep_kernel, out_shape=[shape(CX + 4, 2, ROWS, LANES), sh...]
    ppermute x4 -> x0, starting transfers between devices: 7.21 us -> none  [send(): return lax.ppermute(value, ('gx', 'gy'), pairs)]
    ppermute x6, waiting for transfers between devices: 0.02 us -> 6.65 us  [send(): return lax.ppermute(value, 'gx', [(i, (i + dx) % nx) for i in range(nx)])]
    ppermute x6, starting transfers between devices: 17.3 us -> 11.9 us  [send(): return lax.ppermute(value, 'gy', [(i, (i + dy) % ny) for i in range(ny)])]
  transfers between devices with their start and end apart: 16 -> 12, of which waited for: 5 -> 7; matrix products, arithmetic and copies ran while one was open for 3% -> 5% of each run, Pallas kernels for 24% -> 16%
where the time goes in v1:
time: 140 us; the launch traced here: 139 us
  Pallas kernels  60.8 us (43%)
  waiting for transfers between devices  29.4 us (21%)
  blocking collectives  19.8 us (14%)
  starting transfers between devices  18 us (13%)
  local copies, waits for them, and re-layouts  8.41 us (6%)
  other arithmetic  1.59 us (1%)
    pallas_call x1, Pallas kernels, extend(): pl.pallas_call(extend_kernel, out_shape=[shape(CX, CY, z), shape(COMPS, C...  26.8 us
    ppermute x6, waiting for transfers between devices, send(): return lax.ppermute(value, 'gy', [(i, (i + dy) % ny) for i in range(ny)])  22.8 us
    pallas_call x1, Pallas kernels, sweeps(): pl.pallas_call(sweep_kernel, out_shape=[shape(CX + 4, 2, ROWS, LANES), sh...  22 us
    all_to_all x1, blocking collectives, on_device(): parts = lax.all_to_all(copies, ('gx', 'gy'), 0, 0, tiled=True)  19.8 us
    ppermute x6, starting transfers between devices, send(): return lax.ppermute(value, 'gy', [(i, (i + dy) % ny) for i in range(ny)])  11.9 us
    pallas_call x1, Pallas kernels, advect(): pl.pallas_call(advect_kernel, out_shape=[shape(CX, CY, z)] + [shape(8, CY...  11.9 us
    ppermute x6, waiting for transfers between devices, send(): return lax.ppermute(value, 'gx', [(i, (i + dx) % nx) for i in range(nx)])  6.65 us
    ppermute x6, starting transfers between devices, send(): return lax.ppermute(value, 'gx', [(i, (i + dx) % nx) for i in range(nx)])  6.03 us
  transfers between devices with their start and end apart: 12, of which 7 were waited for; matrix products, arithmetic and copies ran while one was open for 5% of the time, Pallas kernels for 16%

profile of v1, /device:TPU:0, one launch (start us, length us, event | category | flops | bytes accessed | tf_op | source)
XLA Modules:
  0.0 138.8 jit_solution(14301629577581391892)
XLA Ops:
  0.6 1.0 fusion.3
  1.6 2.5 %collective-permute-start.1 = (f32[3,32,256]{2,1,0:T(8,128)S(1)}, f32[3,32,256]{2,1,0:T(8,128)S(1)}, u32[]{:S(2)}, u32[]{:S(2)}) collective-permute-start(f32[3,32,256]{2,1,0:T(8,128)S(1)} %get-tuple-element.30), channel_id=1, source_target_pairs={{0,112},{16,0},{32,16},{48,32},{64,48},{80,64},{96,80},{112,96},{1... | collective-permute-start | bytes 294920 | tf_op jit(solution)/shard_map/ppermute | solution.py:439
  4.1 0.0 collective-permute-start
  4.1 1.1 fusion.2
  5.2 6.3 %collective-permute-start.3 = (f32[32,3,256]{2,1,0:T(4,128)S(1)}, f32[32,3,256]{2,1,0:T(4,128)S(1)}, u32[]{:S(2)}, u32[]{:S(2)}) collective-permute-start(f32[32,3,256]{2,1,0:T(4,128)S(1)} %get-tuple-element.28), channel_id=1, source_target_pairs={{0,15},{1,0},{2,1},{3,2},{4,3},{5,4},{6,5},{7,6},{8,7},{9,8},{10,9... | collective-permute-start | bytes 294920 | tf_op jit(solution)/shard_map/ppermute | solution.py:441
  11.5 0.0 collective-permute-start.2
  11.5 0.0 collective-permute-done.1.xhi
  11.5 0.0 copy-start.11
  11.5 0.0 collective-permute-done.xlo
  11.6 0.0 copy-start.12
  11.6 2.5 %collective-permute-done.3.yhi = f32[32,3,256]{2,1,0:T(4,128)S(1)} collective-permute-done((f32[32,3,256]{2,1,0:T(4,128)S(1)}, f32[32,3,256]{2,1,0:T(4,128)S(1)}, u32[]{:S(2)}, u32[]{:S(2)}) %collective-permute-start.3) | collective-permute-done | bytes 98336 | tf_op jit(solution)/shard_map/ppermute | solution.py:441
  14.0 0.0 copy-start.9
  14.0 5.8 %collective-permute-done.2.ylo = f32[32,3,256]{2,1,0:T(4,128)S(1)} collective-permute-done((f32[32,3,256]{2,1,0:T(4,128)S(1)}, f32[32,3,256]{2,1,0:T(4,128)S(1)}, u32[]{:S(2)}, u32[]{:S(2)}) %collective-permute-start.2) | collective-permute-done | bytes 98336 | tf_op jit(solution)/shard_map/ppermute | solution.py:441
  19.8 0.0 copy-done.11
  19.8 0.0 copy-done.12
  19.8 0.0 copy-done.9
  19.8 0.0 copy-start.10
  19.8 0.6 copy-done.10
  20.5 11.9 %advect.1 = (f32[32,32,256]{2,1,0:T(8,128)}, f32[8,32,256]{2,1,0:T(8,128)}, f32[8,32,256]{2,1,0:T(8,128)}, f32[32,8,256]{2,1,0:T(8,128)}, f32[32,8,256]{2,1,0:T(8,128)}) custom-call(s32[1,1,32]{2,1,0:T(1,128)} %tiles.3, f32[32,32,256]{2,1,0:T(8,128)} %level.1, f32[3,32,256]{2,1,0:T(8,128)} %copy-done.12, f32[3,32,256]{2,1,0:T(8,128)} %copy-done.11, ...), custom_call_target="tpu_custom_call" | custom-call | tf_op jit(solution)/shard_map/advect/pallas_call | solution.py:140
  32.4 0.0 copy-start.8
  32.4 0.0 collective-permute-start.4
  32.4 2.9 %collective-permute-start.5 = (f32[8,32,256]{2,1,0:T(8,128)}, f32[8,32,256]{2,1,0:T(8,128)S(1)}, u32[]{:S(2)}, u32[]{:S(2)}) collective-permute-start(f32[8,32,256]{2,1,0:T(8,128)} %get-tuple-element.17), channel_id=1, source_target_pairs={{0,112},{16,0},{32,16},{48,32},{64,48},{80,64},{96,80},{112,96},{1... | collective-permute-start | bytes 786440 | tf_op jit(solution)/shard_map/ppermute | solution.py:439
  35.4 2.2 %fusion = (f32[6,32,2,256]{3,2,1,0:T(2,128)S(1)}, f32[6,32,2,256]{3,2,1,0:T(2,128)S(1)}) fusion(f32[6,32,32,256]{3,2,1,0:T(8,128)} %stress.1), kind=kLoop, calls=%fused_computation.14 | loop fusion | bytes 1572864 | tf_op jit(solution)/shard_map/slice | solution.py:462
  37.6 1.2 fusion.1
  38.7 0.0 collective-permute-start.9
  38.8 0.5 collective-permute-start.8
  39.3 0.4 collective-permute-done.4.xlo
  39.6 0.0 copy-start
  39.6 0.0 collective-permute-done.5.xhi
  39.7 0.0 copy-start.1
  39.7 0.1 slice_select_fusion
  39.8 1.0 pad_maximum_fusion.2
  40.8 0.1 collective-permute-start.6
  40.9 3.1 %collective-permute-done.9.xhi = f32[6,2,32,256]{3,2,1,0:T(8,128)S(1)} collective-permute-done((f32[6,2,32,256]{3,2,1,0:T(8,128)S(1)}, f32[6,2,32,256]{3,2,1,0:T(8,128)S(1)}, u32[]{:S(2)}, u32[]{:S(2)}) %collective-permute-start.9) | collective-permute-done | bytes 393248 | tf_op jit(solution)/shard_map/ppermute | solution.py:439
  44.1 0.0 copy-start.2
  44.1 3.1 %collective-permute-done.8.xlo = f32[6,2,32,256]{3,2,1,0:T(8,128)S(1)} collective-permute-done((f32[6,2,32,256]{3,2,1,0:T(8,128)S(1)}, f32[6,2,32,256]{3,2,1,0:T(8,128)S(1)}, u32[]{:S(2)}, u32[]{:S(2)}) %collective-permute-start.8) | collective-permute-done | bytes 393248 | tf_op jit(solution)/shard_map/ppermute | solution.py:439
  47.2 0.0 copy-start.3
  47.2 0.2 pad_maximum_fusion
  47.4 0.1 collective-permute-start.10
  47.5 0.2 pad_maximum_fusion.1
  47.7 5.4 %collective-permute-start.11 = (f32[6,36,2,256]{3,2,1,0:T(2,128)S(1)}, f32[6,36,2,256]{3,2,1,0:T(2,128)S(1)}, u32[]{:S(2)}, u32[]{:S(2)}) collective-permute-start(f32[6,36,2,256]{3,2,1,0:T(2,128)S(1)} %pad_maximum_fusion.1), channel_id=1, source_target_pairs={{0,15},{1,0},{2,1},{3,2},{4,3},{5,4},{6,5},{7,6},{8,7},{9,8},{10,9... | collective-permute-start | bytes 1327112 | tf_op jit(solution)/shard_map/ppermute | solution.py:441
  53.1 0.0 copy-done.8
  53.2 0.1 collective-permute-start.7
  53.3 2.6 %collective-permute-done.6.ylo = f32[46,8,256]{2,1,0:T(8,128)S(1)} collective-permute-done((f32[46,8,256]{2,1,0:T(8,128)S(1)}, f32[46,8,256]{2,1,0:T(8,128)S(1)}, u32[]{:S(2)}, u32[]{:S(2)}) %collective-permute-start.6) | collective-permute-done | bytes 376864 | tf_op jit(solution)/shard_map/ppermute | solution.py:441
  55.8 0.0 copy-start.6
  55.8 11.9 %collective-permute-done.7.yhi = f32[46,8,256]{2,1,0:T(8,128)S(1)} collective-permute-done((f32[46,8,256]{2,1,0:T(8,128)S(1)}, f32[46,8,256]{2,1,0:T(8,128)S(1)}, u32[]{:S(2)}, u32[]{:S(2)}) %collective-permute-start.7) | collective-permute-done | bytes 376864 | tf_op jit(solution)/shard_map/ppermute | solution.py:441
  67.8 0.0 copy-start.7
  67.8 0.0 copy-done
  67.8 0.0 copy-done.1
  67.8 0.0 copy-done.6
  67.8 0.7 copy-done.7
  68.5 22.0 %sweeps.1 = (f32[36,2,64,128]{3,2,1,0:T(8,128)}, f32[46,2,64,128]{3,2,1,0:T(8,128)}, f32[1,128]{1,0:T(1,128)}) custom-call(s32[1,1,32]{2,1,0:T(1,128)} %tiles.3, f32[32,32,256]{2,1,0:T(8,128)} %get-tuple-element.13.adv, f32[8,32,256]{2,1,0:T(8,128)} %copy-done, f32[8,32,256]{2,1,0:T(8,128)} %copy-done.1, f32[46,8,256]{2,1,0:T(8,128)} %copy-done.6, ...), custom_call_target="tpu_custom_call" | custom-call | tf_op jit(solution)/shard_map/sweeps/pallas_call | solution.py:294
  90.6 0.7 broadcast_in_dim.73
  91.3 19.8 %all_to_all.5.parts = f32[128,1,128]{2,1,0:T(1,128)} all-to-all(f32[128,1,128]{2,1,0:T(1,128)S(1)} %broadcast_in_dim.73), channel_id=1, replica_groups=mesh['gx'=8,'gy'=16] {'gx','gy'}, dimensions={0} | all-to-all | bytes 131072 | tf_op jit(solution)/shard_map/all_to_all | solution.py:468
  111.0 0.0 collective-permute-done.10.ylo
  111.0 0.0 copy-start.4
  111.1 0.0 collective-permute-done.11.yhi
  111.1 0.0 copy-start.5
  111.1 0.0 copy-done.2
  111.1 0.0 copy-done.3
  111.1 0.7 copy-done.4
  111.8 0.1 copy-done.5
  112.0 26.8 %extend.1 = (f32[32,32,256]{2,1,0:T(8,128)}, f32[6,32,32,256]{3,2,1,0:T(8,128)}) custom-call(f32[128,1,128]{2,1,0:T(1,128)} %all_to_all.5.parts, f32[36,2,64,128]{3,2,1,0:T(8,128)} %get-tuple-element.21.cur, f32[46,2,64,128]{3,2,1,0:T(8,128)} %get-tuple-element.22.weight, f32[6,32,32,256]{3,2,1,0:T(8,128)} %stress.1, f32[6,2,32,256]{3,2,1,0:T(8,128)} %copy-done.3, ...), custom_call_target="tpu_custom_call" | custom-call | tf_op jit(solution)/shard_map/extend/pallas_call | solution.py:418
  (6 shorter events, 0.1 us)
Async XLA Ops:
  1.6 9.9 %collective-permute-start.1 = (f32[3,32,256]{2,1,0:T(8,128)S(1)}, f32[3,32,256]{2,1,0:T(8,128)S(1)}, u32[]{:S(2)}, u32[]{:S(2)}) collective-permute-start(f32[3,32,256]{2,1,0:T(8,128)S(1)} %get-tuple-element.30), channel_id=1, source_target_pairs={{0,112},{16,0},{32,16},{48,32},{64,48},{80,64},{96,80},{112,96},{1... | collective-permute-start | bytes 294920 | tf_op jit(solution)/shard_map/ppermute | solution.py:439
  4.1 7.4 %collective-permute-start = (f32[3,32,256]{2,1,0:T(8,128)S(1)}, f32[3,32,256]{2,1,0:T(8,128)S(1)}, u32[]{:S(2)}, u32[]{:S(2)}) collective-permute-start(f32[3,32,256]{2,1,0:T(8,128)S(1)} %get-tuple-element.31), channel_id=1, source_target_pairs={{0,16},{16,32},{32,48},{48,64},{64,80},{80,96},{96,112},{112,0},{1... | collective-permute-start | bytes 294920 | tf_op jit(solution)/shard_map/ppermute | solution.py:439
  5.2 8.8 %collective-permute-start.3 = (f32[32,3,256]{2,1,0:T(4,128)S(1)}, f32[32,3,256]{2,1,0:T(4,128)S(1)}, u32[]{:S(2)}, u32[]{:S(2)}) collective-permute-start(f32[32,3,256]{2,1,0:T(4,128)S(1)} %get-tuple-element.28), channel_id=1, source_target_pairs={{0,15},{1,0},{2,1},{3,2},{4,3},{5,4},{6,5},{7,6},{8,7},{9,8},{10,9... | collective-permute-start | bytes 294920 | tf_op jit(solution)/shard_map/ppermute | solution.py:441
  11.5 8.3 %collective-permute-start.2 = (f32[32,3,256]{2,1,0:T(4,128)S(1)}, f32[32,3,256]{2,1,0:T(4,128)S(1)}, u32[]{:S(2)}, u32[]{:S(2)}) collective-permute-start(f32[32,3,256]{2,1,0:T(4,128)S(1)} %get-tuple-element.29), channel_id=1, source_target_pairs={{0,1},{1,2},{2,3},{3,4},{4,5},{5,6},{6,7},{7,8},{8,9},{9,10},{10,1... | collective-permute-start | bytes 294920 | tf_op jit(solution)/shard_map/ppermute | solution.py:441
  11.5 8.3 %copy-start.11 = (f32[3,32,256]{2,1,0:T(8,128)}, f32[3,32,256]{2,1,0:T(8,128)S(1)}, u32[]{:S(2)}) copy-start(f32[3,32,256]{2,1,0:T(8,128)S(1)} %collective-permute-done.1.xhi) | copy-start | bytes 294916
  11.6 8.3 %copy-start.12 = (f32[3,32,256]{2,1,0:T(8,128)}, f32[3,32,256]{2,1,0:T(8,128)S(1)}, u32[]{:S(2)}) copy-start(f32[3,32,256]{2,1,0:T(8,128)S(1)} %collective-permute-done.xlo) | copy-start | bytes 294916
  14.0 5.8 %copy-start.9 = (f32[32,3,256]{2,1,0:T(4,128)}, f32[32,3,256]{2,1,0:T(4,128)S(1)}, u32[]{:S(2)}) copy-start(f32[32,3,256]{2,1,0:T(4,128)S(1)} %collective-permute-done.3.yhi) | copy-start | bytes 294916
  19.8 0.6 copy-start.10
  32.4 20.7 %copy-start.8 = (f32[32,8,256]{2,1,0:T(8,128)S(1)}, f32[32,8,256]{2,1,0:T(8,128)}, u32[]{:S(2)}) copy-start(f32[32,8,256]{2,1,0:T(8,128)} %get-tuple-element.19) | copy-start | bytes 786436
  32.4 7.2 %collective-permute-start.4 = (f32[8,32,256]{2,1,0:T(8,128)}, f32[8,32,256]{2,1,0:T(8,128)S(1)}, u32[]{:S(2)}, u32[]{:S(2)}) collective-permute-start(f32[8,32,256]{2,1,0:T(8,128)} %get-tuple-element.16), channel_id=1, source_target_pairs={{0,16},{16,32},{32,48},{48,64},{64,80},{80,96},{96,112},{112,0},{1... | collective-permute-start | bytes 786440 | tf_op jit(solution)/shard_map/ppermute | solution.py:439
  32.4 7.2 %collective-permute-start.5 = (f32[8,32,256]{2,1,0:T(8,128)}, f32[8,32,256]{2,1,0:T(8,128)S(1)}, u32[]{:S(2)}, u32[]{:S(2)}) collective-permute-start(f32[8,32,256]{2,1,0:T(8,128)} %get-tuple-element.17), channel_id=1, source_target_pairs={{0,112},{16,0},{32,16},{48,32},{64,48},{80,64},{96,80},{112,96},{1... | collective-permute-start | bytes 786440 | tf_op jit(solution)/shard_map/ppermute | solution.py:439
  38.7 5.3 %collective-permute-start.9 = (f32[6,2,32,256]{3,2,1,0:T(8,128)S(1)}, f32[6,2,32,256]{3,2,1,0:T(8,128)S(1)}, u32[]{:S(2)}, u32[]{:S(2)}) collective-permute-start(f32[6,2,32,256]{3,2,1,0:T(8,128)S(1)} %get-tuple-element.26), channel_id=1, source_target_pairs={{0,112},{16,0},{32,16},{48,32},{64,48},{80,64},{96,80},{112,96},{1... | collective-permute-start | bytes 1179656 | tf_op jit(solution)/shard_map/ppermute | solution.py:439
  38.8 8.4 %collective-permute-start.8 = (f32[6,2,32,256]{3,2,1,0:T(8,128)S(1)}, f32[6,2,32,256]{3,2,1,0:T(8,128)S(1)}, u32[]{:S(2)}, u32[]{:S(2)}) collective-permute-start(f32[6,2,32,256]{3,2,1,0:T(8,128)S(1)} %get-tuple-element.27), channel_id=1, source_target_pairs={{0,16},{16,32},{32,48},{48,64},{64,80},{80,96},{96,112},{112,0},{1... | collective-permute-start | bytes 1179656 | tf_op jit(solution)/shard_map/ppermute | solution.py:439
  39.6 28.1 %copy-start = (f32[8,32,256]{2,1,0:T(8,128)}, f32[8,32,256]{2,1,0:T(8,128)S(1)}, u32[]{:S(2)}) copy-start(f32[8,32,256]{2,1,0:T(8,128)S(1)} %collective-permute-done.4.xlo) | copy-start | bytes 786436
  39.7 28.1 %copy-start.1 = (f32[8,32,256]{2,1,0:T(8,128)}, f32[8,32,256]{2,1,0:T(8,128)S(1)}, u32[]{:S(2)}) copy-start(f32[8,32,256]{2,1,0:T(8,128)S(1)} %collective-permute-done.5.xhi) | copy-start | bytes 786436
  40.8 15.0 %collective-permute-start.6 = (f32[46,8,256]{2,1,0:T(8,128)S(1)}, f32[46,8,256]{2,1,0:T(8,128)S(1)}, u32[]{:S(2)}, u32[]{:S(2)}) collective-permute-start(f32[46,8,256]{2,1,0:T(8,128)S(1)} %pad_maximum_fusion.2), channel_id=1, source_target_pairs={{0,1},{1,2},{2,3},{3,4},{4,5},{5,6},{6,7},{7,8},{8,9},{9,10},{10,1... | collective-permute-start | bytes 1130504 | tf_op jit(solution)/shard_map/ppermute | solution.py:441
  44.1 67.0 %copy-start.2 = (f32[6,2,32,256]{3,2,1,0:T(8,128)}, f32[6,2,32,256]{3,2,1,0:T(8,128)S(1)}, u32[]{:S(2)}) copy-start(f32[6,2,32,256]{3,2,1,0:T(8,128)S(1)} %collective-permute-done.9.xhi) | copy-start | bytes 1179652
  47.2 63.9 %copy-start.3 = (f32[6,2,32,256]{3,2,1,0:T(8,128)}, f32[6,2,32,256]{3,2,1,0:T(8,128)S(1)}, u32[]{:S(2)}) copy-start(f32[6,2,32,256]{3,2,1,0:T(8,128)S(1)} %collective-permute-done.8.xlo) | copy-start | bytes 1179652
  47.4 63.6 %collective-permute-start.10 = (f32[6,36,2,256]{3,2,1,0:T(2,128)S(1)}, f32[6,36,2,256]{3,2,1,0:T(2,128)S(1)}, u32[]{:S(2)}, u32[]{:S(2)}) collective-permute-start(f32[6,36,2,256]{3,2,1,0:T(2,128)S(1)} %pad_maximum_fusion), channel_id=1, source_target_pairs={{0,1},{1,2},{2,3},{3,4},{4,5},{5,6},{6,7},{7,8},{8,9},{9,10},{10,1... | collective-permute-start | bytes 1327112 | tf_op jit(solution)/shard_map/ppermute | solution.py:441
  47.7 63.3 %collective-permute-start.11 = (f32[6,36,2,256]{3,2,1,0:T(2,128)S(1)}, f32[6,36,2,256]{3,2,1,0:T(2,128)S(1)}, u32[]{:S(2)}, u32[]{:S(2)}) collective-permute-start(f32[6,36,2,256]{3,2,1,0:T(2,128)S(1)} %pad_maximum_fusion.1), channel_id=1, source_target_pairs={{0,15},{1,0},{2,1},{3,2},{4,3},{5,4},{6,5},{7,6},{8,7},{9,8},{10,9... | collective-permute-start | bytes 1327112 | tf_op jit(solution)/shard_map/ppermute | solution.py:441
  53.2 14.6 %collective-permute-start.7 = (f32[46,8,256]{2,1,0:T(8,128)S(1)}, f32[46,8,256]{2,1,0:T(8,128)S(1)}, u32[]{:S(2)}, u32[]{:S(2)}) collective-permute-start(f32[46,8,256]{2,1,0:T(8,128)S(1)} %pad_maximum_fusion.3), channel_id=1, source_target_pairs={{0,15},{1,0},{2,1},{3,2},{4,3},{5,4},{6,5},{7,6},{8,7},{9,8},{10,9... | collective-permute-start | bytes 1130504 | tf_op jit(solution)/shard_map/ppermute | solution.py:441
  55.8 12.0 %copy-start.6 = (f32[46,8,256]{2,1,0:T(8,128)}, f32[46,8,256]{2,1,0:T(8,128)S(1)}, u32[]{:S(2)}) copy-start(f32[46,8,256]{2,1,0:T(8,128)S(1)} %collective-permute-done.6.ylo) | copy-start | bytes 1130500
  67.8 0.7 copy-start.7
  111.0 0.8 copy-start.4
  111.1 0.9 copy-start.5

commit v2 on v1

--- a/solution.py
+++ b/solution.py
@@ -73,8 +73,79 @@
     return flags
 
 
+def derivative(line, speed):
+    return speed * weno([line[k + 1] - line[k] for k in range(6)], speed > 0)
+
+
+def along_x(pad, x, h, at, size):
+    return [pad[x + k, h, pl.ds(at, size), :] for k in range(-3, 4)]
+
+
+def along_y(pad, x, h, at, size):
+    return [pad[x, h, pl.ds(at + k, size), :] for k in range(-3, 4)]
+
+
+def inner_kernel(level, speed, drift, pad, sems):
+    copies = [
+        pltpu.make_async_copy(level.at[:, :, half(h)], pad.at[:, h], sems.at[h]) for h in range(2)
+    ]
+    for copy in copies:
+        copy.start()
+    for copy in copies:
+        copy.wait()
+
+    def plane(x, with_x):
+        for unit in range(CY // UNIT):
+            rows = pl.ds(unit * UNIT, UNIT)
+            v = [[speed[d, x, rows, half(h)].astype(F32) for h in range(2)] for d in range(3)]
+            for part in range(UNIT // 8):
+                at = unit * UNIT + 8 * part
+                cut = slice(8 * part, 8 * part + 8)
+                center = [pad[x, h, pl.ds(at, 8), :] for h in range(2)]
+                ups = [lane_shift(center, k) for k in (1, 2, 3)]
+                downs = [lane_shift(center, -k) for k in (3, 2, 1)]
+                for h in range(2):
+                    line = [s[h] for s in downs] + [center[h]] + [s[h] for s in ups]
+                    total = derivative(line, v[2][h][cut])
+                    if with_x:
+                        total = total + derivative(along_x(pad, x, h, at, 8), v[0][h][cut])
+                    if 8 <= at < CY - 8:
+                        total = total + derivative(along_y(pad, x, h, at, 8), v[1][h][cut])
+                    drift[x, pl.ds(at, 8), half(h)] = total
+
+    def inner(x, carry):
+        plane(x, True)
+        return carry
+
+    def outer(x, carry):
+        plane(x, False)
+        plane(x + CX - 3, False)
+        return carry
+
+    lax.fori_loop(0, 3, outer, 0)
+    lax.fori_loop(3, CX - 3, inner, 0, unroll=2)
+
+
+def inner_drift(level, speed):
+    return pl.pallas_call(
+        inner_kernel,
+        out_shape=jax.ShapeDtypeStruct(level.shape, F32),
+        in_specs=[ANY, VMEM],
+        out_specs=VMEM,
+        scratch_shapes=[
+            pltpu.VMEM((CX, 2, CY, LANES), F32),
+            pltpu.SemaphoreType.DMA((2,)),
+        ],
+        compiler_params=pltpu.CompilerParams(vmem_limit_bytes=LIMIT),
+        cost_estimate=pl.CostEstimate(
+            flops=180 * level.size, bytes_accessed=14 * level.size, transcendentals=9 * level.size
+        ),
+        name="inner_drift",
+    )(level, speed)
+
+
 def advect_kernel(
-    tiles, level, xlo, xhi, ylo, yhi, speed,
+    tiles, level, xlo, xhi, ylo, yhi, speed, drift,
     adv, to_xp, to_xn, to_yp, to_yn,
     pad, table, sems,
 ):
@@ -89,33 +160,41 @@
     for copy in copies:
         copy.start()
     table[...] = band_table(tiles)
-    for copy in copies:
-        copy.wait()
     for h in range(2):
         pad[3 : CX + 3, h, 5:8, :] = ylo[:, :, half(h)]
         pad[3 : CX + 3, h, 8 + CY : 11 + CY, :] = yhi[:, :, half(h)]
-
-    def plane(x, carry):
+    for copy in copies:
+        copy.wait()
+
+    def plane(x, with_x):
         for unit in range(CY // UNIT):
-            at = 8 + unit * UNIT
             rows = pl.ds(unit * UNIT, UNIT)
-            center = [pad[x + 3, h, pl.ds(at, UNIT), :] for h in range(2)]
-            ups = [lane_shift(center, k) for k in (1, 2, 3)]
-            downs = [lane_shift(center, -k) for k in (3, 2, 1)]
             for h in range(2):
-                v = [speed[d, x, rows, half(h)].astype(F32) for d in range(3)]
-                lx = [pad[x + 3 + k, h, pl.ds(at, UNIT), :] for k in range(-3, 4)]
-                ly = [pad[x + 3, h, pl.ds(at + k, UNIT), :] for k in range(-3, 4)]
-                lz = [s[h] for s in downs] + [center[h]] + [s[h] for s in ups]
-                drift = None
-                for vd, line in zip(v, (lx, ly, lz)):
-                    steps = [line[k + 1] - line[k] for k in range(6)]
-                    term = vd * weno(steps, vd > 0)
-                    drift = term if drift is None else drift + term
-                adv[x, rows, half(h)] = center[h] - TIME_STEP * drift
+                vx = speed[0, x, rows, half(h)].astype(F32) if with_x else None
+                vy = speed[1, x, rows, half(h)].astype(F32)
+                for part in range(UNIT // 8):
+                    at = unit * UNIT + 8 * part
+                    cut = slice(8 * part, 8 * part + 8)
+                    total = drift[x, pl.ds(at, 8), half(h)]
+                    if with_x:
+                        total = total + derivative(along_x(pad, x + 3, h, at + 8, 8), vx[cut])
+                    if at in (0, CY - 8):
+                        total = total + derivative(along_y(pad, x + 3, h, at + 8, 8), vy[cut])
+                    adv[x, pl.ds(at, 8), half(h)] = (
+                        pad[x + 3, h, pl.ds(at + 8, 8), :] - TIME_STEP * total
+                    )
+
+    def inner(x, carry):
+        plane(x, False)
         return carry
 
-    lax.fori_loop(0, CX, plane, 0, unroll=2)
+    def outer(x, carry):
+        plane(x, True)
+        plane(x + CX - 3, True)
+        return carry
+
+    lax.fori_loop(0, 3, outer, 0)
+    lax.fori_loop(3, CX - 3, inner, 0, unroll=2)
     low, high = CX - DEEP, CX
     to_xp[0:DEEP] = adv[0:DEEP]
     to_xn[0:DEEP] = adv[low:high]
@@ -134,7 +213,7 @@
                 to_yn[x, :, half(h)] = jnp.where(row8 == 0, last, adv[x, CY - 8 : CY, half(h)])
 
 
-def advect(tiles, level, xlo, xhi, ylo, yhi, speed):
+def advect(tiles, level, xlo, xhi, ylo, yhi, speed, drift):
     shape = lambda *s: jax.ShapeDtypeStruct(s, F32)
     z = 2 * LANES
     return pl.pallas_call(
@@ -142,7 +221,7 @@
         out_shape=[shape(CX, CY, z)]
         + [shape(8, CY, z)] * 2
         + [shape(CX, 8, z)] * 2,
-        in_specs=[SMEM, ANY, ANY, ANY, VMEM, VMEM, VMEM],
+        in_specs=[SMEM, ANY, ANY, ANY, VMEM, VMEM, VMEM, VMEM],
         out_specs=[VMEM] * 5,
         scratch_shapes=[
             pltpu.VMEM((CX + 6, 2, 48, LANES), F32),
@@ -151,7 +230,7 @@
         ],
         compiler_params=pltpu.CompilerParams(vmem_limit_bytes=LIMIT),
         name="advect",
-    )(tiles, level, xlo, xhi, ylo, yhi, speed)
+    )(tiles, level, xlo, xhi, ylo, yhi, speed, drift)
 
 
 WIDE = CX + 2 * DEEP
@@ -192,8 +271,9 @@
     for copy in copies:
         copy.wait()
 
-    def prepare(x, bands):
+    def prepare(x, bands, keep):
         for h in range(2):
+            saved = {}
             for group in range(-1, 5):
                 rows = pl.ds(OWN + 8 * group, 8)
                 value = first[x, h, rows, :]
@@ -207,7 +287,11 @@
                 weight = band * recip(1.0 + square * (1.0 / 36.0))
                 sign = value * lax.rsqrt(square + 1.0)
                 factor[x, h, rows, :] = PSEUDO_STEP * sign * weight
-                weight_out[x, h, rows, :] = weight
+                saved[group] = weight
+            if keep:
+                saved[4] = jnp.where(row8 < 4, saved[4], saved[-1])
+                for group in range(5):
+                    weight_out[x - DEEP + 1, h, pl.ds(OWN + 8 * group, 8), :] = saved[group]
 
     def halo_bands(n):
         return lambda group, h: masks[n, h, pl.ds(8 * group, 8), :]
@@ -219,17 +303,21 @@
 
         return bands
 
-    def run(start, stop, bands):
+    row8 = lax.broadcasted_iota(jnp.int32, (8, LANES), 0)
+
+    def run(start, stop, bands, keep):
         def body(x, carry):
-            prepare(x, bands)
+            prepare(x, bands, keep)
             return carry
 
-        lax.fori_loop(start, stop, body, 0)
-
-    run(0, DEEP, halo_bands(0))
-    run(DEEP, DEEP + TILE, own_bands(0))
-    run(DEEP + TILE, DEEP + CX, own_bands(1))
-    run(DEEP + CX, WIDE, halo_bands(1))
+        lax.fori_loop(start, stop, body, 0, unroll=2)
+
+    run(1, DEEP - 1, halo_bands(0), False)
+    prepare(DEEP - 1, halo_bands(0), True)
+    run(DEEP, DEEP + TILE, own_bands(0), True)
+    run(DEEP + TILE, DEEP + CX, own_bands(1), True)
+    prepare(DEEP + CX, halo_bands(1), True)
+    run(DEEP + CX + 1, WIDE - 1, halo_bands(1), False)
 
     def sweep_plane(src, x):
         for unit in range(3):
@@ -268,8 +356,15 @@
     shift = SWEEPS
 
     def last(x, carry):
+        values = [{}, {}]
         for unit, h, value in sweep_plane(source, x):
-            cur_out[x - shift, h, pl.ds(OWN - 8 + unit * UNIT, UNIT), :] = value
+            values[h][2 * unit], values[h][2 * unit + 1] = value[:8], value[8:]
+        for h in range(2):
+            v = values[h]
+            v[5] = jnp.where(row8 < 4, v[5], v[0])
+            v[0], v[6] = v[5], v[1]
+            for n in range(7):
+                cur_out[x - shift, h, pl.ds(OWN - 8 + 8 * n, 8), :] = v[n]
         return carry
 
     lax.fori_loop(shift, WIDE - shift, last, 0, unroll=2)
@@ -293,7 +388,7 @@
     shape = lambda *s: jax.ShapeDtypeStruct(s, F32)
     return pl.pallas_call(
         sweep_kernel,
-        out_shape=[shape(CX + 4, 2, ROWS, LANES), shape(WIDE, 2, ROWS, LANES), shape(1, LANES)],
+        out_shape=[shape(CX + 4, 2, ROWS, LANES), shape(CX + 2, 2, ROWS, LANES), shape(1, LANES)],
         in_specs=[SMEM, VMEM] + [ANY] * 4,
         out_specs=[VMEM] * 3,
         scratch_shapes=[
@@ -310,31 +405,46 @@
     )(tiles, adv, *halos)
 
 
+CHUNKS = ((0, 10), (10, 18), (18, 26), (26, 32))
+
+
 def extend_kernel(
     parts, cur, weight, stress, xlo, xhi, ylo, yhi,
     level_out, stress_out,
-    pad, ring, mix, sems,
+    pad, ring, mix, stage, sems, out_sems,
 ):
-    copies = []
-    for h in range(2):
-        for n, (src, at, size) in enumerate(((stress, 2, CX), (xlo, 0, 2), (xhi, CX + 2, 2))):
-            copies.append(
-                pltpu.make_async_copy(
-                    src.at[:, :, :, half(h)],
-                    pad.at[:, pl.ds(at, size), h, pl.ds(OWN, CY), :],
-                    sems.at[h, n],
-                )
-            )
-    for copy in copies:
-        copy.start()
+    def chunk(n):
+        start, stop = CHUNKS[n]
+        pieces = [(stress.at[:, pl.ds(start, stop - start)], start + 2, stop - start)]
+        if n == 0:
+            pieces.append((xlo, 0, 2))
+        if n == len(CHUNKS) - 1:
+            pieces.append((xhi, CX + 2, 2))
+        copies = []
+        for h in range(2):
+            for m, (src, at, size) in enumerate(pieces):
+                for k, (y, ny, row) in enumerate(((0, CY, OWN), (0, 8, OWN + CY + 8))):
+                    copies.append(
+                        pltpu.make_async_copy(
+                            src.at[:, :, pl.ds(y, ny), half(h)],
+                            pad.at[:, pl.ds(at, size), h, pl.ds(row, ny), :],
+                            sems.at[n, h, m, k],
+                        )
+                    )
+        return copies
+
+    chunks = [chunk(n) for n in range(len(CHUNKS))]
+    for copies in chunks:
+        for copy in copies:
+            copy.start()
     sums = jnp.sum(parts[...], axis=0)
     shift = sums[:, 0:1] / sums[:, 64:65]
-    for copy in copies:
-        copy.wait()
     for h in range(2):
         for c in range(COMPS):
-            pad[c, :, h, OWN - 2 : OWN, :] = ylo[c, :, :, half(h)]
-            pad[c, :, h, OWN + CY : OWN + CY + 2, :] = yhi[c, :, :, half(h)]
+            low, high = ylo[c, :, :, half(h)], yhi[c, :, :, half(h)]
+            pad[c, :, h, OWN - 2 : OWN, :] = low
+            pad[c, :, h, OWN + CY + 6 : OWN + CY + 8, :] = low
+            pad[c, :, h, OWN + CY : OWN + CY + 2, :] = high
 
     def neighbours(load, at):
         center = [load(0, h, at) for h in range(2)]
@@ -347,11 +457,17 @@
             for h in range(2)
         ]
 
-    def first_step(i, slot):
-        for unit in range(3):
-            at = OWN - 8 + unit * UNIT
-            rows = pl.ds(at, UNIT)
-            center, around = neighbours(lambda dx, h, r: cur[i + 1 + dx, h, pl.ds(r, UNIT), :], at)
+    def blend(mixes, center, around):
+        value = mixes[6] * center
+        for n in range(6):
+            value = value + mixes[n] * around[n]
+        return value
+
+    def first_step(i, slot, groups=5):
+        for group in range(groups):
+            at = OWN + 8 * group
+            rows = pl.ds(at, 8)
+            center, around = neighbours(lambda dx, h, r: cur[i + 1 + dx, h, pl.ds(r, 8), :], at)
             mixes = []
             for h in range(2):
                 c = center[h]
@@ -360,56 +476,62 @@
                     for n in around[h]
                 ]
                 total = w[0] + w[1] + w[2] + w[3] + w[4] + w[5]
-                gate = weight[i + DEEP - 1, h, rows, :] * 0.5 * (1.0 + jnp.tanh(2.0 * (c - shift)))
+                gate = weight[i, h, rows, :] * 0.5 * (1.0 + jnp.tanh(2.0 * (c - shift)))
                 scaled = gate * recip(total)
                 w = [scaled * n for n in w] + [1.0 - gate]
                 mixes.append(w)
-                for n in range(7):
-                    mix[slot % 2, n, h, rows, :] = w[n]
+                if group < 4:
+                    for n in range(7):
+                        mix[slot % 2, n, h, rows, :] = w[n]
             for comp in range(COMPS):
                 center, around = neighbours(
-                    lambda dx, h, r: pad[comp, i + 1 + dx, h, pl.ds(r, UNIT), :], at
+                    lambda dx, h, r: pad[comp, i + 1 + dx, h, pl.ds(r, 8), :], at
                 )
                 for h in range(2):
-                    value = mixes[h][6] * center[h]
-                    for n in range(6):
-                        value = value + mixes[h][n] * around[h][n]
+                    value = blend(mixes[h], center[h], around[h])
                     ring[slot, comp, h, rows, :] = value
+                    if group == 4:
+                        ring[slot, comp, h, pl.ds(OWN - 8, 8), :] = value
 
     def second_step(x, slot):
         slots = {dx: (slot + dx) % 4 for dx in (-1, 0, 1)}
-        for unit in range(CY // UNIT):
-            at = OWN + unit * UNIT
-            rows = pl.ds(at, UNIT)
-            own = pl.ds(unit * UNIT, UNIT)
+        for group in range(CY // 8):
+            at = OWN + 8 * group
+            rows = pl.ds(at, 8)
+            own = pl.ds(8 * group, 8)
             mixes = [[mix[slot % 2, n, h, rows, :] for n in range(7)] for h in range(2)]
             for comp in range(COMPS):
                 center, around = neighbours(
-                    lambda dx, h, r: ring[slots[dx], comp, h, pl.ds(r, UNIT), :], at
+                    lambda dx, h, r: ring[slots[dx], comp, h, pl.ds(r, 8), :], at
                 )
                 for h in range(2):
-                    value = mixes[h][6] * center[h]
-                    for n in range(6):
-                        value = value + mixes[h][n] * around[h][n]
-                    stress_out[comp, x, own, half(h)] = value
+                    stage[comp, x, own, half(h)] = blend(mixes[h], center[h], around[h])
             for h in range(2):
                 level_out[x, own, half(h)] = cur[x + 2, h, rows, :] - shift
 
-    def body(group, carry):
-        for k in range(4):
-            i = group * 4 + k
-            first_step(i, k)
-
-            @pl.when(i >= 2)
-            def _():
-                second_step(i - 2, (k + 3) % 4)
-
-        return carry
-
-    lax.fori_loop(0, 8, body, 0)
-    for i in (32, 33):
-        first_step(i, i % 4)
-        second_step(i - 2, (i + 3) % 4)
+    outs = []
+    for n in range(len(CHUNKS)):
+        for copy in chunks[n]:
+            copy.wait()
+        if n == 0:
+            first_step(0, 0, groups=4)
+            first_step(1, 1)
+
+        def body(group, carry):
+            for k in range(4):
+                i = group * 4 + k + 2
+                first_step(i, (k + 2) % 4)
+                second_step(i - 2, (k + 1) % 4)
+            return carry
+
+        lax.fori_loop(2 * n, 2 * n + 2, body, 0)
+        planes = pl.ds(8 * n, 8)
+        outs.append(
+            pltpu.make_async_copy(stage.at[:, planes], stress_out.at[:, planes], out_sems.at[n])
+        )
+        outs[-1].start()
+    for copy in outs:
+        copy.wait()
 
 
 def extend(parts, cur, weight, stress, halos):
@@ -419,12 +541,14 @@
         extend_kernel,
         out_shape=[shape(CX, CY, z), shape(COMPS, CX, CY, z)],
         in_specs=[VMEM, VMEM, VMEM, ANY, ANY, ANY, VMEM, VMEM],
-        out_specs=[VMEM] * 2,
+        out_specs=[VMEM, ANY],
         scratch_shapes=[
             pltpu.VMEM((COMPS, CX + 4, 2, ROWS, LANES), F32),
             pltpu.VMEM((4, COMPS, 2, ROWS, LANES), F32),
             pltpu.VMEM((2, 7, 2, ROWS, LANES), F32),
-            pltpu.SemaphoreType.DMA((2, 3)),
+            pltpu.VMEM((COMPS, CX, CY, z), F32),
+            pltpu.SemaphoreType.DMA((4, 2, 2, 2)),
+            pltpu.SemaphoreType.DMA((4,)),
         ],
         compiler_params=pltpu.CompilerParams(vmem_limit_bytes=LIMIT),
         name="extend",
@@ -448,24 +572,26 @@
     xhi = send(level[:3], -1, 0)
     ylo = send(level[:, -3:], 0, 1)
     yhi = send(level[:, :3], 0, -1)
-    adv, to_xp, to_xn, to_yp, to_yn = advect(tiles, level, xlo, xhi, ylo, yhi, velocity)
-    stress_after, to_xp, to_xn = lax.optimization_barrier((stress, to_xp, to_xn))
+    drift = inner_drift(level, velocity)
+    adv, to_xp, to_xn, to_yp, to_yn = advect(tiles, level, xlo, xhi, ylo, yhi, velocity, drift)
     axlo, axhi = send(to_xn, 1, 0), send(to_xp, -1, 0)
-    sxlo = send(stress_after[:, -2:], 1, 0)
-    sxhi = send(stress_after[:, :2], -1, 0)
     row = lax.broadcasted_iota(jnp.int32, (1, 8, 1), 1)
     low = lambda face: jnp.where(row == 7, face[DEEP:, :8], face[:DEEP, :8])
     high = lambda face: jnp.where(row == 0, face[DEEP:, -8:], face[:DEEP, -8:])
     aylo = send(jnp.concatenate((high(axlo), to_yn, high(axhi)), axis=0), 0, 1)
     ayhi = send(jnp.concatenate((low(axlo), to_yp, low(axhi)), axis=0), 0, -1)
-    edge = lambda s: jnp.concatenate(
-        (sxlo[:, :, s], stress_after[:, :, s], sxhi[:, :, s]), axis=1
-    )
-    sylo = send(edge(slice(-2, None)), 0, 1)
-    syhi = send(edge(slice(0, 2)), 0, -1)
+    faces = (stress[:, -2:], stress[:, :2])
+    faces, _, _ = lax.optimization_barrier((faces, axlo, axhi))
+    sxlo, sxhi = send(faces[0], 1, 0), send(faces[1], -1, 0)
+    edge = lambda s: jnp.concatenate((sxlo[:, :, s], stress[:, :, s], sxhi[:, :, s]), axis=1)
+    edges = (edge(slice(-2, None)), edge(slice(0, 2)))
+    edges, aylo, ayhi = lax.optimization_barrier((edges, aylo, ayhi))
+    sylo, syhi = send(edges[0], 0, 1), send(edges[1], 0, -1)
     cur, weight, part = sweeps(tiles, adv, (axlo, axhi, aylo, ayhi))
-    copies = jnp.broadcast_to(part[None], (nx * ny, 1, LANES))
-    parts = lax.all_to_all(copies, ("gx", "gy"), 0, 0, tiled=True)
+    for axis, count in (("gx", nx), ("gy", ny)):
+        copies = jnp.broadcast_to(part[None], (count, 1, LANES))
+        parts = lax.all_to_all(copies, axis, 0, 0, tiled=True)
+        part = jnp.sum(parts, axis=0)
     return extend(parts, cur, weight, stress, (sxlo, sxhi, sylo, syhi))
 
 

time: 140 us -> 127 us (0.907)
  waiting for transfers between devices: 29.4 us -> 8.33 us
  starting transfers between devices: 18 us -> 26.1 us
    ppermute x6, waiting for transfers between devices: 22.8 us -> 5.23 us  [send(): return lax.ppermute(value, 'gy', [(i, (i + dy) % ny) for i in range(ny)])]
    pallas_call x0 -> x1, Pallas kernels: none -> 9.59 us  [inner_drift(): pl.pallas_call(inner_kernel, out_shape=jax.ShapeDtypeStruct(level.shape,...]
    ppermute x6, starting transfers between devices: 11.9 us -> 17.6 us  [send(): return lax.ppermute(value, 'gy', [(i, (i + dy) % ny) for i in range(ny)])]
    pallas_call x1, Pallas kernels: 11.9 us -> 6.41 us  [advect(): pl.pallas_call(advect_kernel, out_shape=[shape(CX, CY, z)] + [shape(8, CY...]
    pallas_call x1, Pallas kernels: 26.8 us -> 22.6 us  [extend(): pl.pallas_call(extend_kernel, out_shape=[shape(CX, CY, z), shape(COMPS, C...]
    ppermute x6, waiting for transfers between devices: 6.65 us -> 3.1 us  [send(): return lax.ppermute(value, 'gx', [(i, (i + dx) % nx) for i in range(nx)])]
    ppermute x6, starting transfers between devices: 6.03 us -> 8.47 us  [send(): return lax.ppermute(value, 'gx', [(i, (i + dx) % nx) for i in range(nx)])]
    all_to_all x1 -> x2, blocking collectives: 19.8 us -> 20.5 us  [on_device(): parts = lax.all_to_all(copies, axis, 0, 0, tiled=True)]
  transfers between devices with their start and end apart: 12 -> 12, of which waited for: 7 -> 3; matrix products, arithmetic and copies ran while one was open for 5% -> 6% of each run, Pallas kernels for 16% -> 24%
where the time goes in v2:
time: 127 us
  Pallas kernels  60 us (47%)
  starting transfers between devices  26.1 us (21%)
  blocking collectives  20.5 us (16%)
  local copies, waits for them, and re-layouts  8.35 us (7%)
  waiting for transfers between devices  8.33 us (7%)
  other arithmetic  2.52 us (2%)
    pallas_call x1, Pallas kernels, extend(): pl.pallas_call(extend_kernel, out_shape=[shape(CX, CY, z), shape(COMPS, C...  22.6 us
    pallas_call x1, Pallas kernels, sweeps(): pl.pallas_call(sweep_kernel, out_shape=[shape(CX + 4, 2, ROWS, LANES), sh...  21.5 us
    all_to_all x2, blocking collectives, on_device(): parts = lax.all_to_all(copies, axis, 0, 0, tiled=True)  20.5 us
    ppermute x6, starting transfers between devices, send(): return lax.ppermute(value, 'gy', [(i, (i + dy) % ny) for i in range(ny)])  17.6 us
    pallas_call x1, Pallas kernels, inner_drift(): pl.pallas_call(inner_kernel, out_shape=jax.ShapeDtypeStruct(level.shape,...  9.59 us
    ppermute x6, starting transfers between devices, send(): return lax.ppermute(value, 'gx', [(i, (i + dx) % nx) for i in range(nx)])  8.47 us
    pallas_call x1, Pallas kernels, advect(): pl.pallas_call(advect_kernel, out_shape=[shape(CX, CY, z)] + [shape(8, CY...  6.41 us
    ppermute x6, waiting for transfers between devices, send(): return lax.ppermute(value, 'gy', [(i, (i + dy) % ny) for i in range(ny)])  5.23 us
  transfers between devices with their start and end apart: 12, of which 3 were waited for; matrix products, arithmetic and copies ran while one was open for 6% of the time, Pallas kernels for 24%

profile of v2, /device:TPU:0, one launch (start us, length us, event | category | flops | bytes accessed | tf_op | source)
XLA Modules:
  0.0 126.8 jit_solution(1434749113802467467)
XLA Ops:
  0.6 1.0 fusion.3
  1.6 2.5 %collective-permute-start.1 = (f32[3,32,256]{2,1,0:T(8,128)S(1)}, f32[3,32,256]{2,1,0:T(8,128)S(1)}, u32[]{:S(2)}, u32[]{:S(2)}) collective-permute-start(f32[3,32,256]{2,1,0:T(8,128)S(1)} %get-tuple-element.36), channel_id=1, source_target_pairs={{0,112},{16,0},{32,16},{48,32},{64,48},{80,64},{96,80},{112,96},{1... | collective-permute-start | bytes 294920 | tf_op jit(solution)/shard_map/ppermute | solution.py:563
  4.1 0.0 collective-permute-start
  4.1 1.1 fusion.2
  5.2 6.3 %collective-permute-start.3 = (f32[32,3,256]{2,1,0:T(4,128)S(1)}, f32[32,3,256]{2,1,0:T(4,128)S(1)}, u32[]{:S(2)}, u32[]{:S(2)}) collective-permute-start(f32[32,3,256]{2,1,0:T(4,128)S(1)} %get-tuple-element.34), channel_id=1, source_target_pairs={{0,15},{1,0},{2,1},{3,2},{4,3},{5,4},{6,5},{7,6},{8,7},{9,8},{10,9... | collective-permute-start | bytes 294920 | tf_op jit(solution)/shard_map/ppermute | solution.py:565
  11.5 0.0 collective-permute-start.2
  11.5 2.2 %fusion = (f32[6,32,2,256]{3,2,1,0:T(2,128)S(1)}, f32[6,32,2,256]{3,2,1,0:T(2,128)S(1)}) fusion(f32[6,32,32,256]{3,2,1,0:T(8,128)} %stress.1), kind=kLoop, calls=%fused_computation.14 | loop fusion | bytes 1572864 | tf_op jit(solution)/shard_map/slice | solution.py:586
  13.7 9.6 %inner_drift.1.drift = f32[32,32,256]{2,1,0:T(8,128)} custom-call(f32[32,32,256]{2,1,0:T(8,128)} %level.3, bf16[3,32,32,256]{3,2,1,0:T(8,128)(2,1)} %speed.3), custom_call_target="tpu_custom_call" | custom-call | flops 47185920 | bytes 3670016 | tf_op jit(solution)/shard_map/inner_drift/pallas_call | solution.py:130
  23.3 0.0 collective-permute-done.1.xhi
  23.3 0.0 copy-start.10
  23.3 0.0 collective-permute-done.xlo
  23.3 0.0 copy-start.11
  23.3 0.0 collective-permute-done.3.yhi
  23.4 0.0 copy-start.8
  23.4 0.0 collective-permute-done.2.ylo
  23.4 0.6 copy-done.10
  24.0 0.0 copy-done.11
  24.0 0.0 copy-done.8
  24.0 0.0 copy-start.9
  24.0 0.7 copy-done.9
  24.7 6.4 %advect.1 = (f32[32,32,256]{2,1,0:T(8,128)}, f32[8,32,256]{2,1,0:T(8,128)}, f32[8,32,256]{2,1,0:T(8,128)}, f32[32,8,256]{2,1,0:T(8,128)}, f32[32,8,256]{2,1,0:T(8,128)}) custom-call(s32[1,1,32]{2,1,0:T(1,128)} %tiles.3, f32[32,32,256]{2,1,0:T(8,128)} %level.3, f32[3,32,256]{2,1,0:T(8,128)} %copy-done.11, f32[3,32,256]{2,1,0:T(8,128)} %copy-done.10, ...), custom_call_target="tpu_custom_call" | custom-call | tf_op jit(solution)/shard_map/advect/pallas_call | solution.py:219
  31.1 0.0 collective-permute-start.4
  31.1 2.9 %collective-permute-start.5 = (f32[8,32,256]{2,1,0:T(8,128)}, f32[8,32,256]{2,1,0:T(8,128)S(1)}, u32[]{:S(2)}, u32[]{:S(2)}) collective-permute-start(f32[8,32,256]{2,1,0:T(8,128)} %get-tuple-element.18), channel_id=1, source_target_pairs={{0,112},{16,0},{32,16},{48,32},{64,48},{80,64},{96,80},{112,96},{1... | collective-permute-start | bytes 786440 | tf_op jit(solution)/shard_map/ppermute | solution.py:563
  34.1 1.2 fusion.1
  35.3 3.1 %collective-permute-done.4.xlo = f32[8,32,256]{2,1,0:T(8,128)S(1)} collective-permute-done((f32[8,32,256]{2,1,0:T(8,128)}, f32[8,32,256]{2,1,0:T(8,128)S(1)}, u32[]{:S(2)}, u32[]{:S(2)}) %collective-permute-start.4) | collective-permute-done | bytes 262176 | tf_op jit(solution)/shard_map/ppermute | solution.py:563
  38.4 0.0 copy-start
  38.4 0.0 collective-permute-done.5.xhi
  38.4 0.0 copy-start.1
  38.4 0.0 collective-permute-start.6
  38.4 2.9 %collective-permute-start.7 = (f32[6,2,32,256]{3,2,1,0:T(8,128)S(1)}, f32[6,2,32,256]{3,2,1,0:T(8,128)S(1)}, u32[]{:S(2)}, u32[]{:S(2)}) collective-permute-start(f32[6,2,32,256]{3,2,1,0:T(8,128)S(1)} %get-tuple-element.20), channel_id=1, source_target_pairs={{0,112},{16,0},{32,16},{48,32},{64,48},{80,64},{96,80},{112,96},{1... | collective-permute-start | bytes 1179656 | tf_op jit(solution)/shard_map/ppermute | solution.py:563
  41.3 0.1 slice_select_fusion
  41.4 1.0 pad_maximum_fusion.2
  42.4 0.1 collective-permute-start.8
  42.5 1.0 pad_maximum_fusion.3
  43.5 5.4 %collective-permute-start.9 = (f32[46,8,256]{2,1,0:T(8,128)S(1)}, f32[46,8,256]{2,1,0:T(8,128)S(1)}, u32[]{:S(2)}, u32[]{:S(2)}) collective-permute-start(f32[46,8,256]{2,1,0:T(8,128)S(1)} %pad_maximum_fusion.3), channel_id=1, source_target_pairs={{0,15},{1,0},{2,1},{3,2},{4,3},{5,4},{6,5},{7,6},{8,7},{9,8},{10,9... | collective-permute-start | bytes 1130504 | tf_op jit(solution)/shard_map/ppermute | solution.py:565
  48.9 0.0 collective-permute-done.6.xlo
  48.9 0.0 copy-start.2
  48.9 0.0 collective-permute-done.7.xhi
  48.9 0.0 copy-start.3
  49.0 0.5 pad_maximum_fusion
  49.4 4.9 %collective-permute-done.8.ylo = f32[46,8,256]{2,1,0:T(8,128)S(1)} collective-permute-done((f32[46,8,256]{2,1,0:T(8,128)S(1)}, f32[46,8,256]{2,1,0:T(8,128)S(1)}, u32[]{:S(2)}, u32[]{:S(2)}) %collective-permute-start.8) | collective-permute-done | bytes 376864 | tf_op jit(solution)/shard_map/ppermute | solution.py:565
  54.3 0.0 copy-start.6
  54.3 0.3 collective-permute-done.9.yhi
  54.6 0.0 copy-start.7
  54.6 0.0 collective-permute-start.10
  54.6 5.8 %collective-permute-start.11 = (f32[6,36,2,256]{3,2,1,0:T(2,128)S(1)}, f32[6,36,2,256]{3,2,1,0:T(2,128)S(1)}, u32[]{:S(2)}, u32[]{:S(2)}) collective-permute-start(f32[6,36,2,256]{3,2,1,0:T(2,128)S(1)} %get-tuple-element.29), channel_id=1, source_target_pairs={{0,15},{1,0},{2,1},{3,2},{4,3},{5,4},{6,5},{7,6},{8,7},{9,8},{10,9... | collective-permute-start | bytes 1327112 | tf_op jit(solution)/shard_map/ppermute | solution.py:565
  60.5 0.0 copy-done.6
  60.5 0.0 copy-done.7
  60.5 0.0 copy-done
  60.5 0.0 copy-done.1
  60.5 21.5 %sweeps.1 = (f32[36,2,64,128]{3,2,1,0:T(8,128)}, f32[34,2,64,128]{3,2,1,0:T(8,128)}, f32[1,128]{1,0:T(1,128)}) custom-call(s32[1,1,32]{2,1,0:T(1,128)} %tiles.3, f32[32,32,256]{2,1,0:T(8,128)} %get-tuple-element.16.adv, f32[8,32,256]{2,1,0:T(8,128)} %copy-done, f32[8,32,256]{2,1,0:T(8,128)} %copy-done.1, f32[46,8,256]{2,1,0:T(8,128)} %copy-done.6, ...), custom_call_target="tpu_custom_call" | custom-call | tf_op jit(solution)/shard_map/sweeps/pallas_call | solution.py:389
  81.9 0.7 broadcast_in_dim.79
  82.6 9.6 %all_to_all.10 = f32[8,1,128]{2,1,0:T(1,128)S(1)} all-to-all(f32[8,1,128]{2,1,0:T(1,128)S(1)} %broadcast_in_dim.79), channel_id=1, replica_groups=mesh['gx'=8,'gy'=16] {'gx'}, dimensions={0} | all-to-all | bytes 8192 | tf_op jit(solution)/shard_map/all_to_all | solution.py:593
  92.3 10.9 %all_to_all.11.parts = f32[16,1,128]{2,1,0:T(1,128)} all-to-all(f32[16,1,128]{2,1,0:T(1,128)S(1)} %broadcast_in_dim.80), channel_id=1, replica_groups=mesh['gx'=8,'gy'=16] {'gy'}, dimensions={0} | all-to-all | bytes 16384 | tf_op jit(solution)/shard_map/all_to_all | solution.py:593
  103.1 0.0 collective-permute-done.10.ylo
  103.1 0.0 copy-start.4
  103.1 0.0 collective-permute-done.11.yhi
  103.1 0.0 copy-start.5
  103.1 0.0 copy-done.2
  103.2 0.0 copy-done.3
  103.2 0.7 copy-done.4
  103.9 0.2 copy-done.5
  104.1 22.6 %extend.1 = (f32[32,32,256]{2,1,0:T(8,128)}, f32[6,32,32,256]{3,2,1,0:T(8,128)}) custom-call(f32[16,1,128]{2,1,0:T(1,128)} %all_to_all.11.parts, f32[36,2,64,128]{3,2,1,0:T(8,128)} %get-tuple-element.26.cur, f32[34,2,64,128]{3,2,1,0:T(8,128)} %get-tuple-element.27.weight, f32[6,32,32,256]{3,2,1,0:T(8,128)} %stress.1, f32[6,2,32,256]{3,2,1,0:T(8,128)} %copy-done.2, ...), custom_call_target="tpu_custom_call" | custom-call | tf_op jit(solution)/shard_map/extend/pallas_call | solution.py:540
  (7 shorter events, 0.1 us)
Async XLA Ops:
  1.6 21.7 %collective-permute-start.1 = (f32[3,32,256]{2,1,0:T(8,128)S(1)}, f32[3,32,256]{2,1,0:T(8,128)S(1)}, u32[]{:S(2)}, u32[]{:S(2)}) collective-permute-start(f32[3,32,256]{2,1,0:T(8,128)S(1)} %get-tuple-element.36), channel_id=1, source_target_pairs={{0,112},{16,0},{32,16},{48,32},{64,48},{80,64},{96,80},{112,96},{1... | collective-permute-start | bytes 294920 | tf_op jit(solution)/shard_map/ppermute | solution.py:563
  4.1 19.2 %collective-permute-start = (f32[3,32,256]{2,1,0:T(8,128)S(1)}, f32[3,32,256]{2,1,0:T(8,128)S(1)}, u32[]{:S(2)}, u32[]{:S(2)}) collective-permute-start(f32[3,32,256]{2,1,0:T(8,128)S(1)} %get-tuple-element.37), channel_id=1, source_target_pairs={{0,16},{16,32},{32,48},{48,64},{64,80},{80,96},{96,112},{112,0},{1... | collective-permute-start | bytes 294920 | tf_op jit(solution)/shard_map/ppermute | solution.py:563
  5.2 18.1 %collective-permute-start.3 = (f32[32,3,256]{2,1,0:T(4,128)S(1)}, f32[32,3,256]{2,1,0:T(4,128)S(1)}, u32[]{:S(2)}, u32[]{:S(2)}) collective-permute-start(f32[32,3,256]{2,1,0:T(4,128)S(1)} %get-tuple-element.34), channel_id=1, source_target_pairs={{0,15},{1,0},{2,1},{3,2},{4,3},{5,4},{6,5},{7,6},{8,7},{9,8},{10,9... | collective-permute-start | bytes 294920 | tf_op jit(solution)/shard_map/ppermute | solution.py:565
  11.5 11.8 %collective-permute-start.2 = (f32[32,3,256]{2,1,0:T(4,128)S(1)}, f32[32,3,256]{2,1,0:T(4,128)S(1)}, u32[]{:S(2)}, u32[]{:S(2)}) collective-permute-start(f32[32,3,256]{2,1,0:T(4,128)S(1)} %get-tuple-element.35), channel_id=1, source_target_pairs={{0,1},{1,2},{2,3},{3,4},{4,5},{5,6},{6,7},{7,8},{8,9},{9,10},{10,1... | collective-permute-start | bytes 294920 | tf_op jit(solution)/shard_map/ppermute | solution.py:565
  23.3 0.7 copy-start.10
  23.3 0.7 copy-start.11
  23.4 0.7 copy-start.8
  24.0 0.7 copy-start.9
  31.1 7.2 %collective-permute-start.4 = (f32[8,32,256]{2,1,0:T(8,128)}, f32[8,32,256]{2,1,0:T(8,128)S(1)}, u32[]{:S(2)}, u32[]{:S(2)}) collective-permute-start(f32[8,32,256]{2,1,0:T(8,128)} %get-tuple-element.17), channel_id=1, source_target_pairs={{0,16},{16,32},{32,48},{48,64},{64,80},{80,96},{96,112},{112,0},{1... | collective-permute-start | bytes 786440 | tf_op jit(solution)/shard_map/ppermute | solution.py:563
  31.1 7.2 %collective-permute-start.5 = (f32[8,32,256]{2,1,0:T(8,128)}, f32[8,32,256]{2,1,0:T(8,128)S(1)}, u32[]{:S(2)}, u32[]{:S(2)}) collective-permute-start(f32[8,32,256]{2,1,0:T(8,128)} %get-tuple-element.18), channel_id=1, source_target_pairs={{0,112},{16,0},{32,16},{48,32},{64,48},{80,64},{96,80},{112,96},{1... | collective-permute-start | bytes 786440 | tf_op jit(solution)/shard_map/ppermute | solution.py:563
  38.4 22.1 %copy-start = (f32[8,32,256]{2,1,0:T(8,128)}, f32[8,32,256]{2,1,0:T(8,128)S(1)}, u32[]{:S(2)}) copy-start(f32[8,32,256]{2,1,0:T(8,128)S(1)} %collective-permute-done.4.xlo) | copy-start | bytes 786436
  38.4 22.1 %copy-start.1 = (f32[8,32,256]{2,1,0:T(8,128)}, f32[8,32,256]{2,1,0:T(8,128)S(1)}, u32[]{:S(2)}) copy-start(f32[8,32,256]{2,1,0:T(8,128)S(1)} %collective-permute-done.5.xhi) | copy-start | bytes 786436
  38.4 10.5 %collective-permute-start.6 = (f32[6,2,32,256]{3,2,1,0:T(8,128)S(1)}, f32[6,2,32,256]{3,2,1,0:T(8,128)S(1)}, u32[]{:S(2)}, u32[]{:S(2)}) collective-permute-start(f32[6,2,32,256]{3,2,1,0:T(8,128)S(1)} %get-tuple-element.19), channel_id=1, source_target_pairs={{0,16},{16,32},{32,48},{48,64},{64,80},{80,96},{96,112},{112,0},{1... | collective-permute-start | bytes 1179656 | tf_op jit(solution)/shard_map/ppermute | solution.py:563
  38.4 10.5 %collective-permute-start.7 = (f32[6,2,32,256]{3,2,1,0:T(8,128)S(1)}, f32[6,2,32,256]{3,2,1,0:T(8,128)S(1)}, u32[]{:S(2)}, u32[]{:S(2)}) collective-permute-start(f32[6,2,32,256]{3,2,1,0:T(8,128)S(1)} %get-tuple-element.20), channel_id=1, source_target_pairs={{0,112},{16,0},{32,16},{48,32},{64,48},{80,64},{96,80},{112,96},{1... | collective-permute-start | bytes 1179656 | tf_op jit(solution)/shard_map/ppermute | solution.py:563
  42.4 11.9 %collective-permute-start.8 = (f32[46,8,256]{2,1,0:T(8,128)S(1)}, f32[46,8,256]{2,1,0:T(8,128)S(1)}, u32[]{:S(2)}, u32[]{:S(2)}) collective-permute-start(f32[46,8,256]{2,1,0:T(8,128)S(1)} %pad_maximum_fusion.2), channel_id=1, source_target_pairs={{0,1},{1,2},{2,3},{3,4},{4,5},{5,6},{6,7},{7,8},{8,9},{9,10},{10,1... | collective-permute-start | bytes 1130504 | tf_op jit(solution)/shard_map/ppermute | solution.py:565
  43.5 11.2 %collective-permute-start.9 = (f32[46,8,256]{2,1,0:T(8,128)S(1)}, f32[46,8,256]{2,1,0:T(8,128)S(1)}, u32[]{:S(2)}, u32[]{:S(2)}) collective-permute-start(f32[46,8,256]{2,1,0:T(8,128)S(1)} %pad_maximum_fusion.3), channel_id=1, source_target_pairs={{0,15},{1,0},{2,1},{3,2},{4,3},{5,4},{6,5},{7,6},{8,7},{9,8},{10,9... | collective-permute-start | bytes 1130504 | tf_op jit(solution)/shard_map/ppermute | solution.py:565
  48.9 54.3 %copy-start.2 = (f32[6,2,32,256]{3,2,1,0:T(8,128)}, f32[6,2,32,256]{3,2,1,0:T(8,128)S(1)}, u32[]{:S(2)}) copy-start(f32[6,2,32,256]{3,2,1,0:T(8,128)S(1)} %collective-permute-done.6.xlo) | copy-start | bytes 1179652
  48.9 54.2 %copy-start.3 = (f32[6,2,32,256]{3,2,1,0:T(8,128)}, f32[6,2,32,256]{3,2,1,0:T(8,128)S(1)}, u32[]{:S(2)}) copy-start(f32[6,2,32,256]{3,2,1,0:T(8,128)S(1)} %collective-permute-done.7.xhi) | copy-start | bytes 1179652
  54.3 6.1 %copy-start.6 = (f32[46,8,256]{2,1,0:T(8,128)}, f32[46,8,256]{2,1,0:T(8,128)S(1)}, u32[]{:S(2)}) copy-start(f32[46,8,256]{2,1,0:T(8,128)S(1)} %collective-permute-done.8.ylo) | copy-start | bytes 1130500
  54.6 5.8 %copy-start.7 = (f32[46,8,256]{2,1,0:T(8,128)}, f32[46,8,256]{2,1,0:T(8,128)S(1)}, u32[]{:S(2)}) copy-start(f32[46,8,256]{2,1,0:T(8,128)S(1)} %collective-permute-done.9.yhi) | copy-start | bytes 1130500
  54.6 48.5 %collective-permute-start.10 = (f32[6,36,2,256]{3,2,1,0:T(2,128)S(1)}, f32[6,36,2,256]{3,2,1,0:T(2,128)S(1)}, u32[]{:S(2)}, u32[]{:S(2)}) collective-permute-start(f32[6,36,2,256]{3,2,1,0:T(2,128)S(1)} %get-tuple-element.28), channel_id=1, source_target_pairs={{0,1},{1,2},{2,3},{3,4},{4,5},{5,6},{6,7},{7,8},{8,9},{9,10},{10,1... | collective-permute-start | bytes 1327112 | tf_op jit(solution)/shard_map/ppermute | solution.py:565
  54.6 48.5 %collective-permute-start.11 = (f32[6,36,2,256]{3,2,1,0:T(2,128)S(1)}, f32[6,36,2,256]{3,2,1,0:T(2,128)S(1)}, u32[]{:S(2)}, u32[]{:S(2)}) collective-permute-start(f32[6,36,2,256]{3,2,1,0:T(2,128)S(1)} %get-tuple-element.29), channel_id=1, source_target_pairs={{0,15},{1,0},{2,1},{3,2},{4,3},{5,4},{6,5},{7,6},{8,7},{9,8},{10,9... | collective-permute-start | bytes 1327112 | tf_op jit(solution)/shard_map/ppermute | solution.py:565
  103.1 0.8 copy-start.4
  103.1 0.9 copy-start.5

commit v3 on v2

--- a/solution.py
+++ b/solution.py
@@ -237,7 +237,7 @@
 
 
 def sweep_kernel(
-    tiles, adv, xlo, xhi, ylo, yhi,
+    tiles, adv, xlo, xhi, ylo, yhi, clo, chi,
     cur_out, weight_out, part,
     first, second, factor, masks, table, sums, sems,
 ):
@@ -247,8 +247,12 @@
             (adv, DEEP, CX, OWN, CY),
             (xlo.at[pl.ds(0, DEEP)], 0, DEEP, OWN, CY),
             (xhi.at[pl.ds(0, DEEP)], DEEP + CX, DEEP, OWN, CY),
-            (ylo, 0, WIDE, OWN - 8, 8),
-            (yhi, 0, WIDE, OWN + CY, 8),
+            (ylo, DEEP, CX, OWN - 8, 8),
+            (yhi, DEEP, CX, OWN + CY, 8),
+            (clo.at[pl.ds(0, DEEP)], 0, DEEP, OWN - 8, 8),
+            (clo.at[pl.ds(DEEP, DEEP)], DEEP + CX, DEEP, OWN - 8, 8),
+            (chi.at[pl.ds(0, DEEP)], 0, DEEP, OWN + CY, 8),
+            (chi.at[pl.ds(DEEP, DEEP)], DEEP + CX, DEEP, OWN + CY, 8),
         )
         for n, (src, x, nx, y, ny) in enumerate(pieces):
             copies.append(
@@ -261,7 +265,7 @@
         for n, src in enumerate((xlo, xhi)):
             copies.append(
                 pltpu.make_async_copy(
-                    src.at[pl.ds(DEEP, 1), :, half(h)], masks.at[pl.ds(n, 1), h], sems.at[h, 5 + n]
+                    src.at[pl.ds(DEEP, 1), :, half(h)], masks.at[pl.ds(n, 1), h], sems.at[h, 9 + n]
                 )
             )
     for copy in copies:
@@ -273,7 +277,6 @@
 
     def prepare(x, bands, keep):
         for h in range(2):
-            saved = {}
             for group in range(-1, 5):
                 rows = pl.ds(OWN + 8 * group, 8)
                 value = first[x, h, rows, :]
@@ -287,11 +290,8 @@
                 weight = band * recip(1.0 + square * (1.0 / 36.0))
                 sign = value * lax.rsqrt(square + 1.0)
                 factor[x, h, rows, :] = PSEUDO_STEP * sign * weight
-                saved[group] = weight
-            if keep:
-                saved[4] = jnp.where(row8 < 4, saved[4], saved[-1])
-                for group in range(5):
-                    weight_out[x - DEEP + 1, h, pl.ds(OWN + 8 * group, 8), :] = saved[group]
+                if keep:
+                    weight_out[x - DEEP + 1, h, rows, :] = weight
 
     def halo_bands(n):
         return lambda group, h: masks[n, h, pl.ds(8 * group, 8), :]
@@ -302,8 +302,6 @@
             return jnp.broadcast_to(table[r : r + 1, :], (8, LANES))
 
         return bands
-
-    row8 = lax.broadcasted_iota(jnp.int32, (8, LANES), 0)
 
     def run(start, stop, bands, keep):
         def body(x, carry):
@@ -319,19 +317,20 @@
     prepare(DEEP + CX, halo_bands(1), True)
     run(DEEP + CX + 1, WIDE - 1, halo_bands(1), False)
 
-    def sweep_plane(src, x):
-        for unit in range(3):
-            at = OWN - 8 + unit * UNIT
-            rows = pl.ds(at, UNIT)
-            center = [src[x, h, rows, :] for h in range(2)]
+    def sweep_plane(src, x, dst, y, groups):
+        start = OWN + CY // 2 - 4 * groups
+        rows = [pl.ds(start + k, 8, stride=groups) for k in range(-1, groups + 1)]
+        lines = [[src[x, h, r, :] for r in rows] for h in range(2)]
+        for k in range(1, groups + 1):
+            center = [lines[h][k] for h in range(2)]
             up, down = lane_shift(center, 1), lane_shift(center, -1)
             for h in range(2):
                 c = center[h]
-                step = factor[x, h, rows, :]
+                step = factor[x, h, rows[k], :]
                 positive = step > 0
                 pairs = (
-                    (src[x - 1, h, rows, :], src[x + 1, h, rows, :]),
-                    (src[x, h, pl.ds(at - 1, UNIT), :], src[x, h, pl.ds(at + 1, UNIT), :]),
+                    (src[x - 1, h, rows[k], :], src[x + 1, h, rows[k], :]),
+                    (lines[h][k - 1], lines[h][k + 1]),
                     (down[h], up[h]),
                 )
                 total = None
@@ -340,34 +339,19 @@
                     high = jnp.maximum(jnp.maximum(l, r), c)
                     diff = c - jnp.where(positive, low, high)
                     total = diff * diff if total is None else total + diff * diff
-                yield unit, h, c - step * (jnp.sqrt(total) - 1.0)
+                dst[y, h, rows[k], :] = c - step * (jnp.sqrt(total) - 1.0)
 
     source, target = first, second
-    for sweep in range(1, SWEEPS):
-
-        def body(x, carry, source=source, target=target):
-            for unit, h, value in sweep_plane(source, x):
-                target[x, h, pl.ds(OWN - 8 + unit * UNIT, UNIT), :] = value
+    for sweep in range(1, SWEEPS + 1):
+        offset, dst = (0, target) if sweep < SWEEPS else (SWEEPS, cur_out)
+        groups = 6 if DEEP - sweep > 4 else 5
+
+        def body(x, carry, source=source, dst=dst, offset=offset, groups=groups):
+            sweep_plane(source, x, dst, x - offset, groups)
             return carry
 
         lax.fori_loop(sweep, WIDE - sweep, body, 0, unroll=2)
         source, target = target, source
-
-    shift = SWEEPS
-
-    def last(x, carry):
-        values = [{}, {}]
-        for unit, h, value in sweep_plane(source, x):
-            values[h][2 * unit], values[h][2 * unit + 1] = value[:8], value[8:]
-        for h in range(2):
-            v = values[h]
-            v[5] = jnp.where(row8 < 4, v[5], v[0])
-            v[0], v[6] = v[5], v[1]
-            for n in range(7):
-                cur_out[x - shift, h, pl.ds(OWN - 8 + 8 * n, 8), :] = v[n]
-        return carry
-
-    lax.fori_loop(shift, WIDE - shift, last, 0, unroll=2)
 
     def count(x, carry):
         for h in range(2):
@@ -389,7 +373,7 @@
     return pl.pallas_call(
         sweep_kernel,
         out_shape=[shape(CX + 4, 2, ROWS, LANES), shape(CX + 2, 2, ROWS, LANES), shape(1, LANES)],
-        in_specs=[SMEM, VMEM] + [ANY] * 4,
+        in_specs=[SMEM, VMEM] + [ANY] * 6,
         out_specs=[VMEM] * 3,
         scratch_shapes=[
             pltpu.VMEM((WIDE, 2, ROWS, LANES), F32),
@@ -398,7 +382,7 @@
             pltpu.VMEM((2, 2, CY, LANES), F32),
             pltpu.VMEM((8, LANES), F32),
             pltpu.VMEM((2, UNIT, LANES), F32),
-            pltpu.SemaphoreType.DMA((2, 7)),
+            pltpu.SemaphoreType.DMA((2, 11)),
         ],
         compiler_params=pltpu.CompilerParams(vmem_limit_bytes=LIMIT),
         name="sweeps",
@@ -409,7 +393,7 @@
 
 
 def extend_kernel(
-    parts, cur, weight, stress, xlo, xhi, ylo, yhi,
+    parts, cur, weight, stress, xlo, xhi, ylo, yhi, clo, chi,
     level_out, stress_out,
     pad, ring, mix, stage, sems, out_sems,
 ):
@@ -420,42 +404,30 @@
             pieces.append((xlo, 0, 2))
         if n == len(CHUNKS) - 1:
             pieces.append((xhi, CX + 2, 2))
-        copies = []
-        for h in range(2):
-            for m, (src, at, size) in enumerate(pieces):
-                for k, (y, ny, row) in enumerate(((0, CY, OWN), (0, 8, OWN + CY + 8))):
-                    copies.append(
-                        pltpu.make_async_copy(
-                            src.at[:, :, pl.ds(y, ny), half(h)],
-                            pad.at[:, pl.ds(at, size), h, pl.ds(row, ny), :],
-                            sems.at[n, h, m, k],
-                        )
-                    )
-        return copies
+        return [
+            pltpu.make_async_copy(
+                src.at[:, :, :, half(h)],
+                pad.at[:, pl.ds(at, size), h, pl.ds(OWN, CY), :],
+                sems.at[n, h, m],
+            )
+            for h in range(2)
+            for m, (src, at, size) in enumerate(pieces)
+        ]
 
     chunks = [chunk(n) for n in range(len(CHUNKS))]
     for copies in chunks:
         for copy in copies:
             copy.start()
-    sums = jnp.sum(parts[...], axis=0)
+    sums = parts[...]
     shift = sums[:, 0:1] / sums[:, 64:65]
     for h in range(2):
         for c in range(COMPS):
-            low, high = ylo[c, :, :, half(h)], yhi[c, :, :, half(h)]
-            pad[c, :, h, OWN - 2 : OWN, :] = low
-            pad[c, :, h, OWN + CY + 6 : OWN + CY + 8, :] = low
-            pad[c, :, h, OWN + CY : OWN + CY + 2, :] = high
-
-    def neighbours(load, at):
-        center = [load(0, h, at) for h in range(2)]
-        up, down = lane_shift(center, 1), lane_shift(center, -1)
-        return center, [
-            [
-                load(-1, h, at), load(1, h, at), load(0, h, at - 1), load(0, h, at + 1),
-                down[h], up[h],
-            ]
-            for h in range(2)
-        ]
+            pad[c, 2 : CX + 2, h, OWN - 2 : OWN, :] = ylo[c, :, :, half(h)]
+            pad[c, 2 : CX + 2, h, OWN + CY : OWN + CY + 2, :] = yhi[c, :, :, half(h)]
+            for corner, row in ((clo, OWN - 1), (chi, OWN + CY)):
+                for x, n in ((1, c), (CX + 2, COMPS + c)):
+                    at = 2 * DEEP + n // 8
+                    pad[c, x, h, row : row + 1, :] = corner[at, n % 8 : n % 8 + 1, half(h)]
 
     def blend(mixes, center, around):
         value = mixes[6] * center
@@ -463,11 +435,28 @@
             value = value + mixes[n] * around[n]
         return value
 
+    def neighbours(load, groups):
+        start = OWN + CY // 2 - 4 * groups
+        rows = [pl.ds(start + k, 8, stride=groups) for k in range(-1, groups + 1)]
+        lines = [[load(0, h, r) for r in rows] for h in range(2)]
+        for k in range(1, groups + 1):
+            center = [lines[h][k] for h in range(2)]
+            up, down = lane_shift(center, 1), lane_shift(center, -1)
+            yield rows[k], center, [
+                [
+                    load(-1, h, rows[k]), load(1, h, rows[k]), lines[h][k - 1], lines[h][k + 1],
+                    down[h], up[h],
+                ]
+                for h in range(2)
+            ]
+
     def first_step(i, slot, groups=5):
-        for group in range(groups):
-            at = OWN + 8 * group
-            rows = pl.ds(at, 8)
-            center, around = neighbours(lambda dx, h, r: cur[i + 1 + dx, h, pl.ds(r, 8), :], at)
+        levels = neighbours(lambda dx, h, r: cur[i + 1 + dx, h, r, :], groups)
+        comps = [
+            neighbours(lambda dx, h, r, c=c: pad[c, i + 1 + dx, h, r, :], groups)
+            for c in range(COMPS)
+        ]
+        for rows, center, around in levels:
             mixes = []
             for h in range(2):
                 c = center[h]
@@ -480,34 +469,31 @@
                 scaled = gate * recip(total)
                 w = [scaled * n for n in w] + [1.0 - gate]
                 mixes.append(w)
-                if group < 4:
-                    for n in range(7):
-                        mix[slot % 2, n, h, rows, :] = w[n]
+                for n in range(7):
+                    mix[slot % 2, n, h, rows, :] = w[n]
             for comp in range(COMPS):
-                center, around = neighbours(
-                    lambda dx, h, r: pad[comp, i + 1 + dx, h, pl.ds(r, 8), :], at
-                )
+                _, center, around = next(comps[comp])
                 for h in range(2):
-                    value = blend(mixes[h], center[h], around[h])
-                    ring[slot, comp, h, rows, :] = value
-                    if group == 4:
-                        ring[slot, comp, h, pl.ds(OWN - 8, 8), :] = value
+                    ring[slot, comp, h, rows, :] = blend(mixes[h], center[h], around[h])
 
     def second_step(x, slot):
         slots = {dx: (slot + dx) % 4 for dx in (-1, 0, 1)}
-        for group in range(CY // 8):
-            at = OWN + 8 * group
-            rows = pl.ds(at, 8)
-            own = pl.ds(8 * group, 8)
+        groups = CY // 8
+        comps = [
+            neighbours(lambda dx, h, r, c=c: ring[slots[dx], c, h, r, :], groups)
+            for c in range(COMPS)
+        ]
+        for k in range(groups):
+            rows = pl.ds(OWN + k, 8, stride=groups)
             mixes = [[mix[slot % 2, n, h, rows, :] for n in range(7)] for h in range(2)]
             for comp in range(COMPS):
-                center, around = neighbours(
-                    lambda dx, h, r: ring[slots[dx], comp, h, pl.ds(r, 8), :], at
-                )
+                _, center, around = next(comps[comp])
                 for h in range(2):
-                    stage[comp, x, own, half(h)] = blend(mixes[h], center[h], around[h])
-            for h in range(2):
-                level_out[x, own, half(h)] = cur[x + 2, h, rows, :] - shift
+                    stage[comp, x, h, pl.ds(k, 8, stride=groups), :] = blend(
+                        mixes[h], center[h], around[h]
+                    )
+        for h in range(2):
+            level_out[x, :, half(h)] = cur[x + 2, h, OWN : OWN + CY, :] - shift
 
     outs = []
     for n in range(len(CHUNKS)):
@@ -526,10 +512,12 @@
 
         lax.fori_loop(2 * n, 2 * n + 2, body, 0)
         planes = pl.ds(8 * n, 8)
-        outs.append(
-            pltpu.make_async_copy(stage.at[:, planes], stress_out.at[:, planes], out_sems.at[n])
-        )
-        outs[-1].start()
+        for h in range(2):
+            copy = pltpu.make_async_copy(
+                stage.at[:, planes, h], stress_out.at[:, planes, :, half(h)], out_sems.at[n, h]
+            )
+            copy.start()
+            outs.append(copy)
     for copy in outs:
         copy.wait()
 
@@ -540,15 +528,15 @@
     return pl.pallas_call(
         extend_kernel,
         out_shape=[shape(CX, CY, z), shape(COMPS, CX, CY, z)],
-        in_specs=[VMEM, VMEM, VMEM, ANY, ANY, ANY, VMEM, VMEM],
+        in_specs=[VMEM, VMEM, VMEM, ANY, ANY, ANY, VMEM, VMEM, VMEM, VMEM],
         out_specs=[VMEM, ANY],
         scratch_shapes=[
             pltpu.VMEM((COMPS, CX + 4, 2, ROWS, LANES), F32),
             pltpu.VMEM((4, COMPS, 2, ROWS, LANES), F32),
             pltpu.VMEM((2, 7, 2, ROWS, LANES), F32),
-            pltpu.VMEM((COMPS, CX, CY, z), F32),
-            pltpu.SemaphoreType.DMA((4, 2, 2, 2)),
-            pltpu.SemaphoreType.DMA((4,)),
+            pltpu.VMEM((COMPS, CX, 2, CY, LANES), F32),
+            pltpu.SemaphoreType.DMA((4, 2, 2)),
+            pltpu.SemaphoreType.DMA((4, 2)),
         ],
         compiler_params=pltpu.CompilerParams(vmem_limit_bytes=LIMIT),
         name="extend",
@@ -568,31 +556,43 @@
         ]
         return lax.ppermute(value, ("gx", "gy"), pairs)
 
+    def total(value):
+        rounds = (
+            ("gx", [[i ^ 1 for i in range(nx)]]),
+            ("gx", [[(i + 2 * k) % nx for i in range(nx)] for k in range(1, nx // 2)]),
+            ("gy", [[i // 4 * 4 + (i + k) % 4 for i in range(ny)] for k in range(1, 4)]),
+            ("gy", [[(i + 4 * k) % ny for i in range(ny)] for k in range(1, ny // 4)]),
+        )
+        for axis, moves in rounds:
+            moved = [lax.ppermute(value, axis, list(enumerate(move))) for move in moves]
+            for other in moved:
+                value = value + other
+        return value
+
     xlo = send(level[-3:], 1, 0)
     xhi = send(level[:3], -1, 0)
     ylo = send(level[:, -3:], 0, 1)
     yhi = send(level[:, :3], 0, -1)
+    sxlo, sxhi = send(stress[:, -2:], 1, 0), send(stress[:, :2], -1, 0)
+    sylo, syhi = send(stress[:, :, -2:], 0, 1), send(stress[:, :, :2], 0, -1)
     drift = inner_drift(level, velocity)
     adv, to_xp, to_xn, to_yp, to_yn = advect(tiles, level, xlo, xhi, ylo, yhi, velocity, drift)
     axlo, axhi = send(to_xn, 1, 0), send(to_xp, -1, 0)
+    aylo, ayhi = send(to_yn, 0, 1), send(to_yp, 0, -1)
     row = lax.broadcasted_iota(jnp.int32, (1, 8, 1), 1)
-    low = lambda face: jnp.where(row == 7, face[DEEP:, :8], face[:DEEP, :8])
-    high = lambda face: jnp.where(row == 0, face[DEEP:, -8:], face[:DEEP, -8:])
-    aylo = send(jnp.concatenate((high(axlo), to_yn, high(axhi)), axis=0), 0, 1)
-    ayhi = send(jnp.concatenate((low(axlo), to_yp, low(axhi)), axis=0), 0, -1)
-    faces = (stress[:, -2:], stress[:, :2])
-    faces, _, _ = lax.optimization_barrier((faces, axlo, axhi))
-    sxlo, sxhi = send(faces[0], 1, 0), send(faces[1], -1, 0)
-    edge = lambda s: jnp.concatenate((sxlo[:, :, s], stress[:, :, s], sxhi[:, :, s]), axis=1)
-    edges = (edge(slice(-2, None)), edge(slice(0, 2)))
-    edges, aylo, ayhi = lax.optimization_barrier((edges, aylo, ayhi))
-    sylo, syhi = send(edges[0], 0, 1), send(edges[1], 0, -1)
-    cur, weight, part = sweeps(tiles, adv, (axlo, axhi, aylo, ayhi))
-    for axis, count in (("gx", nx), ("gy", ny)):
-        copies = jnp.broadcast_to(part[None], (count, 1, LANES))
-        parts = lax.all_to_all(copies, axis, 0, 0, tiled=True)
-        part = jnp.sum(parts, axis=0)
-    return extend(parts, cur, weight, stress, (sxlo, sxhi, sylo, syhi))
+    none = jnp.zeros((4, 2 * LANES), F32)
+
+    def corners(rows, mark, y):
+        faces = [jnp.where(row == mark, f[DEEP:, rows], f[:DEEP, rows]) for f in (axlo, axhi)]
+        tail = jnp.concatenate((sxlo[:, 1, y], sxhi[:, 0, y], none), axis=0)
+        return jnp.concatenate(faces + [tail.reshape(2, 8, 2 * LANES)], axis=0)
+
+    clo = send(corners(slice(-8, None), 0, CY - 1), 0, 1)
+    chi = send(corners(slice(0, 8), 7, 0), 0, -1)
+    cur, weight, part = sweeps(tiles, adv, (axlo, axhi, aylo, ayhi, clo, chi))
+    return extend(
+        total(part), cur, weight, stress, (sxlo, sxhi, sylo, syhi, clo, chi)
+    )
 
 
 def solution(mesh):

time: 127 us -> 127 us (level)
  blocking collectives: 20.5 us -> 0 us
  starting transfers between devices: 26.1 us -> 38.6 us
  waiting for transfers between devices: 8.33 us -> 18.3 us
  Pallas kernels: 60 us -> 58.3 us
    all_to_all x2 -> x0, blocking collectives: 20.5 us -> none  [on_device(): parts = lax.all_to_all(copies, axis, 0, 0, tiled=True)]
    ppermute x0 -> x10, waiting for transfers between devices: none -> 9.33 us  [total(): moved = [lax.ppermute(value, axis, list(enumerate(move))) for move in moves]]
    ppermute x6 -> x8, starting transfers between devices: 17.6 us -> 23.9 us  [send(): return lax.ppermute(value, 'gy', [(i, (i + dy) % ny) for i in range(ny)])]
    ppermute x0 -> x10, starting transfers between devices: none -> 6.24 us  [total(): moved = [lax.ppermute(value, axis, list(enumerate(move))) for move in moves]]
    ppermute x6 -> x8, waiting for transfers between devices: 5.23 us -> 7.76 us  [send(): return lax.ppermute(value, 'gy', [(i, (i + dy) % ny) for i in range(ny)])]
    concatenate x3 -> x2, other arithmetic: 2.41 us -> 0.02 us  [corners(): return jnp.concatenate(faces + [tail.reshape(2, 8, 2 * LANES)], axis=0)]
    ppermute x6, waiting for transfers between devices: 3.1 us -> 1.17 us  [send(): return lax.ppermute(value, 'gx', [(i, (i + dx) % nx) for i in range(nx)])]
    unnamed x24 -> x29, local copies, waits for them, and re-layouts: 2.25 us -> 2.99 us
  transfers between devices with their start and end apart: 12 -> 24, of which waited for: 3 -> 8; matrix products, arithmetic and copies ran while one was open for 6% -> 5% of each run, Pallas kernels for 24% -> 8%
where the time goes in v3:
time: 127 us
  Pallas kernels  58.3 us (46%)
  starting transfers between devices  38.6 us (30%)
  waiting for transfers between devices  18.3 us (14%)
  local copies, waits for them, and re-layouts  9.34 us (7%)
  other arithmetic  1.37 us (1%)
    ppermute x8, starting transfers between devices, send(): return lax.ppermute(value, 'gy', [(i, (i + dy) % ny) for i in range(ny)])  23.9 us
    pallas_call x1, Pallas kernels, extend(): pl.pallas_call(extend_kernel, out_shape=[shape(CX, CY, z), shape(COMPS, C...  21.7 us
    pallas_call x1, Pallas kernels, sweeps(): pl.pallas_call(sweep_kernel, out_shape=[shape(CX + 4, 2, ROWS, LANES), sh...  20.5 us
    pallas_call x1, Pallas kernels, inner_drift(): pl.pallas_call(inner_kernel, out_shape=jax.ShapeDtypeStruct(level.shape,...  9.59 us
    ppermute x10, waiting for transfers between devices, total(): moved = [lax.ppermute(value, axis, list(enumerate(move))) for move in moves]  9.33 us
    ppermute x6, starting transfers between devices, send(): return lax.ppermute(value, 'gx', [(i, (i + dx) % nx) for i in range(nx)])  8.48 us
    ppermute x8, waiting for transfers between devices, send(): return lax.ppermute(value, 'gy', [(i, (i + dy) % ny) for i in range(ny)])  7.76 us
    pallas_call x1, Pallas kernels, advect(): pl.pallas_call(advect_kernel, out_shape=[shape(CX, CY, z)] + [shape(8, CY...  6.43 us
  transfers between devices with their start and end apart: 24, of which 8 were waited for; matrix products, arithmetic and copies ran while one was open for 5% of the time, Pallas kernels for 8%

profile of v3, /device:TPU:0, one launch (start us, length us, event | category | flops | bytes accessed | tf_op | source)
XLA Modules:
  0.0 126.9 jit_solution(159682127787146646)
XLA Ops:
  0.6 1.0 fusion.3
  1.6 2.5 %collective-permute-start.1 = (f32[3,32,256]{2,1,0:T(8,128)S(1)}, f32[3,32,256]{2,1,0:T(8,128)S(1)}, u32[]{:S(2)}, u32[]{:S(2)}) collective-permute-start(f32[3,32,256]{2,1,0:T(8,128)S(1)} %get-tuple-element.24), channel_id=1, source_target_pairs={{0,112},{16,0},{32,16},{48,32},{64,48},{80,64},{96,80},{112,96},{1... | collective-permute-start | bytes 294920 | tf_op jit(solution)/shard_map/ppermute | solution.py:551
  4.1 0.0 collective-permute-start
  4.1 1.1 fusion.2
  5.2 6.3 %collective-permute-start.3 = (f32[32,3,256]{2,1,0:T(4,128)S(1)}, f32[32,3,256]{2,1,0:T(4,128)S(1)}, u32[]{:S(2)}, u32[]{:S(2)}) collective-permute-start(f32[32,3,256]{2,1,0:T(4,128)S(1)} %get-tuple-element.22), channel_id=1, source_target_pairs={{0,15},{1,0},{2,1},{3,2},{4,3},{5,4},{6,5},{7,6},{8,7},{9,8},{10,9... | collective-permute-start | bytes 294920 | tf_op jit(solution)/shard_map/ppermute | solution.py:553
  11.5 0.0 collective-permute-start.2
  11.5 9.6 %inner_drift.1.drift = f32[32,32,256]{2,1,0:T(8,128)} custom-call(f32[32,32,256]{2,1,0:T(8,128)} %level.3, bf16[3,32,32,256]{3,2,1,0:T(8,128)(2,1)} %speed.3), custom_call_target="tpu_custom_call" | custom-call | flops 47185920 | bytes 3670016 | tf_op jit(solution)/shard_map/inner_drift/pallas_call | solution.py:130
  21.1 0.0 collective-permute-done.1.xhi
  21.1 0.0 collective-permute-done.xlo
  21.2 0.0 collective-permute-done.3.yhi
  21.2 0.0 collective-permute-done.2.ylo
  21.2 0.6 copy-done.11
  21.8 0.0 copy-done.12
  21.8 0.0 copy-done.9
  21.9 0.6 copy-done.10
  22.5 6.4 %advect.1 = (f32[32,32,256]{2,1,0:T(8,128)}, f32[8,32,256]{2,1,0:T(8,128)}, f32[8,32,256]{2,1,0:T(8,128)}, f32[32,8,256]{2,1,0:T(8,128)}, f32[32,8,256]{2,1,0:T(8,128)}) custom-call(s32[1,1,32]{2,1,0:T(1,128)} %tiles.3, f32[32,32,256]{2,1,0:T(8,128)} %level.3, f32[3,32,256]{2,1,0:T(8,128)} %copy-done.12, f32[3,32,256]{2,1,0:T(8,128)} %copy-done.11, ...), custom_call_target="tpu_custom_call" | custom-call | tf_op jit(solution)/shard_map/advect/pallas_call | solution.py:219
  28.9 0.0 collective-permute-start.4
  29.0 1.2 fusion.1
  30.1 2.9 %collective-permute-start.9 = (f32[6,2,32,256]{3,2,1,0:T(8,128)S(1)}, f32[6,2,32,256]{3,2,1,0:T(8,128)S(1)}, u32[]{:S(2)}, u32[]{:S(2)}) collective-permute-start(f32[6,2,32,256]{3,2,1,0:T(8,128)S(1)} %get-tuple-element.21), channel_id=1, source_target_pairs={{0,112},{16,0},{32,16},{48,32},{64,48},{80,64},{96,80},{112,96},{1... | collective-permute-start | bytes 1179656 | tf_op jit(solution)/shard_map/ppermute | solution.py:551
  33.1 0.2 copy.10
  33.3 0.0 collective-permute-start.8
  33.4 2.9 %collective-permute-start.5 = (f32[8,32,256]{2,1,0:T(8,128)}, f32[8,32,256]{2,1,0:T(8,128)S(1)}, u32[]{:S(2)}, u32[]{:S(2)}) collective-permute-start(f32[8,32,256]{2,1,0:T(8,128)} %get-tuple-element.12), channel_id=1, source_target_pairs={{0,112},{16,0},{32,16},{48,32},{64,48},{80,64},{96,80},{112,96},{1... | collective-permute-start | bytes 786440 | tf_op jit(solution)/shard_map/ppermute | solution.py:551
  36.3 0.1 pad.11.clone
  36.4 0.0 collective-permute-start.6
  36.4 0.0 collective-permute-done.4.xlo
  36.4 0.0 copy-start
  36.4 5.4 %collective-permute-start.7 = (f32[32,8,256]{2,1,0:T(8,128)}, f32[32,8,256]{2,1,0:T(8,128)S(1)}, u32[]{:S(2)}, u32[]{:S(2)}) collective-permute-start(f32[32,8,256]{2,1,0:T(8,128)} %get-tuple-element.14), channel_id=1, source_target_pairs={{0,15},{1,0},{2,1},{3,2},{4,3},{5,4},{6,5},{7,6},{8,7},{9,8},{10,9... | collective-permute-start | bytes 786440 | tf_op jit(solution)/shard_map/ppermute | solution.py:553
  41.8 0.0 collective-permute-done.5.xhi
  41.9 0.1 slice_select_fusion
  42.0 1.2 collective-permute-done.8
  43.2 0.1 maximum_bitcast_fusion.1
  43.3 0.1 collective-permute-start.10
  43.4 5.4 %collective-permute-start.11 = (f32[16,8,256]{2,1,0:T(8,128)S(1)}, f32[16,8,256]{2,1,0:T(8,128)S(1)}, u32[]{:S(2)}, u32[]{:S(2)}) collective-permute-start(f32[16,8,256]{2,1,0:T(8,128)S(1)} %pad_maximum_fusion.1), channel_id=1, source_target_pairs={{0,15},{1,0},{2,1},{3,2},{4,3},{5,4},{6,5},{7,6},{8,7},{9,8},{10,9... | collective-permute-start | bytes 393224 | tf_op jit(solution)/shard_map/ppermute | solution.py:553
  48.8 0.0 collective-permute-done.6.ylo
  48.8 0.0 collective-permute-done.7.yhi
  48.8 2.8 %collective-permute-done.10.clo = f32[16,8,256]{2,1,0:T(8,128)S(1)} collective-permute-done((f32[16,8,256]{2,1,0:T(8,128)S(1)}, f32[16,8,256]{2,1,0:T(8,128)S(1)}, u32[]{:S(2)}, u32[]{:S(2)}) %collective-permute-start.10) | collective-permute-done | bytes 131104 | tf_op jit(solution)/shard_map/ppermute | solution.py:553
  51.7 0.6 copy-done.2
  52.3 0.1 copy-done.3
  52.3 20.5 %sweeps.1 = (f32[36,2,64,128]{3,2,1,0:T(8,128)}, f32[34,2,64,128]{3,2,1,0:T(8,128)}, f32[1,128]{1,0:T(1,128)}) custom-call(s32[1,1,32]{2,1,0:T(1,128)} %tiles.3, f32[32,32,256]{2,1,0:T(8,128)} %get-tuple-element.10.adv, f32[8,32,256]{2,1,0:T(8,128)} %copy-done, f32[8,32,256]{2,1,0:T(8,128)} %copy-done.1, f32[32,8,256]{2,1,0:T(8,128)} %copy-done.7, ...), custom_call_target="tpu_custom_call" | custom-call | tf_op jit(solution)/shard_map/sweeps/pallas_call | solution.py:373
  72.9 0.1 collective-permute-start.12
  73.0 1.3 %collective-permute-done.12 = f32[1,128]{1,0:T(1,128)S(1)} collective-permute-done((f32[1,128]{1,0:T(1,128)}, f32[1,128]{1,0:T(1,128)S(1)}, u32[]{:S(2)}, u32[]{:S(2)}) %collective-permute-start.12) | collective-permute-done | bytes 544 | tf_op jit(solution)/shard_map/ppermute | solution.py:567
  74.3 0.6 add.30
  74.9 0.8 collective-permute-start.15
  75.7 0.0 collective-permute-start.14
  75.7 1.2 collective-permute-start.13
  76.9 1.5 %collective-permute-done.15 = f32[1,128]{1,0:T(1,128)S(1)} collective-permute-done((f32[1,128]{1,0:T(1,128)S(1)}, f32[1,128]{1,0:T(1,128)S(1)}, u32[]{:S(2)}, u32[]{:S(2)}) %collective-permute-start.15) | collective-permute-done | bytes 544 | tf_op jit(solution)/shard_map/ppermute | solution.py:567
  78.4 2.4 %collective-permute-done.14 = f32[1,128]{1,0:T(1,128)S(1)} collective-permute-done((f32[1,128]{1,0:T(1,128)S(1)}, f32[1,128]{1,0:T(1,128)S(1)}, u32[]{:S(2)}, u32[]{:S(2)}) %collective-permute-start.14) | collective-permute-done | bytes 544 | tf_op jit(solution)/shard_map/ppermute | solution.py:567
  80.8 0.3 collective-permute-done.13
  81.1 0.8 collective-permute-start.18
  81.9 0.0 collective-permute-start.17
  81.9 1.3 collective-permute-start.16
  83.1 2.2 %fusion = (f32[6,32,2,256]{3,2,1,0:T(2,128)S(1)}, f32[6,32,2,256]{3,2,1,0:T(2,128)S(1)}) fusion(f32[6,32,32,256]{3,2,1,0:T(8,128)} %stress.1), kind=kLoop, calls=%fused_computation.21 | loop fusion | bytes 1572864 | tf_op jit(solution)/shard_map/slice | solution.py:577
  85.3 6.7 %collective-permute-start.23 = (f32[6,32,2,256]{3,2,1,0:T(2,128)S(1)}, f32[6,32,2,256]{3,2,1,0:T(2,128)S(1)}, u32[]{:S(2)}, u32[]{:S(2)}) collective-permute-start(f32[6,32,2,256]{3,2,1,0:T(2,128)S(1)} %get-tuple-element.18), channel_id=1, source_target_pairs={{0,15},{1,0},{2,1},{3,2},{4,3},{5,4},{6,5},{7,6},{8,7},{9,8},{10,9... | collective-permute-start | bytes 1179656 | tf_op jit(solution)/shard_map/ppermute | solution.py:553
  92.0 0.0 collective-permute-done.16
  92.0 1.0 collective-permute-start.21
  93.0 1.1 collective-permute-start.19
  94.1 0.9 copy.8.xlo
  95.0 3.8 %collective-permute-done.21 = f32[1,128]{1,0:T(1,128)S(1)} collective-permute-done((f32[1,128]{1,0:T(1,128)S(1)}, f32[1,128]{1,0:T(1,128)S(1)}, u32[]{:S(2)}, u32[]{:S(2)}) %collective-permute-start.21) | collective-permute-done | bytes 544 | tf_op jit(solution)/shard_map/ppermute | solution.py:567
  98.8 0.0 collective-permute-done.20
  98.8 0.0 collective-permute-done.19
  98.8 0.6 add_add_fusion.parts
  99.4 4.9 %collective-permute-done.22.ylo = f32[6,32,2,256]{3,2,1,0:T(2,128)S(1)} collective-permute-done((f32[6,32,2,256]{3,2,1,0:T(2,128)S(1)}, f32[6,32,2,256]{3,2,1,0:T(2,128)S(1)}, u32[]{:S(2)}, u32[]{:S(2)}) %collective-permute-start.22) | collective-permute-done | bytes 393248 | tf_op jit(solution)/shard_map/ppermute | solution.py:553
  104.3 0.7 copy-done.6
  105.0 21.7 %extend.1 = (f32[32,32,256]{2,1,0:T(8,128)}, f32[6,32,32,256]{3,2,1,0:T(8,128)}) custom-call(f32[1,128]{1,0:T(1,128)} %add_add_fusion.parts, f32[36,2,64,128]{3,2,1,0:T(8,128)} %get-tuple-element.16.cur, f32[34,2,64,128]{3,2,1,0:T(8,128)} %get-tuple-element.17.weight, f32[6,32,32,256]{3,2,1,0:T(8,128)} %stress.1, f32[6,2,32,256]{3,2,1,0:T(8,128)} %copy.8.xlo, ...), custom_call_target="tpu_custom_call" | custom-call | tf_op jit(solution)/shard_map/extend/pallas_call | solution.py:528
  (37 shorter events, 0.1 us)
Async XLA Ops:
  1.6 19.5 %collective-permute-start.1 = (f32[3,32,256]{2,1,0:T(8,128)S(1)}, f32[3,32,256]{2,1,0:T(8,128)S(1)}, u32[]{:S(2)}, u32[]{:S(2)}) collective-permute-start(f32[3,32,256]{2,1,0:T(8,128)S(1)} %get-tuple-element.24), channel_id=1, source_target_pairs={{0,112},{16,0},{32,16},{48,32},{64,48},{80,64},{96,80},{112,96},{1... | collective-permute-start | bytes 294920 | tf_op jit(solution)/shard_map/ppermute | solution.py:551
  4.1 17.0 %collective-permute-start = (f32[3,32,256]{2,1,0:T(8,128)S(1)}, f32[3,32,256]{2,1,0:T(8,128)S(1)}, u32[]{:S(2)}, u32[]{:S(2)}) collective-permute-start(f32[3,32,256]{2,1,0:T(8,128)S(1)} %get-tuple-element.25), channel_id=1, source_target_pairs={{0,16},{16,32},{32,48},{48,64},{64,80},{80,96},{96,112},{112,0},{1... | collective-permute-start | bytes 294920 | tf_op jit(solution)/shard_map/ppermute | solution.py:551
  5.2 15.9 %collective-permute-start.3 = (f32[32,3,256]{2,1,0:T(4,128)S(1)}, f32[32,3,256]{2,1,0:T(4,128)S(1)}, u32[]{:S(2)}, u32[]{:S(2)}) collective-permute-start(f32[32,3,256]{2,1,0:T(4,128)S(1)} %get-tuple-element.22), channel_id=1, source_target_pairs={{0,15},{1,0},{2,1},{3,2},{4,3},{5,4},{6,5},{7,6},{8,7},{9,8},{10,9... | collective-permute-start | bytes 294920 | tf_op jit(solution)/shard_map/ppermute | solution.py:553
  11.5 9.7 %collective-permute-start.2 = (f32[32,3,256]{2,1,0:T(4,128)S(1)}, f32[32,3,256]{2,1,0:T(4,128)S(1)}, u32[]{:S(2)}, u32[]{:S(2)}) collective-permute-start(f32[32,3,256]{2,1,0:T(4,128)S(1)} %get-tuple-element.23), channel_id=1, source_target_pairs={{0,1},{1,2},{2,3},{3,4},{4,5},{5,6},{6,7},{7,8},{8,9},{9,10},{10,1... | collective-permute-start | bytes 294920 | tf_op jit(solution)/shard_map/ppermute | solution.py:553
  21.1 0.6 copy-start.11
  21.2 0.7 copy-start.12
  21.2 0.7 copy-start.9
  21.9 0.6 copy-start.10
  28.9 7.5 %collective-permute-start.4 = (f32[8,32,256]{2,1,0:T(8,128)}, f32[8,32,256]{2,1,0:T(8,128)S(1)}, u32[]{:S(2)}, u32[]{:S(2)}) collective-permute-start(f32[8,32,256]{2,1,0:T(8,128)} %get-tuple-element.11), channel_id=1, source_target_pairs={{0,16},{16,32},{32,48},{48,64},{64,80},{80,96},{96,112},{112,0},{1... | collective-permute-start | bytes 786440 | tf_op jit(solution)/shard_map/ppermute | solution.py:551
  30.1 11.8 %collective-permute-start.9 = (f32[6,2,32,256]{3,2,1,0:T(8,128)S(1)}, f32[6,2,32,256]{3,2,1,0:T(8,128)S(1)}, u32[]{:S(2)}, u32[]{:S(2)}) collective-permute-start(f32[6,2,32,256]{3,2,1,0:T(8,128)S(1)} %get-tuple-element.21), channel_id=1, source_target_pairs={{0,112},{16,0},{32,16},{48,32},{64,48},{80,64},{96,80},{112,96},{1... | collective-permute-start | bytes 1179656 | tf_op jit(solution)/shard_map/ppermute | solution.py:551
  33.3 9.8 %collective-permute-start.8 = (f32[6,2,32,256]{3,0,2,1:T(8,128)S(1)}, f32[6,2,32,256]{3,0,2,1:T(8,128)S(1)}, u32[]{:S(2)}, u32[]{:S(2)}) collective-permute-start(f32[6,2,32,256]{3,0,2,1:T(8,128)S(1)} %copy.10), channel_id=1, source_target_pairs={{0,16},{16,32},{32,48},{48,64},{64,80},{80,96},{96,112},{112,0},{1... | collective-permute-start | bytes 1179656 | tf_op jit(solution)/shard_map/ppermute | solution.py:551
  33.4 8.5 %collective-permute-start.5 = (f32[8,32,256]{2,1,0:T(8,128)}, f32[8,32,256]{2,1,0:T(8,128)S(1)}, u32[]{:S(2)}, u32[]{:S(2)}) collective-permute-start(f32[8,32,256]{2,1,0:T(8,128)} %get-tuple-element.12), channel_id=1, source_target_pairs={{0,112},{16,0},{32,16},{48,32},{64,48},{80,64},{96,80},{112,96},{1... | collective-permute-start | bytes 786440 | tf_op jit(solution)/shard_map/ppermute | solution.py:551
  36.4 12.4 %collective-permute-start.6 = (f32[32,8,256]{2,1,0:T(8,128)}, f32[32,8,256]{2,1,0:T(8,128)S(1)}, u32[]{:S(2)}, u32[]{:S(2)}) collective-permute-start(f32[32,8,256]{2,1,0:T(8,128)} %get-tuple-element.13), channel_id=1, source_target_pairs={{0,1},{1,2},{2,3},{3,4},{4,5},{5,6},{6,7},{7,8},{8,9},{9,10},{10,1... | collective-permute-start | bytes 786440 | tf_op jit(solution)/shard_map/ppermute | solution.py:553
  36.4 15.2 %copy-start = (f32[8,32,256]{2,1,0:T(8,128)}, f32[8,32,256]{2,1,0:T(8,128)S(1)}, u32[]{:S(2)}) copy-start(f32[8,32,256]{2,1,0:T(8,128)S(1)} %collective-permute-done.4.xlo) | copy-start | bytes 786436
  36.4 12.4 %collective-permute-start.7 = (f32[32,8,256]{2,1,0:T(8,128)}, f32[32,8,256]{2,1,0:T(8,128)S(1)}, u32[]{:S(2)}, u32[]{:S(2)}) collective-permute-start(f32[32,8,256]{2,1,0:T(8,128)} %get-tuple-element.14), channel_id=1, source_target_pairs={{0,15},{1,0},{2,1},{3,2},{4,3},{5,4},{6,5},{7,6},{8,7},{9,8},{10,9... | collective-permute-start | bytes 786440 | tf_op jit(solution)/shard_map/ppermute | solution.py:553
  41.8 9.8 %copy-start.1 = (f32[8,32,256]{2,1,0:T(8,128)}, f32[8,32,256]{2,1,0:T(8,128)S(1)}, u32[]{:S(2)}) copy-start(f32[8,32,256]{2,1,0:T(8,128)S(1)} %collective-permute-done.5.xhi) | copy-start | bytes 786436
  42.0 62.3 %copy-start.4 = (f32[6,2,32,256]{3,2,1,0:T(8,128)}, f32[6,2,32,256]{3,2,1,0:T(8,128)S(1)}, u32[]{:S(2)}) copy-start(f32[6,2,32,256]{3,2,1,0:T(8,128)S(1)} %collective-permute-done.9.xhi) | copy-start | bytes 1179652
  43.3 8.4 %collective-permute-start.10 = (f32[16,8,256]{2,1,0:T(8,128)S(1)}, f32[16,8,256]{2,1,0:T(8,128)S(1)}, u32[]{:S(2)}, u32[]{:S(2)}) collective-permute-start(f32[16,8,256]{2,1,0:T(8,128)S(1)} %pad_maximum_fusion), channel_id=1, source_target_pairs={{0,1},{1,2},{2,3},{3,4},{4,5},{5,6},{6,7},{7,8},{8,9},{9,10},{10,1... | collective-permute-start | bytes 393224 | tf_op jit(solution)/shard_map/ppermute | solution.py:553
  43.4 8.3 %collective-permute-start.11 = (f32[16,8,256]{2,1,0:T(8,128)S(1)}, f32[16,8,256]{2,1,0:T(8,128)S(1)}, u32[]{:S(2)}, u32[]{:S(2)}) collective-permute-start(f32[16,8,256]{2,1,0:T(8,128)S(1)} %pad_maximum_fusion.1), channel_id=1, source_target_pairs={{0,15},{1,0},{2,1},{3,2},{4,3},{5,4},{6,5},{7,6},{8,7},{9,8},{10,9... | collective-permute-start | bytes 393224 | tf_op jit(solution)/shard_map/ppermute | solution.py:553
  48.8 2.9 %copy-start.7 = (f32[32,8,256]{2,1,0:T(8,128)}, f32[32,8,256]{2,1,0:T(8,128)S(1)}, u32[]{:S(2)}) copy-start(f32[32,8,256]{2,1,0:T(8,128)S(1)} %collective-permute-done.6.ylo) | copy-start | bytes 786436
  48.8 2.9 %copy-start.8 = (f32[32,8,256]{2,1,0:T(8,128)}, f32[32,8,256]{2,1,0:T(8,128)S(1)}, u32[]{:S(2)}) copy-start(f32[32,8,256]{2,1,0:T(8,128)S(1)} %collective-permute-done.7.yhi) | copy-start | bytes 786436
  51.6 0.7 copy-start.2
  51.6 0.7 copy-start.3
  72.9 1.4 %collective-permute-start.12 = (f32[1,128]{1,0:T(1,128)}, f32[1,128]{1,0:T(1,128)S(1)}, u32[]{:S(2)}, u32[]{:S(2)}) collective-permute-start(f32[1,128]{1,0:T(1,128)} %get-tuple-element.15), channel_id=1, source_target_pairs={{0,16},{16,0},{32,48},{48,32},{64,80},{80,64},{96,112},{112,96},{1... | collective-permute-start | bytes 1544 | tf_op jit(solution)/shard_map/ppermute | solution.py:567
  74.9 3.5 %collective-permute-start.15 = (f32[1,128]{1,0:T(1,128)S(1)}, f32[1,128]{1,0:T(1,128)S(1)}, u32[]{:S(2)}, u32[]{:S(2)}) collective-permute-start(f32[1,128]{1,0:T(1,128)S(1)} %add.30), channel_id=1, source_target_pairs={{0,96},{16,112},{32,0},{48,16},{64,32},{80,48},{96,64},{112,80},{1... | collective-permute-start | bytes 1544 | tf_op jit(solution)/shard_map/ppermute | solution.py:567
  75.7 5.0 %collective-permute-start.14 = (f32[1,128]{1,0:T(1,128)S(1)}, f32[1,128]{1,0:T(1,128)S(1)}, u32[]{:S(2)}, u32[]{:S(2)}) collective-permute-start(f32[1,128]{1,0:T(1,128)S(1)} %add.30), channel_id=1, source_target_pairs={{0,64},{16,80},{32,96},{48,112},{64,0},{80,16},{96,32},{112,48},{1... | collective-permute-start | bytes 1544 | tf_op jit(solution)/shard_map/ppermute | solution.py:567
  75.7 5.4 %collective-permute-start.13 = (f32[1,128]{1,0:T(1,128)S(1)}, f32[1,128]{1,0:T(1,128)S(1)}, u32[]{:S(2)}, u32[]{:S(2)}) collective-permute-start(f32[1,128]{1,0:T(1,128)S(1)} %add.30), channel_id=1, source_target_pairs={{0,32},{16,48},{32,64},{48,80},{64,96},{80,112},{96,0},{112,16},{1... | collective-permute-start | bytes 1544 | tf_op jit(solution)/shard_map/ppermute | solution.py:567
  81.1 10.9 %collective-permute-start.18 = (f32[1,128]{1,0:T(1,128)S(1)}, f32[1,128]{1,0:T(1,128)S(1)}, u32[]{:S(2)}, u32[]{:S(2)}) collective-permute-start(f32[1,128]{1,0:T(1,128)S(1)} %add_add_fusion.2), channel_id=1, source_target_pairs={{0,3},{1,0},{2,1},{3,2},{4,7},{5,4},{6,5},{7,6},{8,11},{9,8},{10,9... | collective-permute-start | bytes 1544 | tf_op jit(solution)/shard_map/ppermute | solution.py:567
  81.9 10.1 %collective-permute-start.17 = (f32[1,128]{1,0:T(1,128)S(1)}, f32[1,128]{1,0:T(1,128)S(1)}, u32[]{:S(2)}, u32[]{:S(2)}) collective-permute-start(f32[1,128]{1,0:T(1,128)S(1)} %add_add_fusion.2), channel_id=1, source_target_pairs={{0,2},{1,3},{2,0},{3,1},{4,6},{5,7},{6,4},{7,5},{8,10},{9,11},{10,... | collective-permute-start | bytes 1544 | tf_op jit(solution)/shard_map/ppermute | solution.py:567
  81.9 10.1 %collective-permute-start.16 = (f32[1,128]{1,0:T(1,128)S(1)}, f32[1,128]{1,0:T(1,128)S(1)}, u32[]{:S(2)}, u32[]{:S(2)}) collective-permute-start(f32[1,128]{1,0:T(1,128)S(1)} %add_add_fusion.2), channel_id=1, source_target_pairs={{0,1},{1,2},{2,3},{3,0},{4,5},{5,6},{6,7},{7,4},{8,9},{9,10},{10,1... | collective-permute-start | bytes 1544 | tf_op jit(solution)/shard_map/ppermute | solution.py:567
  85.3 14.0 %collective-permute-start.23 = (f32[6,32,2,256]{3,2,1,0:T(2,128)S(1)}, f32[6,32,2,256]{3,2,1,0:T(2,128)S(1)}, u32[]{:S(2)}, u32[]{:S(2)}) collective-permute-start(f32[6,32,2,256]{3,2,1,0:T(2,128)S(1)} %get-tuple-element.18), channel_id=1, source_target_pairs={{0,15},{1,0},{2,1},{3,2},{4,3},{5,4},{6,5},{7,6},{8,7},{9,8},{10,9... | collective-permute-start | bytes 1179656 | tf_op jit(solution)/shard_map/ppermute | solution.py:553
  92.0 12.3 %collective-permute-start.22 = (f32[6,32,2,256]{3,2,1,0:T(2,128)S(1)}, f32[6,32,2,256]{3,2,1,0:T(2,128)S(1)}, u32[]{:S(2)}, u32[]{:S(2)}) collective-permute-start(f32[6,32,2,256]{3,2,1,0:T(2,128)S(1)} %get-tuple-element.19), channel_id=1, source_target_pairs={{0,1},{1,2},{2,3},{3,4},{4,5},{5,6},{6,7},{7,8},{8,9},{9,10},{10,1... | collective-permute-start | bytes 1179656 | tf_op jit(solution)/shard_map/ppermute | solution.py:553
  92.0 6.8 %collective-permute-start.21 = (f32[1,128]{1,0:T(1,128)S(1)}, f32[1,128]{1,0:T(1,128)S(1)}, u32[]{:S(2)}, u32[]{:S(2)}) collective-permute-start(f32[1,128]{1,0:T(1,128)S(1)} %add_add_fusion.1), channel_id=1, source_target_pairs={{0,12},{1,13},{2,14},{3,15},{4,0},{5,1},{6,2},{7,3},{8,4},{9,5},{1... | collective-permute-start | bytes 1544 | tf_op jit(solution)/shard_map/ppermute | solution.py:567
  93.0 5.8 %collective-permute-start.20 = (f32[1,128]{1,0:T(1,128)S(1)}, f32[1,128]{1,0:T(1,128)S(1)}, u32[]{:S(2)}, u32[]{:S(2)}) collective-permute-start(f32[1,128]{1,0:T(1,128)S(1)} %add_add_fusion.1), channel_id=1, source_target_pairs={{0,8},{1,9},{2,10},{3,11},{4,12},{5,13},{6,14},{7,15},{8,0},{9,1},... | collective-permute-start | bytes 1544 | tf_op jit(solution)/shard_map/ppermute | solution.py:567
  93.0 5.8 %collective-permute-start.19 = (f32[1,128]{1,0:T(1,128)S(1)}, f32[1,128]{1,0:T(1,128)S(1)}, u32[]{:S(2)}, u32[]{:S(2)}) collective-permute-start(f32[1,128]{1,0:T(1,128)S(1)} %add_add_fusion.1), channel_id=1, source_target_pairs={{0,4},{1,5},{2,6},{3,7},{4,8},{5,9},{6,10},{7,11},{8,12},{9,13},{1... | collective-permute-start | bytes 1544 | tf_op jit(solution)/shard_map/ppermute | solution.py:567
  99.4 4.9 %copy-start.5 = (f32[6,32,2,256]{3,2,1,0:T(2,128)}, f32[6,32,2,256]{3,2,1,0:T(2,128)S(1)}, u32[]{:S(2)}) copy-start(f32[6,32,2,256]{3,2,1,0:T(2,128)S(1)} %collective-permute-done.23.yhi) | copy-start | bytes 1179652
  104.3 0.8 copy-start.6

commit v4 on v3

--- a/solution.py
+++ b/solution.py
@@ -22,6 +22,7 @@
 UNIT = 16
 COMPS = 6
 F32 = jnp.float32
+DOUBLED = 2.0 * 1.4426950408889634
 LIMIT = 60 * 1024 * 1024
 ANY = pl.BlockSpec(memory_space=pl.ANY)
 VMEM = pl.BlockSpec(memory_space=pltpu.VMEM)
@@ -83,6 +84,68 @@
 
 def along_y(pad, x, h, at, size):
     return [pad[x, h, pl.ds(at + k, size), :] for k in range(-3, 4)]
+
+
+def cut_kernel(level, stress, to_xp, to_xn, to_yp, to_yn, faces, x_sems, y_sems):
+    copies = []
+    for n, (out, at) in enumerate(((to_xp, 0), (to_xn, CX))):
+        deep = lambda size: pl.ds(at and at - size, size)
+        copies.append(pltpu.make_async_copy(level.at[deep(3)], out.at[pl.ds(0, 3)], x_sems.at[n, 0]))
+        for c in range(COMPS):
+            copies.append(
+                pltpu.make_async_copy(
+                    stress.at[c, deep(2)], out.at[pl.ds(3 + 2 * c, 2)], x_sems.at[n, 1 + c]
+                )
+            )
+    for copy in copies:
+        copy.start()
+    sides = []
+    for n, y in enumerate((0, CY - 8)):
+        side = []
+        for h in range(2):
+            for m in range(1 + COMPS):
+                src = stress.at[m - 1] if m else level
+                side.append(
+                    pltpu.make_async_copy(
+                        src.at[:, pl.ds(y, 8), half(h)], faces.at[m, n, h], y_sems.at[m, n, h]
+                    )
+                )
+        for copy in side:
+            copy.start()
+        sides.append(side)
+    flat = faces.reshape(1 + COMPS, 2, 2, CX * 8, LANES)
+    for n, out in enumerate((to_yp, to_yn)):
+        for copy in sides[n]:
+            copy.wait()
+        for h in range(2):
+            for m in range(1 + COMPS):
+                depth = 2 if m else 3
+                first = 1 + 2 * m if m else 0
+                for k in range(depth):
+                    row = k if n == 0 else 8 - depth + k
+                    for x in range(0, CX, 8):
+                        out[first + k, x : x + 8, half(h)] = flat[
+                            m, n, h, pl.ds(8 * x + row, 8, stride=8), :
+                        ]
+    for copy in copies:
+        copy.wait()
+
+
+def cut(level, stress):
+    message = jax.ShapeDtypeStruct((3 + 2 * COMPS, CX, 2 * LANES), F32)
+    return pl.pallas_call(
+        cut_kernel,
+        out_shape=[message] * 4,
+        in_specs=[ANY] * 2,
+        out_specs=[ANY] * 2 + [VMEM] * 2,
+        scratch_shapes=[
+            pltpu.VMEM((1 + COMPS, 2, 2, CX, 8, LANES), F32),
+            pltpu.SemaphoreType.DMA((2, 1 + COMPS)),
+            pltpu.SemaphoreType.DMA((1 + COMPS, 2, 2)),
+        ],
+        compiler_params=pltpu.CompilerParams(vmem_limit_bytes=LIMIT),
+        name="cut",
+    )(level, stress)
 
 
 def inner_kernel(level, speed, drift, pad, sems):
@@ -147,24 +210,32 @@
 def advect_kernel(
     tiles, level, xlo, xhi, ylo, yhi, speed, drift,
     adv, to_xp, to_xn, to_yp, to_yn,
-    pad, table, sems,
+    pad, table, faces, sems, y_sems,
 ):
     copies = []
     for h in range(2):
         for n, (src, at, size) in enumerate(((level, 3, CX), (xlo, 0, 3), (xhi, CX + 3, 3))):
             copies.append(
                 pltpu.make_async_copy(
-                    src.at[:, :, half(h)], pad.at[pl.ds(at, size), h, pl.ds(8, CY), :], sems.at[h, n]
+                    src.at[pl.ds(0, size), :, half(h)],
+                    pad.at[pl.ds(at, size), h, pl.ds(8, CY), :],
+                    sems.at[h, n],
                 )
             )
+    for n, src in enumerate((ylo, yhi)):
+        copies.append(pltpu.make_async_copy(src.at[pl.ds(0, 3)], faces.at[n], y_sems.at[n]))
     for copy in copies:
         copy.start()
     table[...] = band_table(tiles)
-    for h in range(2):
-        pad[3 : CX + 3, h, 5:8, :] = ylo[:, :, half(h)]
-        pad[3 : CX + 3, h, 8 + CY : 11 + CY, :] = yhi[:, :, half(h)]
     for copy in copies:
         copy.wait()
+    flat = pad.reshape((CX + 6) * 2 * 48, LANES)
+    for n, row in enumerate((5, 8 + CY)):
+        for h in range(2):
+            for k in range(3):
+                for x in range(0, CX, 8):
+                    rows = pl.ds(((x + 3) * 2 + h) * 48 + row + k, 8, stride=96)
+                    flat[rows, :] = faces[n, k, x : x + 8, half(h)]
 
     def plane(x, with_x):
         for unit in range(CY // UNIT):
@@ -221,12 +292,14 @@
         out_shape=[shape(CX, CY, z)]
         + [shape(8, CY, z)] * 2
         + [shape(CX, 8, z)] * 2,
-        in_specs=[SMEM, ANY, ANY, ANY, VMEM, VMEM, VMEM, VMEM],
+        in_specs=[SMEM, ANY, ANY, ANY, ANY, ANY, VMEM, VMEM],
         out_specs=[VMEM] * 5,
         scratch_shapes=[
             pltpu.VMEM((CX + 6, 2, 48, LANES), F32),
             pltpu.VMEM((8, LANES), F32),
+            pltpu.VMEM((2, 3, CX, z), F32),
             pltpu.SemaphoreType.DMA((2, 3)),
+            pltpu.SemaphoreType.DMA((2,)),
         ],
         compiler_params=pltpu.CompilerParams(vmem_limit_bytes=LIMIT),
         name="advect",
@@ -339,7 +412,8 @@
                     high = jnp.maximum(jnp.maximum(l, r), c)
                     diff = c - jnp.where(positive, low, high)
                     total = diff * diff if total is None else total + diff * diff
-                dst[y, h, rows[k], :] = c - step * (jnp.sqrt(total) - 1.0)
+                slope = total * lax.rsqrt(jnp.maximum(total, 1e-36))
+                dst[y, h, rows[k], :] = c - step * (slope - 1.0)
 
     source, target = first, second
     for sweep in range(1, SWEEPS + 1):
@@ -395,24 +469,32 @@
 def extend_kernel(
     parts, cur, weight, stress, xlo, xhi, ylo, yhi, clo, chi,
     level_out, stress_out,
-    pad, ring, mix, stage, sems, out_sems,
+    pad, ring, mix, stage, sems, x_sems, out_sems,
 ):
     def chunk(n):
         start, stop = CHUNKS[n]
-        pieces = [(stress.at[:, pl.ds(start, stop - start)], start + 2, stop - start)]
-        if n == 0:
-            pieces.append((xlo, 0, 2))
-        if n == len(CHUNKS) - 1:
-            pieces.append((xhi, CX + 2, 2))
-        return [
+        own = stress.at[:, pl.ds(start, stop - start)]
+        copies = [
             pltpu.make_async_copy(
-                src.at[:, :, :, half(h)],
-                pad.at[:, pl.ds(at, size), h, pl.ds(OWN, CY), :],
-                sems.at[n, h, m],
+                own.at[:, :, :, half(h)],
+                pad.at[:, pl.ds(start + 2, stop - start), h, pl.ds(OWN, CY), :],
+                sems.at[n, h],
             )
             for h in range(2)
-            for m, (src, at, size) in enumerate(pieces)
         ]
+        for side, src in ((0, xlo), (3, xhi)):
+            if n == side:
+                at = 0 if n == 0 else CX + 2
+                for h in range(2):
+                    for c in range(COMPS):
+                        copies.append(
+                            pltpu.make_async_copy(
+                                src.at[pl.ds(3 + 2 * c, 2), :, half(h)],
+                                pad.at[c, pl.ds(at, 2), h, pl.ds(OWN, CY), :],
+                                x_sems.at[side % 2, h, c],
+                            )
+                        )
+        return copies
 
     chunks = [chunk(n) for n in range(len(CHUNKS))]
     for copies in chunks:
@@ -420,10 +502,16 @@
             copy.start()
     sums = parts[...]
     shift = sums[:, 0:1] / sums[:, 64:65]
+    flat = pad.reshape(COMPS, (CX + 4) * 2 * ROWS, LANES)
     for h in range(2):
         for c in range(COMPS):
-            pad[c, 2 : CX + 2, h, OWN - 2 : OWN, :] = ylo[c, :, :, half(h)]
-            pad[c, 2 : CX + 2, h, OWN + CY : OWN + CY + 2, :] = yhi[c, :, :, half(h)]
+            for face, row in ((ylo, OWN - 2), (yhi, OWN + CY)):
+                for k in range(2):
+                    for x in range(0, CX, 8):
+                        at = ((x + 2) * 2 + h) * ROWS + row + k
+                        flat[c, pl.ds(at, 8, stride=2 * ROWS), :] = face[
+                            3 + 2 * c + k, x : x + 8, half(h)
+                        ]
             for corner, row in ((clo, OWN - 1), (chi, OWN + CY)):
                 for x, n in ((1, c), (CX + 2, COMPS + c)):
                     at = 2 * DEEP + n // 8
@@ -451,7 +539,7 @@
             ]
 
     def first_step(i, slot, groups=5):
-        levels = neighbours(lambda dx, h, r: cur[i + 1 + dx, h, r, :], groups)
+        levels = neighbours(lambda dx, h, r: cur[i + 1 + dx, h, r, :] * DOUBLED, groups)
         comps = [
             neighbours(lambda dx, h, r, c=c: pad[c, i + 1 + dx, h, r, :], groups)
             for c in range(COMPS)
@@ -460,12 +548,9 @@
             mixes = []
             for h in range(2):
                 c = center[h]
-                w = [
-                    recip(1.0 + jnp.exp(jnp.minimum(2.0 * (n - c), 87.0)))
-                    for n in around[h]
-                ]
+                w = [recip(1.0 + jnp.exp2(jnp.minimum(n - c, 125.5))) for n in around[h]]
                 total = w[0] + w[1] + w[2] + w[3] + w[4] + w[5]
-                gate = weight[i, h, rows, :] * 0.5 * (1.0 + jnp.tanh(2.0 * (c - shift)))
+                gate = weight[i, h, rows, :] * 0.5 * (1.0 + jnp.tanh(c * (2.0 / DOUBLED) - 2.0 * shift))
                 scaled = gate * recip(total)
                 w = [scaled * n for n in w] + [1.0 - gate]
                 mixes.append(w)
@@ -535,7 +620,8 @@
             pltpu.VMEM((4, COMPS, 2, ROWS, LANES), F32),
             pltpu.VMEM((2, 7, 2, ROWS, LANES), F32),
             pltpu.VMEM((COMPS, CX, 2, CY, LANES), F32),
-            pltpu.SemaphoreType.DMA((4, 2, 2)),
+            pltpu.SemaphoreType.DMA((4, 2)),
+            pltpu.SemaphoreType.DMA((2, 2, COMPS)),
             pltpu.SemaphoreType.DMA((4, 2)),
         ],
         compiler_params=pltpu.CompilerParams(vmem_limit_bytes=LIMIT),
@@ -569,12 +655,9 @@
                 value = value + other
         return value
 
-    xlo = send(level[-3:], 1, 0)
-    xhi = send(level[:3], -1, 0)
-    ylo = send(level[:, -3:], 0, 1)
-    yhi = send(level[:, :3], 0, -1)
-    sxlo, sxhi = send(stress[:, -2:], 1, 0), send(stress[:, :2], -1, 0)
-    sylo, syhi = send(stress[:, :, -2:], 0, 1), send(stress[:, :, :2], 0, -1)
+    to_xp, to_xn, to_yp, to_yn = cut(level, stress)
+    xlo, xhi = send(to_xn, 1, 0), send(to_xp, -1, 0)
+    ylo, yhi = send(to_yn, 0, 1), send(to_yp, 0, -1)
     drift = inner_drift(level, velocity)
     adv, to_xp, to_xn, to_yp, to_yn = advect(tiles, level, xlo, xhi, ylo, yhi, velocity, drift)
     axlo, axhi = send(to_xn, 1, 0), send(to_xp, -1, 0)
@@ -584,14 +667,14 @@
 
     def corners(rows, mark, y):
         faces = [jnp.where(row == mark, f[DEEP:, rows], f[:DEEP, rows]) for f in (axlo, axhi)]
-        tail = jnp.concatenate((sxlo[:, 1, y], sxhi[:, 0, y], none), axis=0)
+        tail = jnp.concatenate((xlo[4::2, y], xhi[3:-1:2, y], none), axis=0)
         return jnp.concatenate(faces + [tail.reshape(2, 8, 2 * LANES)], axis=0)
 
     clo = send(corners(slice(-8, None), 0, CY - 1), 0, 1)
     chi = send(corners(slice(0, 8), 7, 0), 0, -1)
     cur, weight, part = sweeps(tiles, adv, (axlo, axhi, aylo, ayhi, clo, chi))
     return extend(
-        total(part), cur, weight, stress, (sxlo, sxhi, sylo, syhi, clo, chi)
+        total(part), cur, weight, stress, (xlo, xhi, ylo, yhi, clo, chi)
     )
 
 

time: 127 us -> 147 us (1.16)
  Pallas kernels: 58.3 us -> 89 us
  starting transfers between devices: 38.6 us -> 32.7 us
  local copies, waits for them, and re-layouts: 9.34 us -> 5.74 us
  waiting for transfers between devices: 18.3 us -> 16.6 us
    pallas_call x0 -> x1, Pallas kernels: none -> 32.2 us  [cut(): pl.pallas_call(cut_kernel, out_shape=[message] * 4, in_specs=[ANY] * 2, o...]
    ppermute x8 -> x6, starting transfers between devices: 23.9 us -> 17.2 us  [send(): return lax.ppermute(value, 'gy', [(i, (i + dy) % ny) for i in range(ny)])]
    ppermute x8 -> x6, waiting for transfers between devices: 7.76 us -> 2.85 us  [send(): return lax.ppermute(value, 'gy', [(i, (i + dy) % ny) for i in range(ny)])]
    slice x5 -> x3, local copies, waits for them, and re-layouts: 5.4 us -> 0.86 us  [corners(): tail = jnp.concatenate((xlo[4::2, y], xhi[3:-1:2, y], none), axis=0)]
    ppermute x10, waiting for transfers between devices: 9.33 us -> 13.7 us  [total(): moved = [lax.ppermute(value, axis, list(enumerate(move))) for move in moves]]
    ppermute x10, starting transfers between devices: 6.24 us -> 9.99 us  [total(): moved = [lax.ppermute(value, axis, list(enumerate(move))) for move in moves]]
    ppermute x6 -> x4, starting transfers between devices: 8.48 us -> 5.53 us  [send(): return lax.ppermute(value, 'gx', [(i, (i + dx) % nx) for i in range(nx)])]
    unnamed x29 -> x18, local copies, waits for them, and re-layouts: 2.99 us -> 2.39 us
  transfers between devices with their start and end apart: 24 -> 20, of which waited for: 8 -> 10; matrix products, arithmetic and copies ran while one was open for 5% -> 2% of each run, Pallas kernels for 8% -> 7%
where the time goes in v4:
time: 147 us; the launch traced here: 146 us
  Pallas kernels  89 us (61%)
  starting transfers between devices  32.7 us (22%)
  waiting for transfers between devices  16.6 us (11%)
  local copies, waits for them, and re-layouts  5.74 us (4%)
    pallas_call x1, Pallas kernels, cut(): pl.pallas_call(cut_kernel, out_shape=[message] * 4, in_specs=[ANY] * 2, o...  32.2 us
    pallas_call x1, Pallas kernels, extend(): pl.pallas_call(extend_kernel, out_shape=[shape(CX, CY, z), shape(COMPS, C...  21 us
    pallas_call x1, Pallas kernels, sweeps(): pl.pallas_call(sweep_kernel, out_shape=[shape(CX + 4, 2, ROWS, LANES), sh...  19.6 us
    ppermute x6, starting transfers between devices, send(): return lax.ppermute(value, 'gy', [(i, (i + dy) % ny) for i in range(ny)])  17.2 us
    ppermute x10, waiting for transfers between devices, total(): moved = [lax.ppermute(value, axis, list(enumerate(move))) for move in moves]  13.7 us
    ppermute x10, starting transfers between devices, total(): moved = [lax.ppermute(value, axis, list(enumerate(move))) for move in moves]  9.99 us
    pallas_call x1, Pallas kernels, inner_drift(): pl.pallas_call(inner_kernel, out_shape=jax.ShapeDtypeStruct(level.shape,...  9.59 us
    pallas_call x1, Pallas kernels, advect(): pl.pallas_call(advect_kernel, out_shape=[shape(CX, CY, z)] + [shape(8, CY...  6.53 us
  transfers between devices with their start and end apart: 20, of which 10 were waited for; matrix products, arithmetic and copies ran while one was open for 2% of the time, Pallas kernels for 7%

profile of v4, /device:TPU:0, one launch (start us, length us, event | category | flops | bytes accessed | tf_op | source)
XLA Modules:
  0.0 146.4 jit_solution(17165253681100821024)
XLA Ops:
  0.6 32.2 %cut.1 = (f32[15,32,256]{2,1,0:T(8,128)}, f32[15,32,256]{2,1,0:T(8,128)}, f32[15,32,256]{2,1,0:T(8,128)}, f32[15,32,256]{2,1,0:T(8,128)}) custom-call(f32[32,32,256]{2,1,0:T(8,128)} %level.5, f32[6,32,32,256]{3,2,1,0:T(8,128)} %stress.3), custom_call_target="tpu_custom_call" | custom-call | tf_op jit(solution)/shard_map/cut/pallas_call | solution.py:136
  32.9 2.5 %collective-permute-start.1 = (f32[15,32,256]{2,1,0:T(8,128)}, f32[15,32,256]{2,1,0:T(8,128)S(1)}, u32[]{:S(2)}, u32[]{:S(2)}) collective-permute-start(f32[15,32,256]{2,1,0:T(8,128)} %get-tuple-element.15), channel_id=1, source_target_pairs={{0,112},{16,0},{32,16},{48,32},{64,48},{80,64},{96,80},{112,96},{1... | collective-permute-start | bytes 1474568 | tf_op jit(solution)/shard_map/ppermute | solution.py:637
  35.4 1.3 copy.6
  36.7 0.0 collective-permute-start
  36.8 2.0 %collective-permute-start.2 = (f32[15,32,256]{2,1,0:T(8,128)}, f32[15,32,256]{2,1,0:T(8,128)S(1)}, u32[]{:S(2)}, u32[]{:S(2)}) collective-permute-start(f32[15,32,256]{2,1,0:T(8,128)} %get-tuple-element.16), channel_id=1, source_target_pairs={{0,1},{1,2},{2,3},{3,4},{4,5},{5,6},{6,7},{7,8},{8,9},{9,10},{10,1... | collective-permute-start | bytes 1474568 | tf_op jit(solution)/shard_map/ppermute | solution.py:639
  38.7 4.4 %collective-permute-start.3 = (f32[15,32,256]{2,1,0:T(8,128)}, f32[15,32,256]{2,1,0:T(8,128)S(1)}, u32[]{:S(2)}, u32[]{:S(2)}) collective-permute-start(f32[15,32,256]{2,1,0:T(8,128)} %get-tuple-element.17), channel_id=1, source_target_pairs={{0,15},{1,0},{2,1},{3,2},{4,3},{5,4},{6,5},{7,6},{8,7},{9,8},{10,9... | collective-permute-start | bytes 1474568 | tf_op jit(solution)/shard_map/ppermute | solution.py:639
  43.1 0.1 pad.11.clone
  43.2 9.6 %inner_drift.1.drift = f32[32,32,256]{2,1,0:T(8,128)} custom-call(f32[32,32,256]{2,1,0:T(8,128)} %level.5, bf16[3,32,32,256]{3,2,1,0:T(8,128)(2,1)} %speed.3), custom_call_target="tpu_custom_call" | custom-call | flops 47185920 | bytes 3670016 | tf_op jit(solution)/shard_map/inner_drift/pallas_call | solution.py:193
  52.8 0.0 collective-permute-done
  52.8 1.1 copy.7.xlo
  53.9 0.0 collective-permute-done.1.xhi
  53.9 0.0 collective-permute-done.2.ylo
  53.9 0.0 copy-start.1
  53.9 0.0 collective-permute-done.3.yhi
  53.9 0.8 copy-done
  54.7 0.2 copy-done.1
  54.9 0.8 copy-done.2
  55.7 6.5 %advect.1 = (f32[32,32,256]{2,1,0:T(8,128)}, f32[8,32,256]{2,1,0:T(8,128)}, f32[8,32,256]{2,1,0:T(8,128)}, f32[32,8,256]{2,1,0:T(8,128)}, f32[32,8,256]{2,1,0:T(8,128)}) custom-call(s32[1,1,32]{2,1,0:T(1,128)} %tiles.3, f32[32,32,256]{2,1,0:T(8,128)} %level.5, f32[15,32,256]{2,1,0:T(8,128)} %copy.7.xlo, f32[15,32,256]{2,1,0:T(8,128)} %copy-done, ...), custom_call_target="tpu_custom_call" | custom-call | tf_op jit(solution)/shard_map/advect/pallas_call | solution.py:290
  62.2 0.0 collective-permute-start.4
  62.2 2.9 %collective-permute-start.5 = (f32[8,32,256]{2,1,0:T(8,128)}, f32[8,32,256]{2,1,0:T(8,128)S(1)}, u32[]{:S(2)}, u32[]{:S(2)}) collective-permute-start(f32[8,32,256]{2,1,0:T(8,128)} %get-tuple-element.20), channel_id=1, source_target_pairs={{0,112},{16,0},{32,16},{48,32},{64,48},{80,64},{96,80},{112,96},{1... | collective-permute-start | bytes 786440 | tf_op jit(solution)/shard_map/ppermute | solution.py:637
  65.2 0.0 collective-permute-start.6
  65.2 5.3 %collective-permute-start.7 = (f32[32,8,256]{2,1,0:T(8,128)}, f32[32,8,256]{2,1,0:T(8,128)S(1)}, u32[]{:S(2)}, u32[]{:S(2)}) collective-permute-start(f32[32,8,256]{2,1,0:T(8,128)} %get-tuple-element.22), channel_id=1, source_target_pairs={{0,15},{1,0},{2,1},{3,2},{4,3},{5,4},{6,5},{7,6},{8,7},{9,8},{10,9... | collective-permute-start | bytes 786440 | tf_op jit(solution)/shard_map/ppermute | solution.py:639
  70.5 0.8 fusion
  71.4 0.1 maximum_bitcast_fusion.1
  71.5 0.0 collective-permute-done.4.xlo
  71.5 0.0 collective-permute-done.5.xhi
  71.5 0.0 copy-start.4
  71.5 0.1 slice_select_fusion
  71.6 0.1 collective-permute-start.8
  71.7 5.4 %collective-permute-start.9 = (f32[16,8,256]{2,1,0:T(8,128)S(1)}, f32[16,8,256]{2,1,0:T(8,128)S(1)}, u32[]{:S(2)}, u32[]{:S(2)}) collective-permute-start(f32[16,8,256]{2,1,0:T(8,128)S(1)} %pad_maximum_fusion.1), channel_id=1, source_target_pairs={{0,15},{1,0},{2,1},{3,2},{4,3},{5,4},{6,5},{7,6},{8,7},{9,8},{10,9... | collective-permute-start | bytes 393224 | tf_op jit(solution)/shard_map/ppermute | solution.py:639
  77.1 0.0 collective-permute-done.6.ylo
  77.1 0.0 collective-permute-done.7.yhi
  77.1 0.0 copy-start.8
  77.1 2.8 %collective-permute-done.8.clo = f32[16,8,256]{2,1,0:T(8,128)S(1)} collective-permute-done((f32[16,8,256]{2,1,0:T(8,128)S(1)}, f32[16,8,256]{2,1,0:T(8,128)S(1)}, u32[]{:S(2)}, u32[]{:S(2)}) %collective-permute-start.8) | collective-permute-done | bytes 131104 | tf_op jit(solution)/shard_map/ppermute | solution.py:639
  80.0 0.0 collective-permute-done.9.chi
  80.0 0.0 copy-done.4
  80.0 0.0 copy-done.7
  80.0 0.0 copy-done.8
  80.0 0.6 copy-done.5
  80.6 0.0 copy-done.6
  80.7 19.6 %sweeps.1 = (f32[36,2,64,128]{3,2,1,0:T(8,128)}, f32[34,2,64,128]{3,2,1,0:T(8,128)}, f32[1,128]{1,0:T(1,128)}) custom-call(s32[1,1,32]{2,1,0:T(1,128)} %tiles.3, f32[32,32,256]{2,1,0:T(8,128)} %get-tuple-element.18.adv, f32[8,32,256]{2,1,0:T(8,128)} %copy-done.3, f32[8,32,256]{2,1,0:T(8,128)} %copy-done.4, f32[32,8,256]{2,1,0:T(8,128)} %copy-done.7, ...), custom_call_target="tpu_custom_call" | custom-call | tf_op jit(solution)/shard_map/sweeps/pallas_call | solution.py:447
  100.3 0.1 collective-permute-start.10
  100.4 1.3 collective-permute-done.10
  101.7 0.6 add.30
  102.3 0.9 collective-permute-start.13
  103.2 0.9 collective-permute-start.12
  104.0 0.6 collective-permute-start.11
  104.6 1.2 collective-permute-done.13
  105.8 2.4 %collective-permute-done.12 = f32[1,128]{1,0:T(1,128)S(1)} collective-permute-done((f32[1,128]{1,0:T(1,128)S(1)}, f32[1,128]{1,0:T(1,128)S(1)}, u32[]{:S(2)}, u32[]{:S(2)}) %collective-permute-start.12) | collective-permute-done | bytes 544 | tf_op jit(solution)/shard_map/ppermute | solution.py:653
  108.2 0.6 collective-permute-done.11
  108.8 0.6 collective-permute-start.16
  109.4 0.0 collective-permute-start.15
  109.4 1.4 collective-permute-start.14
  110.8 1.5 %collective-permute-done.16 = f32[1,128]{1,0:T(1,128)S(1)} collective-permute-done((f32[1,128]{1,0:T(1,128)S(1)}, f32[1,128]{1,0:T(1,128)S(1)}, u32[]{:S(2)}, u32[]{:S(2)}) %collective-permute-start.16) | collective-permute-done | bytes 544 | tf_op jit(solution)/shard_map/ppermute | solution.py:653
  112.3 2.1 %collective-permute-done.15 = f32[1,128]{1,0:T(1,128)S(1)} collective-permute-done((f32[1,128]{1,0:T(1,128)S(1)}, f32[1,128]{1,0:T(1,128)S(1)}, u32[]{:S(2)}, u32[]{:S(2)}) %collective-permute-start.15) | collective-permute-done | bytes 544 | tf_op jit(solution)/shard_map/ppermute | solution.py:653
  114.5 0.5 collective-permute-done.14
  115.0 4.6 %collective-permute-start.19 = (f32[1,128]{1,0:T(1,128)S(1)}, f32[1,128]{1,0:T(1,128)S(1)}, u32[]{:S(2)}, u32[]{:S(2)}) collective-permute-start(f32[1,128]{1,0:T(1,128)S(1)} %add_add_fusion.1), channel_id=1, source_target_pairs={{0,12},{1,13},{2,14},{3,15},{4,0},{5,1},{6,2},{7,3},{8,4},{9,5},{1... | collective-permute-start | bytes 1544 | tf_op jit(solution)/shard_map/ppermute | solution.py:653
  119.6 0.0 collective-permute-start.18
  119.6 0.9 collective-permute-start.17
  120.5 0.3 collective-permute-done.19
  120.9 3.7 %collective-permute-done.18 = f32[1,128]{1,0:T(1,128)S(1)} collective-permute-done((f32[1,128]{1,0:T(1,128)S(1)}, f32[1,128]{1,0:T(1,128)S(1)}, u32[]{:S(2)}, u32[]{:S(2)}) %collective-permute-start.18) | collective-permute-done | bytes 544 | tf_op jit(solution)/shard_map/ppermute | solution.py:653
  124.6 0.0 collective-permute-done.17
  124.6 0.6 add_add_fusion.parts
  125.2 21.0 %extend.1 = (f32[32,32,256]{2,1,0:T(8,128)}, f32[6,32,32,256]{3,2,1,0:T(8,128)}) custom-call(f32[1,128]{1,0:T(1,128)} %add_add_fusion.parts, f32[36,2,64,128]{3,2,1,0:T(8,128)} %get-tuple-element.24.cur, f32[34,2,64,128]{3,2,1,0:T(8,128)} %get-tuple-element.25.weight, f32[6,32,32,256]{3,2,1,0:T(8,128)} %stress.3, f32[15,32,256]{2,1,0:T(8,128)} %copy.7.xlo, ...), custom_call_target="tpu_custom_call" | custom-call | tf_op jit(solution)/shard_map/extend/pallas_call | solution.py:613
  (18 shorter events, 0.1 us)
Async XLA Ops:
  32.9 21.1 %collective-permute-start.1 = (f32[15,32,256]{2,1,0:T(8,128)}, f32[15,32,256]{2,1,0:T(8,128)S(1)}, u32[]{:S(2)}, u32[]{:S(2)}) collective-permute-start(f32[15,32,256]{2,1,0:T(8,128)} %get-tuple-element.15), channel_id=1, source_target_pairs={{0,112},{16,0},{32,16},{48,32},{64,48},{80,64},{96,80},{112,96},{1... | collective-permute-start | bytes 1474568 | tf_op jit(solution)/shard_map/ppermute | solution.py:637
  36.7 16.1 %collective-permute-start = (f32[15,32,256]{2,0,1:T(8,128)S(1)}, f32[15,32,256]{2,0,1:T(8,128)S(1)}, u32[]{:S(2)}, u32[]{:S(2)}) collective-permute-start(f32[15,32,256]{2,0,1:T(8,128)S(1)} %copy.6), channel_id=1, source_target_pairs={{0,16},{16,32},{32,48},{48,64},{64,80},{80,96},{96,112},{112,0},{1... | collective-permute-start | bytes 1474568 | tf_op jit(solution)/shard_map/ppermute | solution.py:637
  36.8 17.2 %collective-permute-start.2 = (f32[15,32,256]{2,1,0:T(8,128)}, f32[15,32,256]{2,1,0:T(8,128)S(1)}, u32[]{:S(2)}, u32[]{:S(2)}) collective-permute-start(f32[15,32,256]{2,1,0:T(8,128)} %get-tuple-element.16), channel_id=1, source_target_pairs={{0,1},{1,2},{2,3},{3,4},{4,5},{5,6},{6,7},{7,8},{8,9},{9,10},{10,1... | collective-permute-start | bytes 1474568 | tf_op jit(solution)/shard_map/ppermute | solution.py:639
  38.7 15.2 %collective-permute-start.3 = (f32[15,32,256]{2,1,0:T(8,128)}, f32[15,32,256]{2,1,0:T(8,128)S(1)}, u32[]{:S(2)}, u32[]{:S(2)}) collective-permute-start(f32[15,32,256]{2,1,0:T(8,128)} %get-tuple-element.17), channel_id=1, source_target_pairs={{0,15},{1,0},{2,1},{3,2},{4,3},{5,4},{6,5},{7,6},{8,7},{9,8},{10,9... | collective-permute-start | bytes 1474568 | tf_op jit(solution)/shard_map/ppermute | solution.py:639
  53.9 0.8 copy-start
  53.9 0.9 copy-start.1
  54.9 0.8 copy-start.2
  62.2 9.3 %collective-permute-start.4 = (f32[8,32,256]{2,1,0:T(8,128)}, f32[8,32,256]{2,1,0:T(8,128)S(1)}, u32[]{:S(2)}, u32[]{:S(2)}) collective-permute-start(f32[8,32,256]{2,1,0:T(8,128)} %get-tuple-element.19), channel_id=1, source_target_pairs={{0,16},{16,32},{32,48},{48,64},{64,80},{80,96},{96,112},{112,0},{1... | collective-permute-start | bytes 786440 | tf_op jit(solution)/shard_map/ppermute | solution.py:637
  62.2 9.3 %collective-permute-start.5 = (f32[8,32,256]{2,1,0:T(8,128)}, f32[8,32,256]{2,1,0:T(8,128)S(1)}, u32[]{:S(2)}, u32[]{:S(2)}) collective-permute-start(f32[8,32,256]{2,1,0:T(8,128)} %get-tuple-element.20), channel_id=1, source_target_pairs={{0,112},{16,0},{32,16},{48,32},{64,48},{80,64},{96,80},{112,96},{1... | collective-permute-start | bytes 786440 | tf_op jit(solution)/shard_map/ppermute | solution.py:637
  65.2 12.0 %collective-permute-start.6 = (f32[32,8,256]{2,1,0:T(8,128)}, f32[32,8,256]{2,1,0:T(8,128)S(1)}, u32[]{:S(2)}, u32[]{:S(2)}) collective-permute-start(f32[32,8,256]{2,1,0:T(8,128)} %get-tuple-element.21), channel_id=1, source_target_pairs={{0,1},{1,2},{2,3},{3,4},{4,5},{5,6},{6,7},{7,8},{8,9},{9,10},{10,1... | collective-permute-start | bytes 786440 | tf_op jit(solution)/shard_map/ppermute | solution.py:639
  65.2 12.0 %collective-permute-start.7 = (f32[32,8,256]{2,1,0:T(8,128)}, f32[32,8,256]{2,1,0:T(8,128)S(1)}, u32[]{:S(2)}, u32[]{:S(2)}) collective-permute-start(f32[32,8,256]{2,1,0:T(8,128)} %get-tuple-element.22), channel_id=1, source_target_pairs={{0,15},{1,0},{2,1},{3,2},{4,3},{5,4},{6,5},{7,6},{8,7},{9,8},{10,9... | collective-permute-start | bytes 786440 | tf_op jit(solution)/shard_map/ppermute | solution.py:639
  71.5 8.5 %copy-start.3 = (f32[8,32,256]{2,1,0:T(8,128)}, f32[8,32,256]{2,1,0:T(8,128)S(1)}, u32[]{:S(2)}) copy-start(f32[8,32,256]{2,1,0:T(8,128)S(1)} %collective-permute-done.4.xlo) | copy-start | bytes 786436
  71.5 8.5 %copy-start.4 = (f32[8,32,256]{2,1,0:T(8,128)}, f32[8,32,256]{2,1,0:T(8,128)S(1)}, u32[]{:S(2)}) copy-start(f32[8,32,256]{2,1,0:T(8,128)S(1)} %collective-permute-done.5.xhi) | copy-start | bytes 786436
  71.6 8.4 %collective-permute-start.8 = (f32[16,8,256]{2,1,0:T(8,128)S(1)}, f32[16,8,256]{2,1,0:T(8,128)S(1)}, u32[]{:S(2)}, u32[]{:S(2)}) collective-permute-start(f32[16,8,256]{2,1,0:T(8,128)S(1)} %pad_maximum_fusion), channel_id=1, source_target_pairs={{0,1},{1,2},{2,3},{3,4},{4,5},{5,6},{6,7},{7,8},{8,9},{9,10},{10,1... | collective-permute-start | bytes 393224 | tf_op jit(solution)/shard_map/ppermute | solution.py:639
  71.7 8.3 %collective-permute-start.9 = (f32[16,8,256]{2,1,0:T(8,128)S(1)}, f32[16,8,256]{2,1,0:T(8,128)S(1)}, u32[]{:S(2)}, u32[]{:S(2)}) collective-permute-start(f32[16,8,256]{2,1,0:T(8,128)S(1)} %pad_maximum_fusion.1), channel_id=1, source_target_pairs={{0,15},{1,0},{2,1},{3,2},{4,3},{5,4},{6,5},{7,6},{8,7},{9,8},{10,9... | collective-permute-start | bytes 393224 | tf_op jit(solution)/shard_map/ppermute | solution.py:639
  77.1 2.9 %copy-start.7 = (f32[32,8,256]{2,1,0:T(8,128)}, f32[32,8,256]{2,1,0:T(8,128)S(1)}, u32[]{:S(2)}) copy-start(f32[32,8,256]{2,1,0:T(8,128)S(1)} %collective-permute-done.6.ylo) | copy-start | bytes 786436
  77.1 2.9 %copy-start.8 = (f32[32,8,256]{2,1,0:T(8,128)}, f32[32,8,256]{2,1,0:T(8,128)S(1)}, u32[]{:S(2)}) copy-start(f32[32,8,256]{2,1,0:T(8,128)S(1)} %collective-permute-done.7.yhi) | copy-start | bytes 786436
  80.0 0.7 copy-start.5
  80.0 0.7 copy-start.6
  100.3 1.4 collective-permute-start.10
  102.3 3.5 %collective-permute-start.13 = (f32[1,128]{1,0:T(1,128)S(1)}, f32[1,128]{1,0:T(1,128)S(1)}, u32[]{:S(2)}, u32[]{:S(2)}) collective-permute-start(f32[1,128]{1,0:T(1,128)S(1)} %add.30), channel_id=1, source_target_pairs={{0,96},{16,112},{32,0},{48,16},{64,32},{80,48},{96,64},{112,80},{1... | collective-permute-start | bytes 1544 | tf_op jit(solution)/shard_map/ppermute | solution.py:653
  103.2 5.0 %collective-permute-start.12 = (f32[1,128]{1,0:T(1,128)S(1)}, f32[1,128]{1,0:T(1,128)S(1)}, u32[]{:S(2)}, u32[]{:S(2)}) collective-permute-start(f32[1,128]{1,0:T(1,128)S(1)} %add.30), channel_id=1, source_target_pairs={{0,64},{16,80},{32,96},{48,112},{64,0},{80,16},{96,32},{112,48},{1... | collective-permute-start | bytes 1544 | tf_op jit(solution)/shard_map/ppermute | solution.py:653
  104.0 4.8 %collective-permute-start.11 = (f32[1,128]{1,0:T(1,128)S(1)}, f32[1,128]{1,0:T(1,128)S(1)}, u32[]{:S(2)}, u32[]{:S(2)}) collective-permute-start(f32[1,128]{1,0:T(1,128)S(1)} %add.30), channel_id=1, source_target_pairs={{0,32},{16,48},{32,64},{48,80},{64,96},{80,112},{96,0},{112,16},{1... | collective-permute-start | bytes 1544 | tf_op jit(solution)/shard_map/ppermute | solution.py:653
  108.8 3.5 %collective-permute-start.16 = (f32[1,128]{1,0:T(1,128)S(1)}, f32[1,128]{1,0:T(1,128)S(1)}, u32[]{:S(2)}, u32[]{:S(2)}) collective-permute-start(f32[1,128]{1,0:T(1,128)S(1)} %add_add_fusion.2), channel_id=1, source_target_pairs={{0,3},{1,0},{2,1},{3,2},{4,7},{5,4},{6,5},{7,6},{8,11},{9,8},{10,9... | collective-permute-start | bytes 1544 | tf_op jit(solution)/shard_map/ppermute | solution.py:653
  109.4 5.0 %collective-permute-start.15 = (f32[1,128]{1,0:T(1,128)S(1)}, f32[1,128]{1,0:T(1,128)S(1)}, u32[]{:S(2)}, u32[]{:S(2)}) collective-permute-start(f32[1,128]{1,0:T(1,128)S(1)} %add_add_fusion.2), channel_id=1, source_target_pairs={{0,2},{1,3},{2,0},{3,1},{4,6},{5,7},{6,4},{7,5},{8,10},{9,11},{10,... | collective-permute-start | bytes 1544 | tf_op jit(solution)/shard_map/ppermute | solution.py:653
  109.4 5.6 %collective-permute-start.14 = (f32[1,128]{1,0:T(1,128)S(1)}, f32[1,128]{1,0:T(1,128)S(1)}, u32[]{:S(2)}, u32[]{:S(2)}) collective-permute-start(f32[1,128]{1,0:T(1,128)S(1)} %add_add_fusion.2), channel_id=1, source_target_pairs={{0,1},{1,2},{2,3},{3,0},{4,5},{5,6},{6,7},{7,4},{8,9},{9,10},{10,1... | collective-permute-start | bytes 1544 | tf_op jit(solution)/shard_map/ppermute | solution.py:653
  115.0 5.9 %collective-permute-start.19 = (f32[1,128]{1,0:T(1,128)S(1)}, f32[1,128]{1,0:T(1,128)S(1)}, u32[]{:S(2)}, u32[]{:S(2)}) collective-permute-start(f32[1,128]{1,0:T(1,128)S(1)} %add_add_fusion.1), channel_id=1, source_target_pairs={{0,12},{1,13},{2,14},{3,15},{4,0},{5,1},{6,2},{7,3},{8,4},{9,5},{1... | collective-permute-start | bytes 1544 | tf_op jit(solution)/shard_map/ppermute | solution.py:653
  119.6 5.0 %collective-permute-start.18 = (f32[1,128]{1,0:T(1,128)S(1)}, f32[1,128]{1,0:T(1,128)S(1)}, u32[]{:S(2)}, u32[]{:S(2)}) collective-permute-start(f32[1,128]{1,0:T(1,128)S(1)} %add_add_fusion.1), channel_id=1, source_target_pairs={{0,8},{1,9},{2,10},{3,11},{4,12},{5,13},{6,14},{7,15},{8,0},{9,1},... | collective-permute-start | bytes 1544 | tf_op jit(solution)/shard_map/ppermute | solution.py:653
  119.6 5.0 %collective-permute-start.17 = (f32[1,128]{1,0:T(1,128)S(1)}, f32[1,128]{1,0:T(1,128)S(1)}, u32[]{:S(2)}, u32[]{:S(2)}) collective-permute-start(f32[1,128]{1,0:T(1,128)S(1)} %add_add_fusion.1), channel_id=1, source_target_pairs={{0,4},{1,5},{2,6},{3,7},{4,8},{5,9},{6,10},{7,11},{8,12},{9,13},{1... | collective-permute-start | bytes 1544 | tf_op jit(solution)/shard_map/ppermute | solution.py:653

commit v5 on v4

--- a/solution.py
+++ b/solution.py
@@ -23,7 +23,7 @@
 COMPS = 6
 F32 = jnp.float32
 DOUBLED = 2.0 * 1.4426950408889634
-LIMIT = 60 * 1024 * 1024
+MIB = 1024 * 1024
 ANY = pl.BlockSpec(memory_space=pl.ANY)
 VMEM = pl.BlockSpec(memory_space=pltpu.VMEM)
 SMEM = pl.BlockSpec(memory_space=pltpu.SMEM)
@@ -137,13 +137,13 @@
         cut_kernel,
         out_shape=[message] * 4,
         in_specs=[ANY] * 2,
-        out_specs=[ANY] * 2 + [VMEM] * 2,
+        out_specs=[VMEM] * 4,
         scratch_shapes=[
             pltpu.VMEM((1 + COMPS, 2, 2, CX, 8, LANES), F32),
             pltpu.SemaphoreType.DMA((2, 1 + COMPS)),
             pltpu.SemaphoreType.DMA((1 + COMPS, 2, 2)),
         ],
-        compiler_params=pltpu.CompilerParams(vmem_limit_bytes=LIMIT),
+        compiler_params=pltpu.CompilerParams(vmem_limit_bytes=10 * MIB),
         name="cut",
     )(level, stress)
 
@@ -199,7 +199,7 @@
             pltpu.VMEM((CX, 2, CY, LANES), F32),
             pltpu.SemaphoreType.DMA((2,)),
         ],
-        compiler_params=pltpu.CompilerParams(vmem_limit_bytes=LIMIT),
+        compiler_params=pltpu.CompilerParams(vmem_limit_bytes=10 * MIB),
         cost_estimate=pl.CostEstimate(
             flops=180 * level.size, bytes_accessed=14 * level.size, transcendentals=9 * level.size
         ),
@@ -209,8 +209,8 @@
 
 def advect_kernel(
     tiles, level, xlo, xhi, ylo, yhi, speed, drift,
-    adv, to_xp, to_xn, to_yp, to_yn,
-    pad, table, faces, sems, y_sems,
+    adv, to_xp, to_xn, to_yp, to_yn, tail_p, tail_n,
+    pad, table, faces, ends, sems, y_sems, end_sems,
 ):
     copies = []
     for h in range(2):
@@ -224,11 +224,24 @@
             )
     for n, src in enumerate((ylo, yhi)):
         copies.append(pltpu.make_async_copy(src.at[pl.ds(0, 3)], faces.at[n], y_sems.at[n]))
+    for n, src in enumerate((xlo, xhi)):
+        for m, y in enumerate((0, CY - 8)):
+            copies.append(
+                pltpu.make_async_copy(
+                    src.at[pl.ds(3, 2 * COMPS), pl.ds(y, 8)], ends.at[n, m], end_sems.at[n, m]
+                )
+            )
     for copy in copies:
         copy.start()
     table[...] = band_table(tiles)
     for copy in copies:
         copy.wait()
+    for m, (tail, row) in enumerate(((tail_p, 0), (tail_n, 7))):
+        tail[...] = jnp.zeros(tail.shape, F32)
+        for n in range(2):
+            for c in range(COMPS):
+                to = n * COMPS + c
+                tail[to // 8, to % 8 : to % 8 + 1, :] = ends[n, m, 2 * c + 1 - n, row : row + 1, :]
     flat = pad.reshape((CX + 6) * 2 * 48, LANES)
     for n, row in enumerate((5, 8 + CY)):
         for h in range(2):
@@ -291,17 +304,20 @@
         advect_kernel,
         out_shape=[shape(CX, CY, z)]
         + [shape(8, CY, z)] * 2
-        + [shape(CX, 8, z)] * 2,
+        + [shape(CX, 8, z)] * 2
+        + [shape(2, 8, z)] * 2,
         in_specs=[SMEM, ANY, ANY, ANY, ANY, ANY, VMEM, VMEM],
-        out_specs=[VMEM] * 5,
+        out_specs=[VMEM] * 7,
         scratch_shapes=[
             pltpu.VMEM((CX + 6, 2, 48, LANES), F32),
             pltpu.VMEM((8, LANES), F32),
             pltpu.VMEM((2, 3, CX, z), F32),
+            pltpu.VMEM((2, 2, 2 * COMPS, 8, z), F32),
             pltpu.SemaphoreType.DMA((2, 3)),
             pltpu.SemaphoreType.DMA((2,)),
+            pltpu.SemaphoreType.DMA((2, 2)),
         ],
-        compiler_params=pltpu.CompilerParams(vmem_limit_bytes=LIMIT),
+        compiler_params=pltpu.CompilerParams(vmem_limit_bytes=12 * MIB),
         name="advect",
     )(tiles, level, xlo, xhi, ylo, yhi, speed, drift)
 
@@ -439,14 +455,15 @@
 
     lax.fori_loop(0, CX, count, 0, unroll=2)
     lane = lax.broadcasted_iota(jnp.int32, (1, LANES), 1)
-    part[...] = jnp.where(lane < 64, jnp.sum(sums[0]), jnp.sum(sums[1]))
-
-
-def sweeps(tiles, adv, halos):
+    sums_row = jnp.where(lane < 64, jnp.sum(sums[0]), jnp.sum(sums[1]))
+    part[...] = jnp.broadcast_to(sums_row, part.shape)
+
+
+def sweeps(tiles, adv, halos, count):
     shape = lambda *s: jax.ShapeDtypeStruct(s, F32)
     return pl.pallas_call(
         sweep_kernel,
-        out_shape=[shape(CX + 4, 2, ROWS, LANES), shape(CX + 2, 2, ROWS, LANES), shape(1, LANES)],
+        out_shape=[shape(CX + 4, 2, ROWS, LANES), shape(CX + 2, 2, ROWS, LANES), shape(count, 1, LANES)],
         in_specs=[SMEM, VMEM] + [ANY] * 6,
         out_specs=[VMEM] * 3,
         scratch_shapes=[
@@ -458,7 +475,7 @@
             pltpu.VMEM((2, UNIT, LANES), F32),
             pltpu.SemaphoreType.DMA((2, 11)),
         ],
-        compiler_params=pltpu.CompilerParams(vmem_limit_bytes=LIMIT),
+        compiler_params=pltpu.CompilerParams(vmem_limit_bytes=22 * MIB),
         name="sweeps",
     )(tiles, adv, *halos)
 
@@ -500,7 +517,7 @@
     for copies in chunks:
         for copy in copies:
             copy.start()
-    sums = parts[...]
+    sums = jnp.sum(parts[...], axis=0)
     shift = sums[:, 0:1] / sums[:, 64:65]
     flat = pad.reshape(COMPS, (CX + 4) * 2 * ROWS, LANES)
     for h in range(2):
@@ -523,9 +540,17 @@
             value = value + mixes[n] * around[n]
         return value
 
+    def row_groups(groups):
+        start = OWN + CY // 2 - 4 * groups
+        return [pl.ds(start + k, 8, stride=groups) for k in range(-1, groups + 1)]
+
+    def face(here, there):
+        grown = jnp.exp2(jnp.minimum(there - here, 125.5))
+        factor = recip(1.0 + grown)
+        return factor, grown * factor
+
     def neighbours(load, groups):
-        start = OWN + CY // 2 - 4 * groups
-        rows = [pl.ds(start + k, 8, stride=groups) for k in range(-1, groups + 1)]
+        rows = row_groups(groups)
         lines = [[load(0, h, r) for r in rows] for h in range(2)]
         for k in range(1, groups + 1):
             center = [lines[h][k] for h in range(2)]
@@ -539,18 +564,32 @@
             ]
 
     def first_step(i, slot, groups=5):
-        levels = neighbours(lambda dx, h, r: cur[i + 1 + dx, h, r, :] * DOUBLED, groups)
+        load = lambda dx, h, r: cur[i + 1 + dx, h, r, :] * DOUBLED
         comps = [
             neighbours(lambda dx, h, r, c=c: pad[c, i + 1 + dx, h, r, :], groups)
             for c in range(COMPS)
         ]
-        for rows, center, around in levels:
+        rows_of = row_groups(groups)
+        lines = [[load(0, h, r) for r in rows_of] for h in range(2)]
+        below = [face(lines[h][1], lines[h][0])[0] for h in range(2)]
+        for k in range(1, groups + 1):
+            rows = rows_of[k]
+            center = [lines[h][k] for h in range(2)]
+            along_z = [face(c, n) for c, n in zip(center, lane_shift(center, 1))]
+            back_z = lane_shift([back for _, back in along_z], -1)
             mixes = []
             for h in range(2):
                 c = center[h]
-                w = [recip(1.0 + jnp.exp2(jnp.minimum(n - c, 125.5))) for n in around[h]]
+                ahead, back = face(c, lines[h][k + 1])
+                w = [
+                    face(c, load(-1, h, rows))[0], face(c, load(1, h, rows))[0],
+                    below[h], ahead, back_z[h], along_z[h][0],
+                ]
+                below[h] = back
                 total = w[0] + w[1] + w[2] + w[3] + w[4] + w[5]
-                gate = weight[i, h, rows, :] * 0.5 * (1.0 + jnp.tanh(c * (2.0 / DOUBLED) - 2.0 * shift))
+                gate = weight[i, h, rows, :] * 0.5 * (
+                    1.0 + jnp.tanh(c * (2.0 / DOUBLED) - 2.0 * shift)
+                )
                 scaled = gate * recip(total)
                 w = [scaled * n for n in w] + [1.0 - gate]
                 mixes.append(w)
@@ -624,7 +663,7 @@
             pltpu.SemaphoreType.DMA((2, 2, COMPS)),
             pltpu.SemaphoreType.DMA((4, 2)),
         ],
-        compiler_params=pltpu.CompilerParams(vmem_limit_bytes=LIMIT),
+        compiler_params=pltpu.CompilerParams(vmem_limit_bytes=36 * MIB),
         name="extend",
     )(parts, cur, weight, stress, *halos)
 
@@ -642,40 +681,26 @@
         ]
         return lax.ppermute(value, ("gx", "gy"), pairs)
 
-    def total(value):
-        rounds = (
-            ("gx", [[i ^ 1 for i in range(nx)]]),
-            ("gx", [[(i + 2 * k) % nx for i in range(nx)] for k in range(1, nx // 2)]),
-            ("gy", [[i // 4 * 4 + (i + k) % 4 for i in range(ny)] for k in range(1, 4)]),
-            ("gy", [[(i + 4 * k) % ny for i in range(ny)] for k in range(1, ny // 4)]),
-        )
-        for axis, moves in rounds:
-            moved = [lax.ppermute(value, axis, list(enumerate(move))) for move in moves]
-            for other in moved:
-                value = value + other
-        return value
-
     to_xp, to_xn, to_yp, to_yn = cut(level, stress)
     xlo, xhi = send(to_xn, 1, 0), send(to_xp, -1, 0)
     ylo, yhi = send(to_yn, 0, 1), send(to_yp, 0, -1)
     drift = inner_drift(level, velocity)
-    adv, to_xp, to_xn, to_yp, to_yn = advect(tiles, level, xlo, xhi, ylo, yhi, velocity, drift)
+    adv, to_xp, to_xn, to_yp, to_yn, tail_p, tail_n = advect(
+        tiles, level, xlo, xhi, ylo, yhi, velocity, drift
+    )
     axlo, axhi = send(to_xn, 1, 0), send(to_xp, -1, 0)
     aylo, ayhi = send(to_yn, 0, 1), send(to_yp, 0, -1)
     row = lax.broadcasted_iota(jnp.int32, (1, 8, 1), 1)
-    none = jnp.zeros((4, 2 * LANES), F32)
-
-    def corners(rows, mark, y):
+
+    def corners(rows, mark, tail):
         faces = [jnp.where(row == mark, f[DEEP:, rows], f[:DEEP, rows]) for f in (axlo, axhi)]
-        tail = jnp.concatenate((xlo[4::2, y], xhi[3:-1:2, y], none), axis=0)
-        return jnp.concatenate(faces + [tail.reshape(2, 8, 2 * LANES)], axis=0)
-
-    clo = send(corners(slice(-8, None), 0, CY - 1), 0, 1)
-    chi = send(corners(slice(0, 8), 7, 0), 0, -1)
-    cur, weight, part = sweeps(tiles, adv, (axlo, axhi, aylo, ayhi, clo, chi))
-    return extend(
-        total(part), cur, weight, stress, (xlo, xhi, ylo, yhi, clo, chi)
-    )
+        return jnp.concatenate(faces + [tail], axis=0)
+
+    clo = send(corners(slice(-8, None), 0, tail_n), 0, 1)
+    chi = send(corners(slice(0, 8), 7, tail_p), 0, -1)
+    cur, weight, part = sweeps(tiles, adv, (axlo, axhi, aylo, ayhi, clo, chi), nx * ny)
+    parts = lax.all_to_all(part, ("gx", "gy"), 0, 0, tiled=True)
+    return extend(parts, cur, weight, stress, (xlo, xhi, ylo, yhi, clo, chi))
 
 
 def solution(mesh):

time: 147 us -> 107 us (0.73)
  Pallas kernels: 89 us -> 53.6 us
  blocking collectives: 0 us -> 17.8 us
  waiting for transfers between devices: 16.6 us -> 6.87 us
  starting transfers between devices: 32.7 us -> 23.1 us
  local copies, waits for them, and re-layouts: 5.74 us -> 4.04 us
    pallas_call x1, Pallas kernels: 32.2 us -> 2.4 us  [cut(): pl.pallas_call(cut_kernel, out_shape=[message] * 4, in_specs=[ANY] * 2, o...]
    all_to_all x0 -> x1, blocking collectives: none -> 17.8 us  [on_device(): parts = lax.all_to_all(part, ('gx', 'gy'), 0, 0, tiled=True)]
    ppermute x10 -> x0, waiting for transfers between devices: 13.7 us -> none  [total(): moved = [lax.ppermute(value, axis, list(enumerate(move))) for move in moves]]
    ppermute x10 -> x0, starting transfers between devices: 9.99 us -> none  [total(): moved = [lax.ppermute(value, axis, list(enumerate(move))) for move in moves]]
    pallas_call x1, Pallas kernels: 21 us -> 26 us  [extend(): pl.pallas_call(extend_kernel, out_shape=[shape(CX, CY, z), shape(COMPS, C...]
    ppermute x6, waiting for transfers between devices: 2.85 us -> 6.86 us  [send(): return lax.ppermute(value, 'gy', [(i, (i + dy) % ny) for i in range(ny)])]
    pallas_call x1, Pallas kernels: 19.6 us -> 15.8 us  [sweeps(): pl.pallas_call(sweep_kernel, out_shape=[shape(CX + 4, 2, ROWS, LANES), sh...]
    pallas_call x1, Pallas kernels: 9.59 us -> 6.08 us  [inner_drift(): pl.pallas_call(inner_kernel, out_shape=jax.ShapeDtypeStruct(level.shape,...]
  transfers between devices with their start and end apart: 20 -> 10, of which waited for: 10 -> 2; matrix products, arithmetic and copies ran while one was open for 2% -> 0% of each run, Pallas kernels for 7% -> 6%
where the time goes in v5:
time: 107 us; the launch traced here: 106 us
  Pallas kernels  53.6 us (50%)
  starting transfers between devices  23.1 us (22%)
  blocking collectives  17.8 us (17%)
  waiting for transfers between devices  6.87 us (6%)
  local copies, waits for them, and re-layouts  4.04 us (4%)
    pallas_call x1, Pallas kernels, extend(): pl.pallas_call(extend_kernel, out_shape=[shape(CX, CY, z), shape(COMPS, C...  26 us
    all_to_all x1, blocking collectives, on_device(): parts = lax.all_to_all(part, ('gx', 'gy'), 0, 0, tiled=True)  17.8 us
    ppermute x6, starting transfers between devices, send(): return lax.ppermute(value, 'gy', [(i, (i + dy) % ny) for i in range(ny)])  17.1 us
    pallas_call x1, Pallas kernels, sweeps(): pl.pallas_call(sweep_kernel, out_shape=[shape(CX + 4, 2, ROWS, LANES), sh...  15.8 us
    ppermute x6, waiting for transfers between devices, send(): return lax.ppermute(value, 'gy', [(i, (i + dy) % ny) for i in range(ny)])  6.86 us
    pallas_call x1, Pallas kernels, inner_drift(): pl.pallas_call(inner_kernel, out_shape=jax.ShapeDtypeStruct(level.shape,...  6.08 us
    ppermute x4, starting transfers between devices, send(): return lax.ppermute(value, 'gx', [(i, (i + dx) % nx) for i in range(nx)])  5.92 us
    unnamed x14, local copies, waits for them, and re-layouts  4.03 us
  transfers between devices with their start and end apart: 10, of which 2 were waited for; matrix products, arithmetic and copies ran while one was open for 0% of the time, Pallas kernels for 6%

profile of v5, /device:TPU:0, one launch (start us, length us, event | category | flops | bytes accessed | tf_op | source)
XLA Modules:
  0.0 106.5 jit_solution(17485761463463867627)
XLA Ops:
  0.6 0.0 copy-start
  0.6 2.8 %copy-done = f32[6,32,32,256]{3,2,1,0:T(8,128)S(1)} copy-done((f32[6,32,32,256]{3,2,1,0:T(8,128)S(1)}, f32[6,32,32,256]{3,2,1,0:T(8,128)}, u32[]{:S(2)}) %copy-start) | copy-done | bytes 6291480
  3.4 0.0 copy-start.1
  3.4 1.2 %copy-done.1 = f32[32,32,256]{2,1,0:T(8,128)S(1)} copy-done((f32[32,32,256]{2,1,0:T(8,128)S(1)}, f32[32,32,256]{2,1,0:T(8,128)}, u32[]{:S(2)}) %copy-start.1) | copy-done | bytes 1048600
  4.6 0.0 copy-start.3
  4.6 2.4 %cut.1 = (f32[15,32,256]{2,1,0:T(8,128)S(1)}, f32[15,32,256]{2,1,0:T(8,128)S(1)}, f32[15,32,256]{2,1,0:T(8,128)S(1)}, f32[15,32,256]{2,1,0:T(8,128)S(1)}) custom-call(f32[32,32,256]{2,1,0:T(8,128)S(1)} %copy-done.1, f32[6,32,32,256]{3,2,1,0:T(8,128)S(1)} %copy-done), custom_call_target="tpu_custom_call" | custom-call | tf_op jit(solution)/shard_map/cut/pallas_call | solution.py:136
  7.1 0.0 copy-start.2
  7.1 0.0 copy-start.4
  7.1 0.0 collective-permute-start
  7.1 2.9 %collective-permute-start.1 = (f32[15,32,256]{2,1,0:T(8,128)S(1)}, f32[15,32,256]{2,1,0:T(8,128)S(1)}, u32[]{:S(2)}, u32[]{:S(2)}) collective-permute-start(f32[15,32,256]{2,1,0:T(8,128)S(1)} %get-tuple-element.17), channel_id=1, source_target_pairs={{0,112},{16,0},{32,16},{48,32},{64,48},{80,64},{96,80},{112,96},{1... | collective-permute-start | bytes 1474568 | tf_op jit(solution)/shard_map/ppermute | solution.py:676
  10.0 2.0 %collective-permute-start.2 = (f32[15,32,256]{2,1,0:T(8,128)S(1)}, f32[15,32,256]{2,1,0:T(8,128)S(1)}, u32[]{:S(2)}, u32[]{:S(2)}) collective-permute-start(f32[15,32,256]{2,1,0:T(8,128)S(1)} %get-tuple-element.18), channel_id=1, source_target_pairs={{0,1},{1,2},{2,3},{3,4},{4,5},{5,6},{6,7},{7,8},{8,9},{9,10},{10,1... | collective-permute-start | bytes 1474568 | tf_op jit(solution)/shard_map/ppermute | solution.py:678
  12.0 4.3 %collective-permute-start.3 = (f32[15,32,256]{2,1,0:T(8,128)S(1)}, f32[15,32,256]{2,1,0:T(8,128)S(1)}, u32[]{:S(2)}, u32[]{:S(2)}) collective-permute-start(f32[15,32,256]{2,1,0:T(8,128)S(1)} %get-tuple-element.19), channel_id=1, source_target_pairs={{0,15},{1,0},{2,1},{3,2},{4,3},{5,4},{6,5},{7,6},{8,7},{9,8},{10,9... | collective-permute-start | bytes 1474568 | tf_op jit(solution)/shard_map/ppermute | solution.py:678
  16.4 0.0 copy-done.3
  16.4 0.0 slice-start
  16.4 6.1 %inner_drift.1.drift = f32[32,32,256]{2,1,0:T(8,128)S(1)} custom-call(f32[32,32,256]{2,1,0:T(8,128)S(1)} %copy-done.1, bf16[3,32,32,256]{3,2,1,0:T(8,128)(2,1)S(1)} %copy-done.3), custom_call_target="tpu_custom_call" | custom-call | flops 47185920 | bytes 3670016 | tf_op jit(solution)/shard_map/inner_drift/pallas_call | solution.py:193
  22.5 0.0 slice-start.1
  22.5 0.0 collective-permute-done.xlo
  22.5 0.0 collective-permute-done.1.xhi
  22.5 4.0 %collective-permute-done.2.ylo = f32[15,32,256]{2,1,0:T(8,128)S(1)} collective-permute-done((f32[15,32,256]{2,1,0:T(8,128)S(1)}, f32[15,32,256]{2,1,0:T(8,128)S(1)}, u32[]{:S(2)}, u32[]{:S(2)}) %collective-permute-start.2) | collective-permute-done | bytes 491552 | tf_op jit(solution)/shard_map/ppermute | solution.py:678
  26.5 0.0 collective-permute-done.3.yhi
  26.5 0.0 copy-done.2
  26.5 0.0 copy-done.4
  26.5 3.3 %advect.1 = (f32[32,32,256]{2,1,0:T(8,128)S(1)}, f32[8,32,256]{2,1,0:T(8,128)S(1)}, f32[8,32,256]{2,1,0:T(8,128)S(1)}, f32[32,8,256]{2,1,0:T(8,128)S(1)}, f32[32...) custom-call(s32[1,1,32]{2,1,0:T(1,128)S(1)} %copy-done.4, f32[32,32,256]{2,1,0:T(8,128)S(1)} %copy-done.2, ...), custom_call_target="tpu_custom_call" | custom-call | tf_op jit(solution)/shard_map/advect/pallas_call | solution.py:303
  29.8 0.0 collective-permute-start.4
  29.8 2.9 %collective-permute-start.5 = (f32[8,32,256]{2,1,0:T(8,128)S(1)}, f32[8,32,256]{2,1,0:T(8,128)S(1)}, u32[]{:S(2)}, u32[]{:S(2)}) collective-permute-start(f32[8,32,256]{2,1,0:T(8,128)S(1)} %get-tuple-element.22), channel_id=1, source_target_pairs={{0,112},{16,0},{32,16},{48,32},{64,48},{80,64},{96,80},{112,96},{1... | collective-permute-start | bytes 786440 | tf_op jit(solution)/shard_map/ppermute | solution.py:676
  32.8 0.0 collective-permute-start.6
  32.8 5.3 %collective-permute-start.7 = (f32[32,8,256]{2,1,0:T(8,128)S(1)}, f32[32,8,256]{2,1,0:T(8,128)S(1)}, u32[]{:S(2)}, u32[]{:S(2)}) collective-permute-start(f32[32,8,256]{2,1,0:T(8,128)S(1)} %get-tuple-element.24), channel_id=1, source_target_pairs={{0,15},{1,0},{2,1},{3,2},{4,3},{5,4},{6,5},{7,6},{8,7},{9,8},{10,9... | collective-permute-start | bytes 786440 | tf_op jit(solution)/shard_map/ppermute | solution.py:678
  38.1 0.0 collective-permute-done.4.xlo
  38.1 0.0 collective-permute-done.5.xhi
  38.2 0.1 slice_select_fusion
  38.3 0.1 collective-permute-start.8
  38.4 5.4 %collective-permute-start.9 = (f32[16,8,256]{2,1,0:T(8,128)S(1)}, f32[16,8,256]{2,1,0:T(8,128)S(1)}, u32[]{:S(2)}, u32[]{:S(2)}) collective-permute-start(f32[16,8,256]{2,1,0:T(8,128)S(1)} %pad_maximum_fusion.1), channel_id=1, source_target_pairs={{0,15},{1,0},{2,1},{3,2},{4,3},{5,4},{6,5},{7,6},{8,7},{9,8},{10,9... | collective-permute-start | bytes 393224 | tf_op jit(solution)/shard_map/ppermute | solution.py:678
  43.8 0.0 collective-permute-done.6.ylo
  43.8 0.0 collective-permute-done.7.yhi
  43.8 2.9 %collective-permute-done.8.clo = f32[16,8,256]{2,1,0:T(8,128)S(1)} collective-permute-done((f32[16,8,256]{2,1,0:T(8,128)S(1)}, f32[16,8,256]{2,1,0:T(8,128)S(1)}, u32[]{:S(2)}, u32[]{:S(2)}) %collective-permute-start.8) | collective-permute-done | bytes 131104 | tf_op jit(solution)/shard_map/ppermute | solution.py:678
  46.6 0.0 collective-permute-done.9.chi
  46.6 15.8 %sweeps.1 = (f32[36,2,64,128]{3,2,1,0:T(8,128)S(1)}, f32[34,2,64,128]{3,2,1,0:T(8,128)S(1)}, f32[128,1,128]{2,1,0:T(1,128)S(1)}) custom-call(s32[1,1,32]{2,1,0:T(1,128)S(1)} %copy-done.4, f32[32,32,256]{2,1,0:T(8,128)S(1)} %get-tuple-element.20.adv, f32[8,32,256]{2,1,0:T(8,128)S(1)} %collective-permute-done.4.xlo, ...), custom_call_target="tpu_custom_call" | custom-call | tf_op jit(solution)/shard_map/sweeps/pallas_call | solution.py:464
  62.5 17.8 %all_to_all.5.parts = f32[128,1,128]{2,1,0:T(1,128)S(1)} all-to-all(f32[128,1,128]{2,1,0:T(1,128)S(1)} %get-tuple-element.27), channel_id=1, replica_groups=mesh['gx'=8,'gy'=16] {'gx','gy'}, dimensions={0} | all-to-all | bytes 131072 | tf_op jit(solution)/shard_map/all_to_all | solution.py:702
  80.3 0.0 slice-done
  80.3 0.0 slice-done.1
  80.3 26.0 %extend.1 = (f32[32,32,256]{2,1,0:T(8,128)}, f32[6,32,32,256]{3,2,1,0:T(8,128)}) custom-call(f32[128,1,128]{2,1,0:T(1,128)S(1)} %all_to_all.5.parts, f32[36,2,64,128]{3,2,1,0:T(8,128)S(1)} %get-tuple-element.28.cur, f32[34,2,64,128]{3,2,1,0:T(8,128)S(1)} %get-tuple-element.29.weight, f32[6,32,32,256]{3,2,1,0:T(8,128)S(1)} %bitcast.9, ...), custom_call_target="tpu_custom_call" | custom-call | tf_op jit(solution)/shard_map/extend/pallas_call | solution.py:652
  (6 shorter events, 0.0 us)
Async XLA Ops:
  0.6 2.8 %copy-start = (f32[6,32,32,256]{3,2,1,0:T(8,128)S(1)}, f32[6,32,32,256]{3,2,1,0:T(8,128)}, u32[]{:S(2)}) copy-start(f32[6,32,32,256]{3,2,1,0:T(8,128)} %stress.3) | copy-start | bytes 18874372
  3.4 1.2 %copy-start.1 = (f32[32,32,256]{2,1,0:T(8,128)S(1)}, f32[32,32,256]{2,1,0:T(8,128)}, u32[]{:S(2)}) copy-start(f32[32,32,256]{2,1,0:T(8,128)} %level.5) | copy-start | bytes 3145732
  4.6 11.7 %copy-start.3 = (bf16[3,32,32,256]{3,2,1,0:T(8,128)(2,1)S(1)}, bf16[3,32,32,256]{3,2,1,0:T(8,128)(2,1)}, u32[]{:S(2)}) copy-start(bf16[3,32,32,256]{3,2,1,0:T(8,128)(2,1)} %speed.3) | copy-start | bytes 4718596
  7.1 19.4 %copy-start.2 = (f32[32,32,256]{2,1,0:T(8,128)S(1)}, f32[32,32,256]{2,1,0:T(8,128)}, u32[]{:S(2)}) copy-start(f32[32,32,256]{2,1,0:T(8,128)} %level.5) | copy-start | bytes 3145732
  7.1 19.4 %copy-start.4 = (s32[1,1,32]{2,1,0:T(1,128)S(1)}, s32[1,1,32]{2,1,0:T(1,128)}, u32[]{:S(2)}) copy-start(s32[1,1,32]{2,1,0:T(1,128)} %tiles.3) | copy-start | bytes 388
  7.1 15.4 %collective-permute-start = (f32[15,32,256]{2,1,0:T(8,128)S(1)}, f32[15,32,256]{2,1,0:T(8,128)S(1)}, u32[]{:S(2)}, u32[]{:S(2)}) collective-permute-start(f32[15,32,256]{2,1,0:T(8,128)S(1)} %get-tuple-element.16), channel_id=1, source_target_pairs={{0,16},{16,32},{32,48},{48,64},{64,80},{80,96},{96,112},{112,0},{1... | collective-permute-start | bytes 1474568 | tf_op jit(solution)/shard_map/ppermute | solution.py:676
  7.1 15.4 %collective-permute-start.1 = (f32[15,32,256]{2,1,0:T(8,128)S(1)}, f32[15,32,256]{2,1,0:T(8,128)S(1)}, u32[]{:S(2)}, u32[]{:S(2)}) collective-permute-start(f32[15,32,256]{2,1,0:T(8,128)S(1)} %get-tuple-element.17), channel_id=1, source_target_pairs={{0,112},{16,0},{32,16},{48,32},{64,48},{80,64},{96,80},{112,96},{1... | collective-permute-start | bytes 1474568 | tf_op jit(solution)/shard_map/ppermute | solution.py:676
  10.0 16.4 %collective-permute-start.2 = (f32[15,32,256]{2,1,0:T(8,128)S(1)}, f32[15,32,256]{2,1,0:T(8,128)S(1)}, u32[]{:S(2)}, u32[]{:S(2)}) collective-permute-start(f32[15,32,256]{2,1,0:T(8,128)S(1)} %get-tuple-element.18), channel_id=1, source_target_pairs={{0,1},{1,2},{2,3},{3,4},{4,5},{5,6},{6,7},{7,8},{8,9},{9,10},{10,1... | collective-permute-start | bytes 1474568 | tf_op jit(solution)/shard_map/ppermute | solution.py:678
  12.0 14.4 %collective-permute-start.3 = (f32[15,32,256]{2,1,0:T(8,128)S(1)}, f32[15,32,256]{2,1,0:T(8,128)S(1)}, u32[]{:S(2)}, u32[]{:S(2)}) collective-permute-start(f32[15,32,256]{2,1,0:T(8,128)S(1)} %get-tuple-element.19), channel_id=1, source_target_pairs={{0,15},{1,0},{2,1},{3,2},{4,3},{5,4},{6,5},{7,6},{8,7},{9,8},{10,9... | collective-permute-start | bytes 1474568 | tf_op jit(solution)/shard_map/ppermute | solution.py:678
  16.4 63.9 %slice-start = ((s8[6291456]{0:T(1024)(128)(4,1)}), s8[4194304]{0:T(1024)(128)(4,1)S(1)}, s32[]{:S(2)}) async-start(s8[6291456]{0:T(1024)(128)(4,1)} %bitcast.8), calls=%async_computation.1 | async-start | bytes 8388608
  22.5 57.8 %slice-start.1 = ((s8[6291456]{0:T(1024)(128)(4,1)}), s8[2097152]{0:T(1024)(128)(4,1)S(1)}, s32[]{:S(2)}) async-start(s8[6291456]{0:T(1024)(128)(4,1)} %bitcast.8), calls=%async_computation.2 | async-start | bytes 4194304
  29.8 8.3 %collective-permute-start.4 = (f32[8,32,256]{2,1,0:T(8,128)S(1)}, f32[8,32,256]{2,1,0:T(8,128)S(1)}, u32[]{:S(2)}, u32[]{:S(2)}) collective-permute-start(f32[8,32,256]{2,1,0:T(8,128)S(1)} %get-tuple-element.21), channel_id=1, source_target_pairs={{0,16},{16,32},{32,48},{48,64},{64,80},{80,96},{96,112},{112,0},{1... | collective-permute-start | bytes 786440 | tf_op jit(solution)/shard_map/ppermute | solution.py:676
  29.8 8.3 %collective-permute-start.5 = (f32[8,32,256]{2,1,0:T(8,128)S(1)}, f32[8,32,256]{2,1,0:T(8,128)S(1)}, u32[]{:S(2)}, u32[]{:S(2)}) collective-permute-start(f32[8,32,256]{2,1,0:T(8,128)S(1)} %get-tuple-element.22), channel_id=1, source_target_pairs={{0,112},{16,0},{32,16},{48,32},{64,48},{80,64},{96,80},{112,96},{1... | collective-permute-start | bytes 786440 | tf_op jit(solution)/shard_map/ppermute | solution.py:676
  32.8 11.0 %collective-permute-start.6 = (f32[32,8,256]{2,1,0:T(8,128)S(1)}, f32[32,8,256]{2,1,0:T(8,128)S(1)}, u32[]{:S(2)}, u32[]{:S(2)}) collective-permute-start(f32[32,8,256]{2,1,0:T(8,128)S(1)} %get-tuple-element.23), channel_id=1, source_target_pairs={{0,1},{1,2},{2,3},{3,4},{4,5},{5,6},{6,7},{7,8},{8,9},{9,10},{10,1... | collective-permute-start | bytes 786440 | tf_op jit(solution)/shard_map/ppermute | solution.py:678
  32.8 11.0 %collective-permute-start.7 = (f32[32,8,256]{2,1,0:T(8,128)S(1)}, f32[32,8,256]{2,1,0:T(8,128)S(1)}, u32[]{:S(2)}, u32[]{:S(2)}) collective-permute-start(f32[32,8,256]{2,1,0:T(8,128)S(1)} %get-tuple-element.24), channel_id=1, source_target_pairs={{0,15},{1,0},{2,1},{3,2},{4,3},{5,4},{6,5},{7,6},{8,7},{9,8},{10,9... | collective-permute-start | bytes 786440 | tf_op jit(solution)/shard_map/ppermute | solution.py:678
  38.3 8.4 %collective-permute-start.8 = (f32[16,8,256]{2,1,0:T(8,128)S(1)}, f32[16,8,256]{2,1,0:T(8,128)S(1)}, u32[]{:S(2)}, u32[]{:S(2)}) collective-permute-start(f32[16,8,256]{2,1,0:T(8,128)S(1)} %pad_maximum_fusion), channel_id=1, source_target_pairs={{0,1},{1,2},{2,3},{3,4},{4,5},{5,6},{6,7},{7,8},{8,9},{9,10},{10,1... | collective-permute-start | bytes 393224 | tf_op jit(solution)/shard_map/ppermute | solution.py:678
  38.4 8.3 %collective-permute-start.9 = (f32[16,8,256]{2,1,0:T(8,128)S(1)}, f32[16,8,256]{2,1,0:T(8,128)S(1)}, u32[]{:S(2)}, u32[]{:S(2)}) collective-permute-start(f32[16,8,256]{2,1,0:T(8,128)S(1)} %pad_maximum_fusion.1), channel_id=1, source_target_pairs={{0,15},{1,0},{2,1},{3,2},{4,3},{5,4},{6,5},{7,6},{8,7},{9,8},{10,9... | collective-permute-start | bytes 393224 | tf_op jit(solution)/shard_map/ppermute | solution.py:678

commit v6 on v5

--- a/solution.py
+++ b/solution.py
@@ -86,7 +86,9 @@
     return [pad[x, h, pl.ds(at + k, size), :] for k in range(-3, 4)]
 
 
-def cut_kernel(level, stress, to_xp, to_xn, to_yp, to_yn, faces, x_sems, y_sems):
+def cut_kernel(
+    level, stress, to_xp, to_xn, to_yp, to_yn, to_syp, to_syn, faces, x_sems, y_sems
+):
     copies = []
     for n, (out, at) in enumerate(((to_xp, 0), (to_xn, CX))):
         deep = lambda size: pl.ds(at and at - size, size)
@@ -114,13 +116,14 @@
             copy.start()
         sides.append(side)
     flat = faces.reshape(1 + COMPS, 2, 2, CX * 8, LANES)
-    for n, out in enumerate((to_yp, to_yn)):
+    for n, outs in enumerate(((to_yp, to_syp), (to_yn, to_syn))):
         for copy in sides[n]:
             copy.wait()
         for h in range(2):
             for m in range(1 + COMPS):
                 depth = 2 if m else 3
-                first = 1 + 2 * m if m else 0
+                out = outs[min(m, 1)]
+                first = 2 * m - 2 if m else 0
                 for k in range(depth):
                     row = k if n == 0 else 8 - depth + k
                     for x in range(0, CX, 8):
@@ -132,18 +135,18 @@
 
 
 def cut(level, stress):
-    message = jax.ShapeDtypeStruct((3 + 2 * COMPS, CX, 2 * LANES), F32)
+    message = lambda planes: jax.ShapeDtypeStruct((planes, CX, 2 * LANES), F32)
     return pl.pallas_call(
         cut_kernel,
-        out_shape=[message] * 4,
+        out_shape=[message(3 + 2 * COMPS)] * 2 + [message(3)] * 2 + [message(2 * COMPS)] * 2,
         in_specs=[ANY] * 2,
-        out_specs=[VMEM] * 4,
+        out_specs=[VMEM] * 6,
         scratch_shapes=[
             pltpu.VMEM((1 + COMPS, 2, 2, CX, 8, LANES), F32),
             pltpu.SemaphoreType.DMA((2, 1 + COMPS)),
             pltpu.SemaphoreType.DMA((1 + COMPS, 2, 2)),
         ],
-        compiler_params=pltpu.CompilerParams(vmem_limit_bytes=10 * MIB),
+        compiler_params=pltpu.CompilerParams(vmem_limit_bytes=57 * MIB),
         name="cut",
     )(level, stress)
 
@@ -223,7 +226,7 @@
                 )
             )
     for n, src in enumerate((ylo, yhi)):
-        copies.append(pltpu.make_async_copy(src.at[pl.ds(0, 3)], faces.at[n], y_sems.at[n]))
+        copies.append(pltpu.make_async_copy(src, faces.at[n], y_sems.at[n]))
     for n, src in enumerate((xlo, xhi)):
         for m, y in enumerate((0, CY - 8)):
             copies.append(
@@ -527,7 +530,7 @@
                     for x in range(0, CX, 8):
                         at = ((x + 2) * 2 + h) * ROWS + row + k
                         flat[c, pl.ds(at, 8, stride=2 * ROWS), :] = face[
-                            3 + 2 * c + k, x : x + 8, half(h)
+                            2 * c + k, x : x + 8, half(h)
                         ]
             for corner, row in ((clo, OWN - 1), (chi, OWN + CY)):
                 for x, n in ((1, c), (CX + 2, COMPS + c)):
@@ -663,7 +666,7 @@
             pltpu.SemaphoreType.DMA((2, 2, COMPS)),
             pltpu.SemaphoreType.DMA((4, 2)),
         ],
-        compiler_params=pltpu.CompilerParams(vmem_limit_bytes=36 * MIB),
+        compiler_params=pltpu.CompilerParams(vmem_limit_bytes=46 * MIB),
         name="extend",
     )(parts, cur, weight, stress, *halos)
 
@@ -681,7 +684,7 @@
         ]
         return lax.ppermute(value, ("gx", "gy"), pairs)
 
-    to_xp, to_xn, to_yp, to_yn = cut(level, stress)
+    to_xp, to_xn, to_yp, to_yn, to_syp, to_syn = cut(level, stress)
     xlo, xhi = send(to_xn, 1, 0), send(to_xp, -1, 0)
     ylo, yhi = send(to_yn, 0, 1), send(to_yp, 0, -1)
     drift = inner_drift(level, velocity)
@@ -698,9 +701,13 @@
 
     clo = send(corners(slice(-8, None), 0, tail_n), 0, 1)
     chi = send(corners(slice(0, 8), 7, tail_p), 0, -1)
+    to_syp, to_syn, aylo, ayhi, clo, chi = lax.optimization_barrier(
+        (to_syp, to_syn, aylo, ayhi, clo, chi)
+    )
+    sylo, syhi = send(to_syn, 0, 1), send(to_syp, 0, -1)
     cur, weight, part = sweeps(tiles, adv, (axlo, axhi, aylo, ayhi, clo, chi), nx * ny)
     parts = lax.all_to_all(part, ("gx", "gy"), 0, 0, tiled=True)
-    return extend(parts, cur, weight, stress, (xlo, xhi, ylo, yhi, clo, chi))
+    return extend(parts, cur, weight, stress, (xlo, xhi, sylo, syhi, clo, chi))
 
 
 def solution(mesh):

time: 107 us -> 103 us (0.963)
  starting transfers between devices: 23.1 us -> 28.5 us
  local copies, waits for them, and re-layouts: 4.04 us -> 0.03 us
  waiting for transfers between devices: 6.87 us -> 2.88 us
  blocking collectives: 17.8 us -> 14.2 us
  Pallas kernels: 53.6 us -> 55.7 us
    ppermute x6 -> x8, starting transfers between devices: 17.1 us -> 22.6 us  [send(): return lax.ppermute(value, 'gy', [(i, (i + dy) % ny) for i in range(ny)])]
    unnamed x14 -> x10, local copies, waits for them, and re-layouts: 4.03 us -> 0.02 us
    ppermute x6 -> x8, waiting for transfers between devices: 6.86 us -> 2.87 us  [send(): return lax.ppermute(value, 'gy', [(i, (i + dy) % ny) for i in range(ny)])]
    all_to_all x1, blocking collectives: 17.8 us -> 14.2 us  [on_device(): parts = lax.all_to_all(part, ('gx', 'gy'), 0, 0, tiled=True)]
    pallas_call x1, Pallas kernels: 2.4 us -> 4.3 us  [cut(): pl.pallas_call(cut_kernel, out_shape=[message(3 + 2 * COMPS)] * 2 + [mess...]
  transfers between devices with their start and end apart: 10 -> 12, of which waited for: 2 -> 1; matrix products, arithmetic and copies ran while one was open for 0% -> 0% of each run, Pallas kernels for 6% -> 21%
where the time goes in v6:
time: 103 us; the launch traced here: 102 us
  Pallas kernels  55.7 us (54%)
  starting transfers between devices  28.5 us (28%)
  blocking collectives  14.2 us (14%)
  waiting for transfers between devices  2.88 us (3%)
    pallas_call x1, Pallas kernels, extend(): pl.pallas_call(extend_kernel, out_shape=[shape(CX, CY, z), shape(COMPS, C...  26.2 us
    ppermute x8, starting transfers between devices, send(): return lax.ppermute(value, 'gy', [(i, (i + dy) % ny) for i in range(ny)])  22.6 us
    pallas_call x1, Pallas kernels, sweeps(): pl.pallas_call(sweep_kernel, out_shape=[shape(CX + 4, 2, ROWS, LANES), sh...  15.8 us
    all_to_all x1, blocking collectives, on_device(): parts = lax.all_to_all(part, ('gx', 'gy'), 0, 0, tiled=True)  14.2 us
    pallas_call x1, Pallas kernels, inner_drift(): pl.pallas_call(inner_kernel, out_shape=jax.ShapeDtypeStruct(level.shape,...  6.08 us
    ppermute x4, starting transfers between devices, send(): return lax.ppermute(value, 'gx', [(i, (i + dx) % nx) for i in range(nx)])  5.92 us
    pallas_call x1, Pallas kernels, cut(): pl.pallas_call(cut_kernel, out_shape=[message(3 + 2 * COMPS)] * 2 + [mess...  4.3 us
    pallas_call x1, Pallas kernels, advect(): pl.pallas_call(advect_kernel, out_shape=[shape(CX, CY, z)] + [shape(8, CY...  3.29 us
  transfers between devices with their start and end apart: 12, of which 1 were waited for; matrix products, arithmetic and copies ran while one was open for 0% of the time, Pallas kernels for 21%

profile of v6, /device:TPU:0, one launch (start us, length us, event | category | flops | bytes accessed | tf_op | source)
XLA Modules:
  0.0 102.4 jit_solution(11428590731924777006)
XLA Ops:
  0.6 0.0 copy-start
  0.6 0.0 copy-start.1
  0.6 4.3 %cut.1 = (f32[15,32,256]{2,1,0:T(8,128)}, f32[15,32,256]{2,1,0:T(8,128)}, f32[3,32,256]{2,1,0:T(8,128)}, f32[3,32,256]{2,1,0:T(8,128)}, f32[12,32,256]{2,1,0:T(8,128)}, /*index=5*/f32[12,32,256]{2,1,0:T(8,128)}) custom-call(f32[32,32,256]{2,1,0:T(8,128)} %level.5, f32[6,32,32,256]{3,2,1,0:T(8,128)} %stress.3), custom_call_target="tpu_custom_call" | custom-call | tf_op jit(solution)/shard_map/cut/pallas_call | solution.py:139
  5.0 0.0 copy-start.2
  5.0 0.0 collective-permute-start
  5.0 2.9 %collective-permute-start.1 = (f32[15,32,256]{2,1,0:T(8,128)}, f32[15,32,256]{2,1,0:T(8,128)S(1)}, u32[]{:S(2)}, u32[]{:S(2)}) collective-permute-start(f32[15,32,256]{2,1,0:T(8,128)} %get-tuple-element.25), channel_id=1, source_target_pairs={{0,112},{16,0},{32,16},{48,32},{64,48},{80,64},{96,80},{112,96},{1... | collective-permute-start | bytes 1474568 | tf_op jit(solution)/shard_map/ppermute | solution.py:679
  7.9 2.0 %collective-permute-start.2 = (f32[3,32,256]{2,1,0:T(8,128)}, f32[3,32,256]{2,1,0:T(8,128)S(1)}, u32[]{:S(2)}, u32[]{:S(2)}) collective-permute-start(f32[3,32,256]{2,1,0:T(8,128)} %get-tuple-element.26), channel_id=1, source_target_pairs={{0,1},{1,2},{2,3},{3,4},{4,5},{5,6},{6,7},{7,8},{8,9},{9,10},{10,1... | collective-permute-start | bytes 294920 | tf_op jit(solution)/shard_map/ppermute | solution.py:681
  9.9 4.3 %collective-permute-start.3 = (f32[3,32,256]{2,1,0:T(8,128)}, f32[3,32,256]{2,1,0:T(8,128)S(1)}, u32[]{:S(2)}, u32[]{:S(2)}) collective-permute-start(f32[3,32,256]{2,1,0:T(8,128)} %get-tuple-element.27), channel_id=1, source_target_pairs={{0,15},{1,0},{2,1},{3,2},{4,3},{5,4},{6,5},{7,6},{8,7},{9,8},{10,9... | collective-permute-start | bytes 294920 | tf_op jit(solution)/shard_map/ppermute | solution.py:681
  14.3 0.0 copy-done
  14.3 0.0 copy-done.1
  14.3 6.1 %inner_drift.1.drift = f32[32,32,256]{2,1,0:T(8,128)S(1)} custom-call(f32[32,32,256]{2,1,0:T(8,128)S(1)} %copy-done, bf16[3,32,32,256]{3,2,1,0:T(8,128)(2,1)S(1)} %copy-done.1), custom_call_target="tpu_custom_call" | custom-call | flops 47185920 | bytes 3670016 | tf_op jit(solution)/shard_map/inner_drift/pallas_call | solution.py:196
  20.4 0.0 copy-start.4
  20.4 0.0 copy-start.3
  20.4 0.0 collective-permute-done.2.ylo
  20.4 0.0 collective-permute-done.3.yhi
  20.4 0.0 collective-permute-done.xlo
  20.4 0.0 collective-permute-done.1.xhi
  20.4 0.0 copy-done.2
  20.4 3.3 %advect.1 = (f32[32,32,256]{2,1,0:T(8,128)S(1)}, f32[8,32,256]{2,1,0:T(8,128)S(1)}, f32[8,32,256]{2,1,0:T(8,128)S(1)}, f32[32,8,256]{2,1,0:T(8,128)S(1)}, f32[32...) custom-call(s32[1,1,32]{2,1,0:T(1,128)S(1)} %copy-done.2, f32[32,32,256]{2,1,0:T(8,128)S(1)} %copy-done, ...), custom_call_target="tpu_custom_call" | custom-call | tf_op jit(solution)/shard_map/advect/pallas_call | solution.py:306
  23.7 0.0 collective-permute-start.4
  23.7 2.9 %collective-permute-start.5 = (f32[8,32,256]{2,1,0:T(8,128)S(1)}, f32[8,32,256]{2,1,0:T(8,128)S(1)}, u32[]{:S(2)}, u32[]{:S(2)}) collective-permute-start(f32[8,32,256]{2,1,0:T(8,128)S(1)} %get-tuple-element.30), channel_id=1, source_target_pairs={{0,112},{16,0},{32,16},{48,32},{64,48},{80,64},{96,80},{112,96},{1... | collective-permute-start | bytes 786440 | tf_op jit(solution)/shard_map/ppermute | solution.py:679
  26.7 0.0 collective-permute-start.6
  26.7 5.3 %collective-permute-start.7 = (f32[32,8,256]{2,1,0:T(8,128)S(1)}, f32[32,8,256]{2,1,0:T(8,128)S(1)}, u32[]{:S(2)}, u32[]{:S(2)}) collective-permute-start(f32[32,8,256]{2,1,0:T(8,128)S(1)} %get-tuple-element.34), channel_id=1, source_target_pairs={{0,15},{1,0},{2,1},{3,2},{4,3},{5,4},{6,5},{7,6},{8,7},{9,8},{10,9... | collective-permute-start | bytes 786440 | tf_op jit(solution)/shard_map/ppermute | solution.py:681
  32.0 0.0 collective-permute-done.4.xlo
  32.1 0.0 collective-permute-done.5.xhi
  32.1 0.1 slice_select_fusion
  32.2 0.1 collective-permute-start.8
  32.3 5.4 %collective-permute-start.9 = (f32[16,8,256]{2,1,0:T(8,128)S(1)}, f32[16,8,256]{2,1,0:T(8,128)S(1)}, u32[]{:S(2)}, u32[]{:S(2)}) collective-permute-start(f32[16,8,256]{2,1,0:T(8,128)S(1)} %pad_maximum_fusion.1), channel_id=1, source_target_pairs={{0,15},{1,0},{2,1},{3,2},{4,3},{5,4},{6,5},{7,6},{8,7},{9,8},{10,9... | collective-permute-start | bytes 393224 | tf_op jit(solution)/shard_map/ppermute | solution.py:681
  37.7 0.0 collective-permute-done.6.ylo
  37.7 0.0 collective-permute-done.7.yhi
  37.7 2.9 %collective-permute-done.8.clo = f32[16,8,256]{2,1,0:T(8,128)S(1)} collective-permute-done((f32[16,8,256]{2,1,0:T(8,128)S(1)}, f32[16,8,256]{2,1,0:T(8,128)S(1)}, u32[]{:S(2)}, u32[]{:S(2)}) %collective-permute-start.8) | collective-permute-done | bytes 131104 | tf_op jit(solution)/shard_map/ppermute | solution.py:681
  40.5 0.0 collective-permute-done.9.chi
  40.5 0.0 copy-done.4
  40.5 0.0 collective-permute-start.10
  40.6 0.0 copy-done.3
  40.6 5.5 %collective-permute-start.11 = (f32[12,32,256]{2,1,0:T(8,128)S(1)}, f32[12,32,256]{2,1,0:T(8,128)S(1)}, u32[]{:S(2)}, u32[]{:S(2)}) collective-permute-start(f32[12,32,256]{2,1,0:T(8,128)S(1)} %copy-done.3), channel_id=1, source_target_pairs={{0,15},{1,0},{2,1},{3,2},{4,3},{5,4},{6,5},{7,6},{8,7},{9,8},{10,9... | collective-permute-start | bytes 1179656 | tf_op jit(solution)/shard_map/ppermute | solution.py:681
  46.0 15.8 %sweeps.1 = (f32[36,2,64,128]{3,2,1,0:T(8,128)S(1)}, f32[34,2,64,128]{3,2,1,0:T(8,128)S(1)}, f32[128,1,128]{2,1,0:T(1,128)S(1)}) custom-call(s32[1,1,32]{2,1,0:T(1,128)S(1)} %copy-done.2, f32[32,32,256]{2,1,0:T(8,128)S(1)} %get-tuple-element.28.adv, f32[8,32,256]{2,1,0:T(8,128)S(1)} %collective-permute-done.4.xlo, ...), custom_call_target="tpu_custom_call" | custom-call | tf_op jit(solution)/shard_map/sweeps/pallas_call | solution.py:467
  61.9 14.2 %all_to_all.5.parts = f32[128,1,128]{2,1,0:T(1,128)S(1)} all-to-all(f32[128,1,128]{2,1,0:T(1,128)S(1)} %get-tuple-element.41), channel_id=1, replica_groups=mesh['gx'=8,'gy'=16] {'gx','gy'}, dimensions={0} | all-to-all | bytes 131072 | tf_op jit(solution)/shard_map/all_to_all | solution.py:709
  76.1 0.0 collective-permute-done.10.ylo
  76.1 0.0 collective-permute-done.11.yhi
  76.1 26.2 %extend.1 = (f32[32,32,256]{2,1,0:T(8,128)}, f32[6,32,32,256]{3,2,1,0:T(8,128)}) custom-call(f32[128,1,128]{2,1,0:T(1,128)S(1)} %all_to_all.5.parts, f32[36,2,64,128]{3,2,1,0:T(8,128)S(1)} %get-tuple-element.42.cur, f32[34,2,64,128]{3,2,1,0:T(8,128)S(1)} %get-tuple-element.43.weight, f32[6,32,32,256]{3,2,1,0:T(8,128)} %stress.3, ...), custom_call_target="tpu_custom_call" | custom-call | tf_op jit(solution)/shard_map/extend/pallas_call | solution.py:655
  (5 shorter events, 0.0 us)
Async XLA Ops:
  0.6 13.6 %copy-start = (f32[32,32,256]{2,1,0:T(8,128)S(1)}, f32[32,32,256]{2,1,0:T(8,128)}, u32[]{:S(2)}) copy-start(f32[32,32,256]{2,1,0:T(8,128)} %level.5) | copy-start | bytes 3145732
  0.6 13.6 %copy-start.1 = (bf16[3,32,32,256]{3,2,1,0:T(8,128)(2,1)S(1)}, bf16[3,32,32,256]{3,2,1,0:T(8,128)(2,1)}, u32[]{:S(2)}) copy-start(bf16[3,32,32,256]{3,2,1,0:T(8,128)(2,1)} %speed.3) | copy-start | bytes 4718596
  5.0 15.5 %copy-start.2 = (s32[1,1,32]{2,1,0:T(1,128)S(1)}, s32[1,1,32]{2,1,0:T(1,128)}, u32[]{:S(2)}) copy-start(s32[1,1,32]{2,1,0:T(1,128)} %tiles.3) | copy-start | bytes 388
  5.0 15.4 %collective-permute-start = (f32[15,32,256]{2,1,0:T(8,128)}, f32[15,32,256]{2,1,0:T(8,128)S(1)}, u32[]{:S(2)}, u32[]{:S(2)}) collective-permute-start(f32[15,32,256]{2,1,0:T(8,128)} %get-tuple-element.24), channel_id=1, source_target_pairs={{0,16},{16,32},{32,48},{48,64},{64,80},{80,96},{96,112},{112,0},{1... | collective-permute-start | bytes 1474568 | tf_op jit(solution)/shard_map/ppermute | solution.py:679
  5.0 15.4 %collective-permute-start.1 = (f32[15,32,256]{2,1,0:T(8,128)}, f32[15,32,256]{2,1,0:T(8,128)S(1)}, u32[]{:S(2)}, u32[]{:S(2)}) collective-permute-start(f32[15,32,256]{2,1,0:T(8,128)} %get-tuple-element.25), channel_id=1, source_target_pairs={{0,112},{16,0},{32,16},{48,32},{64,48},{80,64},{96,80},{112,96},{1... | collective-permute-start | bytes 1474568 | tf_op jit(solution)/shard_map/ppermute | solution.py:679
  7.9 12.4 %collective-permute-start.2 = (f32[3,32,256]{2,1,0:T(8,128)}, f32[3,32,256]{2,1,0:T(8,128)S(1)}, u32[]{:S(2)}, u32[]{:S(2)}) collective-permute-start(f32[3,32,256]{2,1,0:T(8,128)} %get-tuple-element.26), channel_id=1, source_target_pairs={{0,1},{1,2},{2,3},{3,4},{4,5},{5,6},{6,7},{7,8},{8,9},{9,10},{10,1... | collective-permute-start | bytes 294920 | tf_op jit(solution)/shard_map/ppermute | solution.py:681
  9.9 10.4 %collective-permute-start.3 = (f32[3,32,256]{2,1,0:T(8,128)}, f32[3,32,256]{2,1,0:T(8,128)S(1)}, u32[]{:S(2)}, u32[]{:S(2)}) collective-permute-start(f32[3,32,256]{2,1,0:T(8,128)} %get-tuple-element.27), channel_id=1, source_target_pairs={{0,15},{1,0},{2,1},{3,2},{4,3},{5,4},{6,5},{7,6},{8,7},{9,8},{10,9... | collective-permute-start | bytes 294920 | tf_op jit(solution)/shard_map/ppermute | solution.py:681
  20.4 20.2 %copy-start.4 = (f32[12,32,256]{2,1,0:T(8,128)S(1)}, f32[12,32,256]{2,1,0:T(8,128)}, u32[]{:S(2)}) copy-start(f32[12,32,256]{2,1,0:T(8,128)} %get-tuple-element.44) | copy-start | bytes 1179652
  20.4 20.2 %copy-start.3 = (f32[12,32,256]{2,1,0:T(8,128)S(1)}, f32[12,32,256]{2,1,0:T(8,128)}, u32[]{:S(2)}) copy-start(f32[12,32,256]{2,1,0:T(8,128)} %get-tuple-element.45) | copy-start | bytes 1179652
  23.7 8.3 %collective-permute-start.4 = (f32[8,32,256]{2,1,0:T(8,128)S(1)}, f32[8,32,256]{2,1,0:T(8,128)S(1)}, u32[]{:S(2)}, u32[]{:S(2)}) collective-permute-start(f32[8,32,256]{2,1,0:T(8,128)S(1)} %get-tuple-element.29), channel_id=1, source_target_pairs={{0,16},{16,32},{32,48},{48,64},{64,80},{80,96},{96,112},{112,0},{1... | collective-permute-start | bytes 786440 | tf_op jit(solution)/shard_map/ppermute | solution.py:679
  23.7 8.3 %collective-permute-start.5 = (f32[8,32,256]{2,1,0:T(8,128)S(1)}, f32[8,32,256]{2,1,0:T(8,128)S(1)}, u32[]{:S(2)}, u32[]{:S(2)}) collective-permute-start(f32[8,32,256]{2,1,0:T(8,128)S(1)} %get-tuple-element.30), channel_id=1, source_target_pairs={{0,112},{16,0},{32,16},{48,32},{64,48},{80,64},{96,80},{112,96},{1... | collective-permute-start | bytes 786440 | tf_op jit(solution)/shard_map/ppermute | solution.py:679
  26.7 11.0 %collective-permute-start.6 = (f32[32,8,256]{2,1,0:T(8,128)S(1)}, f32[32,8,256]{2,1,0:T(8,128)S(1)}, u32[]{:S(2)}, u32[]{:S(2)}) collective-permute-start(f32[32,8,256]{2,1,0:T(8,128)S(1)} %get-tuple-element.33), channel_id=1, source_target_pairs={{0,1},{1,2},{2,3},{3,4},{4,5},{5,6},{6,7},{7,8},{8,9},{9,10},{10,1... | collective-permute-start | bytes 786440 | tf_op jit(solution)/shard_map/ppermute | solution.py:681
  26.7 11.0 %collective-permute-start.7 = (f32[32,8,256]{2,1,0:T(8,128)S(1)}, f32[32,8,256]{2,1,0:T(8,128)S(1)}, u32[]{:S(2)}, u32[]{:S(2)}) collective-permute-start(f32[32,8,256]{2,1,0:T(8,128)S(1)} %get-tuple-element.34), channel_id=1, source_target_pairs={{0,15},{1,0},{2,1},{3,2},{4,3},{5,4},{6,5},{7,6},{8,7},{9,8},{10,9... | collective-permute-start | bytes 786440 | tf_op jit(solution)/shard_map/ppermute | solution.py:681
  32.2 8.4 %collective-permute-start.8 = (f32[16,8,256]{2,1,0:T(8,128)S(1)}, f32[16,8,256]{2,1,0:T(8,128)S(1)}, u32[]{:S(2)}, u32[]{:S(2)}) collective-permute-start(f32[16,8,256]{2,1,0:T(8,128)S(1)} %pad_maximum_fusion), channel_id=1, source_target_pairs={{0,1},{1,2},{2,3},{3,4},{4,5},{5,6},{6,7},{7,8},{8,9},{9,10},{10,1... | collective-permute-start | bytes 393224 | tf_op jit(solution)/shard_map/ppermute | solution.py:681
  32.3 8.3 %collective-permute-start.9 = (f32[16,8,256]{2,1,0:T(8,128)S(1)}, f32[16,8,256]{2,1,0:T(8,128)S(1)}, u32[]{:S(2)}, u32[]{:S(2)}) collective-permute-start(f32[16,8,256]{2,1,0:T(8,128)S(1)} %pad_maximum_fusion.1), channel_id=1, source_target_pairs={{0,15},{1,0},{2,1},{3,2},{4,3},{5,4},{6,5},{7,6},{8,7},{9,8},{10,9... | collective-permute-start | bytes 393224 | tf_op jit(solution)/shard_map/ppermute | solution.py:681
  40.5 35.6 %collective-permute-start.10 = (f32[12,32,256]{2,1,0:T(8,128)S(1)}, f32[12,32,256]{2,1,0:T(8,128)S(1)}, u32[]{:S(2)}, u32[]{:S(2)}) collective-permute-start(f32[12,32,256]{2,1,0:T(8,128)S(1)} %copy-done.4), channel_id=1, source_target_pairs={{0,1},{1,2},{2,3},{3,4},{4,5},{5,6},{6,7},{7,8},{8,9},{9,10},{10,1... | collective-permute-start | bytes 1179656 | tf_op jit(solution)/shard_map/ppermute | solution.py:681
  40.6 35.5 %collective-permute-start.11 = (f32[12,32,256]{2,1,0:T(8,128)S(1)}, f32[12,32,256]{2,1,0:T(8,128)S(1)}, u32[]{:S(2)}, u32[]{:S(2)}) collective-permute-start(f32[12,32,256]{2,1,0:T(8,128)S(1)} %copy-done.3), channel_id=1, source_target_pairs={{0,15},{1,0},{2,1},{3,2},{4,3},{5,4},{6,5},{7,6},{8,7},{9,8},{10,9... | collective-permute-start | bytes 1179656 | tf_op jit(solution)/shard_map/ppermute | solution.py:681

commit v7 on v6

--- a/solution.py
+++ b/solution.py
@@ -326,14 +326,129 @@
 
 
 WIDE = CX + 2 * DEEP
+INNER = 48
+SPLIT = 2
+
+
+def sweep_rows(src, factor, x, fx, start, stride, groups, store):
+    span = pl.ds if stride == 1 else functools.partial(pl.ds, stride=stride)
+    rows = [span(start + k, 8) for k in range(-1, groups + 1)]
+    lines = [[src[x, h, r, :] for r in rows] for h in range(2)]
+    for k in range(1, groups + 1):
+        center = [lines[h][k] for h in range(2)]
+        up, down = lane_shift(center, 1), lane_shift(center, -1)
+        for h in range(2):
+            c = center[h]
+            step = factor[fx, h, rows[k], :]
+            positive = step > 0
+            pairs = (
+                (src[x - 1, h, rows[k], :], src[x + 1, h, rows[k], :]),
+                (lines[h][k - 1], lines[h][k + 1]),
+                (down[h], up[h]),
+            )
+            total = None
+            for l, r in pairs:
+                low = jnp.minimum(jnp.minimum(l, r), c)
+                high = jnp.maximum(jnp.maximum(l, r), c)
+                diff = c - jnp.where(positive, low, high)
+                total = diff * diff if total is None else total + diff * diff
+            slope = total * lax.rsqrt(jnp.maximum(total, 1e-36))
+            store(h, rows[k], c - step * (slope - 1.0))
+
+
+def band_step(value, band):
+    square = value * value
+    weight = band * recip(1.0 + square * (1.0 / 36.0))
+    return PSEUDO_STEP * (value * lax.rsqrt(square + 1.0)) * weight, weight
+
+
+def inner_sweeps(source, factor, targets, first):
+    for n, target in enumerate(targets):
+        sweep = first + n
+
+        def body(x, carry, source=source, target=target):
+            def store(h, rows, value):
+                target[x, h, rows, :] = value
+
+            sweep_rows(source, factor, x, x, 8, CY // 8, CY // 8, store)
+            return carry
+
+        lax.fori_loop(sweep, CX - sweep, body, 0, unroll=2)
+        source = target
+
+
+def inner_first_kernel(tiles, adv, done, factor, weight, own, table, sems):
+    copies = [
+        pltpu.make_async_copy(adv.at[:, :, half(h)], own.at[:, h, pl.ds(8, CY), :], sems.at[h])
+        for h in range(2)
+    ]
+    for copy in copies:
+        copy.start()
+    table[...] = band_table(tiles)
+    for copy in copies:
+        copy.wait()
+    for i in range(2):
+
+        def body(x, carry, i=i):
+            for h in range(2):
+                for group in range(CY // 8):
+                    rows = pl.ds(8 + 8 * group, 8)
+                    r = i * 4 + (group // 2) * 2 + h
+                    band = jnp.broadcast_to(table[r : r + 1, :], (8, LANES))
+                    step, value = band_step(own[x, h, rows, :], band)
+                    factor[x, h, rows, :] = step
+                    weight[x, h, rows, :] = value
+            return carry
+
+        lax.fori_loop(i * TILE, (i + 1) * TILE, body, 0, unroll=2)
+    inner_sweeps(own, factor, [done.at[n] for n in range(SPLIT)], 1)
+
+
+def inner_second_kernel(before, factor, done):
+    inner_sweeps(before.at[SPLIT - 1], factor, [done.at[n] for n in range(SWEEPS - SPLIT)], SPLIT + 1)
+
+
+def inner_first(tiles, adv):
+    shape = lambda *s: jax.ShapeDtypeStruct(s + (CX, 2, INNER, LANES), F32)
+    return pl.pallas_call(
+        inner_first_kernel,
+        out_shape=[shape(SPLIT), shape(), shape()],
+        in_specs=[SMEM, ANY],
+        out_specs=[VMEM] * 3,
+        scratch_shapes=[
+            pltpu.VMEM((CX, 2, INNER, LANES), F32),
+            pltpu.VMEM((8, LANES), F32),
+            pltpu.SemaphoreType.DMA((2,)),
+        ],
+        compiler_params=pltpu.CompilerParams(vmem_limit_bytes=12 * MIB),
+        cost_estimate=pl.CostEstimate(
+            flops=100 * adv.size, bytes_accessed=24 * adv.size, transcendentals=4 * adv.size
+        ),
+        name="inner_first",
+    )(tiles, adv)
+
+
+def inner_second(before, factor):
+    return pl.pallas_call(
+        inner_second_kernel,
+        out_shape=jax.ShapeDtypeStruct((SWEEPS - SPLIT, CX, 2, INNER, LANES), F32),
+        in_specs=[VMEM] * 2,
+        out_specs=VMEM,
+        compiler_params=pltpu.CompilerParams(vmem_limit_bytes=12 * MIB),
+        cost_estimate=pl.CostEstimate(
+            flops=60 * factor.size, bytes_accessed=24 * factor.size, transcendentals=2 * factor.size
+        ),
+        name="inner_second",
+    )(before, factor)
 
 
 def sweep_kernel(
-    tiles, adv, xlo, xhi, ylo, yhi, clo, chi,
+    adv, inner1, inner2, own_factor, own_weight, xlo, xhi, ylo, yhi, clo, chi,
     cur_out, weight_out, part,
-    first, second, factor, masks, table, sums, sems,
+    bufs, factor, masks, sums, sems, x_sems,
 ):
     copies = []
+    done = []
     for h in range(2):
         pieces = (
             (adv, DEEP, CX, OWN, CY),
@@ -350,7 +465,7 @@
             copies.append(
                 pltpu.make_async_copy(
                     src.at[:, :, half(h)],
-                    first.at[pl.ds(x, nx), h, pl.ds(y, ny), :],
+                    bufs.at[0, pl.ds(x, nx), h, pl.ds(y, ny), :],
                     sems.at[h, n],
                 )
             )
@@ -360,98 +475,88 @@
                     src.at[pl.ds(DEEP, 1), :, half(h)], masks.at[pl.ds(n, 1), h], sems.at[h, 9 + n]
                 )
             )
-    for copy in copies:
+    own = lambda ref, x: ref.at[pl.ds(x, CX), :, pl.ds(OWN, CY), :]
+    for n, (src, dst) in enumerate(
+        [(own_factor, own(factor, DEEP)), (own_weight, own(weight_out, 1))]
+        + [(inner1.at[n], own(bufs.at[n + 1], DEEP)) for n in range(SPLIT)]
+        + [(inner2.at[n], own(bufs.at[n + 1 + SPLIT], DEEP)) for n in range(SWEEPS - 1 - SPLIT)]
+        + [(inner2.at[SWEEPS - 1 - SPLIT], own(cur_out, 2))]
+    ):
+        done.append(pltpu.make_async_copy(src.at[:, :, pl.ds(8, CY), :], dst, x_sems.at[n]))
+    for copy in copies + done:
         copy.start()
-    table[...] = band_table(tiles)
     sums[...] = jnp.zeros(sums.shape, F32)
-    for copy in copies:
+    for copy in copies + done[:2]:
         copy.wait()
 
-    def prepare(x, bands, keep):
+    def prepare(x, groups, bands, keep):
         for h in range(2):
-            for group in range(-1, 5):
+            for group in groups:
                 rows = pl.ds(OWN + 8 * group, 8)
-                value = first[x, h, rows, :]
+                value = bufs[0, x, h, rows, :]
                 if group == -1:
                     band = jnp.broadcast_to(value[0:1], value.shape)
                 elif group == 4:
                     band = jnp.broadcast_to(value[7:8], value.shape)
                 else:
-                    band = bands(group, h)
-                square = value * value
-                weight = band * recip(1.0 + square * (1.0 / 36.0))
-                sign = value * lax.rsqrt(square + 1.0)
-                factor[x, h, rows, :] = PSEUDO_STEP * sign * weight
+                    band = masks[bands, h, pl.ds(8 * group, 8), :]
+                step, weight = band_step(value, band)
+                factor[x, h, rows, :] = step
                 if keep:
                     weight_out[x - DEEP + 1, h, rows, :] = weight
 
-    def halo_bands(n):
-        return lambda group, h: masks[n, h, pl.ds(8 * group, 8), :]
-
-    def own_bands(i):
-        def bands(group, h):
-            r = i * 4 + (group // 2) * 2 + h
-            return jnp.broadcast_to(table[r : r + 1, :], (8, LANES))
-
-        return bands
-
-    def run(start, stop, bands, keep):
+    def run(start, stop, groups, bands, keep):
         def body(x, carry):
-            prepare(x, bands, keep)
+            prepare(x, groups, bands, keep)
             return carry
 
         lax.fori_loop(start, stop, body, 0, unroll=2)
 
-    run(1, DEEP - 1, halo_bands(0), False)
-    prepare(DEEP - 1, halo_bands(0), True)
-    run(DEEP, DEEP + TILE, own_bands(0), True)
-    run(DEEP + TILE, DEEP + CX, own_bands(1), True)
-    prepare(DEEP + CX, halo_bands(1), True)
-    run(DEEP + CX + 1, WIDE - 1, halo_bands(1), False)
-
-    def sweep_plane(src, x, dst, y, groups):
-        start = OWN + CY // 2 - 4 * groups
-        rows = [pl.ds(start + k, 8, stride=groups) for k in range(-1, groups + 1)]
-        lines = [[src[x, h, r, :] for r in rows] for h in range(2)]
-        for k in range(1, groups + 1):
-            center = [lines[h][k] for h in range(2)]
-            up, down = lane_shift(center, 1), lane_shift(center, -1)
-            for h in range(2):
-                c = center[h]
-                step = factor[x, h, rows[k], :]
-                positive = step > 0
-                pairs = (
-                    (src[x - 1, h, rows[k], :], src[x + 1, h, rows[k], :]),
-                    (lines[h][k - 1], lines[h][k + 1]),
-                    (down[h], up[h]),
-                )
-                total = None
-                for l, r in pairs:
-                    low = jnp.minimum(jnp.minimum(l, r), c)
-                    high = jnp.maximum(jnp.maximum(l, r), c)
-                    diff = c - jnp.where(positive, low, high)
-                    total = diff * diff if total is None else total + diff * diff
-                slope = total * lax.rsqrt(jnp.maximum(total, 1e-36))
-                dst[y, h, rows[k], :] = c - step * (slope - 1.0)
-
-    source, target = first, second
+    everything = tuple(range(-1, 5))
+    run(1, DEEP - 1, everything, 0, False)
+    prepare(DEEP - 1, everything, 0, True)
+    run(DEEP, DEEP + CX, (-1, 4), 0, True)
+    prepare(DEEP + CX, everything, 1, True)
+    run(DEEP + CX + 1, WIDE - 1, everything, 1, False)
+
     for sweep in range(1, SWEEPS + 1):
-        offset, dst = (0, target) if sweep < SWEEPS else (SWEEPS, cur_out)
+        done[sweep + 1].wait()
+        offset, target = (0, bufs.at[sweep]) if sweep < SWEEPS else (SWEEPS, cur_out)
         groups = 6 if DEEP - sweep > 4 else 5
-
-        def body(x, carry, source=source, dst=dst, offset=offset, groups=groups):
-            sweep_plane(source, x, dst, x - offset, groups)
+        source = bufs.at[sweep - 1]
+
+        def whole(x, source=source, target=target, offset=offset, groups=groups):
+            def store(h, rows, value):
+                target[x - offset, h, rows, :] = value
+
+            start = OWN + CY // 2 - 4 * groups
+            sweep_rows(source, factor, x, x, start, groups, groups, store)
+
+        def ends(x, source=source, target=target, offset=offset, sweep=sweep):
+            def store(h, rows, value):
+                target[x - offset, h, rows, :] = value
+
+            for start in (OWN + sweep - 8, OWN + CY - sweep):
+                sweep_rows(source, factor, x, x, start, 1, 1, store)
+
+        def outer(n, carry, whole=whole, sweep=sweep):
+            whole(sweep + n)
+            whole(WIDE - 1 - sweep - n)
             return carry
 
-        lax.fori_loop(sweep, WIDE - sweep, body, 0, unroll=2)
-        source, target = target, source
+        def middle(x, carry, ends=ends):
+            ends(x)
+            return carry
+
+        lax.fori_loop(0, DEEP, outer, 0)
+        lax.fori_loop(DEEP + sweep, DEEP + CX - sweep, middle, 0, unroll=2)
 
     def count(x, carry):
         for h in range(2):
             for unit in range(CY // UNIT):
                 rows = pl.ds(OWN + unit * UNIT, UNIT)
                 after = jnp.tanh(cur_out[x + 2, h, rows, :])
-                before = jnp.tanh(adv[x, pl.ds(unit * UNIT, UNIT), half(h)])
+                before = jnp.tanh(bufs[0, x + DEEP, h, rows, :])
                 sums[0] += after - before
                 sums[1] += 1.0 - after * after
         return carry
@@ -462,25 +567,26 @@
     part[...] = jnp.broadcast_to(sums_row, part.shape)
 
 
-def sweeps(tiles, adv, halos, count):
+def sweeps(adv, inner1, inner2, factor, weight, halos, count):
     shape = lambda *s: jax.ShapeDtypeStruct(s, F32)
     return pl.pallas_call(
         sweep_kernel,
-        out_shape=[shape(CX + 4, 2, ROWS, LANES), shape(CX + 2, 2, ROWS, LANES), shape(count, 1, LANES)],
-        in_specs=[SMEM, VMEM] + [ANY] * 6,
+        out_shape=[
+            shape(CX + 4, 2, ROWS, LANES), shape(CX + 2, 2, ROWS, LANES), shape(count, 1, LANES)
+        ],
+        in_specs=[ANY] * 11,
         out_specs=[VMEM] * 3,
         scratch_shapes=[
-            pltpu.VMEM((WIDE, 2, ROWS, LANES), F32),
-            pltpu.VMEM((WIDE, 2, ROWS, LANES), F32),
+            pltpu.VMEM((SWEEPS, WIDE, 2, ROWS, LANES), F32),
             pltpu.VMEM((WIDE, 2, ROWS, LANES), F32),
             pltpu.VMEM((2, 2, CY, LANES), F32),
-            pltpu.VMEM((8, LANES), F32),
             pltpu.VMEM((2, UNIT, LANES), F32),
             pltpu.SemaphoreType.DMA((2, 11)),
+            pltpu.SemaphoreType.DMA((2 + SWEEPS,)),
         ],
-        compiler_params=pltpu.CompilerParams(vmem_limit_bytes=22 * MIB),
+        compiler_params=pltpu.CompilerParams(vmem_limit_bytes=30 * MIB),
         name="sweeps",
-    )(tiles, adv, *halos)
+    )(adv, inner1, inner2, factor, weight, *halos)
 
 
 CHUNKS = ((0, 10), (10, 18), (18, 26), (26, 32))
@@ -543,52 +649,31 @@
             value = value + mixes[n] * around[n]
         return value
 
-    def row_groups(groups):
+    def neighbours(load, groups):
         start = OWN + CY // 2 - 4 * groups
-        return [pl.ds(start + k, 8, stride=groups) for k in range(-1, groups + 1)]
-
-    def face(here, there):
-        grown = jnp.exp2(jnp.minimum(there - here, 125.5))
-        factor = recip(1.0 + grown)
-        return factor, grown * factor
-
-    def neighbours(load, groups):
-        rows = row_groups(groups)
-        lines = [[load(0, h, r) for r in rows] for h in range(2)]
-        for k in range(1, groups + 1):
-            center = [lines[h][k] for h in range(2)]
+        for k in range(groups):
+            rows, below, above = (pl.ds(start + k + d, 8, stride=groups) for d in (0, -1, 1))
+            center = [load(0, h, rows) for h in range(2)]
             up, down = lane_shift(center, 1), lane_shift(center, -1)
-            yield rows[k], center, [
+            yield rows, center, [
                 [
-                    load(-1, h, rows[k]), load(1, h, rows[k]), lines[h][k - 1], lines[h][k + 1],
+                    load(-1, h, rows), load(1, h, rows), load(0, h, below), load(0, h, above),
                     down[h], up[h],
                 ]
                 for h in range(2)
             ]
 
     def first_step(i, slot, groups=5):
-        load = lambda dx, h, r: cur[i + 1 + dx, h, r, :] * DOUBLED
+        levels = neighbours(lambda dx, h, r: cur[i + 1 + dx, h, r, :] * DOUBLED, groups)
         comps = [
             neighbours(lambda dx, h, r, c=c: pad[c, i + 1 + dx, h, r, :], groups)
             for c in range(COMPS)
         ]
-        rows_of = row_groups(groups)
-        lines = [[load(0, h, r) for r in rows_of] for h in range(2)]
-        below = [face(lines[h][1], lines[h][0])[0] for h in range(2)]
-        for k in range(1, groups + 1):
-            rows = rows_of[k]
-            center = [lines[h][k] for h in range(2)]
-            along_z = [face(c, n) for c, n in zip(center, lane_shift(center, 1))]
-            back_z = lane_shift([back for _, back in along_z], -1)
+        for rows, center, around in levels:
             mixes = []
             for h in range(2):
                 c = center[h]
-                ahead, back = face(c, lines[h][k + 1])
-                w = [
-                    face(c, load(-1, h, rows))[0], face(c, load(1, h, rows))[0],
-                    below[h], ahead, back_z[h], along_z[h][0],
-                ]
-                below[h] = back
+                w = [recip(1.0 + jnp.exp2(jnp.minimum(n - c, 125.5))) for n in around[h]]
                 total = w[0] + w[1] + w[2] + w[3] + w[4] + w[5]
                 gate = weight[i, h, rows, :] * 0.5 * (
                     1.0 + jnp.tanh(c * (2.0 / DOUBLED) - 2.0 * shift)
@@ -699,13 +784,18 @@
         faces = [jnp.where(row == mark, f[DEEP:, rows], f[:DEEP, rows]) for f in (axlo, axhi)]
         return jnp.concatenate(faces + [tail], axis=0)
 
+    inner1, factor, weight = inner_first(tiles, adv)
+    inner1, axlo, axhi = lax.optimization_barrier((inner1, axlo, axhi))
+    inner2 = inner_second(inner1, factor)
     clo = send(corners(slice(-8, None), 0, tail_n), 0, 1)
     chi = send(corners(slice(0, 8), 7, tail_p), 0, -1)
-    to_syp, to_syn, aylo, ayhi, clo, chi = lax.optimization_barrier(
-        (to_syp, to_syn, aylo, ayhi, clo, chi)
+    to_syp, to_syn, aylo, ayhi, clo, chi, inner2 = lax.optimization_barrier(
+        (to_syp, to_syn, aylo, ayhi, clo, chi, inner2)
     )
     sylo, syhi = send(to_syn, 0, 1), send(to_syp, 0, -1)
-    cur, weight, part = sweeps(tiles, adv, (axlo, axhi, aylo, ayhi, clo, chi), nx * ny)
+    cur, weight, part = sweeps(
+        adv, inner1, inner2, factor, weight, (axlo, axhi, aylo, ayhi, clo, chi), nx * ny
+    )
     parts = lax.all_to_all(part, ("gx", "gy"), 0, 0, tiled=True)
     return extend(parts, cur, weight, stress, (xlo, xhi, sylo, syhi, clo, chi))
 

time: 103 us -> 123 us (1.19)
  Pallas kernels: 55.7 us -> 79.8 us
  waiting for transfers between devices: 2.88 us -> 0.03 us
    pallas_call x0 -> x2, Pallas kernels: none -> 18.9 us  [the longest x1 10.5 us: inner_second(): pl.pallas_call(inner_second_kernel, out_shape=jax.ShapeDtypeStruct((SWEEP...]
    pallas_call x1, Pallas kernels: 15.8 us -> 28.3 us  [sweeps(): pl.pallas_call(sweep_kernel, out_shape=[shape(CX + 4, 2, ROWS, LANES), sh...]
    pallas_call x1, Pallas kernels: 26.2 us -> 18.9 us  [extend(): pl.pallas_call(extend_kernel, out_shape=[shape(CX, CY, z), shape(COMPS, C...]
    ppermute x8, waiting for transfers between devices: 2.87 us -> 0.02 us  [send(): return lax.ppermute(value, 'gy', [(i, (i + dy) % ny) for i in range(ny)])]
  transfers between devices with their start and end apart: 12 -> 12, of which waited for: 1 -> 0; matrix products, arithmetic and copies ran while one was open for 0% -> 0% of each run, Pallas kernels for 21% -> 43%
where the time goes in v7:
time: 123 us
  Pallas kernels  79.8 us (65%)
  starting transfers between devices  28.5 us (23%)
  blocking collectives  13.5 us (11%)
    pallas_call x1, Pallas kernels, sweeps(): pl.pallas_call(sweep_kernel, out_shape=[shape(CX + 4, 2, ROWS, LANES), sh...  28.3 us
    ppermute x8, starting transfers between devices, send(): return lax.ppermute(value, 'gy', [(i, (i + dy) % ny) for i in range(ny)])  22.5 us
    pallas_call x1, Pallas kernels, extend(): pl.pallas_call(extend_kernel, out_shape=[shape(CX, CY, z), shape(COMPS, C...  18.9 us
    all_to_all x1, blocking collectives, on_device(): parts = lax.all_to_all(part, ('gx', 'gy'), 0, 0, tiled=True)  13.5 us
    pallas_call x1, Pallas kernels, inner_second(): pl.pallas_call(inner_second_kernel, out_shape=jax.ShapeDtypeStruct((SWEEP...  10.5 us
    pallas_call x1, Pallas kernels, inner_first(): pl.pallas_call(inner_first_kernel, out_shape=[shape(SPLIT), shape(), shap...  8.4 us
    pallas_call x1, Pallas kernels, inner_drift(): pl.pallas_call(inner_kernel, out_shape=jax.ShapeDtypeStruct(level.shape,...  6.08 us
    ppermute x4, starting transfers between devices, send(): return lax.ppermute(value, 'gx', [(i, (i + dx) % nx) for i in range(nx)])  5.92 us
  transfers between devices with their start and end apart: 12, of which 0 were waited for; matrix products, arithmetic and copies ran while one was open for 0% of the time, Pallas kernels for 43%

profile of v7, /device:TPU:0, one launch (start us, length us, event | category | flops | bytes accessed | tf_op | source)
XLA Modules:
  0.0 122.9 jit_solution(16166206020057442469)
XLA Ops:
  0.6 0.0 copy-start
  0.6 0.0 copy-start.1
  0.6 4.3 %cut.1 = (f32[15,32,256]{2,1,0:T(8,128)}, f32[15,32,256]{2,1,0:T(8,128)}, f32[3,32,256]{2,1,0:T(8,128)}, f32[3,32,256]{2,1,0:T(8,128)}, f32[12,32,256]{2,1,0:T(8,128)}, /*index=5*/f32[12,32,256]{2,1,0:T(8,128)}) custom-call(f32[32,32,256]{2,1,0:T(8,128)} %level.5, f32[6,32,32,256]{3,2,1,0:T(8,128)} %stress.3), custom_call_target="tpu_custom_call" | custom-call | tf_op jit(solution)/shard_map/cut/pallas_call | solution.py:139
  5.0 0.0 copy-start.2
  5.0 0.0 collective-permute-start
  5.0 2.9 %collective-permute-start.1 = (f32[15,32,256]{2,1,0:T(8,128)}, f32[15,32,256]{2,1,0:T(8,128)S(1)}, u32[]{:S(2)}, u32[]{:S(2)}) collective-permute-start(f32[15,32,256]{2,1,0:T(8,128)} %get-tuple-element.32), channel_id=1, source_target_pairs={{0,112},{16,0},{32,16},{48,32},{64,48},{80,64},{96,80},{112,96},{1... | collective-permute-start | bytes 1474568 | tf_op jit(solution)/shard_map/ppermute | solution.py:764
  7.9 2.0 %collective-permute-start.2 = (f32[3,32,256]{2,1,0:T(8,128)}, f32[3,32,256]{2,1,0:T(8,128)S(1)}, u32[]{:S(2)}, u32[]{:S(2)}) collective-permute-start(f32[3,32,256]{2,1,0:T(8,128)} %get-tuple-element.33), channel_id=1, source_target_pairs={{0,1},{1,2},{2,3},{3,4},{4,5},{5,6},{6,7},{7,8},{8,9},{9,10},{10,1... | collective-permute-start | bytes 294920 | tf_op jit(solution)/shard_map/ppermute | solution.py:766
  9.9 4.3 %collective-permute-start.3 = (f32[3,32,256]{2,1,0:T(8,128)}, f32[3,32,256]{2,1,0:T(8,128)S(1)}, u32[]{:S(2)}, u32[]{:S(2)}) collective-permute-start(f32[3,32,256]{2,1,0:T(8,128)} %get-tuple-element.34), channel_id=1, source_target_pairs={{0,15},{1,0},{2,1},{3,2},{4,3},{5,4},{6,5},{7,6},{8,7},{9,8},{10,9... | collective-permute-start | bytes 294920 | tf_op jit(solution)/shard_map/ppermute | solution.py:766
  14.3 0.0 copy-done
  14.3 0.0 copy-done.1
  14.3 6.1 %inner_drift.1.drift = f32[32,32,256]{2,1,0:T(8,128)S(1)} custom-call(f32[32,32,256]{2,1,0:T(8,128)S(1)} %copy-done, bf16[3,32,32,256]{3,2,1,0:T(8,128)(2,1)S(1)} %copy-done.1), custom_call_target="tpu_custom_call" | custom-call | flops 47185920 | bytes 3670016 | tf_op jit(solution)/shard_map/inner_drift/pallas_call | solution.py:196
  20.4 0.0 collective-permute-done.2.ylo
  20.4 0.0 collective-permute-done.3.yhi
  20.4 0.0 collective-permute-done.xlo
  20.4 0.0 collective-permute-done.1.xhi
  20.4 0.0 copy-done.2
  20.4 3.3 %advect.1 = (f32[32,32,256]{2,1,0:T(8,128)S(1)}, f32[8,32,256]{2,1,0:T(8,128)S(1)}, f32[8,32,256]{2,1,0:T(8,128)S(1)}, f32[32,8,256]{2,1,0:T(8,128)S(1)}, f32[32...) custom-call(s32[1,1,32]{2,1,0:T(1,128)S(1)} %copy-done.2, f32[32,32,256]{2,1,0:T(8,128)S(1)} %copy-done, ...), custom_call_target="tpu_custom_call" | custom-call | tf_op jit(solution)/shard_map/advect/pallas_call | solution.py:306
  23.7 0.0 collective-permute-start.4
  23.7 2.9 %collective-permute-start.5 = (f32[8,32,256]{2,1,0:T(8,128)S(1)}, f32[8,32,256]{2,1,0:T(8,128)S(1)}, u32[]{:S(2)}, u32[]{:S(2)}) collective-permute-start(f32[8,32,256]{2,1,0:T(8,128)S(1)} %get-tuple-element.38), channel_id=1, source_target_pairs={{0,112},{16,0},{32,16},{48,32},{64,48},{80,64},{96,80},{112,96},{1... | collective-permute-start | bytes 786440 | tf_op jit(solution)/shard_map/ppermute | solution.py:764
  26.7 0.0 collective-permute-start.6
  26.7 5.3 %collective-permute-start.7 = (f32[32,8,256]{2,1,0:T(8,128)S(1)}, f32[32,8,256]{2,1,0:T(8,128)S(1)}, u32[]{:S(2)}, u32[]{:S(2)}) collective-permute-start(f32[32,8,256]{2,1,0:T(8,128)S(1)} %get-tuple-element.43), channel_id=1, source_target_pairs={{0,15},{1,0},{2,1},{3,2},{4,3},{5,4},{6,5},{7,6},{8,7},{9,8},{10,9... | collective-permute-start | bytes 786440 | tf_op jit(solution)/shard_map/ppermute | solution.py:766
  32.0 8.4 %inner_first.1 = (f32[2,32,2,48,128]{4,3,2,1,0:T(8,128)S(1)}, f32[32,2,48,128]{3,2,1,0:T(8,128)S(1)}, f32[32,2,48,128]{3,2,1,0:T(8,128)S(1)}) custom-call(s32[1,1,32]{2,1,0:T(1,128)S(1)} %copy-done.2, f32[32,32,256]{2,1,0:T(8,128)S(1)} %get-tuple-element.35.adv), custom_call_target="tpu_custom_call" | custom-call | flops 26214400 | bytes 6291456 | tf_op jit(solution)/shard_map/inner_first/pallas_call | solution.py:413
  40.5 0.0 collective-permute-done.4.xlo
  40.5 0.0 collective-permute-done.5.xhi
  40.5 0.1 slice_select_fusion
  40.6 0.1 collective-permute-start.8
  40.7 5.4 %collective-permute-start.9 = (f32[16,8,256]{2,1,0:T(8,128)S(1)}, f32[16,8,256]{2,1,0:T(8,128)S(1)}, u32[]{:S(2)}, u32[]{:S(2)}) collective-permute-start(f32[16,8,256]{2,1,0:T(8,128)S(1)} %pad_maximum_fusion.1), channel_id=1, source_target_pairs={{0,15},{1,0},{2,1},{3,2},{4,3},{5,4},{6,5},{7,6},{8,7},{9,8},{10,9... | collective-permute-start | bytes 393224 | tf_op jit(solution)/shard_map/ppermute | solution.py:766
  46.1 0.0 copy-start.4
  46.1 0.0 copy-start.3
  46.1 10.5 %inner_second.1.inner2 = f32[3,32,2,48,128]{4,3,2,1,0:T(8,128)S(1)} custom-call(f32[2,32,2,48,128]{4,3,2,1,0:T(8,128)S(1)} %get-tuple-element.39.before.inner1, f32[32,2,48,128]{3,2,1,0:T(8,128)S(1)} %get-tuple-element.48.factor.own_factor), custom_call_target="tpu_custom_call" | custom-call | flops 23592960 | bytes 9437184 | tf_op jit(solution)/shard_map/inner_second/pallas_call | solution.py:432
  56.6 0.0 collective-permute-done.6.ylo
  56.6 0.0 collective-permute-done.7.yhi
  56.7 0.0 collective-permute-done.8.clo
  56.7 0.0 collective-permute-done.9.chi
  56.7 0.0 copy-done.4
  56.7 0.1 collective-permute-start.10
  56.8 0.0 copy-done.3
  56.8 5.3 %collective-permute-start.11 = (f32[12,32,256]{2,1,0:T(8,128)S(1)}, f32[12,32,256]{2,1,0:T(8,128)S(1)}, u32[]{:S(2)}, u32[]{:S(2)}) collective-permute-start(f32[12,32,256]{2,1,0:T(8,128)S(1)} %copy-done.3), channel_id=1, source_target_pairs={{0,15},{1,0},{2,1},{3,2},{4,3},{5,4},{6,5},{7,6},{8,7},{9,8},{10,9... | collective-permute-start | bytes 1179656 | tf_op jit(solution)/shard_map/ppermute | solution.py:766
  62.1 28.3 %sweeps.1 = (f32[36,2,64,128]{3,2,1,0:T(8,128)S(1)}, f32[34,2,64,128]{3,2,1,0:T(8,128)S(1)}, f32[128,1,128]{2,1,0:T(1,128)S(1)}) custom-call(f32[32,32,256]{2,1,0:T(8,128)S(1)} %get-tuple-element.35.adv, f32[2,32,2,48,128]{4,3,2,1,0:T(8,128)S(1)} %get-tuple-element.39.before.inner1, f32[3,32,2,48,128]{4,3,2,1,0:T(8,128)S(1)} %inner_second.1.inner2, ...), custom_call_target="tpu_custom_call" | custom-call | tf_op jit(solution)/shard_map/sweeps/pallas_call | solution.py:572
  90.4 13.5 %all_to_all.5.parts = f32[128,1,128]{2,1,0:T(1,128)S(1)} all-to-all(f32[128,1,128]{2,1,0:T(1,128)S(1)} %get-tuple-element.55), channel_id=1, replica_groups=mesh['gx'=8,'gy'=16] {'gx','gy'}, dimensions={0} | all-to-all | bytes 131072 | tf_op jit(solution)/shard_map/all_to_all | solution.py:799
  103.8 0.0 collective-permute-done.10.ylo
  103.8 0.0 collective-permute-done.11.yhi
  103.8 18.9 %extend.1 = (f32[32,32,256]{2,1,0:T(8,128)}, f32[6,32,32,256]{3,2,1,0:T(8,128)}) custom-call(f32[128,1,128]{2,1,0:T(1,128)S(1)} %all_to_all.5.parts, f32[36,2,64,128]{3,2,1,0:T(8,128)S(1)} %get-tuple-element.56.cur, f32[34,2,64,128]{3,2,1,0:T(8,128)S(1)} %get-tuple-element.57.weight, f32[6,32,32,256]{3,2,1,0:T(8,128)} %stress.3, ...), custom_call_target="tpu_custom_call" | custom-call | tf_op jit(solution)/shard_map/extend/pallas_call | solution.py:740
  (4 shorter events, 0.0 us)
Async XLA Ops:
  0.6 13.6 %copy-start = (f32[32,32,256]{2,1,0:T(8,128)S(1)}, f32[32,32,256]{2,1,0:T(8,128)}, u32[]{:S(2)}) copy-start(f32[32,32,256]{2,1,0:T(8,128)} %level.5) | copy-start | bytes 3145732
  0.6 13.6 %copy-start.1 = (bf16[3,32,32,256]{3,2,1,0:T(8,128)(2,1)S(1)}, bf16[3,32,32,256]{3,2,1,0:T(8,128)(2,1)}, u32[]{:S(2)}) copy-start(bf16[3,32,32,256]{3,2,1,0:T(8,128)(2,1)} %speed.3) | copy-start | bytes 4718596
  5.0 15.4 %copy-start.2 = (s32[1,1,32]{2,1,0:T(1,128)S(1)}, s32[1,1,32]{2,1,0:T(1,128)}, u32[]{:S(2)}) copy-start(s32[1,1,32]{2,1,0:T(1,128)} %tiles.3) | copy-start | bytes 388
  5.0 15.4 %collective-permute-start = (f32[15,32,256]{2,1,0:T(8,128)}, f32[15,32,256]{2,1,0:T(8,128)S(1)}, u32[]{:S(2)}, u32[]{:S(2)}) collective-permute-start(f32[15,32,256]{2,1,0:T(8,128)} %get-tuple-element.31), channel_id=1, source_target_pairs={{0,16},{16,32},{32,48},{48,64},{64,80},{80,96},{96,112},{112,0},{1... | collective-permute-start | bytes 1474568 | tf_op jit(solution)/shard_map/ppermute | solution.py:764
  5.0 15.4 %collective-permute-start.1 = (f32[15,32,256]{2,1,0:T(8,128)}, f32[15,32,256]{2,1,0:T(8,128)S(1)}, u32[]{:S(2)}, u32[]{:S(2)}) collective-permute-start(f32[15,32,256]{2,1,0:T(8,128)} %get-tuple-element.32), channel_id=1, source_target_pairs={{0,112},{16,0},{32,16},{48,32},{64,48},{80,64},{96,80},{112,96},{1... | collective-permute-start | bytes 1474568 | tf_op jit(solution)/shard_map/ppermute | solution.py:764
  7.9 12.4 %collective-permute-start.2 = (f32[3,32,256]{2,1,0:T(8,128)}, f32[3,32,256]{2,1,0:T(8,128)S(1)}, u32[]{:S(2)}, u32[]{:S(2)}) collective-permute-start(f32[3,32,256]{2,1,0:T(8,128)} %get-tuple-element.33), channel_id=1, source_target_pairs={{0,1},{1,2},{2,3},{3,4},{4,5},{5,6},{6,7},{7,8},{8,9},{9,10},{10,1... | collective-permute-start | bytes 294920 | tf_op jit(solution)/shard_map/ppermute | solution.py:766
  9.9 10.4 %collective-permute-start.3 = (f32[3,32,256]{2,1,0:T(8,128)}, f32[3,32,256]{2,1,0:T(8,128)S(1)}, u32[]{:S(2)}, u32[]{:S(2)}) collective-permute-start(f32[3,32,256]{2,1,0:T(8,128)} %get-tuple-element.34), channel_id=1, source_target_pairs={{0,15},{1,0},{2,1},{3,2},{4,3},{5,4},{6,5},{7,6},{8,7},{9,8},{10,9... | collective-permute-start | bytes 294920 | tf_op jit(solution)/shard_map/ppermute | solution.py:766
  23.7 16.7 %collective-permute-start.4 = (f32[8,32,256]{2,1,0:T(8,128)S(1)}, f32[8,32,256]{2,1,0:T(8,128)S(1)}, u32[]{:S(2)}, u32[]{:S(2)}) collective-permute-start(f32[8,32,256]{2,1,0:T(8,128)S(1)} %get-tuple-element.37), channel_id=1, source_target_pairs={{0,16},{16,32},{32,48},{48,64},{64,80},{80,96},{96,112},{112,0},{1... | collective-permute-start | bytes 786440 | tf_op jit(solution)/shard_map/ppermute | solution.py:764
  23.7 16.7 %collective-permute-start.5 = (f32[8,32,256]{2,1,0:T(8,128)S(1)}, f32[8,32,256]{2,1,0:T(8,128)S(1)}, u32[]{:S(2)}, u32[]{:S(2)}) collective-permute-start(f32[8,32,256]{2,1,0:T(8,128)S(1)} %get-tuple-element.38), channel_id=1, source_target_pairs={{0,112},{16,0},{32,16},{48,32},{64,48},{80,64},{96,80},{112,96},{1... | collective-permute-start | bytes 786440 | tf_op jit(solution)/shard_map/ppermute | solution.py:764
  26.7 29.9 %collective-permute-start.6 = (f32[32,8,256]{2,1,0:T(8,128)S(1)}, f32[32,8,256]{2,1,0:T(8,128)S(1)}, u32[]{:S(2)}, u32[]{:S(2)}) collective-permute-start(f32[32,8,256]{2,1,0:T(8,128)S(1)} %get-tuple-element.42), channel_id=1, source_target_pairs={{0,1},{1,2},{2,3},{3,4},{4,5},{5,6},{6,7},{7,8},{8,9},{9,10},{10,1... | collective-permute-start | bytes 786440 | tf_op jit(solution)/shard_map/ppermute | solution.py:766
  26.7 29.9 %collective-permute-start.7 = (f32[32,8,256]{2,1,0:T(8,128)S(1)}, f32[32,8,256]{2,1,0:T(8,128)S(1)}, u32[]{:S(2)}, u32[]{:S(2)}) collective-permute-start(f32[32,8,256]{2,1,0:T(8,128)S(1)} %get-tuple-element.43), channel_id=1, source_target_pairs={{0,15},{1,0},{2,1},{3,2},{4,3},{5,4},{6,5},{7,6},{8,7},{9,8},{10,9... | collective-permute-start | bytes 786440 | tf_op jit(solution)/shard_map/ppermute | solution.py:766
  40.6 16.1 %collective-permute-start.8 = (f32[16,8,256]{2,1,0:T(8,128)S(1)}, f32[16,8,256]{2,1,0:T(8,128)S(1)}, u32[]{:S(2)}, u32[]{:S(2)}) collective-permute-start(f32[16,8,256]{2,1,0:T(8,128)S(1)} %pad_maximum_fusion), channel_id=1, source_target_pairs={{0,1},{1,2},{2,3},{3,4},{4,5},{5,6},{6,7},{7,8},{8,9},{9,10},{10,1... | collective-permute-start | bytes 393224 | tf_op jit(solution)/shard_map/ppermute | solution.py:766
  40.7 16.0 %collective-permute-start.9 = (f32[16,8,256]{2,1,0:T(8,128)S(1)}, f32[16,8,256]{2,1,0:T(8,128)S(1)}, u32[]{:S(2)}, u32[]{:S(2)}) collective-permute-start(f32[16,8,256]{2,1,0:T(8,128)S(1)} %pad_maximum_fusion.1), channel_id=1, source_target_pairs={{0,15},{1,0},{2,1},{3,2},{4,3},{5,4},{6,5},{7,6},{8,7},{9,8},{10,9... | collective-permute-start | bytes 393224 | tf_op jit(solution)/shard_map/ppermute | solution.py:766
  46.1 10.6 %copy-start.4 = (f32[12,32,256]{2,1,0:T(8,128)S(1)}, f32[12,32,256]{2,1,0:T(8,128)}, u32[]{:S(2)}) copy-start(f32[12,32,256]{2,1,0:T(8,128)} %get-tuple-element.58) | copy-start | bytes 1179652
  46.1 10.7 %copy-start.3 = (f32[12,32,256]{2,1,0:T(8,128)S(1)}, f32[12,32,256]{2,1,0:T(8,128)}, u32[]{:S(2)}) copy-start(f32[12,32,256]{2,1,0:T(8,128)} %get-tuple-element.59) | copy-start | bytes 1179652
  56.7 47.1 %collective-permute-start.10 = (f32[12,32,256]{2,1,0:T(8,128)S(1)}, f32[12,32,256]{2,1,0:T(8,128)S(1)}, u32[]{:S(2)}, u32[]{:S(2)}) collective-permute-start(f32[12,32,256]{2,1,0:T(8,128)S(1)} %copy-done.4), channel_id=1, source_target_pairs={{0,1},{1,2},{2,3},{3,4},{4,5},{5,6},{6,7},{7,8},{8,9},{9,10},{10,1... | collective-permute-start | bytes 1179656 | tf_op jit(solution)/shard_map/ppermute | solution.py:766
  56.8 47.1 %collective-permute-start.11 = (f32[12,32,256]{2,1,0:T(8,128)S(1)}, f32[12,32,256]{2,1,0:T(8,128)S(1)}, u32[]{:S(2)}, u32[]{:S(2)}) collective-permute-start(f32[12,32,256]{2,1,0:T(8,128)S(1)} %copy-done.3), channel_id=1, source_target_pairs={{0,15},{1,0},{2,1},{3,2},{4,3},{5,4},{6,5},{7,6},{8,7},{9,8},{10,9... | collective-permute-start | bytes 1179656 | tf_op jit(solution)/shard_map/ppermute | solution.py:766

commit v8 on v7

--- a/solution.py
+++ b/solution.py
@@ -377,7 +377,7 @@
         source = target
 
 
-def inner_first_kernel(tiles, adv, done, factor, weight, own, table, sems):
+def inner_first_kernel(tiles, adv, done1, done2, factor, weight, own, table, sems):
     copies = [
         pltpu.make_async_copy(adv.at[:, :, half(h)], own.at[:, h, pl.ds(8, CY), :], sems.at[h])
         for h in range(2)
@@ -401,20 +401,19 @@
             return carry
 
         lax.fori_loop(i * TILE, (i + 1) * TILE, body, 0, unroll=2)
-    inner_sweeps(own, factor, [done.at[n] for n in range(SPLIT)], 1)
-
-
-def inner_second_kernel(before, factor, done):
-    inner_sweeps(before.at[SPLIT - 1], factor, [done.at[n] for n in range(SWEEPS - SPLIT)], SPLIT + 1)
+    inner_sweeps(own, factor, (done1, done2), 1)
+
+
+def inner_second_kernel(before, factor, *done):
+    inner_sweeps(before, factor, done, SPLIT + 1)
 
 
 def inner_first(tiles, adv):
-    shape = lambda *s: jax.ShapeDtypeStruct(s + (CX, 2, INNER, LANES), F32)
     return pl.pallas_call(
         inner_first_kernel,
-        out_shape=[shape(SPLIT), shape(), shape()],
+        out_shape=[jax.ShapeDtypeStruct((CX, 2, INNER, LANES), F32)] * (SPLIT + 2),
         in_specs=[SMEM, ANY],
-        out_specs=[VMEM] * 3,
+        out_specs=[VMEM] * (SPLIT + 2),
         scratch_shapes=[
             pltpu.VMEM((CX, 2, INNER, LANES), F32),
             pltpu.VMEM((8, LANES), F32),
@@ -431,9 +430,9 @@
 def inner_second(before, factor):
     return pl.pallas_call(
         inner_second_kernel,
-        out_shape=jax.ShapeDtypeStruct((SWEEPS - SPLIT, CX, 2, INNER, LANES), F32),
+        out_shape=[jax.ShapeDtypeStruct((CX, 2, INNER, LANES), F32)] * (SWEEPS - SPLIT),
         in_specs=[VMEM] * 2,
-        out_specs=VMEM,
+        out_specs=[VMEM] * (SWEEPS - SPLIT),
         compiler_params=pltpu.CompilerParams(vmem_limit_bytes=12 * MIB),
         cost_estimate=pl.CostEstimate(
             flops=60 * factor.size, bytes_accessed=24 * factor.size, transcendentals=2 * factor.size
@@ -443,10 +442,11 @@
 
 
 def sweep_kernel(
-    adv, inner1, inner2, own_factor, own_weight, xlo, xhi, ylo, yhi, clo, chi,
+    adv, in1, in2, in3, in4, in5, own_factor, own_weight, xlo, xhi, ylo, yhi, clo, chi,
     cur_out, weight_out, part,
-    bufs, factor, masks, sums, sems, x_sems,
+    buf0, buf1, buf2, buf3, buf4, factor, masks, sums, sems, x_sems,
 ):
+    bufs = (buf0, buf1, buf2, buf3, buf4)
     copies = []
     done = []
     for h in range(2):
@@ -465,7 +465,7 @@
             copies.append(
                 pltpu.make_async_copy(
                     src.at[:, :, half(h)],
-                    bufs.at[0, pl.ds(x, nx), h, pl.ds(y, ny), :],
+                    buf0.at[pl.ds(x, nx), h, pl.ds(y, ny), :],
                     sems.at[h, n],
                 )
             )
@@ -478,9 +478,8 @@
     own = lambda ref, x: ref.at[pl.ds(x, CX), :, pl.ds(OWN, CY), :]
     for n, (src, dst) in enumerate(
         [(own_factor, own(factor, DEEP)), (own_weight, own(weight_out, 1))]
-        + [(inner1.at[n], own(bufs.at[n + 1], DEEP)) for n in range(SPLIT)]
-        + [(inner2.at[n], own(bufs.at[n + 1 + SPLIT], DEEP)) for n in range(SWEEPS - 1 - SPLIT)]
-        + [(inner2.at[SWEEPS - 1 - SPLIT], own(cur_out, 2))]
+        + [(src, own(buf, DEEP)) for src, buf in zip((in1, in2, in3, in4), bufs[1:])]
+        + [(in5, own(cur_out, 2))]
     ):
         done.append(pltpu.make_async_copy(src.at[:, :, pl.ds(8, CY), :], dst, x_sems.at[n]))
     for copy in copies + done:
@@ -493,7 +492,7 @@
         for h in range(2):
             for group in groups:
                 rows = pl.ds(OWN + 8 * group, 8)
-                value = bufs[0, x, h, rows, :]
+                value = buf0[x, h, rows, :]
                 if group == -1:
                     band = jnp.broadcast_to(value[0:1], value.shape)
                 elif group == 4:
@@ -521,9 +520,9 @@
 
     for sweep in range(1, SWEEPS + 1):
         done[sweep + 1].wait()
-        offset, target = (0, bufs.at[sweep]) if sweep < SWEEPS else (SWEEPS, cur_out)
+        offset, target = (0, bufs[sweep]) if sweep < SWEEPS else (SWEEPS, cur_out)
         groups = 6 if DEEP - sweep > 4 else 5
-        source = bufs.at[sweep - 1]
+        source = bufs[sweep - 1]
 
         def whole(x, source=source, target=target, offset=offset, groups=groups):
             def store(h, rows, value):
@@ -556,7 +555,7 @@
             for unit in range(CY // UNIT):
                 rows = pl.ds(OWN + unit * UNIT, UNIT)
                 after = jnp.tanh(cur_out[x + 2, h, rows, :])
-                before = jnp.tanh(bufs[0, x + DEEP, h, rows, :])
+                before = jnp.tanh(buf0[x + DEEP, h, rows, :])
                 sums[0] += after - before
                 sums[1] += 1.0 - after * after
         return carry
@@ -567,17 +566,17 @@
     part[...] = jnp.broadcast_to(sums_row, part.shape)
 
 
-def sweeps(adv, inner1, inner2, factor, weight, halos, count):
+def sweeps(adv, inner, factor, weight, halos, count):
     shape = lambda *s: jax.ShapeDtypeStruct(s, F32)
     return pl.pallas_call(
         sweep_kernel,
         out_shape=[
             shape(CX + 4, 2, ROWS, LANES), shape(CX + 2, 2, ROWS, LANES), shape(count, 1, LANES)
         ],
-        in_specs=[ANY] * 11,
+        in_specs=[ANY] * (SWEEPS + 9),
         out_specs=[VMEM] * 3,
-        scratch_shapes=[
-            pltpu.VMEM((SWEEPS, WIDE, 2, ROWS, LANES), F32),
+        scratch_shapes=[pltpu.VMEM((WIDE, 2, ROWS, LANES), F32)] * SWEEPS
+        + [
             pltpu.VMEM((WIDE, 2, ROWS, LANES), F32),
             pltpu.VMEM((2, 2, CY, LANES), F32),
             pltpu.VMEM((2, UNIT, LANES), F32),
@@ -586,7 +585,7 @@
         ],
         compiler_params=pltpu.CompilerParams(vmem_limit_bytes=30 * MIB),
         name="sweeps",
-    )(adv, inner1, inner2, factor, weight, *halos)
+    )(adv, *inner, factor, weight, *halos)
 
 
 CHUNKS = ((0, 10), (10, 18), (18, 26), (26, 32))
@@ -595,8 +594,10 @@
 def extend_kernel(
     parts, cur, weight, stress, xlo, xhi, ylo, yhi, clo, chi,
     level_out, stress_out,
-    pad, ring, mix, stage, sems, x_sems, out_sems,
+    pad, ring0, ring1, ring2, ring3, mix0, mix1, stage, sems, x_sems, out_sems,
 ):
+    ring, mix = (ring0, ring1, ring2, ring3), (mix0, mix1)
+
     def chunk(n):
         start, stop = CHUNKS[n]
         own = stress.at[:, pl.ds(start, stop - start)]
@@ -682,22 +683,22 @@
                 w = [scaled * n for n in w] + [1.0 - gate]
                 mixes.append(w)
                 for n in range(7):
-                    mix[slot % 2, n, h, rows, :] = w[n]
+                    mix[slot % 2][n, h, rows, :] = w[n]
             for comp in range(COMPS):
                 _, center, around = next(comps[comp])
                 for h in range(2):
-                    ring[slot, comp, h, rows, :] = blend(mixes[h], center[h], around[h])
+                    ring[slot][comp, h, rows, :] = blend(mixes[h], center[h], around[h])
 
     def second_step(x, slot):
         slots = {dx: (slot + dx) % 4 for dx in (-1, 0, 1)}
         groups = CY // 8
         comps = [
-            neighbours(lambda dx, h, r, c=c: ring[slots[dx], c, h, r, :], groups)
+            neighbours(lambda dx, h, r, c=c: ring[slots[dx]][c, h, r, :], groups)
             for c in range(COMPS)
         ]
         for k in range(groups):
             rows = pl.ds(OWN + k, 8, stride=groups)
-            mixes = [[mix[slot % 2, n, h, rows, :] for n in range(7)] for h in range(2)]
+            mixes = [[mix[slot % 2][n, h, rows, :] for n in range(7)] for h in range(2)]
             for comp in range(COMPS):
                 _, center, around = next(comps[comp])
                 for h in range(2):
@@ -744,8 +745,8 @@
         out_specs=[VMEM, ANY],
         scratch_shapes=[
             pltpu.VMEM((COMPS, CX + 4, 2, ROWS, LANES), F32),
-            pltpu.VMEM((4, COMPS, 2, ROWS, LANES), F32),
-            pltpu.VMEM((2, 7, 2, ROWS, LANES), F32),
+            *[pltpu.VMEM((COMPS, 2, ROWS, LANES), F32)] * 4,
+            *[pltpu.VMEM((7, 2, ROWS, LANES), F32)] * 2,
             pltpu.VMEM((COMPS, CX, 2, CY, LANES), F32),
             pltpu.SemaphoreType.DMA((4, 2)),
             pltpu.SemaphoreType.DMA((2, 2, COMPS)),
@@ -784,17 +785,17 @@
         faces = [jnp.where(row == mark, f[DEEP:, rows], f[:DEEP, rows]) for f in (axlo, axhi)]
         return jnp.concatenate(faces + [tail], axis=0)
 
-    inner1, factor, weight = inner_first(tiles, adv)
-    inner1, axlo, axhi = lax.optimization_barrier((inner1, axlo, axhi))
-    inner2 = inner_second(inner1, factor)
+    *inner, factor, weight = inner_first(tiles, adv)
+    last, axlo, axhi = lax.optimization_barrier((inner[-1], axlo, axhi))
+    more = inner_second(last, factor)
     clo = send(corners(slice(-8, None), 0, tail_n), 0, 1)
     chi = send(corners(slice(0, 8), 7, tail_p), 0, -1)
-    to_syp, to_syn, aylo, ayhi, clo, chi, inner2 = lax.optimization_barrier(
-        (to_syp, to_syn, aylo, ayhi, clo, chi, inner2)
+    to_syp, to_syn, aylo, ayhi, clo, chi, more = lax.optimization_barrier(
+        (to_syp, to_syn, aylo, ayhi, clo, chi, more)
     )
     sylo, syhi = send(to_syn, 0, 1), send(to_syp, 0, -1)
     cur, weight, part = sweeps(
-        adv, inner1, inner2, factor, weight, (axlo, axhi, aylo, ayhi, clo, chi), nx * ny
+        adv, (*inner, *more), factor, weight, (axlo, axhi, aylo, ayhi, clo, chi), nx * ny
     )
     parts = lax.all_to_all(part, ("gx", "gy"), 0, 0, tiled=True)
     return extend(parts, cur, weight, stress, (xlo, xhi, sylo, syhi, clo, chi))

time: 123 us -> 99.6 us (0.81)
  Pallas kernels: 79.8 us -> 56 us
    pallas_call x1, Pallas kernels: 28.3 us -> 14 us  [sweeps(): pl.pallas_call(sweep_kernel, out_shape=[shape(CX + 4, 2, ROWS, LANES), sh...]
    pallas_call x2, Pallas kernels: 18.9 us -> 8.87 us  [the longest x1 4.59 us: inner_first(): pl.pallas_call(inner_first_kernel, out_shape=[jax.ShapeDtypeStruct((CX, 2...]
  transfers between devices with their start and end apart: 12 -> 12, of which waited for: 0 -> 0; matrix products, arithmetic and copies ran while one was open for 0% -> 0% of each run, Pallas kernels for 43% -> 29%
where the time goes in v8:
time: 99.6 us; the launch traced here: 99.1 us
  Pallas kernels  56 us (56%)
  starting transfers between devices  28.5 us (29%)
  blocking collectives  13.5 us (14%)
  between operations  1.02 us (1%)
    ppermute x8, starting transfers between devices, send(): return lax.ppermute(value, 'gy', [(i, (i + dy) % ny) for i in range(ny)])  22.5 us
    pallas_call x1, Pallas kernels, extend(): pl.pallas_call(extend_kernel, out_shape=[shape(CX, CY, z), shape(COMPS, C...  19.4 us
    pallas_call x1, Pallas kernels, sweeps(): pl.pallas_call(sweep_kernel, out_shape=[shape(CX + 4, 2, ROWS, LANES), sh...  14 us
    all_to_all x1, blocking collectives, on_device(): parts = lax.all_to_all(part, ('gx', 'gy'), 0, 0, tiled=True)  13.5 us
    pallas_call x1, Pallas kernels, inner_drift(): pl.pallas_call(inner_kernel, out_shape=jax.ShapeDtypeStruct(level.shape,...  6.08 us
    ppermute x4, starting transfers between devices, send(): return lax.ppermute(value, 'gx', [(i, (i + dx) % nx) for i in range(nx)])  5.92 us
    pallas_call x1, Pallas kernels, inner_first(): pl.pallas_call(inner_first_kernel, out_shape=[jax.ShapeDtypeStruct((CX, 2...  4.59 us
    pallas_call x1, Pallas kernels, cut(): pl.pallas_call(cut_kernel, out_shape=[message(3 + 2 * COMPS)] * 2 + [mess...  4.3 us
  transfers between devices with their start and end apart: 12, of which 0 were waited for; matrix products, arithmetic and copies ran while one was open for 0% of the time, Pallas kernels for 29%

profile of v8, /device:TPU:0, one launch (start us, length us, event | category | flops | bytes accessed | tf_op | source)
XLA Modules:
  0.0 99.1 jit_solution(3441488149839043818)
XLA Ops:
  0.6 0.0 copy-start
  0.6 0.0 copy-start.1
  0.6 4.3 %cut.1 = (f32[15,32,256]{2,1,0:T(8,128)}, f32[15,32,256]{2,1,0:T(8,128)}, f32[3,32,256]{2,1,0:T(8,128)}, f32[3,32,256]{2,1,0:T(8,128)}, f32[12,32,256]{2,1,0:T(8,128)}, /*index=5*/f32[12,32,256]{2,1,0:T(8,128)}) custom-call(f32[32,32,256]{2,1,0:T(8,128)} %level.5, f32[6,32,32,256]{3,2,1,0:T(8,128)} %stress.3), custom_call_target="tpu_custom_call" | custom-call | tf_op jit(solution)/shard_map/cut/pallas_call | solution.py:139
  5.0 0.0 collective-permute-start
  5.0 2.9 %collective-permute-start.1 = (f32[15,32,256]{2,1,0:T(8,128)}, f32[15,32,256]{2,1,0:T(8,128)S(1)}, u32[]{:S(2)}, u32[]{:S(2)}) collective-permute-start(f32[15,32,256]{2,1,0:T(8,128)} %get-tuple-element.38), channel_id=1, source_target_pairs={{0,112},{16,0},{32,16},{48,32},{64,48},{80,64},{96,80},{112,96},{1... | collective-permute-start | bytes 1474568 | tf_op jit(solution)/shard_map/ppermute | solution.py:765
  7.9 2.0 %collective-permute-start.2 = (f32[3,32,256]{2,1,0:T(8,128)}, f32[3,32,256]{2,1,0:T(8,128)S(1)}, u32[]{:S(2)}, u32[]{:S(2)}) collective-permute-start(f32[3,32,256]{2,1,0:T(8,128)} %get-tuple-element.39), channel_id=1, source_target_pairs={{0,1},{1,2},{2,3},{3,4},{4,5},{5,6},{6,7},{7,8},{8,9},{9,10},{10,1... | collective-permute-start | bytes 294920 | tf_op jit(solution)/shard_map/ppermute | solution.py:767
  9.9 0.0 copy-start.2
  9.9 4.3 %collective-permute-start.3 = (f32[3,32,256]{2,1,0:T(8,128)}, f32[3,32,256]{2,1,0:T(8,128)S(1)}, u32[]{:S(2)}, u32[]{:S(2)}) collective-permute-start(f32[3,32,256]{2,1,0:T(8,128)} %get-tuple-element.40), channel_id=1, source_target_pairs={{0,15},{1,0},{2,1},{3,2},{4,3},{5,4},{6,5},{7,6},{8,7},{9,8},{10,9... | collective-permute-start | bytes 294920 | tf_op jit(solution)/shard_map/ppermute | solution.py:767
  14.2 0.0 copy-done
  14.2 0.0 copy-done.1
  14.2 6.1 %inner_drift.1.drift = f32[32,32,256]{2,1,0:T(8,128)S(1)} custom-call(f32[32,32,256]{2,1,0:T(8,128)S(1)} %copy-done, bf16[3,32,32,256]{3,2,1,0:T(8,128)(2,1)S(1)} %copy-done.1), custom_call_target="tpu_custom_call" | custom-call | flops 47185920 | bytes 3670016 | tf_op jit(solution)/shard_map/inner_drift/pallas_call | solution.py:196
  20.3 0.0 collective-permute-done.2.ylo
  20.3 0.0 collective-permute-done.3.yhi
  20.4 0.0 collective-permute-done.xlo
  20.4 0.0 collective-permute-done.1.xhi
  20.4 0.0 copy-done.2
  20.4 3.3 %advect.1 = (f32[32,32,256]{2,1,0:T(8,128)S(1)}, f32[8,32,256]{2,1,0:T(8,128)S(1)}, f32[8,32,256]{2,1,0:T(8,128)S(1)}, f32[32,8,256]{2,1,0:T(8,128)S(1)}, f32[32...) custom-call(s32[1,1,32]{2,1,0:T(1,128)S(1)} %copy-done.2, f32[32,32,256]{2,1,0:T(8,128)S(1)} %copy-done, ...), custom_call_target="tpu_custom_call" | custom-call | tf_op jit(solution)/shard_map/advect/pallas_call | solution.py:306
  23.7 0.0 collective-permute-start.6
  23.7 2.9 %collective-permute-start.7 = (f32[8,32,256]{2,1,0:T(8,128)S(1)}, f32[8,32,256]{2,1,0:T(8,128)S(1)}, u32[]{:S(2)}, u32[]{:S(2)}) collective-permute-start(f32[8,32,256]{2,1,0:T(8,128)S(1)} %get-tuple-element.49), channel_id=1, source_target_pairs={{0,112},{16,0},{32,16},{48,32},{64,48},{80,64},{96,80},{112,96},{1... | collective-permute-start | bytes 786440 | tf_op jit(solution)/shard_map/ppermute | solution.py:765
  26.7 0.0 collective-permute-start.4
  26.7 5.3 %collective-permute-start.5 = (f32[32,8,256]{2,1,0:T(8,128)S(1)}, f32[32,8,256]{2,1,0:T(8,128)S(1)}, u32[]{:S(2)}, u32[]{:S(2)}) collective-permute-start(f32[32,8,256]{2,1,0:T(8,128)S(1)} %get-tuple-element.47), channel_id=1, source_target_pairs={{0,15},{1,0},{2,1},{3,2},{4,3},{5,4},{6,5},{7,6},{8,7},{9,8},{10,9... | collective-permute-start | bytes 786440 | tf_op jit(solution)/shard_map/ppermute | solution.py:767
  32.0 4.6 %inner_first.1 = (f32[32,2,48,128]{3,2,1,0:T(8,128)S(1)}, f32[32,2,48,128]{3,2,1,0:T(8,128)S(1)}, f32[32,2,48,128]{3,2,1,0:T(8,128)S(1)}, f32[32,2,48,128]{3,2,1,0:T(8,128)S(1)}) custom-call(s32[1,1,32]{2,1,0:T(1,128)S(1)} %copy-done.2, f32[32,32,256]{2,1,0:T(8,128)S(1)} %get-tuple-element.41.adv), custom_call_target="tpu_custom_call" | custom-call | flops 26214400 | bytes 6291456 | tf_op jit(solution)/shard_map/inner_first/pallas_call | solution.py:412
  36.6 0.0 collective-permute-done.6.xlo
  36.6 0.0 collective-permute-done.7.xhi
  36.7 0.1 slice_select_fusion
  36.8 0.1 collective-permute-start.8
  36.9 5.4 %collective-permute-start.9 = (f32[16,8,256]{2,1,0:T(8,128)S(1)}, f32[16,8,256]{2,1,0:T(8,128)S(1)}, u32[]{:S(2)}, u32[]{:S(2)}) collective-permute-start(f32[16,8,256]{2,1,0:T(8,128)S(1)} %pad_maximum_fusion.1), channel_id=1, source_target_pairs={{0,15},{1,0},{2,1},{3,2},{4,3},{5,4},{6,5},{7,6},{8,7},{9,8},{10,9... | collective-permute-start | bytes 393224 | tf_op jit(solution)/shard_map/ppermute | solution.py:767
  42.3 0.0 copy-start.4
  42.3 0.0 copy-start.3
  42.3 4.3 %inner_second.1 = (f32[32,2,48,128]{3,2,1,0:T(8,128)S(1)}, f32[32,2,48,128]{3,2,1,0:T(8,128)S(1)}, f32[32,2,48,128]{3,2,1,0:T(8,128)S(1)}) custom-call(f32[32,2,48,128]{3,2,1,0:T(8,128)S(1)} %get-tuple-element.54.before.in2, f32[32,2,48,128]{3,2,1,0:T(8,128)S(1)} %get-tuple-element.55.factor.own_factor), custom_call_target="tpu_custom_call" | custom-call | flops 23592960 | bytes 9437184 | tf_op jit(solution)/shard_map/inner_second/pallas_call | solution.py:431
  46.6 0.0 collective-permute-done.4.ylo
  46.6 0.0 collective-permute-done.5.yhi
  46.6 0.0 collective-permute-done.8.clo
  46.6 0.0 collective-permute-done.9.chi
  46.6 0.0 copy-done.4
  46.6 0.1 collective-permute-start.10
  46.7 0.0 copy-done.3
  46.7 5.3 %collective-permute-start.11 = (f32[12,32,256]{2,1,0:T(8,128)S(1)}, f32[12,32,256]{2,1,0:T(8,128)S(1)}, u32[]{:S(2)}, u32[]{:S(2)}) collective-permute-start(f32[12,32,256]{2,1,0:T(8,128)S(1)} %copy-done.3), channel_id=1, source_target_pairs={{0,15},{1,0},{2,1},{3,2},{4,3},{5,4},{6,5},{7,6},{8,7},{9,8},{10,9... | collective-permute-start | bytes 1179656 | tf_op jit(solution)/shard_map/ppermute | solution.py:767
  52.0 14.0 %sweeps.1 = (f32[36,2,64,128]{3,2,1,0:T(8,128)S(1)}, f32[34,2,64,128]{3,2,1,0:T(8,128)S(1)}, f32[128,1,128]{2,1,0:T(1,128)S(1)}) custom-call(f32[32,32,256]{2,1,0:T(8,128)S(1)} %get-tuple-element.41.adv, f32[32,2,48,128]{3,2,1,0:T(8,128)S(1)} %get-tuple-element.42.in1, f32[32,2,48,128]{3,2,1,0:T(8,128)S(1)} %get-tuple-element.54.before.in2, ...), custom_call_target="tpu_custom_call" | custom-call | tf_op jit(solution)/shard_map/sweeps/pallas_call | solution.py:571
  66.1 13.5 %all_to_all.5.parts = f32[128,1,128]{2,1,0:T(1,128)S(1)} all-to-all(f32[128,1,128]{2,1,0:T(1,128)S(1)} %get-tuple-element.67), channel_id=1, replica_groups=mesh['gx'=8,'gy'=16] {'gx','gy'}, dimensions={0} | all-to-all | bytes 131072 | tf_op jit(solution)/shard_map/all_to_all | solution.py:800
  79.5 0.0 collective-permute-done.10.ylo
  79.5 0.0 collective-permute-done.11.yhi
  79.5 19.4 %extend.1 = (f32[32,32,256]{2,1,0:T(8,128)}, f32[6,32,32,256]{3,2,1,0:T(8,128)}) custom-call(f32[128,1,128]{2,1,0:T(1,128)S(1)} %all_to_all.5.parts, f32[36,2,64,128]{3,2,1,0:T(8,128)S(1)} %get-tuple-element.68.cur, f32[34,2,64,128]{3,2,1,0:T(8,128)S(1)} %get-tuple-element.69.weight, f32[6,32,32,256]{3,2,1,0:T(8,128)} %stress.3, ...), custom_call_target="tpu_custom_call" | custom-call | tf_op jit(solution)/shard_map/extend/pallas_call | solution.py:741
  (4 shorter events, 0.0 us)
Async XLA Ops:
  0.6 13.6 %copy-start = (f32[32,32,256]{2,1,0:T(8,128)S(1)}, f32[32,32,256]{2,1,0:T(8,128)}, u32[]{:S(2)}) copy-start(f32[32,32,256]{2,1,0:T(8,128)} %level.5) | copy-start | bytes 3145732
  0.6 13.6 %copy-start.1 = (bf16[3,32,32,256]{3,2,1,0:T(8,128)(2,1)S(1)}, bf16[3,32,32,256]{3,2,1,0:T(8,128)(2,1)}, u32[]{:S(2)}) copy-start(bf16[3,32,32,256]{3,2,1,0:T(8,128)(2,1)} %speed.3) | copy-start | bytes 4718596
  5.0 15.4 %collective-permute-start = (f32[15,32,256]{2,1,0:T(8,128)}, f32[15,32,256]{2,1,0:T(8,128)S(1)}, u32[]{:S(2)}, u32[]{:S(2)}) collective-permute-start(f32[15,32,256]{2,1,0:T(8,128)} %get-tuple-element.37), channel_id=1, source_target_pairs={{0,16},{16,32},{32,48},{48,64},{64,80},{80,96},{96,112},{112,0},{1... | collective-permute-start | bytes 1474568 | tf_op jit(solution)/shard_map/ppermute | solution.py:765
  5.0 15.4 %collective-permute-start.1 = (f32[15,32,256]{2,1,0:T(8,128)}, f32[15,32,256]{2,1,0:T(8,128)S(1)}, u32[]{:S(2)}, u32[]{:S(2)}) collective-permute-start(f32[15,32,256]{2,1,0:T(8,128)} %get-tuple-element.38), channel_id=1, source_target_pairs={{0,112},{16,0},{32,16},{48,32},{64,48},{80,64},{96,80},{112,96},{1... | collective-permute-start | bytes 1474568 | tf_op jit(solution)/shard_map/ppermute | solution.py:765
  7.9 12.4 %collective-permute-start.2 = (f32[3,32,256]{2,1,0:T(8,128)}, f32[3,32,256]{2,1,0:T(8,128)S(1)}, u32[]{:S(2)}, u32[]{:S(2)}) collective-permute-start(f32[3,32,256]{2,1,0:T(8,128)} %get-tuple-element.39), channel_id=1, source_target_pairs={{0,1},{1,2},{2,3},{3,4},{4,5},{5,6},{6,7},{7,8},{8,9},{9,10},{10,1... | collective-permute-start | bytes 294920 | tf_op jit(solution)/shard_map/ppermute | solution.py:767
  9.9 10.5 %copy-start.2 = (s32[1,1,32]{2,1,0:T(1,128)S(1)}, s32[1,1,32]{2,1,0:T(1,128)}, u32[]{:S(2)}) copy-start(s32[1,1,32]{2,1,0:T(1,128)} %tiles.3) | copy-start | bytes 388
  9.9 10.4 %collective-permute-start.3 = (f32[3,32,256]{2,1,0:T(8,128)}, f32[3,32,256]{2,1,0:T(8,128)S(1)}, u32[]{:S(2)}, u32[]{:S(2)}) collective-permute-start(f32[3,32,256]{2,1,0:T(8,128)} %get-tuple-element.40), channel_id=1, source_target_pairs={{0,15},{1,0},{2,1},{3,2},{4,3},{5,4},{6,5},{7,6},{8,7},{9,8},{10,9... | collective-permute-start | bytes 294920 | tf_op jit(solution)/shard_map/ppermute | solution.py:767
  23.7 12.9 %collective-permute-start.6 = (f32[8,32,256]{2,1,0:T(8,128)S(1)}, f32[8,32,256]{2,1,0:T(8,128)S(1)}, u32[]{:S(2)}, u32[]{:S(2)}) collective-permute-start(f32[8,32,256]{2,1,0:T(8,128)S(1)} %get-tuple-element.48), channel_id=1, source_target_pairs={{0,16},{16,32},{32,48},{48,64},{64,80},{80,96},{96,112},{112,0},{1... | collective-permute-start | bytes 786440 | tf_op jit(solution)/shard_map/ppermute | solution.py:765
  23.7 12.9 %collective-permute-start.7 = (f32[8,32,256]{2,1,0:T(8,128)S(1)}, f32[8,32,256]{2,1,0:T(8,128)S(1)}, u32[]{:S(2)}, u32[]{:S(2)}) collective-permute-start(f32[8,32,256]{2,1,0:T(8,128)S(1)} %get-tuple-element.49), channel_id=1, source_target_pairs={{0,112},{16,0},{32,16},{48,32},{64,48},{80,64},{96,80},{112,96},{1... | collective-permute-start | bytes 786440 | tf_op jit(solution)/shard_map/ppermute | solution.py:765
  26.7 19.9 %collective-permute-start.4 = (f32[32,8,256]{2,1,0:T(8,128)S(1)}, f32[32,8,256]{2,1,0:T(8,128)S(1)}, u32[]{:S(2)}, u32[]{:S(2)}) collective-permute-start(f32[32,8,256]{2,1,0:T(8,128)S(1)} %get-tuple-element.46), channel_id=1, source_target_pairs={{0,1},{1,2},{2,3},{3,4},{4,5},{5,6},{6,7},{7,8},{8,9},{9,10},{10,1... | collective-permute-start | bytes 786440 | tf_op jit(solution)/shard_map/ppermute | solution.py:767
  26.7 19.9 %collective-permute-start.5 = (f32[32,8,256]{2,1,0:T(8,128)S(1)}, f32[32,8,256]{2,1,0:T(8,128)S(1)}, u32[]{:S(2)}, u32[]{:S(2)}) collective-permute-start(f32[32,8,256]{2,1,0:T(8,128)S(1)} %get-tuple-element.47), channel_id=1, source_target_pairs={{0,15},{1,0},{2,1},{3,2},{4,3},{5,4},{6,5},{7,6},{8,7},{9,8},{10,9... | collective-permute-start | bytes 786440 | tf_op jit(solution)/shard_map/ppermute | solution.py:767
  36.8 9.8 %collective-permute-start.8 = (f32[16,8,256]{2,1,0:T(8,128)S(1)}, f32[16,8,256]{2,1,0:T(8,128)S(1)}, u32[]{:S(2)}, u32[]{:S(2)}) collective-permute-start(f32[16,8,256]{2,1,0:T(8,128)S(1)} %pad_maximum_fusion), channel_id=1, source_target_pairs={{0,1},{1,2},{2,3},{3,4},{4,5},{5,6},{6,7},{7,8},{8,9},{9,10},{10,1... | collective-permute-start | bytes 393224 | tf_op jit(solution)/shard_map/ppermute | solution.py:767
  36.9 9.7 %collective-permute-start.9 = (f32[16,8,256]{2,1,0:T(8,128)S(1)}, f32[16,8,256]{2,1,0:T(8,128)S(1)}, u32[]{:S(2)}, u32[]{:S(2)}) collective-permute-start(f32[16,8,256]{2,1,0:T(8,128)S(1)} %pad_maximum_fusion.1), channel_id=1, source_target_pairs={{0,15},{1,0},{2,1},{3,2},{4,3},{5,4},{6,5},{7,6},{8,7},{9,8},{10,9... | collective-permute-start | bytes 393224 | tf_op jit(solution)/shard_map/ppermute | solution.py:767
  42.3 4.3 %copy-start.4 = (f32[12,32,256]{2,1,0:T(8,128)S(1)}, f32[12,32,256]{2,1,0:T(8,128)}, u32[]{:S(2)}) copy-start(f32[12,32,256]{2,1,0:T(8,128)} %get-tuple-element.70) | copy-start | bytes 1179652
  42.3 4.4 %copy-start.3 = (f32[12,32,256]{2,1,0:T(8,128)S(1)}, f32[12,32,256]{2,1,0:T(8,128)}, u32[]{:S(2)}) copy-start(f32[12,32,256]{2,1,0:T(8,128)} %get-tuple-element.71) | copy-start | bytes 1179652
  46.6 32.9 %collective-permute-start.10 = (f32[12,32,256]{2,1,0:T(8,128)S(1)}, f32[12,32,256]{2,1,0:T(8,128)S(1)}, u32[]{:S(2)}, u32[]{:S(2)}) collective-permute-start(f32[12,32,256]{2,1,0:T(8,128)S(1)} %copy-done.4), channel_id=1, source_target_pairs={{0,1},{1,2},{2,3},{3,4},{4,5},{5,6},{6,7},{7,8},{8,9},{9,10},{10,1... | collective-permute-start | bytes 1179656 | tf_op jit(solution)/shard_map/ppermute | solution.py:767
  46.7 32.8 %collective-permute-start.11 = (f32[12,32,256]{2,1,0:T(8,128)S(1)}, f32[12,32,256]{2,1,0:T(8,128)S(1)}, u32[]{:S(2)}, u32[]{:S(2)}) collective-permute-start(f32[12,32,256]{2,1,0:T(8,128)S(1)} %copy-done.3), channel_id=1, source_target_pairs={{0,15},{1,0},{2,1},{3,2},{4,3},{5,4},{6,5},{7,6},{8,7},{9,8},{10,9... | collective-permute-start | bytes 1179656 | tf_op jit(solution)/shard_map/ppermute | solution.py:767

commit v9 on v8

--- a/solution.py
+++ b/solution.py
@@ -211,10 +211,14 @@
 
 
 def advect_kernel(
-    tiles, level, xlo, xhi, ylo, yhi, speed, drift,
+    tiles, level, xlo, xhi, ylo, yhi, speed, drift, stress_p, stress_n,
     adv, to_xp, to_xn, to_yp, to_yn, tail_p, tail_n,
-    pad, table, faces, ends, sems, y_sems, end_sems,
+    pad, table, faces, ends, sems, y_sems, end_sems, ride_sems,
 ):
+    riders = [
+        pltpu.make_async_copy(src, out.at[pl.ds(CX, 8 * COMPS)], ride_sems.at[n])
+        for n, (src, out) in enumerate(((stress_p, to_yp), (stress_n, to_yn)))
+    ]
     copies = []
     for h in range(2):
         for n, (src, at, size) in enumerate(((level, 3, CX), (xlo, 0, 3), (xhi, CX + 3, 3))):
@@ -234,7 +238,7 @@
                     src.at[pl.ds(3, 2 * COMPS), pl.ds(y, 8)], ends.at[n, m], end_sems.at[n, m]
                 )
             )
-    for copy in copies:
+    for copy in copies + riders:
         copy.start()
     table[...] = band_table(tiles)
     for copy in copies:
@@ -298,18 +302,20 @@
             for x in range(i * TILE, i * TILE + TILE):
                 to_yp[x, :, half(h)] = jnp.where(row8 == 7, first, adv[x, 0:8, half(h)])
                 to_yn[x, :, half(h)] = jnp.where(row8 == 0, last, adv[x, CY - 8 : CY, half(h)])
-
-
-def advect(tiles, level, xlo, xhi, ylo, yhi, speed, drift):
+    for copy in riders:
+        copy.wait()
+
+
+def advect(tiles, level, xlo, xhi, ylo, yhi, speed, drift, stress_p, stress_n):
     shape = lambda *s: jax.ShapeDtypeStruct(s, F32)
     z = 2 * LANES
     return pl.pallas_call(
         advect_kernel,
         out_shape=[shape(CX, CY, z)]
         + [shape(8, CY, z)] * 2
-        + [shape(CX, 8, z)] * 2
+        + [shape(CX + 8 * COMPS, 8, z)] * 2
         + [shape(2, 8, z)] * 2,
-        in_specs=[SMEM, ANY, ANY, ANY, ANY, ANY, VMEM, VMEM],
+        in_specs=[SMEM, ANY, ANY, ANY, ANY, ANY, VMEM, VMEM, ANY, ANY],
         out_specs=[VMEM] * 7,
         scratch_shapes=[
             pltpu.VMEM((CX + 6, 2, 48, LANES), F32),
@@ -319,10 +325,11 @@
             pltpu.SemaphoreType.DMA((2, 3)),
             pltpu.SemaphoreType.DMA((2,)),
             pltpu.SemaphoreType.DMA((2, 2)),
+            pltpu.SemaphoreType.DMA((2,)),
         ],
         compiler_params=pltpu.CompilerParams(vmem_limit_bytes=12 * MIB),
         name="advect",
-    )(tiles, level, xlo, xhi, ylo, yhi, speed, drift)
+    )(tiles, level, xlo, xhi, ylo, yhi, speed, drift, stress_p, stress_n)
 
 
 WIDE = CX + 2 * DEEP
@@ -454,8 +461,8 @@
             (adv, DEEP, CX, OWN, CY),
             (xlo.at[pl.ds(0, DEEP)], 0, DEEP, OWN, CY),
             (xhi.at[pl.ds(0, DEEP)], DEEP + CX, DEEP, OWN, CY),
-            (ylo, DEEP, CX, OWN - 8, 8),
-            (yhi, DEEP, CX, OWN + CY, 8),
+            (ylo.at[pl.ds(0, CX)], DEEP, CX, OWN - 8, 8),
+            (yhi.at[pl.ds(0, CX)], DEEP, CX, OWN + CY, 8),
             (clo.at[pl.ds(0, DEEP)], 0, DEEP, OWN - 8, 8),
             (clo.at[pl.ds(DEEP, DEEP)], DEEP + CX, DEEP, OWN - 8, 8),
             (chi.at[pl.ds(0, DEEP)], 0, DEEP, OWN + CY, 8),
@@ -482,11 +489,13 @@
         + [(in5, own(cur_out, 2))]
     ):
         done.append(pltpu.make_async_copy(src.at[:, :, pl.ds(8, CY), :], dst, x_sems.at[n]))
-    for copy in copies + done:
+    for copy in copies + done[:1]:
         copy.start()
     sums[...] = jnp.zeros(sums.shape, F32)
-    for copy in copies + done[:2]:
+    for copy in copies + done[:1]:
         copy.wait()
+    for copy in done[2:] + done[1:2]:
+        copy.start()
 
     def prepare(x, groups, bands, keep):
         for h in range(2):
@@ -548,7 +557,9 @@
             return carry
 
         lax.fori_loop(0, DEEP, outer, 0)
-        lax.fori_loop(DEEP + sweep, DEEP + CX - sweep, middle, 0, unroll=2)
+        count_x = CX - 2 * sweep
+        at_once = max(k for k in range(2, 14) if count_x % k == 0)
+        lax.fori_loop(DEEP + sweep, DEEP + CX - sweep, middle, 0, unroll=at_once)
 
     def count(x, carry):
         for h in range(2):
@@ -561,6 +572,7 @@
         return carry
 
     lax.fori_loop(0, CX, count, 0, unroll=2)
+    done[1].wait()
     lane = lax.broadcasted_iota(jnp.int32, (1, LANES), 1)
     sums_row = jnp.where(lane < 64, jnp.sum(sums[0]), jnp.sum(sums[1]))
     part[...] = jnp.broadcast_to(sums_row, part.shape)
@@ -637,7 +649,7 @@
                     for x in range(0, CX, 8):
                         at = ((x + 2) * 2 + h) * ROWS + row + k
                         flat[c, pl.ds(at, 8, stride=2 * ROWS), :] = face[
-                            2 * c + k, x : x + 8, half(h)
+                            CX + 4 * (2 * c + k) + x // 8, :, half(h)
                         ]
             for corner, row in ((clo, OWN - 1), (chi, OWN + CY)):
                 for x, n in ((1, c), (CX + 2, COMPS + c)):
@@ -775,7 +787,8 @@
     ylo, yhi = send(to_yn, 0, 1), send(to_yp, 0, -1)
     drift = inner_drift(level, velocity)
     adv, to_xp, to_xn, to_yp, to_yn, tail_p, tail_n = advect(
-        tiles, level, xlo, xhi, ylo, yhi, velocity, drift
+        tiles, level, xlo, xhi, ylo, yhi, velocity, drift,
+        to_syp.reshape(8 * COMPS, 8, -1), to_syn.reshape(8 * COMPS, 8, -1),
     )
     axlo, axhi = send(to_xn, 1, 0), send(to_xp, -1, 0)
     aylo, ayhi = send(to_yn, 0, 1), send(to_yp, 0, -1)
@@ -790,15 +803,12 @@
     more = inner_second(last, factor)
     clo = send(corners(slice(-8, None), 0, tail_n), 0, 1)
     chi = send(corners(slice(0, 8), 7, tail_p), 0, -1)
-    to_syp, to_syn, aylo, ayhi, clo, chi, more = lax.optimization_barrier(
-        (to_syp, to_syn, aylo, ayhi, clo, chi, more)
-    )
-    sylo, syhi = send(to_syn, 0, 1), send(to_syp, 0, -1)
+    aylo, ayhi, clo, chi, more = lax.optimization_barrier((aylo, ayhi, clo, chi, more))
     cur, weight, part = sweeps(
         adv, (*inner, *more), factor, weight, (axlo, axhi, aylo, ayhi, clo, chi), nx * ny
     )
     parts = lax.all_to_all(part, ("gx", "gy"), 0, 0, tiled=True)
-    return extend(parts, cur, weight, stress, (xlo, xhi, sylo, syhi, clo, chi))
+    return extend(parts, cur, weight, stress, (xlo, xhi, aylo, ayhi, clo, chi))
 
 
 def solution(mesh):

time: 99.6 us -> 96.2 us (0.966)
  starting transfers between devices: 28.5 us -> 23.1 us
  blocking collectives: 13.5 us -> 18.6 us
  Pallas kernels: 56 us -> 52.4 us
    ppermute x8 -> x6, starting transfers between devices: 22.5 us -> 17.2 us  [send(): return lax.ppermute(value, 'gy', [(i, (i + dy) % ny) for i in range(ny)])]
    all_to_all x1, blocking collectives: 13.5 us -> 18.6 us  [on_device(): parts = lax.all_to_all(part, ('gx', 'gy'), 0, 0, tiled=True)]
    pallas_call x1, Pallas kernels: 14 us -> 10 us  [sweeps(): pl.pallas_call(sweep_kernel, out_shape=[shape(CX + 4, 2, ROWS, LANES), sh...]
  transfers between devices with their start and end apart: 12 -> 10, of which waited for: 0 -> 1; matrix products, arithmetic and copies ran while one was open for 0% -> 0% of each run, Pallas kernels for 29% -> 16%
where the time goes in v9:
time: 96.2 us; the launch traced here: 95.7 us
  Pallas kernels  52.4 us (54%)
  starting transfers between devices  23.1 us (24%)
  blocking collectives  18.6 us (19%)
  between operations  0.99 us (1%)
    pallas_call x1, Pallas kernels, extend(): pl.pallas_call(extend_kernel, out_shape=[shape(CX, CY, z), shape(COMPS, C...  19.4 us
    all_to_all x1, blocking collectives, on_device(): parts = lax.all_to_all(part, ('gx', 'gy'), 0, 0, tiled=True)  18.6 us
    ppermute x6, starting transfers between devices, send(): return lax.ppermute(value, 'gy', [(i, (i + dy) % ny) for i in range(ny)])  17.2 us
    pallas_call x1, Pallas kernels, sweeps(): pl.pallas_call(sweep_kernel, out_shape=[shape(CX + 4, 2, ROWS, LANES), sh...  10 us
    pallas_call x1, Pallas kernels, inner_drift(): pl.pallas_call(inner_kernel, out_shape=jax.ShapeDtypeStruct(level.shape,...  6.08 us
    ppermute x4, starting transfers between devices, send(): return lax.ppermute(value, 'gx', [(i, (i + dx) % nx) for i in range(nx)])  5.92 us
    pallas_call x1, Pallas kernels, inner_first(): pl.pallas_call(inner_first_kernel, out_shape=[jax.ShapeDtypeStruct((CX, 2...  4.59 us
    pallas_call x1, Pallas kernels, cut(): pl.pallas_call(cut_kernel, out_shape=[message(3 + 2 * COMPS)] * 2 + [mess...  4.31 us
  transfers between devices with their start and end apart: 10, of which 1 were waited for; matrix products, arithmetic and copies ran while one was open for 0% of the time, Pallas kernels for 16%

profile of v9, /device:TPU:0, one launch (start us, length us, event | category | flops | bytes accessed | tf_op | source)
XLA Modules:
  0.0 95.7 jit_solution(4548350303517268816)
XLA Ops:
  0.6 0.0 copy-start
  0.6 0.0 copy-start.1
  0.6 4.3 %cut.1 = (f32[15,32,256]{2,1,0:T(8,128)}, f32[15,32,256]{2,1,0:T(8,128)}, f32[3,32,256]{2,1,0:T(8,128)}, f32[3,32,256]{2,1,0:T(8,128)}, f32[12,32,256]{2,1,0:T(8,128)}, /*index=5*/f32[12,32,256]{2,1,0:T(8,128)}) custom-call(f32[32,32,256]{2,1,0:T(8,128)} %level.5, f32[6,32,32,256]{3,2,1,0:T(8,128)} %stress.3), custom_call_target="tpu_custom_call" | custom-call | tf_op jit(solution)/shard_map/cut/pallas_call | solution.py:139
  5.0 0.0 collective-permute-start
  5.0 2.9 %collective-permute-start.1 = (f32[15,32,256]{2,1,0:T(8,128)}, f32[15,32,256]{2,1,0:T(8,128)S(1)}, u32[]{:S(2)}, u32[]{:S(2)}) collective-permute-start(f32[15,32,256]{2,1,0:T(8,128)} %get-tuple-element.36), channel_id=1, source_target_pairs={{0,112},{16,0},{32,16},{48,32},{64,48},{80,64},{96,80},{112,96},{1... | collective-permute-start | bytes 1474568 | tf_op jit(solution)/shard_map/ppermute | solution.py:777
  7.9 2.0 %collective-permute-start.2 = (f32[3,32,256]{2,1,0:T(8,128)}, f32[3,32,256]{2,1,0:T(8,128)S(1)}, u32[]{:S(2)}, u32[]{:S(2)}) collective-permute-start(f32[3,32,256]{2,1,0:T(8,128)} %get-tuple-element.37), channel_id=1, source_target_pairs={{0,1},{1,2},{2,3},{3,4},{4,5},{5,6},{6,7},{7,8},{8,9},{9,10},{10,1... | collective-permute-start | bytes 294920 | tf_op jit(solution)/shard_map/ppermute | solution.py:779
  9.9 0.0 copy-start.2
  9.9 0.0 copy-start.3
  9.9 0.0 copy-start.4
  9.9 4.4 %collective-permute-start.3 = (f32[3,32,256]{2,1,0:T(8,128)}, f32[3,32,256]{2,1,0:T(8,128)S(1)}, u32[]{:S(2)}, u32[]{:S(2)}) collective-permute-start(f32[3,32,256]{2,1,0:T(8,128)} %get-tuple-element.38), channel_id=1, source_target_pairs={{0,15},{1,0},{2,1},{3,2},{4,3},{5,4},{6,5},{7,6},{8,7},{9,8},{10,9... | collective-permute-start | bytes 294920 | tf_op jit(solution)/shard_map/ppermute | solution.py:779
  14.3 0.0 copy-done
  14.3 0.0 copy-done.1
  14.3 6.1 %inner_drift.1.drift = f32[32,32,256]{2,1,0:T(8,128)S(1)} custom-call(f32[32,32,256]{2,1,0:T(8,128)S(1)} %copy-done, bf16[3,32,32,256]{3,2,1,0:T(8,128)(2,1)S(1)} %copy-done.1), custom_call_target="tpu_custom_call" | custom-call | flops 47185920 | bytes 3670016 | tf_op jit(solution)/shard_map/inner_drift/pallas_call | solution.py:196
  20.4 0.0 collective-permute-done.2.ylo
  20.4 0.0 collective-permute-done.3.yhi
  20.4 0.0 collective-permute-done.xlo
  20.5 0.0 collective-permute-done.1.xhi
  20.5 0.0 copy-done.2
  20.5 0.0 copy-done.3
  20.5 0.0 copy-done.4
  20.5 3.7 %advect.1 = (f32[32,32,256]{2,1,0:T(8,128)S(1)}, f32[8,32,256]{2,1,0:T(8,128)S(1)}, f32[8,32,256]{2,1,0:T(8,128)S(1)}, f32[80,8,256]{2,1,0:T(8,128)S(1)}, f32[80...) custom-call(s32[1,1,32]{2,1,0:T(1,128)S(1)} %copy-done.4, f32[32,32,256]{2,1,0:T(8,128)S(1)} %copy-done, ...), custom_call_target="tpu_custom_call" | custom-call | tf_op jit(solution)/shard_map/advect/pallas_call | solution.py:312
  24.2 0.0 collective-permute-start.6
  24.2 2.9 %collective-permute-start.7 = (f32[8,32,256]{2,1,0:T(8,128)S(1)}, f32[8,32,256]{2,1,0:T(8,128)S(1)}, u32[]{:S(2)}, u32[]{:S(2)}) collective-permute-start(f32[8,32,256]{2,1,0:T(8,128)S(1)} %get-tuple-element.47), channel_id=1, source_target_pairs={{0,112},{16,0},{32,16},{48,32},{64,48},{80,64},{96,80},{112,96},{1... | collective-permute-start | bytes 786440 | tf_op jit(solution)/shard_map/ppermute | solution.py:777
  27.2 0.0 collective-permute-start.4
  27.2 5.3 %collective-permute-start.5 = (f32[80,8,256]{2,1,0:T(8,128)S(1)}, f32[80,8,256]{2,1,0:T(8,128)S(1)}, u32[]{:S(2)}, u32[]{:S(2)}) collective-permute-start(f32[80,8,256]{2,1,0:T(8,128)S(1)} %get-tuple-element.45), channel_id=1, source_target_pairs={{0,15},{1,0},{2,1},{3,2},{4,3},{5,4},{6,5},{7,6},{8,7},{9,8},{10,9... | collective-permute-start | bytes 1966088 | tf_op jit(solution)/shard_map/ppermute | solution.py:779
  32.5 4.6 %inner_first.1 = (f32[32,2,48,128]{3,2,1,0:T(8,128)S(1)}, f32[32,2,48,128]{3,2,1,0:T(8,128)S(1)}, f32[32,2,48,128]{3,2,1,0:T(8,128)S(1)}, f32[32,2,48,128]{3,2,1,0:T(8,128)S(1)}) custom-call(s32[1,1,32]{2,1,0:T(1,128)S(1)} %copy-done.4, f32[32,32,256]{2,1,0:T(8,128)S(1)} %get-tuple-element.41.adv), custom_call_target="tpu_custom_call" | custom-call | flops 26214400 | bytes 6291456 | tf_op jit(solution)/shard_map/inner_first/pallas_call | solution.py:419
  37.1 0.0 collective-permute-done.6.xlo
  37.1 0.0 collective-permute-done.7.xhi
  37.1 0.1 slice_select_fusion
  37.3 0.1 collective-permute-start.8
  37.4 5.4 %collective-permute-start.9 = (f32[16,8,256]{2,1,0:T(8,128)S(1)}, f32[16,8,256]{2,1,0:T(8,128)S(1)}, u32[]{:S(2)}, u32[]{:S(2)}) collective-permute-start(f32[16,8,256]{2,1,0:T(8,128)S(1)} %pad_maximum_fusion.1), channel_id=1, source_target_pairs={{0,15},{1,0},{2,1},{3,2},{4,3},{5,4},{6,5},{7,6},{8,7},{9,8},{10,9... | collective-permute-start | bytes 393224 | tf_op jit(solution)/shard_map/ppermute | solution.py:779
  42.8 4.3 %inner_second.1 = (f32[32,2,48,128]{3,2,1,0:T(8,128)S(1)}, f32[32,2,48,128]{3,2,1,0:T(8,128)S(1)}, f32[32,2,48,128]{3,2,1,0:T(8,128)S(1)}) custom-call(f32[32,2,48,128]{3,2,1,0:T(8,128)S(1)} %get-tuple-element.52.before.in2, f32[32,2,48,128]{3,2,1,0:T(8,128)S(1)} %get-tuple-element.53.factor.own_factor), custom_call_target="tpu_custom_call" | custom-call | flops 23592960 | bytes 9437184 | tf_op jit(solution)/shard_map/inner_second/pallas_call | solution.py:438
  47.0 0.5 collective-permute-done.8.clo
  47.5 0.0 collective-permute-done.9.chi
  47.5 0.0 collective-permute-done.4.ylo
  47.5 0.0 collective-permute-done.5.yhi
  47.5 10.0 %sweeps.1 = (f32[36,2,64,128]{3,2,1,0:T(8,128)S(1)}, f32[34,2,64,128]{3,2,1,0:T(8,128)S(1)}, f32[128,1,128]{2,1,0:T(1,128)S(1)}) custom-call(f32[32,32,256]{2,1,0:T(8,128)S(1)} %get-tuple-element.41.adv, f32[32,2,48,128]{3,2,1,0:T(8,128)S(1)} %get-tuple-element.42.in1, f32[32,2,48,128]{3,2,1,0:T(8,128)S(1)} %get-tuple-element.52.before.in2, ...), custom_call_target="tpu_custom_call" | custom-call | tf_op jit(solution)/shard_map/sweeps/pallas_call | solution.py:583
  57.6 18.6 %all_to_all.5.parts = f32[128,1,128]{2,1,0:T(1,128)S(1)} all-to-all(f32[128,1,128]{2,1,0:T(1,128)S(1)} %get-tuple-element.65), channel_id=1, replica_groups=mesh['gx'=8,'gy'=16] {'gx','gy'}, dimensions={0} | all-to-all | bytes 131072 | tf_op jit(solution)/shard_map/all_to_all | solution.py:810
  76.1 19.4 %extend.1 = (f32[32,32,256]{2,1,0:T(8,128)}, f32[6,32,32,256]{3,2,1,0:T(8,128)}) custom-call(f32[128,1,128]{2,1,0:T(1,128)S(1)} %all_to_all.5.parts, f32[36,2,64,128]{3,2,1,0:T(8,128)S(1)} %get-tuple-element.66.cur, f32[34,2,64,128]{3,2,1,0:T(8,128)S(1)} %get-tuple-element.67.weight, f32[6,32,32,256]{3,2,1,0:T(8,128)} %stress.3, ...), custom_call_target="tpu_custom_call" | custom-call | tf_op jit(solution)/shard_map/extend/pallas_call | solution.py:753
  (4 shorter events, 0.0 us)
Async XLA Ops:
  0.6 13.7 %copy-start = (f32[32,32,256]{2,1,0:T(8,128)S(1)}, f32[32,32,256]{2,1,0:T(8,128)}, u32[]{:S(2)}) copy-start(f32[32,32,256]{2,1,0:T(8,128)} %level.5) | copy-start | bytes 3145732
  0.6 13.7 %copy-start.1 = (bf16[3,32,32,256]{3,2,1,0:T(8,128)(2,1)S(1)}, bf16[3,32,32,256]{3,2,1,0:T(8,128)(2,1)}, u32[]{:S(2)}) copy-start(bf16[3,32,32,256]{3,2,1,0:T(8,128)(2,1)} %speed.3) | copy-start | bytes 4718596
  5.0 15.5 %collective-permute-start = (f32[15,32,256]{2,1,0:T(8,128)}, f32[15,32,256]{2,1,0:T(8,128)S(1)}, u32[]{:S(2)}, u32[]{:S(2)}) collective-permute-start(f32[15,32,256]{2,1,0:T(8,128)} %get-tuple-element.35), channel_id=1, source_target_pairs={{0,16},{16,32},{32,48},{48,64},{64,80},{80,96},{96,112},{112,0},{1... | collective-permute-start | bytes 1474568 | tf_op jit(solution)/shard_map/ppermute | solution.py:777
  5.0 15.5 %collective-permute-start.1 = (f32[15,32,256]{2,1,0:T(8,128)}, f32[15,32,256]{2,1,0:T(8,128)S(1)}, u32[]{:S(2)}, u32[]{:S(2)}) collective-permute-start(f32[15,32,256]{2,1,0:T(8,128)} %get-tuple-element.36), channel_id=1, source_target_pairs={{0,112},{16,0},{32,16},{48,32},{64,48},{80,64},{96,80},{112,96},{1... | collective-permute-start | bytes 1474568 | tf_op jit(solution)/shard_map/ppermute | solution.py:777
  7.9 12.5 %collective-permute-start.2 = (f32[3,32,256]{2,1,0:T(8,128)}, f32[3,32,256]{2,1,0:T(8,128)S(1)}, u32[]{:S(2)}, u32[]{:S(2)}) collective-permute-start(f32[3,32,256]{2,1,0:T(8,128)} %get-tuple-element.37), channel_id=1, source_target_pairs={{0,1},{1,2},{2,3},{3,4},{4,5},{5,6},{6,7},{7,8},{8,9},{9,10},{10,1... | collective-permute-start | bytes 294920 | tf_op jit(solution)/shard_map/ppermute | solution.py:779
  9.9 10.5 %copy-start.2 = (f32[12,32,256]{2,1,0:T(8,128)S(1)}, f32[12,32,256]{2,1,0:T(8,128)}, u32[]{:S(2)}) copy-start(f32[12,32,256]{2,1,0:T(8,128)} %get-tuple-element.39) | copy-start | bytes 1179652
  9.9 10.5 %copy-start.3 = (f32[12,32,256]{2,1,0:T(8,128)S(1)}, f32[12,32,256]{2,1,0:T(8,128)}, u32[]{:S(2)}) copy-start(f32[12,32,256]{2,1,0:T(8,128)} %get-tuple-element.40) | copy-start | bytes 1179652
  9.9 10.5 %copy-start.4 = (s32[1,1,32]{2,1,0:T(1,128)S(1)}, s32[1,1,32]{2,1,0:T(1,128)}, u32[]{:S(2)}) copy-start(s32[1,1,32]{2,1,0:T(1,128)} %tiles.3) | copy-start | bytes 388
  9.9 10.5 %collective-permute-start.3 = (f32[3,32,256]{2,1,0:T(8,128)}, f32[3,32,256]{2,1,0:T(8,128)S(1)}, u32[]{:S(2)}, u32[]{:S(2)}) collective-permute-start(f32[3,32,256]{2,1,0:T(8,128)} %get-tuple-element.38), channel_id=1, source_target_pairs={{0,15},{1,0},{2,1},{3,2},{4,3},{5,4},{6,5},{7,6},{8,7},{9,8},{10,9... | collective-permute-start | bytes 294920 | tf_op jit(solution)/shard_map/ppermute | solution.py:779
  24.2 12.9 %collective-permute-start.6 = (f32[8,32,256]{2,1,0:T(8,128)S(1)}, f32[8,32,256]{2,1,0:T(8,128)S(1)}, u32[]{:S(2)}, u32[]{:S(2)}) collective-permute-start(f32[8,32,256]{2,1,0:T(8,128)S(1)} %get-tuple-element.46), channel_id=1, source_target_pairs={{0,16},{16,32},{32,48},{48,64},{64,80},{80,96},{96,112},{112,0},{1... | collective-permute-start | bytes 786440 | tf_op jit(solution)/shard_map/ppermute | solution.py:777
  24.2 12.9 %collective-permute-start.7 = (f32[8,32,256]{2,1,0:T(8,128)S(1)}, f32[8,32,256]{2,1,0:T(8,128)S(1)}, u32[]{:S(2)}, u32[]{:S(2)}) collective-permute-start(f32[8,32,256]{2,1,0:T(8,128)S(1)} %get-tuple-element.47), channel_id=1, source_target_pairs={{0,112},{16,0},{32,16},{48,32},{64,48},{80,64},{96,80},{112,96},{1... | collective-permute-start | bytes 786440 | tf_op jit(solution)/shard_map/ppermute | solution.py:777
  27.2 20.4 %collective-permute-start.4 = (f32[80,8,256]{2,1,0:T(8,128)S(1)}, f32[80,8,256]{2,1,0:T(8,128)S(1)}, u32[]{:S(2)}, u32[]{:S(2)}) collective-permute-start(f32[80,8,256]{2,1,0:T(8,128)S(1)} %get-tuple-element.44), channel_id=1, source_target_pairs={{0,1},{1,2},{2,3},{3,4},{4,5},{5,6},{6,7},{7,8},{8,9},{9,10},{10,1... | collective-permute-start | bytes 1966088 | tf_op jit(solution)/shard_map/ppermute | solution.py:779
  27.2 20.4 %collective-permute-start.5 = (f32[80,8,256]{2,1,0:T(8,128)S(1)}, f32[80,8,256]{2,1,0:T(8,128)S(1)}, u32[]{:S(2)}, u32[]{:S(2)}) collective-permute-start(f32[80,8,256]{2,1,0:T(8,128)S(1)} %get-tuple-element.45), channel_id=1, source_target_pairs={{0,15},{1,0},{2,1},{3,2},{4,3},{5,4},{6,5},{7,6},{8,7},{9,8},{10,9... | collective-permute-start | bytes 1966088 | tf_op jit(solution)/shard_map/ppermute | solution.py:779
  37.3 10.3 %collective-permute-start.8 = (f32[16,8,256]{2,1,0:T(8,128)S(1)}, f32[16,8,256]{2,1,0:T(8,128)S(1)}, u32[]{:S(2)}, u32[]{:S(2)}) collective-permute-start(f32[16,8,256]{2,1,0:T(8,128)S(1)} %pad_maximum_fusion), channel_id=1, source_target_pairs={{0,1},{1,2},{2,3},{3,4},{4,5},{5,6},{6,7},{7,8},{8,9},{9,10},{10,1... | collective-permute-start | bytes 393224 | tf_op jit(solution)/shard_map/ppermute | solution.py:779
  37.4 10.2 %collective-permute-start.9 = (f32[16,8,256]{2,1,0:T(8,128)S(1)}, f32[16,8,256]{2,1,0:T(8,128)S(1)}, u32[]{:S(2)}, u32[]{:S(2)}) collective-permute-start(f32[16,8,256]{2,1,0:T(8,128)S(1)} %pad_maximum_fusion.1), channel_id=1, source_target_pairs={{0,15},{1,0},{2,1},{3,2},{4,3},{5,4},{6,5},{7,6},{8,7},{9,8},{10,9... | collective-permute-start | bytes 393224 | tf_op jit(solution)/shard_map/ppermute | solution.py:779

commit v10 on v9

--- a/solution.py
+++ b/solution.py
@@ -122,8 +122,8 @@
         for h in range(2):
             for m in range(1 + COMPS):
                 depth = 2 if m else 3
-                out = outs[min(m, 1)]
-                first = 2 * m - 2 if m else 0
+                out = outs[m // 4]
+                first = (0, 3, 5, 7, 0, 2, 4)[m]
                 for k in range(depth):
                     row = k if n == 0 else 8 - depth + k
                     for x in range(0, CX, 8):
@@ -138,7 +138,7 @@
     message = lambda planes: jax.ShapeDtypeStruct((planes, CX, 2 * LANES), F32)
     return pl.pallas_call(
         cut_kernel,
-        out_shape=[message(3 + 2 * COMPS)] * 2 + [message(3)] * 2 + [message(2 * COMPS)] * 2,
+        out_shape=[message(3 + 2 * COMPS)] * 2 + [message(3 + COMPS)] * 2 + [message(COMPS)] * 2,
         in_specs=[ANY] * 2,
         out_specs=[VMEM] * 6,
         scratch_shapes=[
@@ -216,7 +216,7 @@
     pad, table, faces, ends, sems, y_sems, end_sems, ride_sems,
 ):
     riders = [
-        pltpu.make_async_copy(src, out.at[pl.ds(CX, 8 * COMPS)], ride_sems.at[n])
+        pltpu.make_async_copy(src, out.at[pl.ds(CX, 4 * COMPS)], ride_sems.at[n])
         for n, (src, out) in enumerate(((stress_p, to_yp), (stress_n, to_yn)))
     ]
     copies = []
@@ -230,7 +230,7 @@
                 )
             )
     for n, src in enumerate((ylo, yhi)):
-        copies.append(pltpu.make_async_copy(src, faces.at[n], y_sems.at[n]))
+        copies.append(pltpu.make_async_copy(src.at[pl.ds(0, 3)], faces.at[n], y_sems.at[n]))
     for n, src in enumerate((xlo, xhi)):
         for m, y in enumerate((0, CY - 8)):
             copies.append(
@@ -313,7 +313,7 @@
         advect_kernel,
         out_shape=[shape(CX, CY, z)]
         + [shape(8, CY, z)] * 2
-        + [shape(CX + 8 * COMPS, 8, z)] * 2
+        + [shape(CX + 4 * COMPS, 8, z)] * 2
         + [shape(2, 8, z)] * 2,
         in_specs=[SMEM, ANY, ANY, ANY, ANY, ANY, VMEM, VMEM, ANY, ANY],
         out_specs=[VMEM] * 7,
@@ -604,7 +604,7 @@
 
 
 def extend_kernel(
-    parts, cur, weight, stress, xlo, xhi, ylo, yhi, clo, chi,
+    parts, cur, weight, stress, xlo, xhi, ylo, yhi, sylo, syhi, clo, chi,
     level_out, stress_out,
     pad, ring0, ring1, ring2, ring3, mix0, mix1, stage, sems, x_sems, out_sems,
 ):
@@ -644,13 +644,15 @@
     flat = pad.reshape(COMPS, (CX + 4) * 2 * ROWS, LANES)
     for h in range(2):
         for c in range(COMPS):
-            for face, row in ((ylo, OWN - 2), (yhi, OWN + CY)):
+            for face, rest, row in ((ylo, sylo, OWN - 2), (yhi, syhi, OWN + CY)):
                 for k in range(2):
                     for x in range(0, CX, 8):
                         at = ((x + 2) * 2 + h) * ROWS + row + k
-                        flat[c, pl.ds(at, 8, stride=2 * ROWS), :] = face[
-                            CX + 4 * (2 * c + k) + x // 8, :, half(h)
-                        ]
+                        if c < 3:
+                            value = face[3 + 2 * c + k, x : x + 8, half(h)]
+                        else:
+                            value = rest[CX + 4 * (2 * c - 6 + k) + x // 8, :, half(h)]
+                        flat[c, pl.ds(at, 8, stride=2 * ROWS), :] = value
             for corner, row in ((clo, OWN - 1), (chi, OWN + CY)):
                 for x, n in ((1, c), (CX + 2, COMPS + c)):
                     at = 2 * DEEP + n // 8
@@ -753,7 +755,7 @@
     return pl.pallas_call(
         extend_kernel,
         out_shape=[shape(CX, CY, z), shape(COMPS, CX, CY, z)],
-        in_specs=[VMEM, VMEM, VMEM, ANY, ANY, ANY, VMEM, VMEM, VMEM, VMEM],
+        in_specs=[VMEM, VMEM, VMEM, ANY, ANY, ANY] + [VMEM] * 6,
         out_specs=[VMEM, ANY],
         scratch_shapes=[
             pltpu.VMEM((COMPS, CX + 4, 2, ROWS, LANES), F32),
@@ -788,7 +790,7 @@
     drift = inner_drift(level, velocity)
     adv, to_xp, to_xn, to_yp, to_yn, tail_p, tail_n = advect(
         tiles, level, xlo, xhi, ylo, yhi, velocity, drift,
-        to_syp.reshape(8 * COMPS, 8, -1), to_syn.reshape(8 * COMPS, 8, -1),
+        to_syp.reshape(4 * COMPS, 8, -1), to_syn.reshape(4 * COMPS, 8, -1),
     )
     axlo, axhi = send(to_xn, 1, 0), send(to_xp, -1, 0)
     aylo, ayhi = send(to_yn, 0, 1), send(to_yp, 0, -1)
@@ -808,7 +810,7 @@
         adv, (*inner, *more), factor, weight, (axlo, axhi, aylo, ayhi, clo, chi), nx * ny
     )
     parts = lax.all_to_all(part, ("gx", "gy"), 0, 0, tiled=True)
-    return extend(parts, cur, weight, stress, (xlo, xhi, aylo, ayhi, clo, chi))
+    return extend(parts, cur, weight, stress, (xlo, xhi, ylo, yhi, aylo, ayhi, clo, chi))
 
 
 def solution(mesh):

time: 96.2 us -> 93.6 us (0.973)
  blocking collectives: 18.6 us -> 16.2 us
    all_to_all x1, blocking collectives: 18.6 us -> 16.2 us  [on_device(): parts = lax.all_to_all(part, ('gx', 'gy'), 0, 0, tiled=True)]
  transfers between devices with their start and end apart: 10 -> 10, of which waited for: 1 -> 0; matrix products, arithmetic and copies ran while one was open for 0% -> 0% of each run, Pallas kernels for 16% -> 16%
where the time goes in v10:
time: 93.6 us; the launch traced here: 93.1 us
  Pallas kernels  52.5 us (56%)
  starting transfers between devices  23.1 us (25%)
  blocking collectives  16.2 us (17%)
  between operations  1.01 us (1%)
    pallas_call x1, Pallas kernels, extend(): pl.pallas_call(extend_kernel, out_shape=[shape(CX, CY, z), shape(COMPS, C...  19.4 us
    ppermute x6, starting transfers between devices, send(): return lax.ppermute(value, 'gy', [(i, (i + dy) % ny) for i in range(ny)])  17.2 us
    all_to_all x1, blocking collectives, on_device(): parts = lax.all_to_all(part, ('gx', 'gy'), 0, 0, tiled=True)  16.2 us
    pallas_call x1, Pallas kernels, sweeps(): pl.pallas_call(sweep_kernel, out_shape=[shape(CX + 4, 2, ROWS, LANES), sh...  10 us
    pallas_call x1, Pallas kernels, inner_drift(): pl.pallas_call(inner_kernel, out_shape=jax.ShapeDtypeStruct(level.shape,...  6.08 us
    ppermute x4, starting transfers between devices, send(): return lax.ppermute(value, 'gx', [(i, (i + dx) % nx) for i in range(nx)])  5.92 us
    pallas_call x1, Pallas kernels, inner_first(): pl.pallas_call(inner_first_kernel, out_shape=[jax.ShapeDtypeStruct((CX, 2...  4.59 us
    pallas_call x1, Pallas kernels, cut(): pl.pallas_call(cut_kernel, out_shape=[message(3 + 2 * COMPS)] * 2 + [mess...  4.3 us
  transfers between devices with their start and end apart: 10, of which 0 were waited for; matrix products, arithmetic and copies ran while one was open for 0% of the time, Pallas kernels for 16%

profile of v10, /device:TPU:0, one launch (start us, length us, event | category | flops | bytes accessed | tf_op | source)
XLA Modules:
  0.0 93.1 jit_solution(269658919062153288)
XLA Ops:
  0.6 0.0 copy-start
  0.6 0.0 copy-start.1
  0.6 4.3 %cut.1 = (f32[15,32,256]{2,1,0:T(8,128)}, f32[15,32,256]{2,1,0:T(8,128)}, f32[9,32,256]{2,1,0:T(8,128)}, f32[9,32,256]{2,1,0:T(8,128)}, f32[6,32,256]{2,1,0:T(8,128)}, /*index=5*/f32[6,32,256]{2,1,0:T(8,128)}) custom-call(f32[32,32,256]{2,1,0:T(8,128)} %level.5, f32[6,32,32,256]{3,2,1,0:T(8,128)} %stress.3), custom_call_target="tpu_custom_call" | custom-call | tf_op jit(solution)/shard_map/cut/pallas_call | solution.py:139
  5.0 0.0 collective-permute-start
  5.0 2.9 %collective-permute-start.1 = (f32[15,32,256]{2,1,0:T(8,128)}, f32[15,32,256]{2,1,0:T(8,128)S(1)}, u32[]{:S(2)}, u32[]{:S(2)}) collective-permute-start(f32[15,32,256]{2,1,0:T(8,128)} %get-tuple-element.36), channel_id=1, source_target_pairs={{0,112},{16,0},{32,16},{48,32},{64,48},{80,64},{96,80},{112,96},{1... | collective-permute-start | bytes 1474568 | tf_op jit(solution)/shard_map/ppermute | solution.py:779
  7.9 2.0 %collective-permute-start.2 = (f32[9,32,256]{2,1,0:T(8,128)}, f32[9,32,256]{2,1,0:T(8,128)S(1)}, u32[]{:S(2)}, u32[]{:S(2)}) collective-permute-start(f32[9,32,256]{2,1,0:T(8,128)} %get-tuple-element.37), channel_id=1, source_target_pairs={{0,1},{1,2},{2,3},{3,4},{4,5},{5,6},{6,7},{7,8},{8,9},{9,10},{10,1... | collective-permute-start | bytes 884744 | tf_op jit(solution)/shard_map/ppermute | solution.py:781
  9.9 0.0 copy-start.2
  9.9 0.0 copy-start.3
  9.9 0.0 copy-start.4
  9.9 4.4 %collective-permute-start.3 = (f32[9,32,256]{2,1,0:T(8,128)}, f32[9,32,256]{2,1,0:T(8,128)S(1)}, u32[]{:S(2)}, u32[]{:S(2)}) collective-permute-start(f32[9,32,256]{2,1,0:T(8,128)} %get-tuple-element.38), channel_id=1, source_target_pairs={{0,15},{1,0},{2,1},{3,2},{4,3},{5,4},{6,5},{7,6},{8,7},{9,8},{10,9... | collective-permute-start | bytes 884744 | tf_op jit(solution)/shard_map/ppermute | solution.py:781
  14.3 0.0 copy-done
  14.3 0.0 copy-done.1
  14.3 6.1 %inner_drift.1.drift = f32[32,32,256]{2,1,0:T(8,128)S(1)} custom-call(f32[32,32,256]{2,1,0:T(8,128)S(1)} %copy-done, bf16[3,32,32,256]{3,2,1,0:T(8,128)(2,1)S(1)} %copy-done.1), custom_call_target="tpu_custom_call" | custom-call | flops 47185920 | bytes 3670016 | tf_op jit(solution)/shard_map/inner_drift/pallas_call | solution.py:196
  20.4 0.0 collective-permute-done.2.ylo
  20.4 0.0 collective-permute-done.3.yhi
  20.4 0.0 collective-permute-done.xlo
  20.4 0.0 collective-permute-done.1.xhi
  20.5 0.0 copy-done.2
  20.5 0.0 copy-done.3
  20.5 0.0 copy-done.4
  20.5 3.8 %advect.1 = (f32[32,32,256]{2,1,0:T(8,128)S(1)}, f32[8,32,256]{2,1,0:T(8,128)S(1)}, f32[8,32,256]{2,1,0:T(8,128)S(1)}, f32[56,8,256]{2,1,0:T(8,128)S(1)}, f32[56...) custom-call(s32[1,1,32]{2,1,0:T(1,128)S(1)} %copy-done.4, f32[32,32,256]{2,1,0:T(8,128)S(1)} %copy-done, ...), custom_call_target="tpu_custom_call" | custom-call | tf_op jit(solution)/shard_map/advect/pallas_call | solution.py:312
  24.3 0.0 collective-permute-start.6
  24.3 2.9 %collective-permute-start.7 = (f32[8,32,256]{2,1,0:T(8,128)S(1)}, f32[8,32,256]{2,1,0:T(8,128)S(1)}, u32[]{:S(2)}, u32[]{:S(2)}) collective-permute-start(f32[8,32,256]{2,1,0:T(8,128)S(1)} %get-tuple-element.47), channel_id=1, source_target_pairs={{0,112},{16,0},{32,16},{48,32},{64,48},{80,64},{96,80},{112,96},{1... | collective-permute-start | bytes 786440 | tf_op jit(solution)/shard_map/ppermute | solution.py:779
  27.3 0.0 collective-permute-start.4
  27.3 5.3 %collective-permute-start.5 = (f32[56,8,256]{2,1,0:T(8,128)S(1)}, f32[56,8,256]{2,1,0:T(8,128)S(1)}, u32[]{:S(2)}, u32[]{:S(2)}) collective-permute-start(f32[56,8,256]{2,1,0:T(8,128)S(1)} %get-tuple-element.45), channel_id=1, source_target_pairs={{0,15},{1,0},{2,1},{3,2},{4,3},{5,4},{6,5},{7,6},{8,7},{9,8},{10,9... | collective-permute-start | bytes 1376264 | tf_op jit(solution)/shard_map/ppermute | solution.py:781
  32.6 4.6 %inner_first.1 = (f32[32,2,48,128]{3,2,1,0:T(8,128)S(1)}, f32[32,2,48,128]{3,2,1,0:T(8,128)S(1)}, f32[32,2,48,128]{3,2,1,0:T(8,128)S(1)}, f32[32,2,48,128]{3,2,1,0:T(8,128)S(1)}) custom-call(s32[1,1,32]{2,1,0:T(1,128)S(1)} %copy-done.4, f32[32,32,256]{2,1,0:T(8,128)S(1)} %get-tuple-element.41.adv), custom_call_target="tpu_custom_call" | custom-call | flops 26214400 | bytes 6291456 | tf_op jit(solution)/shard_map/inner_first/pallas_call | solution.py:419
  37.2 0.0 collective-permute-done.6.xlo
  37.2 0.0 collective-permute-done.7.xhi
  37.3 0.1 slice_select_fusion
  37.4 0.1 collective-permute-start.8
  37.5 5.4 %collective-permute-start.9 = (f32[16,8,256]{2,1,0:T(8,128)S(1)}, f32[16,8,256]{2,1,0:T(8,128)S(1)}, u32[]{:S(2)}, u32[]{:S(2)}) collective-permute-start(f32[16,8,256]{2,1,0:T(8,128)S(1)} %pad_maximum_fusion.1), channel_id=1, source_target_pairs={{0,15},{1,0},{2,1},{3,2},{4,3},{5,4},{6,5},{7,6},{8,7},{9,8},{10,9... | collective-permute-start | bytes 393224 | tf_op jit(solution)/shard_map/ppermute | solution.py:781
  42.9 4.3 %inner_second.1 = (f32[32,2,48,128]{3,2,1,0:T(8,128)S(1)}, f32[32,2,48,128]{3,2,1,0:T(8,128)S(1)}, f32[32,2,48,128]{3,2,1,0:T(8,128)S(1)}) custom-call(f32[32,2,48,128]{3,2,1,0:T(8,128)S(1)} %get-tuple-element.52.before.in2, f32[32,2,48,128]{3,2,1,0:T(8,128)S(1)} %get-tuple-element.53.factor.own_factor), custom_call_target="tpu_custom_call" | custom-call | flops 23592960 | bytes 9437184 | tf_op jit(solution)/shard_map/inner_second/pallas_call | solution.py:438
  47.2 0.0 collective-permute-done.8.clo
  47.2 0.0 collective-permute-done.9.chi
  47.2 0.0 collective-permute-done.4.ylo.sylo
  47.2 0.0 collective-permute-done.5.yhi.syhi
  47.2 10.0 %sweeps.1 = (f32[36,2,64,128]{3,2,1,0:T(8,128)S(1)}, f32[34,2,64,128]{3,2,1,0:T(8,128)S(1)}, f32[128,1,128]{2,1,0:T(1,128)S(1)}) custom-call(f32[32,32,256]{2,1,0:T(8,128)S(1)} %get-tuple-element.41.adv, f32[32,2,48,128]{3,2,1,0:T(8,128)S(1)} %get-tuple-element.42.in1, f32[32,2,48,128]{3,2,1,0:T(8,128)S(1)} %get-tuple-element.52.before.in2, ...), custom_call_target="tpu_custom_call" | custom-call | tf_op jit(solution)/shard_map/sweeps/pallas_call | solution.py:583
  57.3 16.2 %all_to_all.5.parts = f32[128,1,128]{2,1,0:T(1,128)S(1)} all-to-all(f32[128,1,128]{2,1,0:T(1,128)S(1)} %get-tuple-element.65), channel_id=1, replica_groups=mesh['gx'=8,'gy'=16] {'gx','gy'}, dimensions={0} | all-to-all | bytes 131072 | tf_op jit(solution)/shard_map/all_to_all | solution.py:812
  73.5 19.4 %extend.1 = (f32[32,32,256]{2,1,0:T(8,128)}, f32[6,32,32,256]{3,2,1,0:T(8,128)}) custom-call(f32[128,1,128]{2,1,0:T(1,128)S(1)} %all_to_all.5.parts, f32[36,2,64,128]{3,2,1,0:T(8,128)S(1)} %get-tuple-element.66.cur, f32[34,2,64,128]{3,2,1,0:T(8,128)S(1)} %get-tuple-element.67.weight, f32[6,32,32,256]{3,2,1,0:T(8,128)} %stress.3, ...), custom_call_target="tpu_custom_call" | custom-call | tf_op jit(solution)/shard_map/extend/pallas_call | solution.py:755
  (4 shorter events, 0.0 us)
Async XLA Ops:
  0.6 13.7 %copy-start = (f32[32,32,256]{2,1,0:T(8,128)S(1)}, f32[32,32,256]{2,1,0:T(8,128)}, u32[]{:S(2)}) copy-start(f32[32,32,256]{2,1,0:T(8,128)} %level.5) | copy-start | bytes 3145732
  0.6 13.7 %copy-start.1 = (bf16[3,32,32,256]{3,2,1,0:T(8,128)(2,1)S(1)}, bf16[3,32,32,256]{3,2,1,0:T(8,128)(2,1)}, u32[]{:S(2)}) copy-start(bf16[3,32,32,256]{3,2,1,0:T(8,128)(2,1)} %speed.3) | copy-start | bytes 4718596
  5.0 15.5 %collective-permute-start = (f32[15,32,256]{2,1,0:T(8,128)}, f32[15,32,256]{2,1,0:T(8,128)S(1)}, u32[]{:S(2)}, u32[]{:S(2)}) collective-permute-start(f32[15,32,256]{2,1,0:T(8,128)} %get-tuple-element.35), channel_id=1, source_target_pairs={{0,16},{16,32},{32,48},{48,64},{64,80},{80,96},{96,112},{112,0},{1... | collective-permute-start | bytes 1474568 | tf_op jit(solution)/shard_map/ppermute | solution.py:779
  5.0 15.5 %collective-permute-start.1 = (f32[15,32,256]{2,1,0:T(8,128)}, f32[15,32,256]{2,1,0:T(8,128)S(1)}, u32[]{:S(2)}, u32[]{:S(2)}) collective-permute-start(f32[15,32,256]{2,1,0:T(8,128)} %get-tuple-element.36), channel_id=1, source_target_pairs={{0,112},{16,0},{32,16},{48,32},{64,48},{80,64},{96,80},{112,96},{1... | collective-permute-start | bytes 1474568 | tf_op jit(solution)/shard_map/ppermute | solution.py:779
  7.9 12.5 %collective-permute-start.2 = (f32[9,32,256]{2,1,0:T(8,128)}, f32[9,32,256]{2,1,0:T(8,128)S(1)}, u32[]{:S(2)}, u32[]{:S(2)}) collective-permute-start(f32[9,32,256]{2,1,0:T(8,128)} %get-tuple-element.37), channel_id=1, source_target_pairs={{0,1},{1,2},{2,3},{3,4},{4,5},{5,6},{6,7},{7,8},{8,9},{9,10},{10,1... | collective-permute-start | bytes 884744 | tf_op jit(solution)/shard_map/ppermute | solution.py:781
  9.9 10.5 %copy-start.2 = (f32[6,32,256]{2,1,0:T(8,128)S(1)}, f32[6,32,256]{2,1,0:T(8,128)}, u32[]{:S(2)}) copy-start(f32[6,32,256]{2,1,0:T(8,128)} %get-tuple-element.39) | copy-start | bytes 589828
  9.9 10.5 %copy-start.3 = (f32[6,32,256]{2,1,0:T(8,128)S(1)}, f32[6,32,256]{2,1,0:T(8,128)}, u32[]{:S(2)}) copy-start(f32[6,32,256]{2,1,0:T(8,128)} %get-tuple-element.40) | copy-start | bytes 589828
  9.9 10.5 %copy-start.4 = (s32[1,1,32]{2,1,0:T(1,128)S(1)}, s32[1,1,32]{2,1,0:T(1,128)}, u32[]{:S(2)}) copy-start(s32[1,1,32]{2,1,0:T(1,128)} %tiles.3) | copy-start | bytes 388
  9.9 10.5 %collective-permute-start.3 = (f32[9,32,256]{2,1,0:T(8,128)}, f32[9,32,256]{2,1,0:T(8,128)S(1)}, u32[]{:S(2)}, u32[]{:S(2)}) collective-permute-start(f32[9,32,256]{2,1,0:T(8,128)} %get-tuple-element.38), channel_id=1, source_target_pairs={{0,15},{1,0},{2,1},{3,2},{4,3},{5,4},{6,5},{7,6},{8,7},{9,8},{10,9... | collective-permute-start | bytes 884744 | tf_op jit(solution)/shard_map/ppermute | solution.py:781
  24.3 12.9 %collective-permute-start.6 = (f32[8,32,256]{2,1,0:T(8,128)S(1)}, f32[8,32,256]{2,1,0:T(8,128)S(1)}, u32[]{:S(2)}, u32[]{:S(2)}) collective-permute-start(f32[8,32,256]{2,1,0:T(8,128)S(1)} %get-tuple-element.46), channel_id=1, source_target_pairs={{0,16},{16,32},{32,48},{48,64},{64,80},{80,96},{96,112},{112,0},{1... | collective-permute-start | bytes 786440 | tf_op jit(solution)/shard_map/ppermute | solution.py:779
  24.3 12.9 %collective-permute-start.7 = (f32[8,32,256]{2,1,0:T(8,128)S(1)}, f32[8,32,256]{2,1,0:T(8,128)S(1)}, u32[]{:S(2)}, u32[]{:S(2)}) collective-permute-start(f32[8,32,256]{2,1,0:T(8,128)S(1)} %get-tuple-element.47), channel_id=1, source_target_pairs={{0,112},{16,0},{32,16},{48,32},{64,48},{80,64},{96,80},{112,96},{1... | collective-permute-start | bytes 786440 | tf_op jit(solution)/shard_map/ppermute | solution.py:779
  27.3 19.9 %collective-permute-start.4 = (f32[56,8,256]{2,1,0:T(8,128)S(1)}, f32[56,8,256]{2,1,0:T(8,128)S(1)}, u32[]{:S(2)}, u32[]{:S(2)}) collective-permute-start(f32[56,8,256]{2,1,0:T(8,128)S(1)} %get-tuple-element.44), channel_id=1, source_target_pairs={{0,1},{1,2},{2,3},{3,4},{4,5},{5,6},{6,7},{7,8},{8,9},{9,10},{10,1... | collective-permute-start | bytes 1376264 | tf_op jit(solution)/shard_map/ppermute | solution.py:781
  27.3 19.9 %collective-permute-start.5 = (f32[56,8,256]{2,1,0:T(8,128)S(1)}, f32[56,8,256]{2,1,0:T(8,128)S(1)}, u32[]{:S(2)}, u32[]{:S(2)}) collective-permute-start(f32[56,8,256]{2,1,0:T(8,128)S(1)} %get-tuple-element.45), channel_id=1, source_target_pairs={{0,15},{1,0},{2,1},{3,2},{4,3},{5,4},{6,5},{7,6},{8,7},{9,8},{10,9... | collective-permute-start | bytes 1376264 | tf_op jit(solution)/shard_map/ppermute | solution.py:781
  37.4 9.8 %collective-permute-start.8 = (f32[16,8,256]{2,1,0:T(8,128)S(1)}, f32[16,8,256]{2,1,0:T(8,128)S(1)}, u32[]{:S(2)}, u32[]{:S(2)}) collective-permute-start(f32[16,8,256]{2,1,0:T(8,128)S(1)} %pad_maximum_fusion), channel_id=1, source_target_pairs={{0,1},{1,2},{2,3},{3,4},{4,5},{5,6},{6,7},{7,8},{8,9},{9,10},{10,1... | collective-permute-start | bytes 393224 | tf_op jit(solution)/shard_map/ppermute | solution.py:781
  37.5 9.7 %collective-permute-start.9 = (f32[16,8,256]{2,1,0:T(8,128)S(1)}, f32[16,8,256]{2,1,0:T(8,128)S(1)}, u32[]{:S(2)}, u32[]{:S(2)}) collective-permute-start(f32[16,8,256]{2,1,0:T(8,128)S(1)} %pad_maximum_fusion.1), channel_id=1, source_target_pairs={{0,15},{1,0},{2,1},{3,2},{4,3},{5,4},{6,5},{7,6},{8,7},{9,8},{10,9... | collective-permute-start | bytes 393224 | tf_op jit(solution)/shard_map/ppermute | solution.py:781
